TPU v7x, 32 devices: a whole 2x2x4 slice. The times are simulated.
32 devices in a mesh: expert: 16 (over z, y, x), dp: 2 (over core).
Axes of the slice: x: 2, y: 2, z: 4, core: 2. Of those that a mesh axis runs over, the one named last changes fastest.
Arguments:
- tokens: bfloat16 [512, 3584], P(('dp', 'expert')), parts along dimension 0, may hold values from -6 to 6
- expert_ids: int32 [512, 2], P(('dp', 'expert')), parts along dimension 0, may hold values from 0 to 2, as said below
- gate_weights: float32 [512, 2], P(('dp', 'expert')), parts along dimension 0, may hold values from 0.1 to 1
- replica_pick: int32 [512, 2], P(('dp', 'expert')), parts along dimension 0, may hold values from 0 to 1
- placement: int32 [4], replicated, may hold values from 0 to 2, as said below
- w_in: bfloat16 [2, 3584, 4096], P(None, None, 'expert')
- w_out: bfloat16 [4096, 3584], P('expert')
Outputs:
- moe_out: bfloat16 [512, 3584], P(('dp', 'expert')), parts along dimension 0
There are 2 independent parts, one for each index of `dp`. A program takes and returns all parts, laid end to end along the dimension named above; an argument that names none is the same for every part. Nothing has to cross between parts.
Inputs may be any that keep to these rules, and one draw needn't show every extreme that they name: `expert_ids`: each row names 2 different experts. `placement`: every expert is named once or twice, 1 of them twice, at any positions.
All inputs are finite; a program needn't handle non-finite values.
Results may differ from a plain program's by a relative error of at most 0.012.
Values may be sent and summed in bfloat16 or wider, within the bound.
No kernel may reach another device: no remote copies, remote signals or barrier semaphores. Data moves between devices by JAX's collectives and lax.ppermute only.
A program may use at most 64 MiB of HBM per device.

v0:
```python
import jax
import jax.numpy as jnp
from jax import lax
from jax.sharding import PartitionSpec as P


def route_block(expert_ids, replica_pick, gate_weights, placement, slot_count, capacity):
    tok_count, top_count = expert_ids.shape
    copy_index = jnp.arange(slot_count, dtype=jnp.int32)
    same_expert = placement[:, None] == placement[None, :]
    before = jnp.sum(
        (same_expert & (copy_index[:, None] < copy_index[None, :])).astype(jnp.int32), axis=0
    )
    matches = placement[None, None, :] == expert_ids[:, :, None]
    copies = jnp.sum(matches.astype(jnp.int32), axis=-1)
    wanted = replica_pick % copies
    chosen = (matches & (before[None, None, :] == wanted[:, :, None])).astype(jnp.int32)
    flat_hot = chosen.reshape(tok_count * top_count, slot_count)
    earlier = jnp.cumsum(flat_hot, axis=0) - flat_hot
    slot_rank = jnp.sum(earlier * flat_hot, axis=-1).reshape(tok_count, top_count)
    slot_index = jnp.arange(capacity, dtype=jnp.int32)
    in_slot = chosen[:, :, :, None] * (
        slot_rank[:, :, None, None] == slot_index[None, None, None, :]
    ).astype(jnp.int32)
    in_slot = in_slot.astype(jnp.float32)
    pick_rows = jnp.sum(in_slot, axis=1).reshape(tok_count, slot_count * capacity).T
    combine_rows = jnp.sum(in_slot * gate_weights[:, :, None, None], axis=1).reshape(
        tok_count, slot_count * capacity
    )
    return (pick_rows, combine_rows)


def body(tokens, expert_ids, gate_weights, replica_pick, placement, w_in, w_out):
    n_devices = lax.axis_size("expert")
    group_size = min(8, n_devices // 4)
    slot_count = n_devices // group_size
    tok_count, model_width = tokens.shape
    capacity = tok_count * expert_ids.shape[1] // slot_count
    pick_rows, combine_rows = route_block(
        expert_ids, replica_pick, gate_weights, placement, slot_count, capacity
    )
    slot_rows = jnp.dot(
        pick_rows.astype(jnp.bfloat16), tokens, preferred_element_type=jnp.float32
    ).astype(jnp.bfloat16)
    slot_rows = slot_rows.reshape(slot_count, capacity, model_width)
    send_rows = jnp.broadcast_to(
        slot_rows[:, None], (slot_count, group_size, capacity, model_width)
    )
    send_rows = send_rows.reshape(n_devices, capacity, model_width)
    received = lax.all_to_all(send_rows, "expert", split_axis=0, concat_axis=0, tiled=True)
    senders, items, _ = received.shape
    flat_rows = received.reshape(senders * items, model_width)
    gate_up = jnp.einsum("rd,gdf->grf", flat_rows, w_in, preferred_element_type=jnp.float32)
    hidden = (jax.nn.silu(gate_up[0]) * gate_up[1]).astype(jnp.bfloat16)
    partial_value = jnp.dot(hidden, w_out, preferred_element_type=jnp.float32).astype(jnp.bfloat16)
    partial_value = partial_value.reshape(senders, items, model_width)
    returned = lax.all_to_all(partial_value, "expert", split_axis=0, concat_axis=0, tiled=True)
    expert_out = jnp.sum(
        returned.reshape(slot_count, group_size, capacity, model_width).astype(jnp.float32), axis=1
    )
    expert_out = expert_out.reshape(slot_count * capacity, model_width)
    moe_out = jnp.dot(
        combine_rows,
        expert_out,
        precision=lax.Precision.HIGHEST,
        preferred_element_type=jnp.float32,
    )
    return moe_out.astype(jnp.bfloat16)


def solution(mesh):
    in_specs = (
        P(("dp", "expert"), None),
        P(("dp", "expert"), None),
        P(("dp", "expert"), None),
        P(("dp", "expert"), None),
        P(),
        P(None, None, "expert"),
        P("expert", None),
    )
    out_specs = P(("dp", "expert"), None)
    return jax.shard_map(body, mesh=mesh, in_specs=in_specs, out_specs=out_specs, check_vma=False)
```

profile of v0, /device:TPU:0, one launch (start us, length us, event | category | flops | bytes accessed | tf_op | source)
XLA Modules:
  0.0 70.7 jit_solution(18397603467199936629)
XLA Ops:
  0.0 0.0 copy-start
  0.0 0.9 %convert_reduce_fusion.2 = s32[4]{0:T(128)S(1)} fusion(s32[4]{0:T(128)} %param.11), kind=kLoop, calls=%fused_computation.28 | loop fusion | flops 76 | bytes 32 | tf_op jit(solution)/shard_map/reduce_sum | solution.py:11
  0.9 0.8 %fusion.12 = s32[16,2]{0,1:T(2,128)S(1)} fusion(s32[16,2]{0,1:T(2,128)} %param.8, s32[4]{0:T(128)} %param.11), kind=kLoop, calls=%fused_computation.25 | loop fusion | flops 352 | bytes 272 | tf_op jit(solution)/shard_map/reduce_sum | solution.py:15
  1.7 0.8 %copy.18 = s32[16,2]{1,0:T(8,128)S(1)} copy(s32[16,2]{0,1:T(2,128)} %param.8) | data formatting | bytes 256 | tf_op args[1]
  2.4 0.8 %and_select_fusion = s32[16,2]{0,1:T(2,128)S(1)} fusion(s32[16,2]{0,1:T(2,128)} %param.10, s32[16,2]{0,1:T(2,128)S(1)} %fusion.12), kind=kLoop, calls=%fused_computation.31 | loop fusion | flops 320 | bytes 384 | tf_op jit(solution)/shard_map/jit(remainder)/select_n | solution.py:16
  3.2 0.1 copy.19
  3.3 0.8 %fusion.13 = s32[16,2,4]{0,2,1:T(4,128)S(1)} fusion(s32[16,2]{0,1:T(2,128)S(1)} %and_select_fusion, s32[16,2]{0,1:T(2,128)} %param.8, s32[4]{0:T(128)S(1)} %convert_reduce_fusion.2, s32[4]{0:T(128)} %param.11), kind=kLoop, calls=%fused_computation.26 | loop fusion | flops 512 | bytes 800 | tf_op jit(solution)/shard_map/convert_element_type | solution.py:17
  4.1 0.1 eq.104
  4.1 0.1 eq.100
  4.2 0.7 %fusion.8 = s32[32,4]{1,0:T(8,128)S(1)} fusion(s32[4]{0:T(128)S(1)} %convert_reduce_fusion.2, s32[4]{0:T(128)} %param.11, s32[32]{0:T(128)S(1)} %eq.104, s32[32]{0:T(128)S(1)} %eq.100), kind=kLoop, calls=%fused_computation.18 | loop fusion | flops 512 | bytes 800 | tf_op jit(solution)/shard_map/convert_element_type | solution.py:17
  5.0 0.1 reduce_window_sum.11
  5.0 0.8 %select_reduce_fusion = s32[32]{0:T(128)S(1)} fusion(s32[32,4]{1,0:T(8,128)S(1)} %reduce_window_sum.11, s32[4]{0:T(128)S(1)} %convert_reduce_fusion.2, s32[4]{0:T(128)} %param.11, s32[32]{0:T(128)S(1)} %eq.104, s32[32]{0:T(128)S(1)} %eq.100), kind=kLoop, calls=%fused_computation.16 | loop fusion | flops 864 | bytes 928 | tf_op jit(solution)/shard_map/reduce_sum | solution.py:20
  5.9 0.1 eq.107
  5.9 0.1 copy.20
  6.0 0.7 %convert_reduce_fusion.1 = (bf16[16,4,8]{0,2,1:T(8,128)(2,1)S(1)}, f32[16,4,8]{0,2,1:T(8,128)S(1)}) fusion(s32[16,2,8]{0,2,1:T(8,128)S(1)} %fusion.11, s32[16,2,4]{0,2,1:T(4,128)S(1)} %fusion.13, f32[16,2]{0,1:T(2,128)} %param.9), kind=kLoop, calls=%fused_computation.15 | loop fusion | flops 4096 | bytes 4736 | tf_op jit(solution)/shard_map/reduce_sum | solution.py:26
  6.8 1.1 %fusion.1 = bf16[4,8,3584]{2,1,0:T(8,128)(2,1)S(1)} fusion(bf16[16,3584]{1,0:T(8,128)(2,1)} %param.7, bf16[16,4,8]{0,2,1:T(8,128)(2,1)S(1)} %get-tuple-element.5), kind=kOutput, calls=%fused_computation.3 | convolution fusion | flops 3784704 | bytes 345088 | tf_op jit(solution)/shard_map/dot_general | solution.py:42
  7.8 0.1 broadcast_in_dim.10
  7.9 31.9 %all_to_all.10 = bf16[16,8,3584]{2,1,0:T(8,128)(2,1)S(1)} all-to-all(bf16[16,8,3584]{2,1,0:T(8,128)(2,1)S(1)} %bitcast.39), channel_id=1, replica_groups=mesh['expert'=16,'dp'=2] {'expert'}, dimensions={0} | all-to-all | bytes 1835008 | tf_op jit(solution)/shard_map/all_to_all | solution.py:50
  39.8 2.7 %convolution_bitcast_fusion.1 = f32[2,128,256]{2,1,0:T(8,128)S(1)} fusion(bf16[2,3584,256]{2,1,0:T(8,128)(2,1)} %param.12, bf16[16,8,3584]{2,1,0:T(8,128)(2,1)S(1)} %all_to_all.10), kind=kOutput, calls=%fused_computation.7 | convolution fusion | flops 469762048 | bytes 4849664 | tf_op jit(solution)/shard_map/rd,gdf->grf/dot_general | solution.py:53
  42.5 0.0 copy-done
  42.5 0.4 fusion
  43.0 26.5 %all_to_all.11 = bf16[16,8,3584]{2,1,0:T(8,128)(2,1)S(1)} all-to-all(bf16[16,8,3584]{2,1,0:T(8,128)(2,1)S(1)} %fusion), channel_id=1, replica_groups=mesh['expert'=16,'dp'=2] {'expert'}, dimensions={0} | all-to-all | bytes 1835008 | tf_op jit(solution)/shard_map/all_to_all | solution.py:57
  69.5 0.1 convert_reduce_fusion
  69.7 1.0 %fusion.2 = bf16[16,3584]{1,0:T(8,128)(2,1)} fusion(f32[16,4,8]{0,2,1:T(8,128)S(1)} %get-tuple-element.6, f32[4,8,3584]{2,1,0:T(8,128)S(1)} %convert_reduce_fusion), kind=kOutput, calls=%fused_computation.5 | convolution fusion | flops 22077440 | bytes 575488 | tf_op jit(solution)/shard_map/dot_general | solution.py:62
  (1 shorter events, 0.0 us)
Async XLA Ops:
  0.0 42.5 %copy-start = (bf16[256,3584]{1,0:T(8,128)(2,1)S(1)}, bf16[256,3584]{1,0:T(8,128)(2,1)}, u32[]{:S(2)}) copy-start(bf16[256,3584]{1,0:T(8,128)(2,1)} %param.13) | copy-start | bytes 5505028
where the time goes:
time: 71.1 us; the launch traced here: 70.7 us
  blocking collectives  58.5 us (82%)
  other arithmetic  5.68 us (8%)
  matrix products  5.23 us (7%)
  local copies, waits for them, and re-layouts  1.25 us (2%)
    all_to_all x1, blocking collectives, body(): lax.all_to_all(send_rows, 'expert', split_axis=0, concat_axis=0, tiled=True)  31.9 us
    all_to_all x1, blocking collectives, body(): lax.all_to_all(partial_value, 'expert', split_axis=0, concat_axis=0, tile...  26.5 us
    dot_general x1, matrix products, body(): jnp.einsum('rd,gdf->grf', flat_rows, w_in, preferred_element_type=jnp.flo...  2.68 us
    convert_element_type x2, other arithmetic, route_block(): (matches & (before[None, None, :] == wanted[:, :, None])).astype(jnp.int32)  1.48 us

commit v1 on v0

v1 whole, which is shorter than its diff:
```python
import functools

import jax
import jax.numpy as jnp
from jax import lax
from jax.experimental import pallas as pl
from jax.experimental.pallas import tpu as pltpu
from jax.sharding import PartitionSpec as P

VMEM = pl.BlockSpec(memory_space=pltpu.VMEM)
SMEM = pl.BlockSpec(memory_space=pltpu.SMEM)
MIB = 1 << 20


def iota(shape, axis):
    return lax.broadcasted_iota(jnp.int32, shape, axis)


def route_kernel(group_size, placement, expert_ids, replica_pick, gate_weights, tokens, *outs):
    row_outs, combine_out = outs[:-1], outs[-1]
    slot_count, capacity = len(row_outs), row_outs[0].shape[0]
    top_count, tok_count = expert_ids.shape
    own = lax.axis_index("expert") // group_size
    copy_row = iota((slot_count, tok_count), 0)
    named = jnp.zeros_like(copy_row)
    before = jnp.zeros_like(copy_row)
    relative = jnp.zeros_like(copy_row)
    for p in range(slot_count):
        here = copy_row == p
        named = jnp.where(here, placement[p], named)
        relative = jnp.where(here, lax.bitwise_xor(own, p), relative)
        seen = jnp.int32(0)
        for q in range(p):
            seen = seen + (placement[q] == placement[p]).astype(jnp.int32)
        before = jnp.where(here, seen, before)
    chosen = []
    for k in range(top_count):
        matches = named == expert_ids[pl.ds(k, 1), :]
        copies = jnp.sum(matches.astype(jnp.int32), axis=0, keepdims=True)
        pick = replica_pick[pl.ds(k, 1), :]
        wanted = jnp.where(pick >= copies, pick - copies, pick)
        chosen.append((matches & (before == wanted)).astype(jnp.int32))
    total = sum(chosen[1:], chosen[0])
    ahead = (iota((tok_count, tok_count), 0) < iota((tok_count, tok_count), 1)).astype(jnp.bfloat16)
    earlier = jnp.dot(
        total.astype(jnp.bfloat16), ahead, preferred_element_type=jnp.float32
    ).astype(jnp.int32)
    slot_row = iota((slot_count * capacity, tok_count), 0)
    pick_rows = jnp.zeros((slot_count * capacity, tok_count), jnp.float32)
    combine = jnp.zeros((slot_count * capacity, tok_count), jnp.float32)
    for k in range(top_count):
        rank = jnp.sum(chosen[k] * earlier, axis=0, keepdims=True)
        place = jnp.sum(chosen[k] * relative, axis=0, keepdims=True)
        slot = jnp.where(rank < capacity, place * capacity + rank, -1)
        hot = slot_row == slot
        pick_rows = pick_rows + hot.astype(jnp.float32)
        combine = combine + jnp.where(hot, gate_weights[pl.ds(k, 1), :], 0.0)
        earlier = earlier + chosen[k]
    combine_out[...] = combine
    rows = jnp.dot(pick_rows.astype(jnp.bfloat16), tokens[...], preferred_element_type=jnp.float32)
    for d in range(slot_count):
        row_outs[d][...] = rows[d * capacity : (d + 1) * capacity].astype(jnp.bfloat16)


def expert_kernel(count, group_size, *refs):
    chunks, (w_in, w_out), outs = refs[:count], refs[count : count + 2], refs[count + 2 :]
    rows = jnp.concatenate([c[...].astype(jnp.float32) for c in chunks], axis=0)
    rows = rows.astype(jnp.bfloat16)
    gate = jnp.dot(rows, w_in[0], preferred_element_type=jnp.float32)
    upper = jnp.dot(rows, w_in[1], preferred_element_type=jnp.float32)
    hidden = (gate / (1.0 + jnp.exp(-gate)) * upper).astype(jnp.bfloat16)
    partial_value = jnp.dot(hidden, w_out[...], preferred_element_type=jnp.float32)
    each = partial_value.shape[0] // group_size
    for q in range(group_size):
        outs[q][...] = partial_value[q * each : (q + 1) * each].astype(jnp.bfloat16)


def reduce_kernel(count, *refs):
    total = refs[0][...].astype(jnp.float32)
    for r in refs[1:count]:
        total = total + r[...].astype(jnp.float32)
    capacity = refs[count].shape[0]
    for d, out in enumerate(refs[count:]):
        out[...] = total[d * capacity : (d + 1) * capacity].astype(jnp.bfloat16)


def combine_kernel(combine, *refs):
    parts, out = refs[:-1], refs[-1]
    values = jnp.concatenate([p[...].astype(jnp.float32) for p in parts], axis=0)
    out[...] = lax.dot_general(
        combine[...],
        values,
        (((0,), (0,)), ((), ())),
        precision=lax.Precision.HIGHEST,
        preferred_element_type=jnp.float32,
    ).astype(jnp.bfloat16)


def call(kernel, inputs, in_specs, outs, limit):
    return pl.pallas_call(
        kernel,
        out_shape=outs,
        in_specs=in_specs,
        out_specs=jax.tree.map(lambda _: VMEM, outs),
        compiler_params=pltpu.CompilerParams(vmem_limit_bytes=limit),
    )(*inputs)


def body(tokens, expert_ids, gate_weights, replica_pick, placement, w_in, w_out):
    n_devices = lax.axis_size("expert")
    group_size = min(8, n_devices // 4)
    slot_count = n_devices // group_size
    tok_count, width = tokens.shape
    capacity = tok_count * expert_ids.shape[1] // slot_count
    chunk = jax.ShapeDtypeStruct((capacity, width), jnp.bfloat16)

    def swap(value, offset):
        return lax.ppermute(value, "expert", [(e, e ^ offset) for e in range(n_devices)])

    *slot_rows, combine = call(
        functools.partial(route_kernel, group_size),
        (placement, expert_ids.T, replica_pick.T, gate_weights.T, tokens),
        [SMEM] + [VMEM] * 4,
        [chunk] * slot_count
        + [jax.ShapeDtypeStruct((slot_count * capacity, tok_count), jnp.float32)],
        16 * MIB,
    )
    held = {}
    for d in range(slot_count):
        held[0, d] = slot_rows[0] if d == 0 else swap(slot_rows[d], d * group_size)
    for d in range(slot_count):
        for q in range(1, group_size):
            held[q, d] = swap(held[0, d], q)
    order = [(q, d) for q in range(group_size) for d in range(slot_count)]
    partial_value = call(
        functools.partial(expert_kernel, n_devices, group_size),
        [held[i] for i in order] + [w_in, w_out],
        [VMEM] * (n_devices + 2),
        [jax.ShapeDtypeStruct((slot_count * capacity, width), jnp.bfloat16)] * group_size,
        40 * MIB,
    )
    partial_value = [v if q == 0 else swap(v, q) for q, v in enumerate(partial_value)]
    summed = call(
        functools.partial(reduce_kernel, group_size),
        partial_value,
        [VMEM] * group_size,
        [chunk] * slot_count,
        16 * MIB,
    )
    returned = [v if d == 0 else swap(v, d * group_size) for d, v in enumerate(summed)]
    return call(
        combine_kernel,
        [combine] + returned,
        [VMEM] * (slot_count + 1),
        jax.ShapeDtypeStruct((tok_count, width), jnp.bfloat16),
        16 * MIB,
    )


def solution(mesh):
    in_specs = (
        P(("dp", "expert"), None),
        P(("dp", "expert"), None),
        P(("dp", "expert"), None),
        P(("dp", "expert"), None),
        P(),
        P(None, None, "expert"),
        P("expert", None),
    )
    out_specs = P(("dp", "expert"), None)
    return jax.shard_map(body, mesh=mesh, in_specs=in_specs, out_specs=out_specs, check_vma=False)
```

time: 71.1 us -> 54 us (0.76)
  blocking collectives: 58.5 us -> 0 us
  starting transfers between devices: 0 us -> 29.4 us
  waiting for transfers between devices: 0 us -> 14.1 us
  local copies, waits for them, and re-layouts: 1.25 us -> 7.13 us
  other arithmetic: 5.68 us -> 0 us
  matrix products: 5.23 us -> 0 us
  Pallas kernels: 0 us -> 3.11 us
    all_to_all x2 -> x0, blocking collectives: 58.5 us -> none  [the longest x1 31.9 us: body(): lax.all_to_all(send_rows, 'expert', split_axis=0, concat_axis=0, tiled=True)]
    ppermute x0 -> x21, starting transfers between devices: none -> 29.4 us  [swap(): lax.ppermute(value, 'expert', [(e, e ^ offset) for e in range(n_devices)])]
    ppermute x0 -> x21, waiting for transfers between devices: none -> 14.1 us  [swap(): lax.ppermute(value, 'expert', [(e, e ^ offset) for e in range(n_devices)])]
    unnamed x3 -> x14, local copies, waits for them, and re-layouts: 0.76 us -> 7.13 us
    dot_general x4 -> x0, matrix products: 5.23 us -> none  [the longest x1 2.68 us: body(): jnp.einsum('rd,gdf->grf', flat_rows, w_in, preferred_element_type=jnp.flo...]
    reduce_sum x5 -> x0, other arithmetic: 3.34 us -> none  [the longest x1 0.89 us: route_block(): jnp.sum((same_expert & (copy_index[:, None] < copy_index[None, :])).astyp...]
    pallas_call x0 -> x4, Pallas kernels: none -> 3.11 us  [call(): pl.pallas_call(kernel, out_shape=outs, in_specs=in_specs, out_specs=jax.t...]
    convert_element_type x3 -> x0, other arithmetic: 1.49 us -> none  [the longest x2 1.48 us: route_block(): (matches & (before[None, None, :] == wanted[:, :, None])).astype(jnp.int32)]
  transfers between devices with their start and end apart: 0 -> 21, of which waited for: 0 -> 9; matrix products, arithmetic and copies ran while one was open for 0% -> 0% of each run, Pallas kernels for 0% -> 0%
where the time goes in v1:
time: 54 us; the launch traced here: 53.8 us
  starting transfers between devices  29.4 us (54%)
  waiting for transfers between devices  14.1 us (26%)
  local copies, waits for them, and re-layouts  7.13 us (13%)
  Pallas kernels  3.11 us (6%)
    ppermute x21, starting transfers between devices, swap(): lax.ppermute(value, 'expert', [(e, e ^ offset) for e in range(n_devices)])  29.4 us
    ppermute x21, waiting for transfers between devices, swap(): lax.ppermute(value, 'expert', [(e, e ^ offset) for e in range(n_devices)])  14.1 us
    unnamed x14, local copies, waits for them, and re-layouts  7.13 us
    pallas_call x4, Pallas kernels, call(): pl.pallas_call(kernel, out_shape=outs, in_specs=in_specs, out_specs=jax.t...  3.11 us
  transfers between devices with their start and end apart: 21, of which 9 were waited for; matrix products, arithmetic and copies ran while one was open for 0% of the time, Pallas kernels for 0%

profile of v1, /device:TPU:0, one launch (start us, length us, event | category | flops | bytes accessed | tf_op | source)
XLA Modules:
  0.0 53.8 jit_solution(15782334834521969726)
XLA Ops:
  0.0 0.9 %copy-done.2 = bf16[16,3584]{1,0:T(8,128)(2,1)S(1)} copy-done((bf16[16,3584]{1,0:T(8,128)(2,1)S(1)}, bf16[16,3584]{1,0:T(8,128)(2,1)}, u32[]{:S(2)}) %copy-start.2) | copy-done | bytes 114712
  0.9 0.7 %copy-done.3 = s32[16,2]{0,1:T(2,128)S(1)} copy-done((s32[16,2]{0,1:T(2,128)S(1)}, s32[16,2]{0,1:T(2,128)}, u32[]{:S(2)}) %copy-start.3) | copy-done | bytes 152
  1.6 0.7 %copy-done.4 = s32[16,2]{0,1:T(2,128)S(1)} copy-done((s32[16,2]{0,1:T(2,128)S(1)}, s32[16,2]{0,1:T(2,128)}, u32[]{:S(2)}) %copy-start.4) | copy-done | bytes 152
  2.3 0.7 %copy-done.5 = f32[16,2]{0,1:T(2,128)S(1)} copy-done((f32[16,2]{0,1:T(2,128)S(1)}, f32[16,2]{0,1:T(2,128)}, u32[]{:S(2)}) %copy-start.5) | copy-done | bytes 152
  2.9 0.7 %copy-done.6 = s32[4]{0:T(128)S(1)} copy-done((s32[4]{0:T(128)S(1)}, s32[4]{0:T(128)}, u32[]{:S(2)}) %copy-start.6) | copy-done | bytes 40
  3.6 0.9 %shard_map.73 = (bf16[8,3584]{1,0:T(8,128)(2,1)S(1)}, bf16[8,3584]{1,0:T(8,128)(2,1)S(1)}, bf16[8,3584]{1,0:T(8,128)(2,1)S(1)}, bf16[8,3584]{1,0:T(8,128)(2,1)S(1)}, f32[32,16]{1,0:T(8,128)S(1)}) custom-call(s32[4]{0:T(128)S(1)} %copy-done.6, s32[2,16]{1,0:T(2,128)S(1)} %bitcast.3, s32[2,16]{1,0:T(2,128)S(1)} %bitcast.4, f32[2,16]{1,0:T(2,128)S(1)} %bitcast.5, ...), custom_call_target="tpu_custom_call" | custom-call | tf_op jit(solution)/shard_map/pallas_call | solution.py:100
  4.5 3.1 %collective-permute-start = (bf16[8,3584]{1,0:T(8,128)(2,1)S(1)}, bf16[8,3584]{1,0:T(8,128)(2,1)S(1)}, u32[]{:S(2)}, u32[]{:S(2)}) collective-permute-start(bf16[8,3584]{1,0:T(8,128)(2,1)S(1)} %get-tuple-element.20), channel_id=1, source_target_pairs={{0,8},{2,10},{4,12},{6,14},{8,0},{10,2},{12,4},{14,6},{16,24},{18,... | collective-permute-start | bytes 172040 | tf_op jit(solution)/shard_map/ppermute | solution.py:118
  7.6 2.6 %collective-permute-start.1 = (bf16[8,3584]{1,0:T(8,128)(2,1)S(1)}, bf16[8,3584]{1,0:T(8,128)(2,1)S(1)}, u32[]{:S(2)}, u32[]{:S(2)}) collective-permute-start(bf16[8,3584]{1,0:T(8,128)(2,1)S(1)} %get-tuple-element.21), channel_id=1, source_target_pairs={{0,16},{2,18},{4,20},{6,22},{8,24},{10,26},{12,28},{14,30},{16,0},... | collective-permute-start | bytes 172040 | tf_op jit(solution)/shard_map/ppermute | solution.py:118
  10.2 2.7 %collective-permute-start.11 = (bf16[8,3584]{1,0:T(8,128)(2,1)S(1)}, bf16[8,3584]{1,0:T(8,128)(2,1)S(1)}, u32[]{:S(2)}, u32[]{:S(2)}) collective-permute-start(bf16[8,3584]{1,0:T(8,128)(2,1)S(1)} %get-tuple-element.19.refs_0_), channel_id=1, source_target_pairs={{0,6},{2,4},{4,2},{6,0},{8,14},{10,12},{12,10},{14,8},{16,22},{18,... | collective-permute-start | bytes 172040 | tf_op jit(solution)/shard_map/ppermute | solution.py:118
  13.8 2.6 %collective-permute-start.12 = (bf16[8,3584]{1,0:T(8,128)(2,1)S(1)}, bf16[8,3584]{1,0:T(8,128)(2,1)S(1)}, u32[]{:S(2)}, u32[]{:S(2)}) collective-permute-start(bf16[8,3584]{1,0:T(8,128)(2,1)S(1)} %collective-permute-done.refs_1_), channel_id=1, source_target_pairs={{0,6},{2,4},{4,2},{6,0},{8,14},{10,12},{12,10},{14,8},{16,22},{18,... | collective-permute-start | bytes 172040 | tf_op jit(solution)/shard_map/ppermute | solution.py:118
  16.3 1.3 %collective-permute-start.8 = (bf16[8,3584]{1,0:T(8,128)(2,1)S(1)}, bf16[8,3584]{1,0:T(8,128)(2,1)S(1)}, u32[]{:S(2)}, u32[]{:S(2)}) collective-permute-start(bf16[8,3584]{1,0:T(8,128)(2,1)S(1)} %collective-permute-done.refs_1_), channel_id=1, source_target_pairs={{0,4},{2,6},{4,0},{6,2},{8,12},{10,14},{12,8},{14,10},{16,20},{18,... | collective-permute-start | bytes 172040 | tf_op jit(solution)/shard_map/ppermute | solution.py:118
  17.6 1.5 %collective-permute-start.4 = (bf16[8,3584]{1,0:T(8,128)(2,1)S(1)}, bf16[8,3584]{1,0:T(8,128)(2,1)S(1)}, u32[]{:S(2)}, u32[]{:S(2)}) collective-permute-start(bf16[8,3584]{1,0:T(8,128)(2,1)S(1)} %collective-permute-done.refs_1_), channel_id=1, source_target_pairs={{0,2},{2,0},{4,6},{6,4},{8,10},{10,8},{12,14},{14,12},{16,18},{18,... | collective-permute-start | bytes 172040 | tf_op jit(solution)/shard_map/ppermute | solution.py:118
  19.1 0.7 %collective-permute-start.13 = (bf16[8,3584]{1,0:T(8,128)(2,1)S(1)}, bf16[8,3584]{1,0:T(8,128)(2,1)S(1)}, u32[]{:S(2)}, u32[]{:S(2)}) collective-permute-start(bf16[8,3584]{1,0:T(8,128)(2,1)S(1)} %collective-permute-done.1.refs_2_), channel_id=1, source_target_pairs={{0,6},{2,4},{4,2},{6,0},{8,14},{10,12},{12,10},{14,8},{16,22},{18,... | collective-permute-start | bytes 172040 | tf_op jit(solution)/shard_map/ppermute | solution.py:118
  19.8 1.3 %collective-permute-start.9 = (bf16[8,3584]{1,0:T(8,128)(2,1)S(1)}, bf16[8,3584]{1,0:T(8,128)(2,1)S(1)}, u32[]{:S(2)}, u32[]{:S(2)}) collective-permute-start(bf16[8,3584]{1,0:T(8,128)(2,1)S(1)} %collective-permute-done.1.refs_2_), channel_id=1, source_target_pairs={{0,4},{2,6},{4,0},{6,2},{8,12},{10,14},{12,8},{14,10},{16,20},{18,... | collective-permute-start | bytes 172040 | tf_op jit(solution)/shard_map/ppermute | solution.py:118
  21.2 1.5 %collective-permute-start.5 = (bf16[8,3584]{1,0:T(8,128)(2,1)S(1)}, bf16[8,3584]{1,0:T(8,128)(2,1)S(1)}, u32[]{:S(2)}, u32[]{:S(2)}) collective-permute-start(bf16[8,3584]{1,0:T(8,128)(2,1)S(1)} %collective-permute-done.1.refs_2_), channel_id=1, source_target_pairs={{0,2},{2,0},{4,6},{6,4},{8,10},{10,8},{12,14},{14,12},{16,18},{18,... | collective-permute-start | bytes 172040 | tf_op jit(solution)/shard_map/ppermute | solution.py:118
  22.7 1.0 %collective-permute-start.14 = (bf16[8,3584]{1,0:T(8,128)(2,1)S(1)}, bf16[8,3584]{1,0:T(8,128)(2,1)S(1)}, u32[]{:S(2)}, u32[]{:S(2)}) collective-permute-start(bf16[8,3584]{1,0:T(8,128)(2,1)S(1)} %collective-permute-done.2.refs_3_), channel_id=1, source_target_pairs={{0,6},{2,4},{4,2},{6,0},{8,14},{10,12},{12,10},{14,8},{16,22},{18,... | collective-permute-start | bytes 172040 | tf_op jit(solution)/shard_map/ppermute | solution.py:118
  23.7 1.0 %collective-permute-start.10 = (bf16[8,3584]{1,0:T(8,128)(2,1)S(1)}, bf16[8,3584]{1,0:T(8,128)(2,1)S(1)}, u32[]{:S(2)}, u32[]{:S(2)}) collective-permute-start(bf16[8,3584]{1,0:T(8,128)(2,1)S(1)} %collective-permute-done.2.refs_3_), channel_id=1, source_target_pairs={{0,4},{2,6},{4,0},{6,2},{8,12},{10,14},{12,8},{14,10},{16,20},{18,... | collective-permute-start | bytes 172040 | tf_op jit(solution)/shard_map/ppermute | solution.py:118
  24.8 1.4 %collective-permute-start.6 = (bf16[8,3584]{1,0:T(8,128)(2,1)S(1)}, bf16[8,3584]{1,0:T(8,128)(2,1)S(1)}, u32[]{:S(2)}, u32[]{:S(2)}) collective-permute-start(bf16[8,3584]{1,0:T(8,128)(2,1)S(1)} %collective-permute-done.2.refs_3_), channel_id=1, source_target_pairs={{0,2},{2,0},{4,6},{6,4},{8,10},{10,8},{12,14},{14,12},{16,18},{18,... | collective-permute-start | bytes 172040 | tf_op jit(solution)/shard_map/ppermute | solution.py:118
  26.2 1.6 %collective-permute-done.14.refs_15_ = bf16[8,3584]{1,0:T(8,128)(2,1)S(1)} collective-permute-done((bf16[8,3584]{1,0:T(8,128)(2,1)S(1)}, bf16[8,3584]{1,0:T(8,128)(2,1)S(1)}, u32[]{:S(2)}, u32[]{:S(2)}) %collective-permute-start.14) | collective-permute-done | bytes 57376 | tf_op jit(solution)/shard_map/ppermute | solution.py:118
  28.3 0.6 %collective-permute-done.6.refs_7_ = bf16[8,3584]{1,0:T(8,128)(2,1)S(1)} collective-permute-done((bf16[8,3584]{1,0:T(8,128)(2,1)S(1)}, bf16[8,3584]{1,0:T(8,128)(2,1)S(1)}, u32[]{:S(2)}, u32[]{:S(2)}) %collective-permute-start.6) | collective-permute-done | bytes 57376 | tf_op jit(solution)/shard_map/ppermute | solution.py:118
  29.0 2.0 %copy-done = bf16[2,3584,256]{2,1,0:T(8,128)(2,1)S(1)} copy-done((bf16[2,3584,256]{2,1,0:T(8,128)(2,1)S(1)}, bf16[2,3584,256]{2,1,0:T(8,128)(2,1)}, u32[]{:S(2)}) %copy-start) | copy-done | bytes 3670040
  31.0 1.5 %copy-done.1 = bf16[256,3584]{1,0:T(8,128)(2,1)S(1)} copy-done((bf16[256,3584]{1,0:T(8,128)(2,1)S(1)}, bf16[256,3584]{1,0:T(8,128)(2,1)}, u32[]{:S(2)}) %copy-start.1) | copy-done | bytes 1835032
  32.5 1.0 %shard_map.74 = (bf16[32,3584]{1,0:T(8,128)(2,1)S(1)}, bf16[32,3584]{1,0:T(8,128)(2,1)S(1)}, bf16[32,3584]{1,0:T(8,128)(2,1)S(1)}, bf16[32,3584]{1,0:T(8,128)(2,1)S(1)}) custom-call(bf16[8,3584]{1,0:T(8,128)(2,1)S(1)} %get-tuple-element.19.refs_0_, bf16[8,3584]{1,0:T(8,128)(2,1)S(1)} %collective-permute-done.refs_1_, ...), custom_call_target="tpu_custom_call" | custom-call | tf_op jit(solution)/shard_map/pallas_call | solution.py:100
  33.5 1.4 %collective-permute-start.15 = (bf16[32,3584]{1,0:T(8,128)(2,1)S(1)}, bf16[32,3584]{1,0:T(8,128)(2,1)S(1)}, u32[]{:S(2)}, u32[]{:S(2)}) collective-permute-start(bf16[32,3584]{1,0:T(8,128)(2,1)S(1)} %get-tuple-element.24), channel_id=1, source_target_pairs={{0,2},{2,0},{4,6},{6,4},{8,10},{10,8},{12,14},{14,12},{16,18},{18,... | collective-permute-start | bytes 688136 | tf_op jit(solution)/shard_map/ppermute | solution.py:118
  35.5 1.6 %collective-permute-start.17 = (bf16[32,3584]{1,0:T(8,128)(2,1)S(1)}, bf16[32,3584]{1,0:T(8,128)(2,1)S(1)}, u32[]{:S(2)}, u32[]{:S(2)}) collective-permute-start(bf16[32,3584]{1,0:T(8,128)(2,1)S(1)} %get-tuple-element.26), channel_id=1, source_target_pairs={{0,6},{2,4},{4,2},{6,0},{8,14},{10,12},{12,10},{14,8},{16,22},{18,... | collective-permute-start | bytes 688136 | tf_op jit(solution)/shard_map/ppermute | solution.py:118
  37.1 2.5 %collective-permute-done.15.refs_1_ = bf16[32,3584]{1,0:T(8,128)(2,1)S(1)} collective-permute-done((bf16[32,3584]{1,0:T(8,128)(2,1)S(1)}, bf16[32,3584]{1,0:T(8,128)(2,1)S(1)}, u32[]{:S(2)}, u32[]{:S(2)}) %collective-permute-start.15) | collective-permute-done | bytes 229408 | tf_op jit(solution)/shard_map/ppermute | solution.py:118
  39.6 3.8 %collective-permute-done.16.refs_2_ = bf16[32,3584]{1,0:T(8,128)(2,1)S(1)} collective-permute-done((bf16[32,3584]{1,0:T(8,128)(2,1)S(1)}, bf16[32,3584]{1,0:T(8,128)(2,1)S(1)}, u32[]{:S(2)}, u32[]{:S(2)}) %collective-permute-start.16) | collective-permute-done | bytes 229408 | tf_op jit(solution)/shard_map/ppermute | solution.py:118
  43.7 3.0 %collective-permute-start.19 = (bf16[8,3584]{1,0:T(8,128)(2,1)S(1)}, bf16[8,3584]{1,0:T(8,128)(2,1)S(1)}, u32[]{:S(2)}, u32[]{:S(2)}) collective-permute-start(bf16[8,3584]{1,0:T(8,128)(2,1)S(1)} %get-tuple-element.29), channel_id=1, source_target_pairs={{0,16},{2,18},{4,20},{6,22},{8,24},{10,26},{12,28},{14,30},{16,0},... | collective-permute-start | bytes 172040 | tf_op jit(solution)/shard_map/ppermute | solution.py:118
  46.7 1.3 %collective-permute-start.20 = (bf16[8,3584]{1,0:T(8,128)(2,1)S(1)}, bf16[8,3584]{1,0:T(8,128)(2,1)S(1)}, u32[]{:S(2)}, u32[]{:S(2)}) collective-permute-start(bf16[8,3584]{1,0:T(8,128)(2,1)S(1)} %get-tuple-element.30), channel_id=1, source_target_pairs={{0,24},{2,26},{4,28},{6,30},{8,16},{10,18},{12,20},{14,22},{16,8},... | collective-permute-start | bytes 172040 | tf_op jit(solution)/shard_map/ppermute | solution.py:118
  48.0 0.8 %collective-permute-done.19.refs_2_ = bf16[8,3584]{1,0:T(8,128)(2,1)S(1)} collective-permute-done((bf16[8,3584]{1,0:T(8,128)(2,1)S(1)}, bf16[8,3584]{1,0:T(8,128)(2,1)S(1)}, u32[]{:S(2)}, u32[]{:S(2)}) %collective-permute-start.19) | collective-permute-done | bytes 57376 | tf_op jit(solution)/shard_map/ppermute | solution.py:118
  48.9 3.8 %collective-permute-done.20.refs_3_ = bf16[8,3584]{1,0:T(8,128)(2,1)S(1)} collective-permute-done((bf16[8,3584]{1,0:T(8,128)(2,1)S(1)}, bf16[8,3584]{1,0:T(8,128)(2,1)S(1)}, u32[]{:S(2)}, u32[]{:S(2)}) %collective-permute-start.20) | collective-permute-done | bytes 57376 | tf_op jit(solution)/shard_map/ppermute | solution.py:118
  52.7 1.1 %shard_map.76 = bf16[16,3584]{1,0:T(8,128)(2,1)} custom-call(f32[32,16]{1,0:T(8,128)S(1)} %get-tuple-element.18.combine, bf16[8,3584]{1,0:T(8,128)(2,1)S(1)} %get-tuple-element.27.refs_0_, bf16[8,3584]{1,0:T(8,128)(2,1)S(1)} %collective-permute-done.18.refs_1_, bf16[8,3584]{1,0:T(8,128)(2,1)S(1)} %collective-permute-done.19.refs_2_, ...), custom_call_target="tpu_custom_call" | custom-call | tf_op jit(solution)/shard_map/pallas_call | solution.py:100
  (28 shorter events, 2.3 us)
Async XLA Ops:
  0.0 0.9 %copy-start.2 = (bf16[16,3584]{1,0:T(8,128)(2,1)S(1)}, bf16[16,3584]{1,0:T(8,128)(2,1)}, u32[]{:S(2)}) copy-start(bf16[16,3584]{1,0:T(8,128)(2,1)} %tokens.1) | copy-start | bytes 344068
  0.9 0.7 %copy-start.3 = (s32[16,2]{0,1:T(2,128)S(1)}, s32[16,2]{0,1:T(2,128)}, u32[]{:S(2)}) copy-start(s32[16,2]{0,1:T(2,128)} %param.8) | copy-start | bytes 388
  1.6 0.7 %copy-start.4 = (s32[16,2]{0,1:T(2,128)S(1)}, s32[16,2]{0,1:T(2,128)}, u32[]{:S(2)}) copy-start(s32[16,2]{0,1:T(2,128)} %param.10) | copy-start | bytes 388
  2.3 0.7 %copy-start.5 = (f32[16,2]{0,1:T(2,128)S(1)}, f32[16,2]{0,1:T(2,128)}, u32[]{:S(2)}) copy-start(f32[16,2]{0,1:T(2,128)} %param.9) | copy-start | bytes 388
  2.9 0.7 %copy-start.6 = (s32[4]{0:T(128)S(1)}, s32[4]{0:T(128)}, u32[]{:S(2)}) copy-start(s32[4]{0:T(128)} %placement.1) | copy-start | bytes 52
  4.5 8.9 %collective-permute-start = (bf16[8,3584]{1,0:T(8,128)(2,1)S(1)}, bf16[8,3584]{1,0:T(8,128)(2,1)S(1)}, u32[]{:S(2)}, u32[]{:S(2)}) collective-permute-start(bf16[8,3584]{1,0:T(8,128)(2,1)S(1)} %get-tuple-element.20), channel_id=1, source_target_pairs={{0,8},{2,10},{4,12},{6,14},{8,0},{10,2},{12,4},{14,6},{16,24},{18,... | collective-permute-start | bytes 172040 | tf_op jit(solution)/shard_map/ppermute | solution.py:118
  7.6 6.2 %collective-permute-start.1 = (bf16[8,3584]{1,0:T(8,128)(2,1)S(1)}, bf16[8,3584]{1,0:T(8,128)(2,1)S(1)}, u32[]{:S(2)}, u32[]{:S(2)}) collective-permute-start(bf16[8,3584]{1,0:T(8,128)(2,1)S(1)} %get-tuple-element.21), channel_id=1, source_target_pairs={{0,16},{2,18},{4,20},{6,22},{8,24},{10,26},{12,28},{14,30},{16,0},... | collective-permute-start | bytes 172040 | tf_op jit(solution)/shard_map/ppermute | solution.py:118
  10.2 6.2 %collective-permute-start.2 = (bf16[8,3584]{1,0:T(8,128)(2,1)S(1)}, bf16[8,3584]{1,0:T(8,128)(2,1)S(1)}, u32[]{:S(2)}, u32[]{:S(2)}) collective-permute-start(bf16[8,3584]{1,0:T(8,128)(2,1)S(1)} %get-tuple-element.22), channel_id=1, source_target_pairs={{0,24},{2,26},{4,28},{6,30},{8,16},{10,18},{12,20},{14,22},{16,8},... | collective-permute-start | bytes 172040 | tf_op jit(solution)/shard_map/ppermute | solution.py:118
  10.2 7.5 %collective-permute-start.11 = (bf16[8,3584]{1,0:T(8,128)(2,1)S(1)}, bf16[8,3584]{1,0:T(8,128)(2,1)S(1)}, u32[]{:S(2)}, u32[]{:S(2)}) collective-permute-start(bf16[8,3584]{1,0:T(8,128)(2,1)S(1)} %get-tuple-element.19.refs_0_), channel_id=1, source_target_pairs={{0,6},{2,4},{4,2},{6,0},{8,14},{10,12},{12,10},{14,8},{16,22},{18,... | collective-permute-start | bytes 172040 | tf_op jit(solution)/shard_map/ppermute | solution.py:118
  12.8 6.3 %collective-permute-start.7 = (bf16[8,3584]{1,0:T(8,128)(2,1)S(1)}, bf16[8,3584]{1,0:T(8,128)(2,1)S(1)}, u32[]{:S(2)}, u32[]{:S(2)}) collective-permute-start(bf16[8,3584]{1,0:T(8,128)(2,1)S(1)} %get-tuple-element.19.refs_0_), channel_id=1, source_target_pairs={{0,4},{2,6},{4,0},{6,2},{8,12},{10,14},{12,8},{14,10},{16,20},{18,... | collective-permute-start | bytes 172040 | tf_op jit(solution)/shard_map/ppermute | solution.py:118
  13.3 6.5 %collective-permute-start.3 = (bf16[8,3584]{1,0:T(8,128)(2,1)S(1)}, bf16[8,3584]{1,0:T(8,128)(2,1)S(1)}, u32[]{:S(2)}, u32[]{:S(2)}) collective-permute-start(bf16[8,3584]{1,0:T(8,128)(2,1)S(1)} %get-tuple-element.19.refs_0_), channel_id=1, source_target_pairs={{0,2},{2,0},{4,6},{6,4},{8,10},{10,8},{12,14},{14,12},{16,18},{18,... | collective-permute-start | bytes 172040 | tf_op jit(solution)/shard_map/ppermute | solution.py:118
  13.8 7.4 %collective-permute-start.12 = (bf16[8,3584]{1,0:T(8,128)(2,1)S(1)}, bf16[8,3584]{1,0:T(8,128)(2,1)S(1)}, u32[]{:S(2)}, u32[]{:S(2)}) collective-permute-start(bf16[8,3584]{1,0:T(8,128)(2,1)S(1)} %collective-permute-done.refs_1_), channel_id=1, source_target_pairs={{0,6},{2,4},{4,2},{6,0},{8,14},{10,12},{12,10},{14,8},{16,22},{18,... | collective-permute-start | bytes 172040 | tf_op jit(solution)/shard_map/ppermute | solution.py:118
  16.3 6.3 %collective-permute-start.8 = (bf16[8,3584]{1,0:T(8,128)(2,1)S(1)}, bf16[8,3584]{1,0:T(8,128)(2,1)S(1)}, u32[]{:S(2)}, u32[]{:S(2)}) collective-permute-start(bf16[8,3584]{1,0:T(8,128)(2,1)S(1)} %collective-permute-done.refs_1_), channel_id=1, source_target_pairs={{0,4},{2,6},{4,0},{6,2},{8,12},{10,14},{12,8},{14,10},{16,20},{18,... | collective-permute-start | bytes 172040 | tf_op jit(solution)/shard_map/ppermute | solution.py:118
  17.6 6.0 %collective-permute-start.4 = (bf16[8,3584]{1,0:T(8,128)(2,1)S(1)}, bf16[8,3584]{1,0:T(8,128)(2,1)S(1)}, u32[]{:S(2)}, u32[]{:S(2)}) collective-permute-start(bf16[8,3584]{1,0:T(8,128)(2,1)S(1)} %collective-permute-done.refs_1_), channel_id=1, source_target_pairs={{0,2},{2,0},{4,6},{6,4},{8,10},{10,8},{12,14},{14,12},{16,18},{18,... | collective-permute-start | bytes 172040 | tf_op jit(solution)/shard_map/ppermute | solution.py:118
  19.1 5.6 %collective-permute-start.13 = (bf16[8,3584]{1,0:T(8,128)(2,1)S(1)}, bf16[8,3584]{1,0:T(8,128)(2,1)S(1)}, u32[]{:S(2)}, u32[]{:S(2)}) collective-permute-start(bf16[8,3584]{1,0:T(8,128)(2,1)S(1)} %collective-permute-done.1.refs_2_), channel_id=1, source_target_pairs={{0,6},{2,4},{4,2},{6,0},{8,14},{10,12},{12,10},{14,8},{16,22},{18,... | collective-permute-start | bytes 172040 | tf_op jit(solution)/shard_map/ppermute | solution.py:118
  19.8 6.3 %collective-permute-start.9 = (bf16[8,3584]{1,0:T(8,128)(2,1)S(1)}, bf16[8,3584]{1,0:T(8,128)(2,1)S(1)}, u32[]{:S(2)}, u32[]{:S(2)}) collective-permute-start(bf16[8,3584]{1,0:T(8,128)(2,1)S(1)} %collective-permute-done.1.refs_2_), channel_id=1, source_target_pairs={{0,4},{2,6},{4,0},{6,2},{8,12},{10,14},{12,8},{14,10},{16,20},{18,... | collective-permute-start | bytes 172040 | tf_op jit(solution)/shard_map/ppermute | solution.py:118
  21.2 5.0 %collective-permute-start.5 = (bf16[8,3584]{1,0:T(8,128)(2,1)S(1)}, bf16[8,3584]{1,0:T(8,128)(2,1)S(1)}, u32[]{:S(2)}, u32[]{:S(2)}) collective-permute-start(bf16[8,3584]{1,0:T(8,128)(2,1)S(1)} %collective-permute-done.1.refs_2_), channel_id=1, source_target_pairs={{0,2},{2,0},{4,6},{6,4},{8,10},{10,8},{12,14},{14,12},{16,18},{18,... | collective-permute-start | bytes 172040 | tf_op jit(solution)/shard_map/ppermute | solution.py:118
  22.7 5.1 %collective-permute-start.14 = (bf16[8,3584]{1,0:T(8,128)(2,1)S(1)}, bf16[8,3584]{1,0:T(8,128)(2,1)S(1)}, u32[]{:S(2)}, u32[]{:S(2)}) collective-permute-start(bf16[8,3584]{1,0:T(8,128)(2,1)S(1)} %collective-permute-done.2.refs_3_), channel_id=1, source_target_pairs={{0,6},{2,4},{4,2},{6,0},{8,14},{10,12},{12,10},{14,8},{16,22},{18,... | collective-permute-start | bytes 172040 | tf_op jit(solution)/shard_map/ppermute | solution.py:118
  23.7 4.7 %collective-permute-start.10 = (bf16[8,3584]{1,0:T(8,128)(2,1)S(1)}, bf16[8,3584]{1,0:T(8,128)(2,1)S(1)}, u32[]{:S(2)}, u32[]{:S(2)}) collective-permute-start(bf16[8,3584]{1,0:T(8,128)(2,1)S(1)} %collective-permute-done.2.refs_3_), channel_id=1, source_target_pairs={{0,4},{2,6},{4,0},{6,2},{8,12},{10,14},{12,8},{14,10},{16,20},{18,... | collective-permute-start | bytes 172040 | tf_op jit(solution)/shard_map/ppermute | solution.py:118
  24.8 4.2 %collective-permute-start.6 = (bf16[8,3584]{1,0:T(8,128)(2,1)S(1)}, bf16[8,3584]{1,0:T(8,128)(2,1)S(1)}, u32[]{:S(2)}, u32[]{:S(2)}) collective-permute-start(bf16[8,3584]{1,0:T(8,128)(2,1)S(1)} %collective-permute-done.2.refs_3_), channel_id=1, source_target_pairs={{0,2},{2,0},{4,6},{6,4},{8,10},{10,8},{12,14},{14,12},{16,18},{18,... | collective-permute-start | bytes 172040 | tf_op jit(solution)/shard_map/ppermute | solution.py:118
  29.0 2.0 %copy-start = (bf16[2,3584,256]{2,1,0:T(8,128)(2,1)S(1)}, bf16[2,3584,256]{2,1,0:T(8,128)(2,1)}, u32[]{:S(2)}) copy-start(bf16[2,3584,256]{2,1,0:T(8,128)(2,1)} %refs_16_.1) | copy-start | bytes 11010052
  31.0 1.5 %copy-start.1 = (bf16[256,3584]{1,0:T(8,128)(2,1)S(1)}, bf16[256,3584]{1,0:T(8,128)(2,1)}, u32[]{:S(2)}) copy-start(bf16[256,3584]{1,0:T(8,128)(2,1)} %refs_17_.1) | copy-start | bytes 5505028
  33.5 6.1 %collective-permute-start.15 = (bf16[32,3584]{1,0:T(8,128)(2,1)S(1)}, bf16[32,3584]{1,0:T(8,128)(2,1)S(1)}, u32[]{:S(2)}, u32[]{:S(2)}) collective-permute-start(bf16[32,3584]{1,0:T(8,128)(2,1)S(1)} %get-tuple-element.24), channel_id=1, source_target_pairs={{0,2},{2,0},{4,6},{6,4},{8,10},{10,8},{12,14},{14,12},{16,18},{18,... | collective-permute-start | bytes 688136 | tf_op jit(solution)/shard_map/ppermute | solution.py:118
  35.0 8.5 %collective-permute-start.16 = (bf16[32,3584]{1,0:T(8,128)(2,1)S(1)}, bf16[32,3584]{1,0:T(8,128)(2,1)S(1)}, u32[]{:S(2)}, u32[]{:S(2)}) collective-permute-start(bf16[32,3584]{1,0:T(8,128)(2,1)S(1)} %get-tuple-element.25), channel_id=1, source_target_pairs={{0,4},{2,6},{4,0},{6,2},{8,12},{10,14},{12,8},{14,10},{16,20},{18,... | collective-permute-start | bytes 688136 | tf_op jit(solution)/shard_map/ppermute | solution.py:118
  35.5 8.0 %collective-permute-start.17 = (bf16[32,3584]{1,0:T(8,128)(2,1)S(1)}, bf16[32,3584]{1,0:T(8,128)(2,1)S(1)}, u32[]{:S(2)}, u32[]{:S(2)}) collective-permute-start(bf16[32,3584]{1,0:T(8,128)(2,1)S(1)} %get-tuple-element.26), channel_id=1, source_target_pairs={{0,6},{2,4},{4,2},{6,0},{8,14},{10,12},{12,10},{14,8},{16,22},{18,... | collective-permute-start | bytes 688136 | tf_op jit(solution)/shard_map/ppermute | solution.py:118
  43.6 4.5 %collective-permute-start.18 = (bf16[8,3584]{1,0:T(8,128)(2,1)S(1)}, bf16[8,3584]{1,0:T(8,128)(2,1)S(1)}, u32[]{:S(2)}, u32[]{:S(2)}) collective-permute-start(bf16[8,3584]{1,0:T(8,128)(2,1)S(1)} %get-tuple-element.28), channel_id=1, source_target_pairs={{0,8},{2,10},{4,12},{6,14},{8,0},{10,2},{12,4},{14,6},{16,24},{18,... | collective-permute-start | bytes 172040 | tf_op jit(solution)/shard_map/ppermute | solution.py:118
  43.7 5.2 %collective-permute-start.19 = (bf16[8,3584]{1,0:T(8,128)(2,1)S(1)}, bf16[8,3584]{1,0:T(8,128)(2,1)S(1)}, u32[]{:S(2)}, u32[]{:S(2)}) collective-permute-start(bf16[8,3584]{1,0:T(8,128)(2,1)S(1)} %get-tuple-element.29), channel_id=1, source_target_pairs={{0,16},{2,18},{4,20},{6,22},{8,24},{10,26},{12,28},{14,30},{16,0},... | collective-permute-start | bytes 172040 | tf_op jit(solution)/shard_map/ppermute | solution.py:118
  46.7 6.0 %collective-permute-start.20 = (bf16[8,3584]{1,0:T(8,128)(2,1)S(1)}, bf16[8,3584]{1,0:T(8,128)(2,1)S(1)}, u32[]{:S(2)}, u32[]{:S(2)}) collective-permute-start(bf16[8,3584]{1,0:T(8,128)(2,1)S(1)} %get-tuple-element.30), channel_id=1, source_target_pairs={{0,24},{2,26},{4,28},{6,30},{8,16},{10,18},{12,20},{14,22},{16,8},... | collective-permute-start | bytes 172040 | tf_op jit(solution)/shard_map/ppermute | solution.py:118

commit v2 on v1

v2 whole, which is shorter than its diff:
```python
import functools

import jax
import jax.numpy as jnp
from jax import lax
from jax.experimental import pallas as pl
from jax.experimental.pallas import tpu as pltpu
from jax.sharding import PartitionSpec as P

VMEM = pl.BlockSpec(memory_space=pltpu.VMEM)
HBM = pl.BlockSpec(memory_space=pltpu.HBM)
MIB = 1 << 20


def iota(shape, axis):
    return lax.broadcasted_iota(jnp.int32, shape, axis)


def fetch(sources, targets, sems):
    copies = [
        pltpu.make_async_copy(s, t, sems.at[i]) for i, (s, t) in enumerate(zip(sources, targets))
    ]
    for c in copies:
        c.start()
    for c in copies:
        c.wait()


def route_kernel(slot_count, capacity, *refs):
    sources, out, scratch, sems = refs[:5], refs[5], refs[6:11], refs[11]
    fetch(sources, scratch, sems)
    placement, expert_ids, replica_pick, gate_weights, tokens = scratch
    top_count, tok_count = expert_ids.shape
    width = tokens.shape[1]
    copy_row = iota((slot_count, tok_count), 0)
    named = jnp.zeros_like(copy_row)
    before = jnp.zeros_like(copy_row)
    for p in range(slot_count):
        here = copy_row == p
        named = jnp.where(here, placement[p], named)
        seen = jnp.int32(0)
        for q in range(p):
            seen = seen + (placement[q] == placement[p]).astype(jnp.int32)
        before = jnp.where(here, seen, before)
    chosen = []
    for k in range(top_count):
        matches = named == expert_ids[pl.ds(k, 1), :]
        copies = jnp.sum(matches.astype(jnp.int32), axis=0, keepdims=True)
        pick = replica_pick[pl.ds(k, 1), :]
        wanted = jnp.where(pick >= copies, pick - copies, pick)
        chosen.append((matches & (before == wanted)).astype(jnp.int32))
    total = sum(chosen[1:], chosen[0])
    ahead = (iota((tok_count, tok_count), 0) < iota((tok_count, tok_count), 1)).astype(jnp.bfloat16)
    earlier = jnp.dot(
        total.astype(jnp.bfloat16), ahead, preferred_element_type=jnp.float32
    ).astype(jnp.int32)
    weight = jnp.zeros((slot_count, tok_count), jnp.float32)
    for k in range(top_count):
        kept = (chosen[k] > 0) & (earlier < capacity)
        weight = weight + jnp.where(kept, gate_weights[pl.ds(k, 1), :], 0.0)
        earlier = earlier + chosen[k]
    terms = []
    for _ in range(3):
        terms.append(weight.astype(jnp.bfloat16).astype(jnp.float32))
        weight = weight - terms[-1]
    terms = jnp.concatenate(terms, axis=0)
    spread = (iota((3 * slot_count, 128), 0) == iota((3 * slot_count, 128), 1)).astype(jnp.float32)
    out[:, pl.ds(0, width)] = tokens[...]
    out[:, pl.ds(width, 128)] = lax.dot_general(
        terms, spread, (((0,), (0,)), ((), ())), preferred_element_type=jnp.float32
    ).astype(jnp.bfloat16)


def weight_kernel(w_in, w_out, w_in_held, w_out_held, sems):
    fetch((w_in, w_out), (w_in_held, w_out_held), sems)


def expert_kernel(slot_count, group_size, gathered, w_in, w_out, out):
    width = w_out.shape[1]
    own = lax.axis_index("expert") // group_size
    terms = gathered[:, pl.ds(width, 128)].astype(jnp.float32)
    lane = iota(terms.shape, 1)
    wanted = (lane < 3 * slot_count) & (lane % slot_count == own)
    weight = jnp.sum(jnp.where(wanted, terms, 0.0), axis=1, keepdims=True)
    rows = gathered[:, pl.ds(0, width)]
    gate = jnp.dot(rows, w_in[0], preferred_element_type=jnp.float32)
    upper = jnp.dot(rows, w_in[1], preferred_element_type=jnp.float32)
    hidden = (gate / (1.0 + jnp.exp(-gate)) * upper).astype(jnp.bfloat16)
    step = 512
    for c in range(0, width, step):
        value = jnp.dot(hidden, w_out[:, pl.ds(c, step)], preferred_element_type=jnp.float32)
        out[:, pl.ds(c, step)] = jnp.where(weight > 0.0, weight * value, 0.0).astype(jnp.bfloat16)


def call(kernel, inputs, in_specs, outs, limit, scratch=(), moved=0):
    return pl.pallas_call(
        kernel,
        out_shape=outs,
        in_specs=in_specs,
        out_specs=jax.tree.map(lambda _: VMEM, outs),
        scratch_shapes=scratch,
        compiler_params=pltpu.CompilerParams(vmem_limit_bytes=limit),
        cost_estimate=pl.CostEstimate(flops=0, bytes_accessed=moved, transcendentals=0)
        if moved
        else None,
    )(*inputs)


def body(tokens, expert_ids, gate_weights, replica_pick, placement, w_in, w_out):
    n_devices = lax.axis_size("expert")
    group_size = min(8, n_devices // 4)
    slot_count = n_devices // group_size
    tok_count, width = tokens.shape
    capacity = tok_count * expert_ids.shape[1] // slot_count
    sources = (placement, expert_ids.T, replica_pick.T, gate_weights.T, tokens)
    sources = [pltpu.with_memory_space_constraint(s, pltpu.HBM) for s in sources]
    w_in = pltpu.with_memory_space_constraint(w_in, pltpu.HBM)
    w_out = pltpu.with_memory_space_constraint(w_out, pltpu.HBM)
    marked = call(
        functools.partial(route_kernel, slot_count, capacity),
        sources,
        [HBM] * 5,
        jax.ShapeDtypeStruct((tok_count, width + 128), jnp.bfloat16),
        16 * MIB,
        [pltpu.SMEM(placement.shape, jnp.int32)]
        + [pltpu.VMEM(s.shape, s.dtype) for s in sources[1:]]
        + [pltpu.SemaphoreType.DMA((5,))],
    )
    gathered = lax.all_gather(marked, "expert", axis=0, tiled=True)
    w_in, w_out = call(
        weight_kernel,
        (w_in, w_out),
        [HBM] * 2,
        [jax.ShapeDtypeStruct(w.shape, w.dtype) for w in (w_in, w_out)],
        16 * MIB,
        [pltpu.SemaphoreType.DMA((2,))],
        2 * (w_in.size + w_out.size),
    )
    partial_value = call(
        functools.partial(expert_kernel, slot_count, group_size),
        (gathered, w_in, w_out),
        [VMEM] * 3,
        jax.ShapeDtypeStruct((gathered.shape[0], width), jnp.bfloat16),
        40 * MIB,
    )
    return lax.psum_scatter(partial_value, "expert", scatter_dimension=0, tiled=True)


def solution(mesh):
    in_specs = (
        P(("dp", "expert"), None),
        P(("dp", "expert"), None),
        P(("dp", "expert"), None),
        P(("dp", "expert"), None),
        P(),
        P(None, None, "expert"),
        P("expert", None),
    )
    out_specs = P(("dp", "expert"), None)
    return jax.shard_map(body, mesh=mesh, in_specs=in_specs, out_specs=out_specs, check_vma=False)
```

time: 54 us -> 165 us (3.06)
  waiting for transfers between devices: 14.1 us -> 138 us
  starting transfers between devices: 29.4 us -> 0.04 us
  between operations: 0.06 us -> 13.4 us
  Pallas kernels: 3.11 us -> 7.53 us
  local copies, waits for them, and re-layouts: 7.13 us -> 5.34 us
    reduce_scatter x0 -> x1, waiting for transfers between devices: none -> 78.9 us  [body(): lax.psum_scatter(partial_value, 'expert', scatter_dimension=0, tiled=True)]
    all_gather x0 -> x1, waiting for transfers between devices: none -> 59.6 us  [body(): gathered = lax.all_gather(marked, 'expert', axis=0, tiled=True)]
    ppermute x21 -> x0, starting transfers between devices: 29.4 us -> none  [swap(): lax.ppermute(value, 'expert', [(e, e ^ offset) for e in range(n_devices)])]
    ppermute x21 -> x0, waiting for transfers between devices: 14.1 us -> none  [swap(): lax.ppermute(value, 'expert', [(e, e ^ offset) for e in range(n_devices)])]
    pallas_call x4 -> x3, Pallas kernels: 3.11 us -> 7.53 us  [call(): pl.pallas_call(kernel, out_shape=outs, in_specs=in_specs, out_specs=jax.t...]
    unnamed x14 -> x6, local copies, waits for them, and re-layouts: 7.13 us -> 5.34 us
  transfers between devices with their start and end apart: 21 -> 2, of which waited for: 9 -> 2; matrix products, arithmetic and copies ran while one was open for 0% -> 0% of each run, Pallas kernels for 0% -> 2%
where the time goes in v2:
time: 165 us
  waiting for transfers between devices  138 us (84%)
  between operations  13.4 us (8%)
  Pallas kernels  7.53 us (5%)
  local copies, waits for them, and re-layouts  5.34 us (3%)
    reduce_scatter x1, waiting for transfers between devices, body(): lax.psum_scatter(partial_value, 'expert', scatter_dimension=0, tiled=True)  78.9 us
    all_gather x1, waiting for transfers between devices, body(): gathered = lax.all_gather(marked, 'expert', axis=0, tiled=True)  59.6 us
    pallas_call x3, Pallas kernels, call(): pl.pallas_call(kernel, out_shape=outs, in_specs=in_specs, out_specs=jax.t...  7.53 us
    unnamed x6, local copies, waits for them, and re-layouts  5.34 us
  transfers between devices with their start and end apart: 2, of which 2 were waited for; matrix products, arithmetic and copies ran while one was open for 0% of the time, Pallas kernels for 2%

profile of v2, /device:TPU:0, one launch (start us, length us, event | category | flops | bytes accessed | tf_op | source)
XLA Modules:
  0.0 164.8 jit_solution(2678128958315368801)
XLA Ops:
  6.5 0.0 all-gather.2.cloned.1.call-start
  6.5 2.0 %shard_map.73 = bf16[16,3712]{1,0:T(8,128)(2,1)} custom-call(s32[4]{0:T(128)} %refs_0_.1, s32[2,16]{1,0:T(2,128)} %bitcast.3, s32[2,16]{1,0:T(2,128)} %bitcast.4, f32[2,16]{1,0:T(2,128)} %bitcast.5, bf16[16,3584]{1,0:T(8,128)(2,1)} %refs_4_.1), custom_call_target="tpu_custom_call" | custom-call | tf_op jit(solution)/shard_map/pallas_call | solution.py:96
  8.5 0.0 all-gather.2.cloned.1.call-update
  8.5 0.0 reduce-scatter.2.cloned.1.call-start
  8.6 2.6 %shard_map.74 = (bf16[2,3584,256]{2,1,0:T(8,128)(2,1)S(1)}, bf16[256,3584]{1,0:T(8,128)(2,1)S(1)}) custom-call(bf16[2,3584,256]{2,1,0:T(8,128)(2,1)} %w_in.1, bf16[256,3584]{1,0:T(8,128)(2,1)} %w_out.1), custom_call_target="tpu_custom_call" | custom-call | bytes 5505024 | tf_op jit(solution)/shard_map/pallas_call | solution.py:96
  11.2 0.0 copy-start
  11.2 1.8 %copy-done = bf16[2,3584,256]{2,1,0:T(8,128)(2,1)} copy-done((bf16[2,3584,256]{2,1,0:T(8,128)(2,1)}, bf16[2,3584,256]{2,1,0:T(8,128)(2,1)S(1)}, u32[]{:S(2)}) %copy-start) | copy-done | bytes 3670040
  13.0 59.6 %all-gather.2.cloned.1.call-done.gathered = bf16[256,3712]{1,0:T(8,128)(2,1)} async-done(((bf16[16,3712]{1,0:T(8,128)(2,1)}), bf16[256,3712]{1,0:T(8,128)(2,1)}) %all-gather.2.cloned.1.call-update) | async-done | bytes 1900560 | tf_op jit(solution)/shard_map/all_gather | solution.py:129
  72.6 0.0 copy-start.1
  72.6 2.0 %copy-done.1 = bf16[2,3584,256]{2,1,0:T(8,128)(2,1)S(1)} copy-done((bf16[2,3584,256]{2,1,0:T(8,128)(2,1)S(1)}, bf16[2,3584,256]{2,1,0:T(8,128)(2,1)}, u32[]{:S(2)}) %copy-start.1) | copy-done | bytes 3670040
  74.6 0.0 copy-start.2
  74.6 1.5 copy-done.2
  76.1 2.9 %shard_map.75 = bf16[256,3584]{1,0:T(8,128)(2,1)} custom-call(bf16[256,3712]{1,0:T(8,128)(2,1)S(1)} %copy-done.2, bf16[2,3584,256]{2,1,0:T(8,128)(2,1)S(1)} %copy-done.1, bf16[256,3584]{1,0:T(8,128)(2,1)S(1)} %get-tuple-element.8.w_out), custom_call_target="tpu_custom_call" | custom-call | tf_op jit(solution)/shard_map/pallas_call | solution.py:96
  79.1 0.0 reduce-scatter.2.cloned.1.call-update
  79.1 78.9 %reduce-scatter.2.cloned.1.call-done = bf16[16,3584]{1,0:T(8,128)(2,1)} async-done(((bf16[256,3584]{1,0:T(8,128)(2,1)}), bf16[16,3584]{1,0:T(8,128)(2,1)}) %reduce-scatter.2.cloned.1.call-update) | async-done | bytes 114704 | tf_op jit(solution)/shard_map/reduce_scatter | solution.py:146
Async XLA Ops:
  6.5 66.1 %all-gather.2.cloned.1.call-start = ((), (), s32[]{:S(2)}) async-start(), calls=%async_computation.1 | async-start | bytes 2019328 | tf_op jit(solution)/shard_map/all_gather | solution.py:129
  8.5 149.4 %reduce-scatter.2.cloned.1.call-start = ((), (), s32[]{:S(2)}) async-start(), calls=%async_computation.2 | async-start | bytes 1949696 | tf_op jit(solution)/shard_map/reduce_scatter | solution.py:146
  11.2 1.8 %copy-start = (bf16[2,3584,256]{2,1,0:T(8,128)(2,1)}, bf16[2,3584,256]{2,1,0:T(8,128)(2,1)S(1)}, u32[]{:S(2)}) copy-start(bf16[2,3584,256]{2,1,0:T(8,128)(2,1)S(1)} %get-tuple-element.7.w_in) | copy-start | bytes 11010052
  72.6 2.0 %copy-start.1 = (bf16[2,3584,256]{2,1,0:T(8,128)(2,1)S(1)}, bf16[2,3584,256]{2,1,0:T(8,128)(2,1)}, u32[]{:S(2)}) copy-start(bf16[2,3584,256]{2,1,0:T(8,128)(2,1)} %copy-done) | copy-start | bytes 11010052
  74.6 1.5 copy-start.2
Sparse Core Ops, SparseCore 0:
  10.1 62.4 all-gather.1
  79.2 78.7 reduce-scatter.1

commit v3 on v2

v3 whole, which is shorter than its diff:
```python
import functools

import jax
import jax.numpy as jnp
from jax import lax
from jax.experimental import pallas as pl
from jax.experimental.pallas import tpu as pltpu
from jax.sharding import PartitionSpec as P

VMEM = pl.BlockSpec(memory_space=pltpu.VMEM)
HBM = pl.BlockSpec(memory_space=pltpu.HBM)
MIB = 1 << 20


def iota(shape, axis):
    return lax.broadcasted_iota(jnp.int32, shape, axis)


def stack(refs):
    return jnp.concatenate([r[...].astype(jnp.float32) for r in refs], axis=0)


def unstack(value, outs):
    start = 0
    for out in outs:
        out[...] = value[start : start + out.shape[0]].astype(out.dtype)
        start += out.shape[0]


def route_kernel(group_size, slot_count, *refs):
    sources, refs = refs[:5], refs[5:]
    row_outs, combine_out, refs = refs[:slot_count], refs[slot_count], refs[slot_count + 1 :]
    scratch, sems = refs[:5], refs[5]
    copies_in = [
        pltpu.make_async_copy(s, t, sems.at[i]) for i, (s, t) in enumerate(zip(sources, scratch))
    ]
    for c in copies_in:
        c.start()
    placement, expert_ids, replica_pick, gate_weights, tokens = scratch
    capacity = row_outs[0].shape[0]
    top_count, tok_count = expert_ids.shape
    own = lax.axis_index("expert") // group_size
    copy_row = iota((slot_count, tok_count), 0)
    named = jnp.zeros_like(copy_row)
    before = jnp.zeros_like(copy_row)
    relative = jnp.zeros_like(copy_row)
    for c in copies_in[:4]:
        c.wait()
    for p in range(slot_count):
        here = copy_row == p
        named = jnp.where(here, placement[p], named)
        relative = jnp.where(here, lax.bitwise_xor(own, p), relative)
        seen = jnp.int32(0)
        for q in range(p):
            seen = seen + (placement[q] == placement[p]).astype(jnp.int32)
        before = jnp.where(here, seen, before)
    chosen = []
    for k in range(top_count):
        matches = named == expert_ids[pl.ds(k, 1), :]
        copies = jnp.sum(matches.astype(jnp.int32), axis=0, keepdims=True)
        pick = replica_pick[pl.ds(k, 1), :]
        wanted = jnp.where(pick >= copies, pick - copies, pick)
        chosen.append((matches & (before == wanted)).astype(jnp.int32))
    total = sum(chosen[1:], chosen[0])
    ahead = (iota((tok_count, tok_count), 0) < iota((tok_count, tok_count), 1)).astype(jnp.bfloat16)
    earlier = jnp.dot(
        total.astype(jnp.bfloat16), ahead, preferred_element_type=jnp.float32
    ).astype(jnp.int32)
    slot_row = iota((slot_count * capacity, tok_count), 0)
    pick_rows = jnp.zeros((slot_count * capacity, tok_count), jnp.float32)
    combine = jnp.zeros((slot_count * capacity, tok_count), jnp.float32)
    for k in range(top_count):
        rank = jnp.sum(chosen[k] * earlier, axis=0, keepdims=True)
        place = jnp.sum(chosen[k] * relative, axis=0, keepdims=True)
        slot = jnp.where(rank < capacity, place * capacity + rank, -1)
        hot = slot_row == slot
        pick_rows = pick_rows + hot.astype(jnp.float32)
        combine = combine + jnp.where(hot, gate_weights[pl.ds(k, 1), :], 0.0)
        earlier = earlier + chosen[k]
    combine_out[...] = combine
    copies_in[4].wait()
    rows = jnp.dot(pick_rows.astype(jnp.bfloat16), tokens[...], preferred_element_type=jnp.float32)
    unstack(rows, row_outs)


def prepare_kernel(w_in, w_out, combine, w_in_held, w_out_held, terms_out, sems):
    first = pltpu.make_async_copy(w_in, w_in_held, sems.at[0])
    second = pltpu.make_async_copy(w_out, w_out_held, sems.at[1])
    first.start()
    second.start()
    rest = combine[...]
    slots = rest.shape[0]
    same = (iota((slots, slots), 0) == iota((slots, slots), 1)).astype(jnp.float32)
    terms = []
    for _ in range(3):
        term = rest.astype(jnp.bfloat16).astype(jnp.float32)
        rest = rest - term
        terms.append(
            lax.dot_general(
                term, same, (((0,), (0,)), ((), ())), preferred_element_type=jnp.float32
            )
        )
    terms_out[...] = jnp.concatenate(terms, axis=0).astype(jnp.bfloat16)
    first.wait()
    second.wait()


def stack_kernel(*refs):
    refs[-1][...] = stack(refs[:-1]).astype(jnp.bfloat16)


def expert_kernel(count, *refs):
    blocks, (w_in, w_out), outs = refs[:count], refs[count : count + 2], refs[count + 2 :]
    rows = stack(blocks).astype(jnp.bfloat16)
    gate = jnp.dot(rows, w_in[0], preferred_element_type=jnp.float32)
    upper = jnp.dot(rows, w_in[1], preferred_element_type=jnp.float32)
    hidden = (gate / (1.0 + jnp.exp(-gate)) * upper).astype(jnp.bfloat16)
    unstack(jnp.dot(hidden, w_out[...], preferred_element_type=jnp.float32), outs)


def sum_kernel(count, *refs):
    total = refs[0][...].astype(jnp.float32)
    for r in refs[1:count]:
        total = total + r[...].astype(jnp.float32)
    unstack(total, refs[count:])


def combine_kernel(terms, *refs):
    parts, out = refs[:-1], refs[-1]
    values = stack(parts).astype(jnp.bfloat16)
    product = jnp.dot(terms[...], values, preferred_element_type=jnp.float32)
    rows = out.shape[0]
    total = product[2 * rows :] + product[rows : 2 * rows] + product[:rows]
    out[...] = total.astype(jnp.bfloat16)


def call(kernel, inputs, in_specs, outs, limit, scratch=(), moved=0):
    return pl.pallas_call(
        kernel,
        out_shape=outs,
        in_specs=in_specs,
        out_specs=jax.tree.map(lambda _: VMEM, outs),
        scratch_shapes=scratch,
        compiler_params=pltpu.CompilerParams(vmem_limit_bytes=limit),
        cost_estimate=pl.CostEstimate(flops=0, bytes_accessed=moved, transcendentals=0)
        if moved
        else None,
    )(*inputs)


def body(tokens, expert_ids, gate_weights, replica_pick, placement, w_in, w_out):
    n_devices = lax.axis_size("expert")
    group_size = min(8, n_devices // 4)
    slot_count = n_devices // group_size
    tok_count, width = tokens.shape
    capacity = tok_count * expert_ids.shape[1] // slot_count
    slots = slot_count * capacity
    near, far = range(slot_count // 2), range(slot_count // 2, slot_count)
    bf16 = jnp.bfloat16
    chunk = jax.ShapeDtypeStruct((capacity, width), bf16)
    half = jax.ShapeDtypeStruct((slots // 2, width), bf16)

    def swap(value, offset):
        return lax.ppermute(value, "expert", [(e, e ^ offset) for e in range(n_devices)])

    def local(kernel, inputs, outs, limit=16 * MIB):
        return call(kernel, inputs, [VMEM] * len(inputs), outs, limit)

    def in_hbm(*arrays):
        return [pltpu.with_memory_space_constraint(a, pltpu.HBM) for a in arrays]

    sources = in_hbm(placement, expert_ids.T, replica_pick.T, gate_weights.T, tokens)
    *chunks, combine = call(
        functools.partial(route_kernel, group_size, slot_count),
        sources,
        [HBM] * 5,
        [chunk] * slot_count + [jax.ShapeDtypeStruct((slots, tok_count), jnp.float32)],
        16 * MIB,
        [pltpu.SMEM(placement.shape, jnp.int32)]
        + [pltpu.VMEM(s.shape, s.dtype) for s in sources[1:]]
        + [pltpu.SemaphoreType.DMA((5,))],
    )
    chunks = [c if d == 0 else swap(c, d * group_size) for d, c in enumerate(chunks)]
    w_in, w_out, terms = call(
        prepare_kernel,
        (*in_hbm(w_in, w_out), combine),
        [HBM] * 2 + [VMEM],
        [
            jax.ShapeDtypeStruct(w_in.shape, bf16),
            jax.ShapeDtypeStruct(w_out.shape, bf16),
            jax.ShapeDtypeStruct((3 * tok_count, slots), bf16),
        ],
        16 * MIB,
        [pltpu.SemaphoreType.DMA((2,))],
        2 * (w_in.size + w_out.size),
    )

    own = [local(stack_kernel, [chunks[d] for d in part], half) for part in (near, far)]
    held = [own] + [[None, None] for _ in range(1, group_size)]
    square = group_size == 4
    for h in range(2):
        for q in (1, 2) if square else range(1, group_size):
            held[q][h] = swap(own[h], q)
    if square:
        held[3] = [swap(held[1][0], 2), swap(held[2][1], 1)]

    result = local(
        functools.partial(expert_kernel, 2 * group_size),
        [held[q][h] for h in range(2) for q in range(group_size)] + [w_in, w_out],
        [half] * (2 * group_size),
        40 * MIB,
    )
    near_sent, far_sent = result[:group_size], result[group_size:]
    if square:
        far_cross, near_cross = swap(far_sent[3], 1), swap(near_sent[3], 2)
        far_terms = [
            far_sent[0],
            swap(far_sent[1], 1),
            swap(local(functools.partial(sum_kernel, 2), [far_sent[2], far_cross], [half])[0], 2),
        ]
        near_terms = [
            near_sent[0],
            swap(near_sent[2], 2),
            swap(local(functools.partial(sum_kernel, 2), [near_sent[1], near_cross], [half])[0], 1),
        ]
    else:
        far_terms = [v if q == 0 else swap(v, q) for q, v in enumerate(far_sent)]
        near_terms = [v if q == 0 else swap(v, q) for q, v in enumerate(near_sent)]
    summed = [
        local(functools.partial(sum_kernel, len(t)), t, [chunk] * (slot_count // 2))
        for t in (near_terms, far_terms)
    ]
    returned = [
        v if d == 0 else swap(v, d * group_size) for d, v in enumerate(summed[0] + summed[1])
    ]
    return local(
        combine_kernel, [terms] + returned, jax.ShapeDtypeStruct((tok_count, width), bf16)
    )


def solution(mesh):
    in_specs = (
        P(("dp", "expert"), None),
        P(("dp", "expert"), None),
        P(("dp", "expert"), None),
        P(("dp", "expert"), None),
        P(),
        P(None, None, "expert"),
        P("expert", None),
    )
    out_specs = P(("dp", "expert"), None)
    return jax.shard_map(body, mesh=mesh, in_specs=in_specs, out_specs=out_specs, check_vma=False)
```

time: 165 us -> 46.2 us (0.28)
  waiting for transfers between devices: 138 us -> 19.3 us
  starting transfers between devices: 0.04 us -> 20.7 us
  between operations: 13.4 us -> 0.11 us
  local copies, waits for them, and re-layouts: 5.34 us -> 0 us
  Pallas kernels: 7.53 us -> 5.87 us
    reduce_scatter x1 -> x0, waiting for transfers between devices: 78.9 us -> none  [body(): lax.psum_scatter(partial_value, 'expert', scatter_dimension=0, tiled=True)]
    all_gather x1 -> x0, waiting for transfers between devices: 59.6 us -> none  [body(): gathered = lax.all_gather(marked, 'expert', axis=0, tiled=True)]
    ppermute x0 -> x18, starting transfers between devices: none -> 20.7 us  [swap(): lax.ppermute(value, 'expert', [(e, e ^ offset) for e in range(n_devices)])]
    ppermute x0 -> x18, waiting for transfers between devices: none -> 19.3 us  [swap(): lax.ppermute(value, 'expert', [(e, e ^ offset) for e in range(n_devices)])]
    unnamed x6 -> x0, local copies, waits for them, and re-layouts: 5.34 us -> none
    pallas_call x3 -> x10, Pallas kernels: 7.53 us -> 5.87 us  [call(): pl.pallas_call(kernel, out_shape=outs, in_specs=in_specs, out_specs=jax.t...]
  transfers between devices with their start and end apart: 2 -> 18, of which waited for: 2 -> 10; matrix products, arithmetic and copies ran while one was open for 0% -> 0% of each run, Pallas kernels for 2% -> 6%
where the time goes in v3:
time: 46.2 us; the launch traced here: 46.1 us
  starting transfers between devices  20.7 us (45%)
  waiting for transfers between devices  19.3 us (42%)
  Pallas kernels  5.87 us (13%)
    ppermute x18, starting transfers between devices, swap(): lax.ppermute(value, 'expert', [(e, e ^ offset) for e in range(n_devices)])  20.7 us
    ppermute x18, waiting for transfers between devices, swap(): lax.ppermute(value, 'expert', [(e, e ^ offset) for e in range(n_devices)])  19.3 us
    pallas_call x10, Pallas kernels, call(): pl.pallas_call(kernel, out_shape=outs, in_specs=in_specs, out_specs=jax.t...  5.87 us
  transfers between devices with their start and end apart: 18, of which 10 were waited for; matrix products, arithmetic and copies ran while one was open for 0% of the time, Pallas kernels for 6%

profile of v3, /device:TPU:0, one launch (start us, length us, event | category | flops | bytes accessed | tf_op | source)
XLA Modules:
  0.0 46.1 jit_solution(17042942878929730699)
XLA Ops:
  0.0 1.2 %shard_map.73 = (bf16[8,3584]{1,0:T(8,128)(2,1)S(1)}, bf16[8,3584]{1,0:T(8,128)(2,1)S(1)}, bf16[8,3584]{1,0:T(8,128)(2,1)S(1)}, bf16[8,3584]{1,0:T(8,128)(2,1)S(1)}, f32[32,16]{1,0:T(8,128)S(1)}) custom-call(s32[4]{0:T(128)} %refs_0_.1, s32[2,16]{1,0:T(2,128)} %bitcast.3, s32[2,16]{1,0:T(2,128)} %bitcast.4, f32[2,16]{1,0:T(2,128)} %bitcast.5, ...), custom_call_target="tpu_custom_call" | custom-call | tf_op jit(solution)/shard_map/pallas_call | solution.py:138
  1.2 4.1 %collective-permute-start.4 = (bf16[8,3584]{1,0:T(8,128)(2,1)S(1)}, bf16[8,3584]{1,0:T(8,128)(2,1)S(1)}, u32[]{:S(2)}, u32[]{:S(2)}) collective-permute-start(bf16[8,3584]{1,0:T(8,128)(2,1)S(1)} %get-tuple-element.29), channel_id=1, source_target_pairs={{0,16},{2,18},{4,20},{6,22},{8,24},{10,26},{12,28},{14,30},{16,0},... | collective-permute-start | bytes 172040 | tf_op jit(solution)/shard_map/ppermute | solution.py:164
  5.3 1.4 %collective-permute-start.5 = (bf16[8,3584]{1,0:T(8,128)(2,1)S(1)}, bf16[8,3584]{1,0:T(8,128)(2,1)S(1)}, u32[]{:S(2)}, u32[]{:S(2)}) collective-permute-start(bf16[8,3584]{1,0:T(8,128)(2,1)S(1)} %get-tuple-element.30), channel_id=1, source_target_pairs={{0,24},{2,26},{4,28},{6,30},{8,16},{10,18},{12,20},{14,22},{16,8},... | collective-permute-start | bytes 172040 | tf_op jit(solution)/shard_map/ppermute | solution.py:164
  6.6 0.2 collective-permute-start
  6.9 1.2 %collective-permute-done.4.refs_0_ = bf16[8,3584]{1,0:T(8,128)(2,1)S(1)} collective-permute-done((bf16[8,3584]{1,0:T(8,128)(2,1)S(1)}, bf16[8,3584]{1,0:T(8,128)(2,1)S(1)}, u32[]{:S(2)}, u32[]{:S(2)}) %collective-permute-start.4) | collective-permute-done | bytes 57376 | tf_op jit(solution)/shard_map/ppermute | solution.py:164
  8.1 3.3 %collective-permute-done.5.refs_1_ = bf16[8,3584]{1,0:T(8,128)(2,1)S(1)} collective-permute-done((bf16[8,3584]{1,0:T(8,128)(2,1)S(1)}, bf16[8,3584]{1,0:T(8,128)(2,1)S(1)}, u32[]{:S(2)}, u32[]{:S(2)}) %collective-permute-start.5) | collective-permute-done | bytes 57376 | tf_op jit(solution)/shard_map/ppermute | solution.py:164
  11.4 1.6 %collective-permute-start.7 = (bf16[16,3584]{1,0:T(8,128)(2,1)S(1)}, bf16[16,3584]{1,0:T(8,128)(2,1)S(1)}, u32[]{:S(2)}, u32[]{:S(2)}) collective-permute-start(bf16[16,3584]{1,0:T(8,128)(2,1)S(1)} %shard_map.76.refs_4_), channel_id=1, source_target_pairs={{0,4},{2,6},{4,0},{6,2},{8,12},{10,14},{12,8},{14,10},{16,20},{18,... | collective-permute-start | bytes 344072 | tf_op jit(solution)/shard_map/ppermute | solution.py:164
  13.0 1.6 %collective-permute-start.1 = (bf16[16,3584]{1,0:T(8,128)(2,1)S(1)}, bf16[16,3584]{1,0:T(8,128)(2,1)S(1)}, u32[]{:S(2)}, u32[]{:S(2)}) collective-permute-start(bf16[16,3584]{1,0:T(8,128)(2,1)S(1)} %shard_map.75.refs_0_), channel_id=1, source_target_pairs={{0,2},{2,0},{4,6},{6,4},{8,10},{10,8},{12,14},{14,12},{16,18},{18,... | collective-permute-start | bytes 344072 | tf_op jit(solution)/shard_map/ppermute | solution.py:164
  14.6 0.5 %collective-permute-start.6 = (bf16[16,3584]{1,0:T(8,128)(2,1)S(1)}, bf16[16,3584]{1,0:T(8,128)(2,1)S(1)}, u32[]{:S(2)}, u32[]{:S(2)}) collective-permute-start(bf16[16,3584]{1,0:T(8,128)(2,1)S(1)} %shard_map.76.refs_4_), channel_id=1, source_target_pairs={{0,2},{2,0},{4,6},{6,4},{8,10},{10,8},{12,14},{14,12},{16,18},{18,... | collective-permute-start | bytes 344072 | tf_op jit(solution)/shard_map/ppermute | solution.py:164
  15.1 0.5 %collective-permute-start.2 = (bf16[16,3584]{1,0:T(8,128)(2,1)S(1)}, bf16[16,3584]{1,0:T(8,128)(2,1)S(1)}, u32[]{:S(2)}, u32[]{:S(2)}) collective-permute-start(bf16[16,3584]{1,0:T(8,128)(2,1)S(1)} %shard_map.75.refs_0_), channel_id=1, source_target_pairs={{0,4},{2,6},{4,0},{6,2},{8,12},{10,14},{12,8},{14,10},{16,20},{18,... | collective-permute-start | bytes 344072 | tf_op jit(solution)/shard_map/ppermute | solution.py:164
  15.6 1.7 %collective-permute-done.7.refs_6_ = bf16[16,3584]{1,0:T(8,128)(2,1)S(1)} collective-permute-done((bf16[16,3584]{1,0:T(8,128)(2,1)S(1)}, bf16[16,3584]{1,0:T(8,128)(2,1)S(1)}, u32[]{:S(2)}, u32[]{:S(2)}) %collective-permute-start.7) | collective-permute-done | bytes 114720 | tf_op jit(solution)/shard_map/ppermute | solution.py:164
  17.3 1.5 %collective-permute-start.8 = (bf16[16,3584]{1,0:T(8,128)(2,1)S(1)}, bf16[16,3584]{1,0:T(8,128)(2,1)S(1)}, u32[]{:S(2)}, u32[]{:S(2)}) collective-permute-start(bf16[16,3584]{1,0:T(8,128)(2,1)S(1)} %collective-permute-done.7.refs_6_), channel_id=1, source_target_pairs={{0,2},{2,0},{4,6},{6,4},{8,10},{10,8},{12,14},{14,12},{16,18},{18,... | collective-permute-start | bytes 344072 | tf_op jit(solution)/shard_map/ppermute | solution.py:164
  18.8 1.0 %collective-permute-start.3 = (bf16[16,3584]{1,0:T(8,128)(2,1)S(1)}, bf16[16,3584]{1,0:T(8,128)(2,1)S(1)}, u32[]{:S(2)}, u32[]{:S(2)}) collective-permute-start(bf16[16,3584]{1,0:T(8,128)(2,1)S(1)} %collective-permute-done.1.refs_1_), channel_id=1, source_target_pairs={{0,4},{2,6},{4,0},{6,2},{8,12},{10,14},{12,8},{14,10},{16,20},{18,... | collective-permute-start | bytes 344072 | tf_op jit(solution)/shard_map/ppermute | solution.py:164
  19.9 2.6 %shard_map.74 = (bf16[2,3584,256]{2,1,0:T(8,128)(2,1)S(1)}, bf16[256,3584]{1,0:T(8,128)(2,1)S(1)}, bf16[48,32]{1,0:T(8,128)(2,1)S(1)}) custom-call(bf16[2,3584,256]{2,1,0:T(8,128)(2,1)} %w_in.1, bf16[256,3584]{1,0:T(8,128)(2,1)} %w_out.1, f32[32,16]{1,0:T(8,128)S(1)} %get-tuple-element.25.combine), custom_call_target="tpu_custom_call" | custom-call | bytes 5505024 | tf_op jit(solution)/shard_map/pallas_call | solution.py:138
  22.6 1.7 %collective-permute-done.3.refs_3_ = bf16[16,3584]{1,0:T(8,128)(2,1)S(1)} collective-permute-done((bf16[16,3584]{1,0:T(8,128)(2,1)S(1)}, bf16[16,3584]{1,0:T(8,128)(2,1)S(1)}, u32[]{:S(2)}, u32[]{:S(2)}) %collective-permute-start.3) | collective-permute-done | bytes 114720 | tf_op jit(solution)/shard_map/ppermute | solution.py:164
  24.3 1.0 %shard_map.77 = (bf16[16,3584]{1,0:T(8,128)(2,1)S(1)}, bf16[16,3584]{1,0:T(8,128)(2,1)S(1)}, bf16[16,3584]{1,0:T(8,128)(2,1)S(1)}, bf16[16,3584]{1,0:T(8,128)(2,...) custom-call(bf16[16,3584]{1,0:T(8,128)(2,1)S(1)} %shard_map.75.refs_, ...), custom_call_target="tpu_custom_call" | custom-call | tf_op jit(solution)/shard_map/pallas_call | solution.py:138
  25.3 0.4 collective-permute-start.10
  25.8 1.2 %collective-permute-start.14 = (bf16[16,3584]{1,0:T(8,128)(2,1)S(1)}, bf16[16,3584]{1,0:T(8,128)(2,1)S(1)}, u32[]{:S(2)}, u32[]{:S(2)}) collective-permute-start(bf16[16,3584]{1,0:T(8,128)(2,1)S(1)} %get-tuple-element.42), channel_id=1, source_target_pairs={{0,2},{2,0},{4,6},{6,4},{8,10},{10,8},{12,14},{14,12},{16,18},{18,... | collective-permute-start | bytes 344072 | tf_op jit(solution)/shard_map/ppermute | solution.py:164
  27.0 1.9 %collective-permute-start.9 = (bf16[16,3584]{1,0:T(8,128)(2,1)S(1)}, bf16[16,3584]{1,0:T(8,128)(2,1)S(1)}, u32[]{:S(2)}, u32[]{:S(2)}) collective-permute-start(bf16[16,3584]{1,0:T(8,128)(2,1)S(1)} %get-tuple-element.34), channel_id=1, source_target_pairs={{0,4},{2,6},{4,0},{6,2},{8,12},{10,14},{12,8},{14,10},{16,20},{18,... | collective-permute-start | bytes 344072 | tf_op jit(solution)/shard_map/ppermute | solution.py:164
  28.9 2.5 %collective-permute-done.10.refs_1_ = bf16[16,3584]{1,0:T(8,128)(2,1)S(1)} collective-permute-done((bf16[16,3584]{1,0:T(8,128)(2,1)S(1)}, bf16[16,3584]{1,0:T(8,128)(2,1)S(1)}, u32[]{:S(2)}, u32[]{:S(2)}) %collective-permute-start.10) | collective-permute-done | bytes 114720 | tf_op jit(solution)/shard_map/ppermute | solution.py:164
  31.4 1.4 %collective-permute-start.11 = (bf16[16,3584]{1,0:T(8,128)(2,1)S(1)}, bf16[16,3584]{1,0:T(8,128)(2,1)S(1)}, u32[]{:S(2)}, u32[]{:S(2)}) collective-permute-start(bf16[16,3584]{1,0:T(8,128)(2,1)S(1)} %shard_map.78), channel_id=1, source_target_pairs={{0,2},{2,0},{4,6},{6,4},{8,10},{10,8},{12,14},{14,12},{16,18},{18,... | collective-permute-start | bytes 344072 | tf_op jit(solution)/shard_map/ppermute | solution.py:164
  32.8 0.7 %collective-permute-start.13 = (bf16[16,3584]{1,0:T(8,128)(2,1)S(1)}, bf16[16,3584]{1,0:T(8,128)(2,1)S(1)}, u32[]{:S(2)}, u32[]{:S(2)}) collective-permute-start(bf16[16,3584]{1,0:T(8,128)(2,1)S(1)} %get-tuple-element.40), channel_id=1, source_target_pairs={{0,2},{2,0},{4,6},{6,4},{8,10},{10,8},{12,14},{14,12},{16,18},{18,... | collective-permute-start | bytes 344072 | tf_op jit(solution)/shard_map/ppermute | solution.py:164
  33.6 0.1 collective-permute-start.15
  33.6 2.6 %collective-permute-done.11.refs_2_ = bf16[16,3584]{1,0:T(8,128)(2,1)S(1)} collective-permute-done((bf16[16,3584]{1,0:T(8,128)(2,1)S(1)}, bf16[16,3584]{1,0:T(8,128)(2,1)S(1)}, u32[]{:S(2)}, u32[]{:S(2)}) %collective-permute-start.11) | collective-permute-done | bytes 114720 | tf_op jit(solution)/shard_map/ppermute | solution.py:164
  36.3 0.1 collective-permute-start.12
  36.4 1.2 %collective-permute-done.13.refs_1_ = bf16[16,3584]{1,0:T(8,128)(2,1)S(1)} collective-permute-done((bf16[16,3584]{1,0:T(8,128)(2,1)S(1)}, bf16[16,3584]{1,0:T(8,128)(2,1)S(1)}, u32[]{:S(2)}, u32[]{:S(2)}) %collective-permute-start.13) | collective-permute-done | bytes 114720 | tf_op jit(solution)/shard_map/ppermute | solution.py:164
  37.6 0.8 %collective-permute-done.15.refs_2_ = bf16[16,3584]{1,0:T(8,128)(2,1)S(1)} collective-permute-done((bf16[16,3584]{1,0:T(8,128)(2,1)S(1)}, bf16[16,3584]{1,0:T(8,128)(2,1)S(1)}, u32[]{:S(2)}, u32[]{:S(2)}) %collective-permute-start.15) | collective-permute-done | bytes 114720 | tf_op jit(solution)/shard_map/ppermute | solution.py:164
  38.5 0.7 %collective-permute-start.16 = (bf16[8,3584]{1,0:T(8,128)(2,1)S(1)}, bf16[8,3584]{1,0:T(8,128)(2,1)S(1)}, u32[]{:S(2)}, u32[]{:S(2)}) collective-permute-start(bf16[8,3584]{1,0:T(8,128)(2,1)S(1)} %get-tuple-element.43), channel_id=1, source_target_pairs={{0,16},{2,18},{4,20},{6,22},{8,24},{10,26},{12,28},{14,30},{16,0},... | collective-permute-start | bytes 172040 | tf_op jit(solution)/shard_map/ppermute | solution.py:164
  39.2 1.7 %collective-permute-start.17 = (bf16[8,3584]{1,0:T(8,128)(2,1)S(1)}, bf16[8,3584]{1,0:T(8,128)(2,1)S(1)}, u32[]{:S(2)}, u32[]{:S(2)}) collective-permute-start(bf16[8,3584]{1,0:T(8,128)(2,1)S(1)} %get-tuple-element.44), channel_id=1, source_target_pairs={{0,24},{2,26},{4,28},{6,30},{8,16},{10,18},{12,20},{14,22},{16,8},... | collective-permute-start | bytes 172040 | tf_op jit(solution)/shard_map/ppermute | solution.py:164
  40.9 2.8 %collective-permute-done.16.refs_2_ = bf16[8,3584]{1,0:T(8,128)(2,1)S(1)} collective-permute-done((bf16[8,3584]{1,0:T(8,128)(2,1)S(1)}, bf16[8,3584]{1,0:T(8,128)(2,1)S(1)}, u32[]{:S(2)}, u32[]{:S(2)}) %collective-permute-start.16) | collective-permute-done | bytes 57376 | tf_op jit(solution)/shard_map/ppermute | solution.py:164
  43.7 1.5 %collective-permute-done.17.refs_3_ = bf16[8,3584]{1,0:T(8,128)(2,1)S(1)} collective-permute-done((bf16[8,3584]{1,0:T(8,128)(2,1)S(1)}, bf16[8,3584]{1,0:T(8,128)(2,1)S(1)}, u32[]{:S(2)}, u32[]{:S(2)}) %collective-permute-start.17) | collective-permute-done | bytes 57376 | tf_op jit(solution)/shard_map/ppermute | solution.py:164
  45.2 0.9 %shard_map.82 = bf16[16,3584]{1,0:T(8,128)(2,1)} custom-call(bf16[48,32]{1,0:T(8,128)(2,1)S(1)} %get-tuple-element.26.terms, bf16[8,3584]{1,0:T(8,128)(2,1)S(1)} %get-tuple-element.37.refs_0_, bf16[8,3584]{1,0:T(8,128)(2,1)S(1)} %collective-permute-done.12.refs_1_, bf16[8,3584]{1,0:T(8,128)(2,1)S(1)} %collective-permute-done.16.refs_2_, ...), custom_call_target="tpu_custom_call" | custom-call | tf_op jit(solution)/shard_map/pallas_call | solution.py:138
  (14 shorter events, 0.2 us)
Async XLA Ops:
  1.2 6.9 %collective-permute-start.4 = (bf16[8,3584]{1,0:T(8,128)(2,1)S(1)}, bf16[8,3584]{1,0:T(8,128)(2,1)S(1)}, u32[]{:S(2)}, u32[]{:S(2)}) collective-permute-start(bf16[8,3584]{1,0:T(8,128)(2,1)S(1)} %get-tuple-element.29), channel_id=1, source_target_pairs={{0,16},{2,18},{4,20},{6,22},{8,24},{10,26},{12,28},{14,30},{16,0},... | collective-permute-start | bytes 172040 | tf_op jit(solution)/shard_map/ppermute | solution.py:164
  5.3 6.1 %collective-permute-start.5 = (bf16[8,3584]{1,0:T(8,128)(2,1)S(1)}, bf16[8,3584]{1,0:T(8,128)(2,1)S(1)}, u32[]{:S(2)}, u32[]{:S(2)}) collective-permute-start(bf16[8,3584]{1,0:T(8,128)(2,1)S(1)} %get-tuple-element.30), channel_id=1, source_target_pairs={{0,24},{2,26},{4,28},{6,30},{8,16},{10,18},{12,20},{14,22},{16,8},... | collective-permute-start | bytes 172040 | tf_op jit(solution)/shard_map/ppermute | solution.py:164
  6.6 6.4 %collective-permute-start = (bf16[8,3584]{1,0:T(8,128)(2,1)S(1)}, bf16[8,3584]{1,0:T(8,128)(2,1)S(1)}, u32[]{:S(2)}, u32[]{:S(2)}) collective-permute-start(bf16[8,3584]{1,0:T(8,128)(2,1)S(1)} %get-tuple-element.28), channel_id=1, source_target_pairs={{0,8},{2,10},{4,12},{6,14},{8,0},{10,2},{12,4},{14,6},{16,24},{18,... | collective-permute-start | bytes 172040 | tf_op jit(solution)/shard_map/ppermute | solution.py:164
  11.4 5.9 %collective-permute-start.7 = (bf16[16,3584]{1,0:T(8,128)(2,1)S(1)}, bf16[16,3584]{1,0:T(8,128)(2,1)S(1)}, u32[]{:S(2)}, u32[]{:S(2)}) collective-permute-start(bf16[16,3584]{1,0:T(8,128)(2,1)S(1)} %shard_map.76.refs_4_), channel_id=1, source_target_pairs={{0,4},{2,6},{4,0},{6,2},{8,12},{10,14},{12,8},{14,10},{16,20},{18,... | collective-permute-start | bytes 344072 | tf_op jit(solution)/shard_map/ppermute | solution.py:164
  13.0 5.8 %collective-permute-start.1 = (bf16[16,3584]{1,0:T(8,128)(2,1)S(1)}, bf16[16,3584]{1,0:T(8,128)(2,1)S(1)}, u32[]{:S(2)}, u32[]{:S(2)}) collective-permute-start(bf16[16,3584]{1,0:T(8,128)(2,1)S(1)} %shard_map.75.refs_0_), channel_id=1, source_target_pairs={{0,2},{2,0},{4,6},{6,4},{8,10},{10,8},{12,14},{14,12},{16,18},{18,... | collective-permute-start | bytes 344072 | tf_op jit(solution)/shard_map/ppermute | solution.py:164
  14.6 7.9 %collective-permute-start.6 = (bf16[16,3584]{1,0:T(8,128)(2,1)S(1)}, bf16[16,3584]{1,0:T(8,128)(2,1)S(1)}, u32[]{:S(2)}, u32[]{:S(2)}) collective-permute-start(bf16[16,3584]{1,0:T(8,128)(2,1)S(1)} %shard_map.76.refs_4_), channel_id=1, source_target_pairs={{0,2},{2,0},{4,6},{6,4},{8,10},{10,8},{12,14},{14,12},{16,18},{18,... | collective-permute-start | bytes 344072 | tf_op jit(solution)/shard_map/ppermute | solution.py:164
  15.1 7.4 %collective-permute-start.2 = (bf16[16,3584]{1,0:T(8,128)(2,1)S(1)}, bf16[16,3584]{1,0:T(8,128)(2,1)S(1)}, u32[]{:S(2)}, u32[]{:S(2)}) collective-permute-start(bf16[16,3584]{1,0:T(8,128)(2,1)S(1)} %shard_map.75.refs_0_), channel_id=1, source_target_pairs={{0,4},{2,6},{4,0},{6,2},{8,12},{10,14},{12,8},{14,10},{16,20},{18,... | collective-permute-start | bytes 344072 | tf_op jit(solution)/shard_map/ppermute | solution.py:164
  17.3 5.3 %collective-permute-start.8 = (bf16[16,3584]{1,0:T(8,128)(2,1)S(1)}, bf16[16,3584]{1,0:T(8,128)(2,1)S(1)}, u32[]{:S(2)}, u32[]{:S(2)}) collective-permute-start(bf16[16,3584]{1,0:T(8,128)(2,1)S(1)} %collective-permute-done.7.refs_6_), channel_id=1, source_target_pairs={{0,2},{2,0},{4,6},{6,4},{8,10},{10,8},{12,14},{14,12},{16,18},{18,... | collective-permute-start | bytes 344072 | tf_op jit(solution)/shard_map/ppermute | solution.py:164
  18.8 5.5 %collective-permute-start.3 = (bf16[16,3584]{1,0:T(8,128)(2,1)S(1)}, bf16[16,3584]{1,0:T(8,128)(2,1)S(1)}, u32[]{:S(2)}, u32[]{:S(2)}) collective-permute-start(bf16[16,3584]{1,0:T(8,128)(2,1)S(1)} %collective-permute-done.1.refs_1_), channel_id=1, source_target_pairs={{0,4},{2,6},{4,0},{6,2},{8,12},{10,14},{12,8},{14,10},{16,20},{18,... | collective-permute-start | bytes 344072 | tf_op jit(solution)/shard_map/ppermute | solution.py:164
  25.3 6.1 %collective-permute-start.10 = (bf16[16,3584]{1,0:T(8,128)(2,1)S(1)}, bf16[16,3584]{1,0:T(8,128)(2,1)S(1)}, u32[]{:S(2)}, u32[]{:S(2)}) collective-permute-start(bf16[16,3584]{1,0:T(8,128)(2,1)S(1)} %get-tuple-element.36), channel_id=1, source_target_pairs={{0,4},{2,6},{4,0},{6,2},{8,12},{10,14},{12,8},{14,10},{16,20},{18,... | collective-permute-start | bytes 344072 | tf_op jit(solution)/shard_map/ppermute | solution.py:164
  25.8 7.8 %collective-permute-start.14 = (bf16[16,3584]{1,0:T(8,128)(2,1)S(1)}, bf16[16,3584]{1,0:T(8,128)(2,1)S(1)}, u32[]{:S(2)}, u32[]{:S(2)}) collective-permute-start(bf16[16,3584]{1,0:T(8,128)(2,1)S(1)} %get-tuple-element.42), channel_id=1, source_target_pairs={{0,2},{2,0},{4,6},{6,4},{8,10},{10,8},{12,14},{14,12},{16,18},{18,... | collective-permute-start | bytes 344072 | tf_op jit(solution)/shard_map/ppermute | solution.py:164
  27.0 6.6 %collective-permute-start.9 = (bf16[16,3584]{1,0:T(8,128)(2,1)S(1)}, bf16[16,3584]{1,0:T(8,128)(2,1)S(1)}, u32[]{:S(2)}, u32[]{:S(2)}) collective-permute-start(bf16[16,3584]{1,0:T(8,128)(2,1)S(1)} %get-tuple-element.34), channel_id=1, source_target_pairs={{0,4},{2,6},{4,0},{6,2},{8,12},{10,14},{12,8},{14,10},{16,20},{18,... | collective-permute-start | bytes 344072 | tf_op jit(solution)/shard_map/ppermute | solution.py:164
  31.4 4.9 %collective-permute-start.11 = (bf16[16,3584]{1,0:T(8,128)(2,1)S(1)}, bf16[16,3584]{1,0:T(8,128)(2,1)S(1)}, u32[]{:S(2)}, u32[]{:S(2)}) collective-permute-start(bf16[16,3584]{1,0:T(8,128)(2,1)S(1)} %shard_map.78), channel_id=1, source_target_pairs={{0,2},{2,0},{4,6},{6,4},{8,10},{10,8},{12,14},{14,12},{16,18},{18,... | collective-permute-start | bytes 344072 | tf_op jit(solution)/shard_map/ppermute | solution.py:164
  32.8 4.8 %collective-permute-start.13 = (bf16[16,3584]{1,0:T(8,128)(2,1)S(1)}, bf16[16,3584]{1,0:T(8,128)(2,1)S(1)}, u32[]{:S(2)}, u32[]{:S(2)}) collective-permute-start(bf16[16,3584]{1,0:T(8,128)(2,1)S(1)} %get-tuple-element.40), channel_id=1, source_target_pairs={{0,2},{2,0},{4,6},{6,4},{8,10},{10,8},{12,14},{14,12},{16,18},{18,... | collective-permute-start | bytes 344072 | tf_op jit(solution)/shard_map/ppermute | solution.py:164
  33.6 4.9 %collective-permute-start.15 = (bf16[16,3584]{1,0:T(8,128)(2,1)S(1)}, bf16[16,3584]{1,0:T(8,128)(2,1)S(1)}, u32[]{:S(2)}, u32[]{:S(2)}) collective-permute-start(bf16[16,3584]{1,0:T(8,128)(2,1)S(1)} %shard_map.80), channel_id=1, source_target_pairs={{0,4},{2,6},{4,0},{6,2},{8,12},{10,14},{12,8},{14,10},{16,20},{18,... | collective-permute-start | bytes 344072 | tf_op jit(solution)/shard_map/ppermute | solution.py:164
  36.3 4.6 %collective-permute-start.12 = (bf16[8,3584]{1,0:T(8,128)(2,1)S(1)}, bf16[8,3584]{1,0:T(8,128)(2,1)S(1)}, u32[]{:S(2)}, u32[]{:S(2)}) collective-permute-start(bf16[8,3584]{1,0:T(8,128)(2,1)S(1)} %get-tuple-element.38), channel_id=1, source_target_pairs={{0,8},{2,10},{4,12},{6,14},{8,0},{10,2},{12,4},{14,6},{16,24},{18,... | collective-permute-start | bytes 172040 | tf_op jit(solution)/shard_map/ppermute | solution.py:164
  38.5 5.2 %collective-permute-start.16 = (bf16[8,3584]{1,0:T(8,128)(2,1)S(1)}, bf16[8,3584]{1,0:T(8,128)(2,1)S(1)}, u32[]{:S(2)}, u32[]{:S(2)}) collective-permute-start(bf16[8,3584]{1,0:T(8,128)(2,1)S(1)} %get-tuple-element.43), channel_id=1, source_target_pairs={{0,16},{2,18},{4,20},{6,22},{8,24},{10,26},{12,28},{14,30},{16,0},... | collective-permute-start | bytes 172040 | tf_op jit(solution)/shard_map/ppermute | solution.py:164
  39.2 6.0 %collective-permute-start.17 = (bf16[8,3584]{1,0:T(8,128)(2,1)S(1)}, bf16[8,3584]{1,0:T(8,128)(2,1)S(1)}, u32[]{:S(2)}, u32[]{:S(2)}) collective-permute-start(bf16[8,3584]{1,0:T(8,128)(2,1)S(1)} %get-tuple-element.44), channel_id=1, source_target_pairs={{0,24},{2,26},{4,28},{6,30},{8,16},{10,18},{12,20},{14,22},{16,8},... | collective-permute-start | bytes 172040 | tf_op jit(solution)/shard_map/ppermute | solution.py:164

commit v4 on v3

--- a/solution.py
+++ b/solution.py
@@ -105,8 +105,8 @@
     second.wait()
 
 
-def stack_kernel(*refs):
-    refs[-1][...] = stack(refs[:-1]).astype(jnp.bfloat16)
+def stack_kernel(count, *refs):
+    refs[-1][...] = stack(refs[:count]).astype(jnp.bfloat16)
 
 
 def expert_kernel(count, *refs):
@@ -155,10 +155,9 @@
     tok_count, width = tokens.shape
     capacity = tok_count * expert_ids.shape[1] // slot_count
     slots = slot_count * capacity
-    near, far = range(slot_count // 2), range(slot_count // 2, slot_count)
     bf16 = jnp.bfloat16
     chunk = jax.ShapeDtypeStruct((capacity, width), bf16)
-    half = jax.ShapeDtypeStruct((slots // 2, width), bf16)
+    block = jax.ShapeDtypeStruct((slots, width), bf16)
 
     def swap(value, offset):
         return lax.ppermute(value, "expert", [(e, e ^ offset) for e in range(n_devices)])
@@ -194,45 +193,17 @@
         [pltpu.SemaphoreType.DMA((2,))],
         2 * (w_in.size + w_out.size),
     )
-
-    own = [local(stack_kernel, [chunks[d] for d in part], half) for part in (near, far)]
-    held = [own] + [[None, None] for _ in range(1, group_size)]
-    square = group_size == 4
-    for h in range(2):
-        for q in (1, 2) if square else range(1, group_size):
-            held[q][h] = swap(own[h], q)
-    if square:
-        held[3] = [swap(held[1][0], 2), swap(held[2][1], 1)]
-
+    own = local(functools.partial(stack_kernel, slot_count), chunks + [terms], block)
+    held = [own if q == 0 else swap(own, q) for q in range(group_size)]
     result = local(
-        functools.partial(expert_kernel, 2 * group_size),
-        [held[q][h] for h in range(2) for q in range(group_size)] + [w_in, w_out],
-        [half] * (2 * group_size),
+        functools.partial(expert_kernel, group_size),
+        held + [w_in, w_out],
+        [block] * group_size,
         40 * MIB,
     )
-    near_sent, far_sent = result[:group_size], result[group_size:]
-    if square:
-        far_cross, near_cross = swap(far_sent[3], 1), swap(near_sent[3], 2)
-        far_terms = [
-            far_sent[0],
-            swap(far_sent[1], 1),
-            swap(local(functools.partial(sum_kernel, 2), [far_sent[2], far_cross], [half])[0], 2),
-        ]
-        near_terms = [
-            near_sent[0],
-            swap(near_sent[2], 2),
-            swap(local(functools.partial(sum_kernel, 2), [near_sent[1], near_cross], [half])[0], 1),
-        ]
-    else:
-        far_terms = [v if q == 0 else swap(v, q) for q, v in enumerate(far_sent)]
-        near_terms = [v if q == 0 else swap(v, q) for q, v in enumerate(near_sent)]
-    summed = [
-        local(functools.partial(sum_kernel, len(t)), t, [chunk] * (slot_count // 2))
-        for t in (near_terms, far_terms)
-    ]
-    returned = [
-        v if d == 0 else swap(v, d * group_size) for d, v in enumerate(summed[0] + summed[1])
-    ]
+    result = [v if q == 0 else swap(v, q) for q, v in enumerate(result)]
+    summed = local(functools.partial(sum_kernel, group_size), result, [chunk] * slot_count)
+    returned = [v if d == 0 else swap(v, d * group_size) for d, v in enumerate(summed)]
     return local(
         combine_kernel, [terms] + returned, jax.ShapeDtypeStruct((tok_count, width), bf16)
     )

time: 46.2 us -> 47.9 us (1.037)
  waiting for transfers between devices: 19.3 us -> 24.6 us
  starting transfers between devices: 20.7 us -> 17.2 us
    ppermute x18 -> x12, waiting for transfers between devices: 19.3 us -> 24.6 us  [swap(): lax.ppermute(value, 'expert', [(e, e ^ offset) for e in range(n_devices)])]
    ppermute x18 -> x12, starting transfers between devices: 20.7 us -> 17.2 us  [swap(): lax.ppermute(value, 'expert', [(e, e ^ offset) for e in range(n_devices)])]
    pallas_call x10 -> x6, Pallas kernels: 5.87 us -> 5.84 us  [call(): pl.pallas_call(kernel, out_shape=outs, in_specs=in_specs, out_specs=jax.t...]
  transfers between devices with their start and end apart: 18 -> 12, of which waited for: 10 -> 9; matrix products, arithmetic and copies ran while one was open for 0% -> 0% of each run, Pallas kernels for 6% -> 5%
where the time goes in v4:
time: 47.9 us; the launch traced here: 47.8 us
  waiting for transfers between devices  24.6 us (51%)
  starting transfers between devices  17.2 us (36%)
  Pallas kernels  5.84 us (12%)
    ppermute x12, waiting for transfers between devices, swap(): lax.ppermute(value, 'expert', [(e, e ^ offset) for e in range(n_devices)])  24.6 us
    ppermute x12, starting transfers between devices, swap(): lax.ppermute(value, 'expert', [(e, e ^ offset) for e in range(n_devices)])  17.2 us
    pallas_call x6, Pallas kernels, call(): pl.pallas_call(kernel, out_shape=outs, in_specs=in_specs, out_specs=jax.t...  5.84 us
  transfers between devices with their start and end apart: 12, of which 9 were waited for; matrix products, arithmetic and copies ran while one was open for 0% of the time, Pallas kernels for 5%

profile of v4, /device:TPU:0, one launch (start us, length us, event | category | flops | bytes accessed | tf_op | source)
XLA Modules:
  0.0 47.8 jit_solution(9059980345907404305)
XLA Ops:
  0.0 1.2 %shard_map.73 = (bf16[8,3584]{1,0:T(8,128)(2,1)S(1)}, bf16[8,3584]{1,0:T(8,128)(2,1)S(1)}, bf16[8,3584]{1,0:T(8,128)(2,1)S(1)}, bf16[8,3584]{1,0:T(8,128)(2,1)S(1)}, f32[32,16]{1,0:T(8,128)S(1)}) custom-call(s32[4]{0:T(128)} %refs_0_.1, s32[2,16]{1,0:T(2,128)} %bitcast.3, s32[2,16]{1,0:T(2,128)} %bitcast.4, f32[2,16]{1,0:T(2,128)} %bitcast.5, ...), custom_call_target="tpu_custom_call" | custom-call | tf_op jit(solution)/shard_map/pallas_call | solution.py:138
  1.2 3.1 %collective-permute-start = (bf16[8,3584]{1,0:T(8,128)(2,1)S(1)}, bf16[8,3584]{1,0:T(8,128)(2,1)S(1)}, u32[]{:S(2)}, u32[]{:S(2)}) collective-permute-start(bf16[8,3584]{1,0:T(8,128)(2,1)S(1)} %get-tuple-element.24), channel_id=1, source_target_pairs={{0,8},{2,10},{4,12},{6,14},{8,0},{10,2},{12,4},{14,6},{16,24},{18,... | collective-permute-start | bytes 172040 | tf_op jit(solution)/shard_map/ppermute | solution.py:163
  4.3 2.6 %collective-permute-start.1 = (bf16[8,3584]{1,0:T(8,128)(2,1)S(1)}, bf16[8,3584]{1,0:T(8,128)(2,1)S(1)}, u32[]{:S(2)}, u32[]{:S(2)}) collective-permute-start(bf16[8,3584]{1,0:T(8,128)(2,1)S(1)} %get-tuple-element.25), channel_id=1, source_target_pairs={{0,16},{2,18},{4,20},{6,22},{8,24},{10,26},{12,28},{14,30},{16,0},... | collective-permute-start | bytes 172040 | tf_op jit(solution)/shard_map/ppermute | solution.py:163
  6.9 0.0 collective-permute-start.2
  6.9 2.6 %shard_map.74 = (bf16[2,3584,256]{2,1,0:T(8,128)(2,1)S(1)}, bf16[256,3584]{1,0:T(8,128)(2,1)S(1)}, bf16[48,32]{1,0:T(8,128)(2,1)S(1)}) custom-call(bf16[2,3584,256]{2,1,0:T(8,128)(2,1)} %w_in.1, bf16[256,3584]{1,0:T(8,128)(2,1)} %w_out.1, f32[32,16]{1,0:T(8,128)S(1)} %get-tuple-element.21.combine), custom_call_target="tpu_custom_call" | custom-call | bytes 5505024 | tf_op jit(solution)/shard_map/pallas_call | solution.py:138
  9.5 0.0 collective-permute-done.refs_1_
  9.5 0.9 %collective-permute-done.1.refs_2_ = bf16[8,3584]{1,0:T(8,128)(2,1)S(1)} collective-permute-done((bf16[8,3584]{1,0:T(8,128)(2,1)S(1)}, bf16[8,3584]{1,0:T(8,128)(2,1)S(1)}, u32[]{:S(2)}, u32[]{:S(2)}) %collective-permute-start.1) | collective-permute-done | bytes 57376 | tf_op jit(solution)/shard_map/ppermute | solution.py:163
  10.5 2.4 %collective-permute-done.2.refs_3_ = bf16[8,3584]{1,0:T(8,128)(2,1)S(1)} collective-permute-done((bf16[8,3584]{1,0:T(8,128)(2,1)S(1)}, bf16[8,3584]{1,0:T(8,128)(2,1)S(1)}, u32[]{:S(2)}, u32[]{:S(2)}) %collective-permute-start.2) | collective-permute-done | bytes 57376 | tf_op jit(solution)/shard_map/ppermute | solution.py:163
  12.9 2.5 %collective-permute-start.5 = (bf16[32,3584]{1,0:T(8,128)(2,1)S(1)}, bf16[32,3584]{1,0:T(8,128)(2,1)S(1)}, u32[]{:S(2)}, u32[]{:S(2)}) collective-permute-start(bf16[32,3584]{1,0:T(8,128)(2,1)S(1)} %shard_map.75.refs_0_), channel_id=1, source_target_pairs={{0,6},{2,4},{4,2},{6,0},{8,14},{10,12},{12,10},{14,8},{16,22},{18,... | collective-permute-start | bytes 688136 | tf_op jit(solution)/shard_map/ppermute | solution.py:163
  15.4 0.5 %collective-permute-start.4 = (bf16[32,3584]{1,0:T(8,128)(2,1)S(1)}, bf16[32,3584]{1,0:T(8,128)(2,1)S(1)}, u32[]{:S(2)}, u32[]{:S(2)}) collective-permute-start(bf16[32,3584]{1,0:T(8,128)(2,1)S(1)} %shard_map.75.refs_0_), channel_id=1, source_target_pairs={{0,4},{2,6},{4,0},{6,2},{8,12},{10,14},{12,8},{14,10},{16,20},{18,... | collective-permute-start | bytes 688136 | tf_op jit(solution)/shard_map/ppermute | solution.py:163
  15.9 0.5 %collective-permute-start.3 = (bf16[32,3584]{1,0:T(8,128)(2,1)S(1)}, bf16[32,3584]{1,0:T(8,128)(2,1)S(1)}, u32[]{:S(2)}, u32[]{:S(2)}) collective-permute-start(bf16[32,3584]{1,0:T(8,128)(2,1)S(1)} %shard_map.75.refs_0_), channel_id=1, source_target_pairs={{0,2},{2,0},{4,6},{6,4},{8,10},{10,8},{12,14},{14,12},{16,18},{18,... | collective-permute-start | bytes 688136 | tf_op jit(solution)/shard_map/ppermute | solution.py:163
  16.4 5.6 %collective-permute-done.5.refs_3_ = bf16[32,3584]{1,0:T(8,128)(2,1)S(1)} collective-permute-done((bf16[32,3584]{1,0:T(8,128)(2,1)S(1)}, bf16[32,3584]{1,0:T(8,128)(2,1)S(1)}, u32[]{:S(2)}, u32[]{:S(2)}) %collective-permute-start.5) | collective-permute-done | bytes 229408 | tf_op jit(solution)/shard_map/ppermute | solution.py:163
  22.1 2.4 %collective-permute-done.4.refs_2_ = bf16[32,3584]{1,0:T(8,128)(2,1)S(1)} collective-permute-done((bf16[32,3584]{1,0:T(8,128)(2,1)S(1)}, bf16[32,3584]{1,0:T(8,128)(2,1)S(1)}, u32[]{:S(2)}, u32[]{:S(2)}) %collective-permute-start.4) | collective-permute-done | bytes 229408 | tf_op jit(solution)/shard_map/ppermute | solution.py:163
  24.5 0.1 collective-permute-done.3.refs_1_
  24.6 1.0 %shard_map.76 = (bf16[32,3584]{1,0:T(8,128)(2,1)S(1)}, bf16[32,3584]{1,0:T(8,128)(2,1)S(1)}, bf16[32,3584]{1,0:T(8,128)(2,1)S(1)}, bf16[32,3584]{1,0:T(8,128)(2,1)S(1)}) custom-call(bf16[32,3584]{1,0:T(8,128)(2,1)S(1)} %shard_map.75.refs_0_, bf16[32,3584]{1,0:T(8,128)(2,1)S(1)} %collective-permute-done.3.refs_1_, ...), custom_call_target="tpu_custom_call" | custom-call | tf_op jit(solution)/shard_map/pallas_call | solution.py:138
  25.6 1.6 %collective-permute-start.6 = (bf16[32,3584]{1,0:T(8,128)(2,1)S(1)}, bf16[32,3584]{1,0:T(8,128)(2,1)S(1)}, u32[]{:S(2)}, u32[]{:S(2)}) collective-permute-start(bf16[32,3584]{1,0:T(8,128)(2,1)S(1)} %get-tuple-element.30), channel_id=1, source_target_pairs={{0,2},{2,0},{4,6},{6,4},{8,10},{10,8},{12,14},{14,12},{16,18},{18,... | collective-permute-start | bytes 688136 | tf_op jit(solution)/shard_map/ppermute | solution.py:163
  27.2 0.7 %collective-permute-start.7 = (bf16[32,3584]{1,0:T(8,128)(2,1)S(1)}, bf16[32,3584]{1,0:T(8,128)(2,1)S(1)}, u32[]{:S(2)}, u32[]{:S(2)}) collective-permute-start(bf16[32,3584]{1,0:T(8,128)(2,1)S(1)} %get-tuple-element.31), channel_id=1, source_target_pairs={{0,4},{2,6},{4,0},{6,2},{8,12},{10,14},{12,8},{14,10},{16,20},{18,... | collective-permute-start | bytes 688136 | tf_op jit(solution)/shard_map/ppermute | solution.py:163
  27.9 1.3 %collective-permute-start.8 = (bf16[32,3584]{1,0:T(8,128)(2,1)S(1)}, bf16[32,3584]{1,0:T(8,128)(2,1)S(1)}, u32[]{:S(2)}, u32[]{:S(2)}) collective-permute-start(bf16[32,3584]{1,0:T(8,128)(2,1)S(1)} %get-tuple-element.32), channel_id=1, source_target_pairs={{0,6},{2,4},{4,2},{6,0},{8,14},{10,12},{12,10},{14,8},{16,22},{18,... | collective-permute-start | bytes 688136 | tf_op jit(solution)/shard_map/ppermute | solution.py:163
  29.2 5.1 %collective-permute-done.6.refs_1_ = bf16[32,3584]{1,0:T(8,128)(2,1)S(1)} collective-permute-done((bf16[32,3584]{1,0:T(8,128)(2,1)S(1)}, bf16[32,3584]{1,0:T(8,128)(2,1)S(1)}, u32[]{:S(2)}, u32[]{:S(2)}) %collective-permute-start.6) | collective-permute-done | bytes 229408 | tf_op jit(solution)/shard_map/ppermute | solution.py:163
  34.2 4.4 %collective-permute-done.7.refs_2_ = bf16[32,3584]{1,0:T(8,128)(2,1)S(1)} collective-permute-done((bf16[32,3584]{1,0:T(8,128)(2,1)S(1)}, bf16[32,3584]{1,0:T(8,128)(2,1)S(1)}, u32[]{:S(2)}, u32[]{:S(2)}) %collective-permute-start.7) | collective-permute-done | bytes 229408 | tf_op jit(solution)/shard_map/ppermute | solution.py:163
  38.6 0.0 collective-permute-done.8.refs_3_
  38.6 0.1 shard_map.77
  38.8 0.1 collective-permute-start.9
  38.8 1.9 %collective-permute-start.10 = (bf16[8,3584]{1,0:T(8,128)(2,1)S(1)}, bf16[8,3584]{1,0:T(8,128)(2,1)S(1)}, u32[]{:S(2)}, u32[]{:S(2)}) collective-permute-start(bf16[8,3584]{1,0:T(8,128)(2,1)S(1)} %get-tuple-element.35), channel_id=1, source_target_pairs={{0,16},{2,18},{4,20},{6,22},{8,24},{10,26},{12,28},{14,30},{16,0},... | collective-permute-start | bytes 172040 | tf_op jit(solution)/shard_map/ppermute | solution.py:163
  40.8 2.4 %collective-permute-start.11 = (bf16[8,3584]{1,0:T(8,128)(2,1)S(1)}, bf16[8,3584]{1,0:T(8,128)(2,1)S(1)}, u32[]{:S(2)}, u32[]{:S(2)}) collective-permute-start(bf16[8,3584]{1,0:T(8,128)(2,1)S(1)} %get-tuple-element.36), channel_id=1, source_target_pairs={{0,24},{2,26},{4,28},{6,30},{8,16},{10,18},{12,20},{14,22},{16,8},... | collective-permute-start | bytes 172040 | tf_op jit(solution)/shard_map/ppermute | solution.py:163
  43.2 0.0 collective-permute-done.9.refs_1_
  43.2 1.6 %collective-permute-done.10.refs_2_ = bf16[8,3584]{1,0:T(8,128)(2,1)S(1)} collective-permute-done((bf16[8,3584]{1,0:T(8,128)(2,1)S(1)}, bf16[8,3584]{1,0:T(8,128)(2,1)S(1)}, u32[]{:S(2)}, u32[]{:S(2)}) %collective-permute-start.10) | collective-permute-done | bytes 57376 | tf_op jit(solution)/shard_map/ppermute | solution.py:163
  44.9 2.0 %collective-permute-done.11.refs_3_ = bf16[8,3584]{1,0:T(8,128)(2,1)S(1)} collective-permute-done((bf16[8,3584]{1,0:T(8,128)(2,1)S(1)}, bf16[8,3584]{1,0:T(8,128)(2,1)S(1)}, u32[]{:S(2)}, u32[]{:S(2)}) %collective-permute-start.11) | collective-permute-done | bytes 57376 | tf_op jit(solution)/shard_map/ppermute | solution.py:163
  46.9 0.9 %shard_map.78 = bf16[16,3584]{1,0:T(8,128)(2,1)} custom-call(bf16[48,32]{1,0:T(8,128)(2,1)S(1)} %get-tuple-element.22.refs_4_.terms, bf16[8,3584]{1,0:T(8,128)(2,1)S(1)} %get-tuple-element.33.refs_0_, bf16[8,3584]{1,0:T(8,128)(2,1)S(1)} %collective-permute-done.9.refs_1_, bf16[8,3584]{1,0:T(8,128)(2,1)S(1)} %collective-permute-done.10.refs_2_, ...), custom_call_target="tpu_custom_call" | custom-call | tf_op jit(solution)/shard_map/pallas_call | solution.py:138
  (1 shorter events, 0.0 us)
Async XLA Ops:
  1.2 8.3 %collective-permute-start = (bf16[8,3584]{1,0:T(8,128)(2,1)S(1)}, bf16[8,3584]{1,0:T(8,128)(2,1)S(1)}, u32[]{:S(2)}, u32[]{:S(2)}) collective-permute-start(bf16[8,3584]{1,0:T(8,128)(2,1)S(1)} %get-tuple-element.24), channel_id=1, source_target_pairs={{0,8},{2,10},{4,12},{6,14},{8,0},{10,2},{12,4},{14,6},{16,24},{18,... | collective-permute-start | bytes 172040 | tf_op jit(solution)/shard_map/ppermute | solution.py:163
  4.3 6.2 %collective-permute-start.1 = (bf16[8,3584]{1,0:T(8,128)(2,1)S(1)}, bf16[8,3584]{1,0:T(8,128)(2,1)S(1)}, u32[]{:S(2)}, u32[]{:S(2)}) collective-permute-start(bf16[8,3584]{1,0:T(8,128)(2,1)S(1)} %get-tuple-element.25), channel_id=1, source_target_pairs={{0,16},{2,18},{4,20},{6,22},{8,24},{10,26},{12,28},{14,30},{16,0},... | collective-permute-start | bytes 172040 | tf_op jit(solution)/shard_map/ppermute | solution.py:163
  6.9 6.0 %collective-permute-start.2 = (bf16[8,3584]{1,0:T(8,128)(2,1)S(1)}, bf16[8,3584]{1,0:T(8,128)(2,1)S(1)}, u32[]{:S(2)}, u32[]{:S(2)}) collective-permute-start(bf16[8,3584]{1,0:T(8,128)(2,1)S(1)} %get-tuple-element.26), channel_id=1, source_target_pairs={{0,24},{2,26},{4,28},{6,30},{8,16},{10,18},{12,20},{14,22},{16,8},... | collective-permute-start | bytes 172040 | tf_op jit(solution)/shard_map/ppermute | solution.py:163
  12.9 9.2 %collective-permute-start.5 = (bf16[32,3584]{1,0:T(8,128)(2,1)S(1)}, bf16[32,3584]{1,0:T(8,128)(2,1)S(1)}, u32[]{:S(2)}, u32[]{:S(2)}) collective-permute-start(bf16[32,3584]{1,0:T(8,128)(2,1)S(1)} %shard_map.75.refs_0_), channel_id=1, source_target_pairs={{0,6},{2,4},{4,2},{6,0},{8,14},{10,12},{12,10},{14,8},{16,22},{18,... | collective-permute-start | bytes 688136 | tf_op jit(solution)/shard_map/ppermute | solution.py:163
  15.4 9.1 %collective-permute-start.4 = (bf16[32,3584]{1,0:T(8,128)(2,1)S(1)}, bf16[32,3584]{1,0:T(8,128)(2,1)S(1)}, u32[]{:S(2)}, u32[]{:S(2)}) collective-permute-start(bf16[32,3584]{1,0:T(8,128)(2,1)S(1)} %shard_map.75.refs_0_), channel_id=1, source_target_pairs={{0,4},{2,6},{4,0},{6,2},{8,12},{10,14},{12,8},{14,10},{16,20},{18,... | collective-permute-start | bytes 688136 | tf_op jit(solution)/shard_map/ppermute | solution.py:163
  15.9 8.7 %collective-permute-start.3 = (bf16[32,3584]{1,0:T(8,128)(2,1)S(1)}, bf16[32,3584]{1,0:T(8,128)(2,1)S(1)}, u32[]{:S(2)}, u32[]{:S(2)}) collective-permute-start(bf16[32,3584]{1,0:T(8,128)(2,1)S(1)} %shard_map.75.refs_0_), channel_id=1, source_target_pairs={{0,2},{2,0},{4,6},{6,4},{8,10},{10,8},{12,14},{14,12},{16,18},{18,... | collective-permute-start | bytes 688136 | tf_op jit(solution)/shard_map/ppermute | solution.py:163
  25.6 8.6 %collective-permute-start.6 = (bf16[32,3584]{1,0:T(8,128)(2,1)S(1)}, bf16[32,3584]{1,0:T(8,128)(2,1)S(1)}, u32[]{:S(2)}, u32[]{:S(2)}) collective-permute-start(bf16[32,3584]{1,0:T(8,128)(2,1)S(1)} %get-tuple-element.30), channel_id=1, source_target_pairs={{0,2},{2,0},{4,6},{6,4},{8,10},{10,8},{12,14},{14,12},{16,18},{18,... | collective-permute-start | bytes 688136 | tf_op jit(solution)/shard_map/ppermute | solution.py:163
  27.2 11.5 %collective-permute-start.7 = (bf16[32,3584]{1,0:T(8,128)(2,1)S(1)}, bf16[32,3584]{1,0:T(8,128)(2,1)S(1)}, u32[]{:S(2)}, u32[]{:S(2)}) collective-permute-start(bf16[32,3584]{1,0:T(8,128)(2,1)S(1)} %get-tuple-element.31), channel_id=1, source_target_pairs={{0,4},{2,6},{4,0},{6,2},{8,12},{10,14},{12,8},{14,10},{16,20},{18,... | collective-permute-start | bytes 688136 | tf_op jit(solution)/shard_map/ppermute | solution.py:163
  27.9 10.8 %collective-permute-start.8 = (bf16[32,3584]{1,0:T(8,128)(2,1)S(1)}, bf16[32,3584]{1,0:T(8,128)(2,1)S(1)}, u32[]{:S(2)}, u32[]{:S(2)}) collective-permute-start(bf16[32,3584]{1,0:T(8,128)(2,1)S(1)} %get-tuple-element.32), channel_id=1, source_target_pairs={{0,6},{2,4},{4,2},{6,0},{8,14},{10,12},{12,10},{14,8},{16,22},{18,... | collective-permute-start | bytes 688136 | tf_op jit(solution)/shard_map/ppermute | solution.py:163
  38.8 4.5 %collective-permute-start.9 = (bf16[8,3584]{1,0:T(8,128)(2,1)S(1)}, bf16[8,3584]{1,0:T(8,128)(2,1)S(1)}, u32[]{:S(2)}, u32[]{:S(2)}) collective-permute-start(bf16[8,3584]{1,0:T(8,128)(2,1)S(1)} %get-tuple-element.34), channel_id=1, source_target_pairs={{0,8},{2,10},{4,12},{6,14},{8,0},{10,2},{12,4},{14,6},{16,24},{18,... | collective-permute-start | bytes 172040 | tf_op jit(solution)/shard_map/ppermute | solution.py:163
  38.8 6.0 %collective-permute-start.10 = (bf16[8,3584]{1,0:T(8,128)(2,1)S(1)}, bf16[8,3584]{1,0:T(8,128)(2,1)S(1)}, u32[]{:S(2)}, u32[]{:S(2)}) collective-permute-start(bf16[8,3584]{1,0:T(8,128)(2,1)S(1)} %get-tuple-element.35), channel_id=1, source_target_pairs={{0,16},{2,18},{4,20},{6,22},{8,24},{10,26},{12,28},{14,30},{16,0},... | collective-permute-start | bytes 172040 | tf_op jit(solution)/shard_map/ppermute | solution.py:163
  40.8 6.1 %collective-permute-start.11 = (bf16[8,3584]{1,0:T(8,128)(2,1)S(1)}, bf16[8,3584]{1,0:T(8,128)(2,1)S(1)}, u32[]{:S(2)}, u32[]{:S(2)}) collective-permute-start(bf16[8,3584]{1,0:T(8,128)(2,1)S(1)} %get-tuple-element.36), channel_id=1, source_target_pairs={{0,24},{2,26},{4,28},{6,30},{8,16},{10,18},{12,20},{14,22},{16,8},... | collective-permute-start | bytes 172040 | tf_op jit(solution)/shard_map/ppermute | solution.py:163

commit v5 on v4

--- a/solution.py
+++ b/solution.py
@@ -84,10 +84,15 @@
 
 
 def prepare_kernel(w_in, w_out, combine, w_in_held, w_out_held, terms_out, sems):
-    first = pltpu.make_async_copy(w_in, w_in_held, sems.at[0])
-    second = pltpu.make_async_copy(w_out, w_out_held, sems.at[1])
-    first.start()
-    second.start()
+    half = w_in.shape[1] // 2
+    rows = [pl.ds(0, half), pl.ds(half, half)]
+    copies = [
+        pltpu.make_async_copy(w_in.at[i, r], w_in_held.at[i, r], sems.at[2 * i + j])
+        for i in range(2)
+        for j, r in enumerate(rows)
+    ] + [pltpu.make_async_copy(w_out, w_out_held, sems.at[4])]
+    for c in copies:
+        c.start()
     rest = combine[...]
     slots = rest.shape[0]
     same = (iota((slots, slots), 0) == iota((slots, slots), 1)).astype(jnp.float32)
@@ -101,8 +106,8 @@
             )
         )
     terms_out[...] = jnp.concatenate(terms, axis=0).astype(jnp.bfloat16)
-    first.wait()
-    second.wait()
+    for c in copies:
+        c.wait()
 
 
 def stack_kernel(count, *refs):
@@ -155,12 +160,22 @@
     tok_count, width = tokens.shape
     capacity = tok_count * expert_ids.shape[1] // slot_count
     slots = slot_count * capacity
+    square = group_size == 4
     bf16 = jnp.bfloat16
     chunk = jax.ShapeDtypeStruct((capacity, width), bf16)
     block = jax.ShapeDtypeStruct((slots, width), bf16)
 
     def swap(value, offset):
         return lax.ppermute(value, "expert", [(e, e ^ offset) for e in range(n_devices)])
+
+    def turn(value, even, odd):
+        parts = lax.axis_size("dp")
+        pairs = [
+            (e * parts + part, (e ^ (odd if part % 2 else even)) * parts + part)
+            for e in range(n_devices)
+            for part in range(parts)
+        ]
+        return lax.ppermute(value, ("expert", "dp"), pairs)
 
     def local(kernel, inputs, outs, limit=16 * MIB):
         return call(kernel, inputs, [VMEM] * len(inputs), outs, limit)
@@ -190,19 +205,30 @@
             jax.ShapeDtypeStruct((3 * tok_count, slots), bf16),
         ],
         16 * MIB,
-        [pltpu.SemaphoreType.DMA((2,))],
+        [pltpu.SemaphoreType.DMA((5,))],
         2 * (w_in.size + w_out.size),
     )
     own = local(functools.partial(stack_kernel, slot_count), chunks + [terms], block)
-    held = [own if q == 0 else swap(own, q) for q in range(group_size)]
+    if square:
+        first, second = turn(own, 1, 2), turn(own, 2, 1)
+        held = [own, first, second, turn(first, 2, 1)]
+    else:
+        held = [own if q == 0 else swap(own, q) for q in range(group_size)]
     result = local(
         functools.partial(expert_kernel, group_size),
         held + [w_in, w_out],
         [block] * group_size,
         40 * MIB,
     )
-    result = [v if q == 0 else swap(v, q) for q, v in enumerate(result)]
-    summed = local(functools.partial(sum_kernel, group_size), result, [chunk] * slot_count)
+    if square:
+        mine, first, second, cross = result
+        cross = turn(cross, 1, 2)
+        first = turn(first, 1, 2)
+        second = local(functools.partial(sum_kernel, 2), [second, cross], [block])[0]
+        result = [mine, first, turn(second, 2, 1)]
+    else:
+        result = [v if q == 0 else swap(v, q) for q, v in enumerate(result)]
+    summed = local(functools.partial(sum_kernel, len(result)), result, [chunk] * slot_count)
     returned = [v if d == 0 else swap(v, d * group_size) for d, v in enumerate(summed)]
     return local(
         combine_kernel, [terms] + returned, jax.ShapeDtypeStruct((tok_count, width), bf16)

time: 47.9 us -> 52.3 us (1.092)
  waiting for transfers between devices: 24.6 us -> 30.8 us
  starting transfers between devices: 17.2 us -> 15.4 us
    ppermute x0 -> x6, waiting for transfers between devices: none -> 24 us  [turn(): return lax.ppermute(value, ('expert', 'dp'), pairs)]
    ppermute x12 -> x6, waiting for transfers between devices: 24.6 us -> 6.77 us  [swap(): lax.ppermute(value, 'expert', [(e, e ^ offset) for e in range(n_devices)])]
    ppermute x12 -> x6, starting transfers between devices: 17.2 us -> 10.1 us  [swap(): lax.ppermute(value, 'expert', [(e, e ^ offset) for e in range(n_devices)])]
    ppermute x0 -> x6, starting transfers between devices: none -> 5.25 us  [turn(): return lax.ppermute(value, ('expert', 'dp'), pairs)]
    pallas_call x6 -> x7, Pallas kernels: 5.84 us -> 5.9 us  [call(): pl.pallas_call(kernel, out_shape=outs, in_specs=in_specs, out_specs=jax.t...]
where the time goes in v5:
time: 52.3 us; the launch traced here: 52.1 us
  waiting for transfers between devices  30.8 us (59%)
  starting transfers between devices  15.4 us (29%)
  Pallas kernels  5.9 us (11%)
    ppermute x6, waiting for transfers between devices, turn(): return lax.ppermute(value, ('expert', 'dp'), pairs)  24 us
    ppermute x6, starting transfers between devices, swap(): lax.ppermute(value, 'expert', [(e, e ^ offset) for e in range(n_devices)])  10.1 us
    ppermute x6, waiting for transfers between devices, swap(): lax.ppermute(value, 'expert', [(e, e ^ offset) for e in range(n_devices)])  6.77 us
    pallas_call x7, Pallas kernels, call(): pl.pallas_call(kernel, out_shape=outs, in_specs=in_specs, out_specs=jax.t...  5.9 us
    ppermute x6, starting transfers between devices, turn(): return lax.ppermute(value, ('expert', 'dp'), pairs)  5.25 us
  transfers between devices with their start and end apart: 12, of which 9 were waited for; matrix products, arithmetic and copies ran while one was open for 0% of the time, Pallas kernels for 5%

profile of v5, /device:TPU:0, one launch (start us, length us, event | category | flops | bytes accessed | tf_op | source)
XLA Modules:
  0.0 52.1 jit_solution(1238524589972020549)
XLA Ops:
  0.0 1.2 %shard_map.73 = (bf16[8,3584]{1,0:T(8,128)(2,1)S(1)}, bf16[8,3584]{1,0:T(8,128)(2,1)S(1)}, bf16[8,3584]{1,0:T(8,128)(2,1)S(1)}, bf16[8,3584]{1,0:T(8,128)(2,1)S(1)}, f32[32,16]{1,0:T(8,128)S(1)}) custom-call(s32[4]{0:T(128)} %refs_0_.1, s32[2,16]{1,0:T(2,128)} %bitcast.3, s32[2,16]{1,0:T(2,128)} %bitcast.4, f32[2,16]{1,0:T(2,128)} %bitcast.5, ...), custom_call_target="tpu_custom_call" | custom-call | tf_op jit(solution)/shard_map/pallas_call | solution.py:143
  1.2 3.1 %collective-permute-start = (bf16[8,3584]{1,0:T(8,128)(2,1)S(1)}, bf16[8,3584]{1,0:T(8,128)(2,1)S(1)}, u32[]{:S(2)}, u32[]{:S(2)}) collective-permute-start(bf16[8,3584]{1,0:T(8,128)(2,1)S(1)} %get-tuple-element.24), channel_id=1, source_target_pairs={{0,8},{2,10},{4,12},{6,14},{8,0},{10,2},{12,4},{14,6},{16,24},{18,... | collective-permute-start | bytes 172040 | tf_op jit(solution)/shard_map/ppermute | solution.py:169
  4.3 2.6 %collective-permute-start.1 = (bf16[8,3584]{1,0:T(8,128)(2,1)S(1)}, bf16[8,3584]{1,0:T(8,128)(2,1)S(1)}, u32[]{:S(2)}, u32[]{:S(2)}) collective-permute-start(bf16[8,3584]{1,0:T(8,128)(2,1)S(1)} %get-tuple-element.25), channel_id=1, source_target_pairs={{0,16},{2,18},{4,20},{6,22},{8,24},{10,26},{12,28},{14,30},{16,0},... | collective-permute-start | bytes 172040 | tf_op jit(solution)/shard_map/ppermute | solution.py:169
  6.9 0.0 collective-permute-start.2
  6.9 2.7 %shard_map.74 = (bf16[2,3584,256]{2,1,0:T(8,128)(2,1)S(1)}, bf16[256,3584]{1,0:T(8,128)(2,1)S(1)}, bf16[48,32]{1,0:T(8,128)(2,1)S(1)}) custom-call(bf16[2,3584,256]{2,1,0:T(8,128)(2,1)} %w_in.1, bf16[256,3584]{1,0:T(8,128)(2,1)} %w_out.1, f32[32,16]{1,0:T(8,128)S(1)} %get-tuple-element.21.combine), custom_call_target="tpu_custom_call" | custom-call | bytes 5505024 | tf_op jit(solution)/shard_map/pallas_call | solution.py:143
  9.5 0.0 collective-permute-done.refs_1_
  9.5 0.9 %collective-permute-done.1.refs_2_ = bf16[8,3584]{1,0:T(8,128)(2,1)S(1)} collective-permute-done((bf16[8,3584]{1,0:T(8,128)(2,1)S(1)}, bf16[8,3584]{1,0:T(8,128)(2,1)S(1)}, u32[]{:S(2)}, u32[]{:S(2)}) %collective-permute-start.1) | collective-permute-done | bytes 57376 | tf_op jit(solution)/shard_map/ppermute | solution.py:169
  10.5 2.4 %collective-permute-done.2.refs_3_ = bf16[8,3584]{1,0:T(8,128)(2,1)S(1)} collective-permute-done((bf16[8,3584]{1,0:T(8,128)(2,1)S(1)}, bf16[8,3584]{1,0:T(8,128)(2,1)S(1)}, u32[]{:S(2)}, u32[]{:S(2)}) %collective-permute-start.2) | collective-permute-done | bytes 57376 | tf_op jit(solution)/shard_map/ppermute | solution.py:169
  12.9 1.6 %collective-permute-start.3 = (bf16[32,3584]{1,0:T(8,128)(2,1)S(1)}, bf16[32,3584]{1,0:T(8,128)(2,1)S(1)}, u32[]{:S(2)}, u32[]{:S(2)}) collective-permute-start(bf16[32,3584]{1,0:T(8,128)(2,1)S(1)} %shard_map.75.refs_0_), channel_id=1, source_target_pairs={{0,2},{1,5},{2,0},{3,7},{4,6},{5,1},{6,4},{7,3},{8,10},{9,13},{10,... | collective-permute-start | bytes 688136 | tf_op jit(solution)/shard_map/ppermute | solution.py:178
  14.4 1.5 %collective-permute-start.4 = (bf16[32,3584]{1,0:T(8,128)(2,1)S(1)}, bf16[32,3584]{1,0:T(8,128)(2,1)S(1)}, u32[]{:S(2)}, u32[]{:S(2)}) collective-permute-start(bf16[32,3584]{1,0:T(8,128)(2,1)S(1)} %shard_map.75.refs_0_), channel_id=1, source_target_pairs={{0,4},{1,3},{2,6},{3,1},{4,0},{5,7},{6,2},{7,5},{8,12},{9,11},{10,... | collective-permute-start | bytes 688136 | tf_op jit(solution)/shard_map/ppermute | solution.py:178
  15.9 5.2 %collective-permute-done.3.refs_1_ = bf16[32,3584]{1,0:T(8,128)(2,1)S(1)} collective-permute-done((bf16[32,3584]{1,0:T(8,128)(2,1)S(1)}, bf16[32,3584]{1,0:T(8,128)(2,1)S(1)}, u32[]{:S(2)}, u32[]{:S(2)}) %collective-permute-start.3) | collective-permute-done | bytes 229408 | tf_op jit(solution)/shard_map/ppermute | solution.py:178
  21.1 0.0 collective-permute-start.5
  21.1 0.0 collective-permute-done.4.refs_2_
  21.1 7.3 %collective-permute-done.5.refs_3_ = bf16[32,3584]{1,0:T(8,128)(2,1)S(1)} collective-permute-done((bf16[32,3584]{1,0:T(8,128)(2,1)S(1)}, bf16[32,3584]{1,0:T(8,128)(2,1)S(1)}, u32[]{:S(2)}, u32[]{:S(2)}) %collective-permute-start.5) | collective-permute-done | bytes 229408 | tf_op jit(solution)/shard_map/ppermute | solution.py:178
  28.4 1.0 %shard_map.76 = (bf16[32,3584]{1,0:T(8,128)(2,1)S(1)}, bf16[32,3584]{1,0:T(8,128)(2,1)S(1)}, bf16[32,3584]{1,0:T(8,128)(2,1)S(1)}, bf16[32,3584]{1,0:T(8,128)(2,1)S(1)}) custom-call(bf16[32,3584]{1,0:T(8,128)(2,1)S(1)} %shard_map.75.refs_0_, bf16[32,3584]{1,0:T(8,128)(2,1)S(1)} %collective-permute-done.3.refs_1_, ...), custom_call_target="tpu_custom_call" | custom-call | tf_op jit(solution)/shard_map/pallas_call | solution.py:143
  29.4 1.6 %collective-permute-start.7 = (bf16[32,3584]{1,0:T(8,128)(2,1)S(1)}, bf16[32,3584]{1,0:T(8,128)(2,1)S(1)}, u32[]{:S(2)}, u32[]{:S(2)}) collective-permute-start(bf16[32,3584]{1,0:T(8,128)(2,1)S(1)} %get-tuple-element.32), channel_id=1, source_target_pairs={{0,2},{1,5},{2,0},{3,7},{4,6},{5,1},{6,4},{7,3},{8,10},{9,13},{10,... | collective-permute-start | bytes 688136 | tf_op jit(solution)/shard_map/ppermute | solution.py:178
  31.0 0.5 %collective-permute-start.6 = (bf16[32,3584]{1,0:T(8,128)(2,1)S(1)}, bf16[32,3584]{1,0:T(8,128)(2,1)S(1)}, u32[]{:S(2)}, u32[]{:S(2)}) collective-permute-start(bf16[32,3584]{1,0:T(8,128)(2,1)S(1)} %get-tuple-element.30), channel_id=1, source_target_pairs={{0,2},{1,5},{2,0},{3,7},{4,6},{5,1},{6,4},{7,3},{8,10},{9,13},{10,... | collective-permute-start | bytes 688136 | tf_op jit(solution)/shard_map/ppermute | solution.py:178
  31.5 5.5 %collective-permute-done.7.refs_1_ = bf16[32,3584]{1,0:T(8,128)(2,1)S(1)} collective-permute-done((bf16[32,3584]{1,0:T(8,128)(2,1)S(1)}, bf16[32,3584]{1,0:T(8,128)(2,1)S(1)}, u32[]{:S(2)}, u32[]{:S(2)}) %collective-permute-start.7) | collective-permute-done | bytes 229408 | tf_op jit(solution)/shard_map/ppermute | solution.py:178
  37.0 0.1 shard_map.77
  37.1 0.1 collective-permute-start.8
  37.2 2.3 %collective-permute-done.6.refs_1_ = bf16[32,3584]{1,0:T(8,128)(2,1)S(1)} collective-permute-done((bf16[32,3584]{1,0:T(8,128)(2,1)S(1)}, bf16[32,3584]{1,0:T(8,128)(2,1)S(1)}, u32[]{:S(2)}, u32[]{:S(2)}) %collective-permute-start.6) | collective-permute-done | bytes 229408 | tf_op jit(solution)/shard_map/ppermute | solution.py:178
  39.5 3.7 %collective-permute-done.8.refs_2_ = bf16[32,3584]{1,0:T(8,128)(2,1)S(1)} collective-permute-done((bf16[32,3584]{1,0:T(8,128)(2,1)S(1)}, bf16[32,3584]{1,0:T(8,128)(2,1)S(1)}, u32[]{:S(2)}, u32[]{:S(2)}) %collective-permute-start.8) | collective-permute-done | bytes 229408 | tf_op jit(solution)/shard_map/ppermute | solution.py:178
  43.2 0.1 shard_map.78
  43.3 0.1 collective-permute-start.9
  43.4 1.9 %collective-permute-start.10 = (bf16[8,3584]{1,0:T(8,128)(2,1)S(1)}, bf16[8,3584]{1,0:T(8,128)(2,1)S(1)}, u32[]{:S(2)}, u32[]{:S(2)}) collective-permute-start(bf16[8,3584]{1,0:T(8,128)(2,1)S(1)} %get-tuple-element.35), channel_id=1, source_target_pairs={{0,16},{2,18},{4,20},{6,22},{8,24},{10,26},{12,28},{14,30},{16,0},... | collective-permute-start | bytes 172040 | tf_op jit(solution)/shard_map/ppermute | solution.py:169
  45.2 2.5 %collective-permute-start.11 = (bf16[8,3584]{1,0:T(8,128)(2,1)S(1)}, bf16[8,3584]{1,0:T(8,128)(2,1)S(1)}, u32[]{:S(2)}, u32[]{:S(2)}) collective-permute-start(bf16[8,3584]{1,0:T(8,128)(2,1)S(1)} %get-tuple-element.36), channel_id=1, source_target_pairs={{0,24},{2,26},{4,28},{6,30},{8,16},{10,18},{12,20},{14,22},{16,8},... | collective-permute-start | bytes 172040 | tf_op jit(solution)/shard_map/ppermute | solution.py:169
  47.7 0.0 collective-permute-done.9.refs_1_
  47.7 0.8 %collective-permute-done.10.refs_2_ = bf16[8,3584]{1,0:T(8,128)(2,1)S(1)} collective-permute-done((bf16[8,3584]{1,0:T(8,128)(2,1)S(1)}, bf16[8,3584]{1,0:T(8,128)(2,1)S(1)}, u32[]{:S(2)}, u32[]{:S(2)}) %collective-permute-start.10) | collective-permute-done | bytes 57376 | tf_op jit(solution)/shard_map/ppermute | solution.py:169
  48.5 2.7 %collective-permute-done.11.refs_3_ = bf16[8,3584]{1,0:T(8,128)(2,1)S(1)} collective-permute-done((bf16[8,3584]{1,0:T(8,128)(2,1)S(1)}, bf16[8,3584]{1,0:T(8,128)(2,1)S(1)}, u32[]{:S(2)}, u32[]{:S(2)}) %collective-permute-start.11) | collective-permute-done | bytes 57376 | tf_op jit(solution)/shard_map/ppermute | solution.py:169
  51.2 0.9 %shard_map.79 = bf16[16,3584]{1,0:T(8,128)(2,1)} custom-call(bf16[48,32]{1,0:T(8,128)(2,1)S(1)} %get-tuple-element.22.refs_4_.terms, bf16[8,3584]{1,0:T(8,128)(2,1)S(1)} %get-tuple-element.33.refs_0_, bf16[8,3584]{1,0:T(8,128)(2,1)S(1)} %collective-permute-done.9.refs_1_, bf16[8,3584]{1,0:T(8,128)(2,1)S(1)} %collective-permute-done.10.refs_2_, ...), custom_call_target="tpu_custom_call" | custom-call | tf_op jit(solution)/shard_map/pallas_call | solution.py:143
  (1 shorter events, 0.0 us)
Async XLA Ops:
  1.2 8.3 %collective-permute-start = (bf16[8,3584]{1,0:T(8,128)(2,1)S(1)}, bf16[8,3584]{1,0:T(8,128)(2,1)S(1)}, u32[]{:S(2)}, u32[]{:S(2)}) collective-permute-start(bf16[8,3584]{1,0:T(8,128)(2,1)S(1)} %get-tuple-element.24), channel_id=1, source_target_pairs={{0,8},{2,10},{4,12},{6,14},{8,0},{10,2},{12,4},{14,6},{16,24},{18,... | collective-permute-start | bytes 172040 | tf_op jit(solution)/shard_map/ppermute | solution.py:169
  4.3 6.2 %collective-permute-start.1 = (bf16[8,3584]{1,0:T(8,128)(2,1)S(1)}, bf16[8,3584]{1,0:T(8,128)(2,1)S(1)}, u32[]{:S(2)}, u32[]{:S(2)}) collective-permute-start(bf16[8,3584]{1,0:T(8,128)(2,1)S(1)} %get-tuple-element.25), channel_id=1, source_target_pairs={{0,16},{2,18},{4,20},{6,22},{8,24},{10,26},{12,28},{14,30},{16,0},... | collective-permute-start | bytes 172040 | tf_op jit(solution)/shard_map/ppermute | solution.py:169
  6.9 6.0 %collective-permute-start.2 = (bf16[8,3584]{1,0:T(8,128)(2,1)S(1)}, bf16[8,3584]{1,0:T(8,128)(2,1)S(1)}, u32[]{:S(2)}, u32[]{:S(2)}) collective-permute-start(bf16[8,3584]{1,0:T(8,128)(2,1)S(1)} %get-tuple-element.26), channel_id=1, source_target_pairs={{0,24},{2,26},{4,28},{6,30},{8,16},{10,18},{12,20},{14,22},{16,8},... | collective-permute-start | bytes 172040 | tf_op jit(solution)/shard_map/ppermute | solution.py:169
  12.9 8.3 %collective-permute-start.3 = (bf16[32,3584]{1,0:T(8,128)(2,1)S(1)}, bf16[32,3584]{1,0:T(8,128)(2,1)S(1)}, u32[]{:S(2)}, u32[]{:S(2)}) collective-permute-start(bf16[32,3584]{1,0:T(8,128)(2,1)S(1)} %shard_map.75.refs_0_), channel_id=1, source_target_pairs={{0,2},{1,5},{2,0},{3,7},{4,6},{5,1},{6,4},{7,3},{8,10},{9,13},{10,... | collective-permute-start | bytes 688136 | tf_op jit(solution)/shard_map/ppermute | solution.py:178
  14.4 6.7 %collective-permute-start.4 = (bf16[32,3584]{1,0:T(8,128)(2,1)S(1)}, bf16[32,3584]{1,0:T(8,128)(2,1)S(1)}, u32[]{:S(2)}, u32[]{:S(2)}) collective-permute-start(bf16[32,3584]{1,0:T(8,128)(2,1)S(1)} %shard_map.75.refs_0_), channel_id=1, source_target_pairs={{0,4},{1,3},{2,6},{3,1},{4,0},{5,7},{6,2},{7,5},{8,12},{9,11},{10,... | collective-permute-start | bytes 688136 | tf_op jit(solution)/shard_map/ppermute | solution.py:178
  21.1 7.3 %collective-permute-start.5 = (bf16[32,3584]{1,0:T(8,128)(2,1)S(1)}, bf16[32,3584]{1,0:T(8,128)(2,1)S(1)}, u32[]{:S(2)}, u32[]{:S(2)}) collective-permute-start(bf16[32,3584]{1,0:T(8,128)(2,1)S(1)} %collective-permute-done.3.refs_1_), channel_id=1, source_target_pairs={{0,4},{1,3},{2,6},{3,1},{4,0},{5,7},{6,2},{7,5},{8,12},{9,11},{10,... | collective-permute-start | bytes 688136 | tf_op jit(solution)/shard_map/ppermute | solution.py:178
  29.4 7.6 %collective-permute-start.7 = (bf16[32,3584]{1,0:T(8,128)(2,1)S(1)}, bf16[32,3584]{1,0:T(8,128)(2,1)S(1)}, u32[]{:S(2)}, u32[]{:S(2)}) collective-permute-start(bf16[32,3584]{1,0:T(8,128)(2,1)S(1)} %get-tuple-element.32), channel_id=1, source_target_pairs={{0,2},{1,5},{2,0},{3,7},{4,6},{5,1},{6,4},{7,3},{8,10},{9,13},{10,... | collective-permute-start | bytes 688136 | tf_op jit(solution)/shard_map/ppermute | solution.py:178
  31.0 8.5 %collective-permute-start.6 = (bf16[32,3584]{1,0:T(8,128)(2,1)S(1)}, bf16[32,3584]{1,0:T(8,128)(2,1)S(1)}, u32[]{:S(2)}, u32[]{:S(2)}) collective-permute-start(bf16[32,3584]{1,0:T(8,128)(2,1)S(1)} %get-tuple-element.30), channel_id=1, source_target_pairs={{0,2},{1,5},{2,0},{3,7},{4,6},{5,1},{6,4},{7,3},{8,10},{9,13},{10,... | collective-permute-start | bytes 688136 | tf_op jit(solution)/shard_map/ppermute | solution.py:178
  37.1 6.1 %collective-permute-start.8 = (bf16[32,3584]{1,0:T(8,128)(2,1)S(1)}, bf16[32,3584]{1,0:T(8,128)(2,1)S(1)}, u32[]{:S(2)}, u32[]{:S(2)}) collective-permute-start(bf16[32,3584]{1,0:T(8,128)(2,1)S(1)} %shard_map.77), channel_id=1, source_target_pairs={{0,4},{1,3},{2,6},{3,1},{4,0},{5,7},{6,2},{7,5},{8,12},{9,11},{10,... | collective-permute-start | bytes 688136 | tf_op jit(solution)/shard_map/ppermute | solution.py:178
  43.3 4.5 %collective-permute-start.9 = (bf16[8,3584]{1,0:T(8,128)(2,1)S(1)}, bf16[8,3584]{1,0:T(8,128)(2,1)S(1)}, u32[]{:S(2)}, u32[]{:S(2)}) collective-permute-start(bf16[8,3584]{1,0:T(8,128)(2,1)S(1)} %get-tuple-element.34), channel_id=1, source_target_pairs={{0,8},{2,10},{4,12},{6,14},{8,0},{10,2},{12,4},{14,6},{16,24},{18,... | collective-permute-start | bytes 172040 | tf_op jit(solution)/shard_map/ppermute | solution.py:169
  43.4 5.1 %collective-permute-start.10 = (bf16[8,3584]{1,0:T(8,128)(2,1)S(1)}, bf16[8,3584]{1,0:T(8,128)(2,1)S(1)}, u32[]{:S(2)}, u32[]{:S(2)}) collective-permute-start(bf16[8,3584]{1,0:T(8,128)(2,1)S(1)} %get-tuple-element.35), channel_id=1, source_target_pairs={{0,16},{2,18},{4,20},{6,22},{8,24},{10,26},{12,28},{14,30},{16,0},... | collective-permute-start | bytes 172040 | tf_op jit(solution)/shard_map/ppermute | solution.py:169
  45.2 6.0 %collective-permute-start.11 = (bf16[8,3584]{1,0:T(8,128)(2,1)S(1)}, bf16[8,3584]{1,0:T(8,128)(2,1)S(1)}, u32[]{:S(2)}, u32[]{:S(2)}) collective-permute-start(bf16[8,3584]{1,0:T(8,128)(2,1)S(1)} %get-tuple-element.36), channel_id=1, source_target_pairs={{0,24},{2,26},{4,28},{6,30},{8,16},{10,18},{12,20},{14,22},{16,8},... | collective-permute-start | bytes 172040 | tf_op jit(solution)/shard_map/ppermute | solution.py:169

commit v6 on v4

--- a/solution.py
+++ b/solution.py
@@ -84,10 +84,15 @@
 
 
 def prepare_kernel(w_in, w_out, combine, w_in_held, w_out_held, terms_out, sems):
-    first = pltpu.make_async_copy(w_in, w_in_held, sems.at[0])
-    second = pltpu.make_async_copy(w_out, w_out_held, sems.at[1])
-    first.start()
-    second.start()
+    half = w_in.shape[1] // 2
+    rows = [pl.ds(0, half), pl.ds(half, half)]
+    copies = [
+        pltpu.make_async_copy(w_in.at[i, r], w_in_held.at[i, r], sems.at[2 * i + j])
+        for i in range(2)
+        for j, r in enumerate(rows)
+    ] + [pltpu.make_async_copy(w_out, w_out_held, sems.at[4])]
+    for c in copies:
+        c.start()
     rest = combine[...]
     slots = rest.shape[0]
     same = (iota((slots, slots), 0) == iota((slots, slots), 1)).astype(jnp.float32)
@@ -101,28 +106,30 @@
             )
         )
     terms_out[...] = jnp.concatenate(terms, axis=0).astype(jnp.bfloat16)
-    first.wait()
-    second.wait()
+    for c in copies:
+        c.wait()
 
 
 def stack_kernel(count, *refs):
-    refs[-1][...] = stack(refs[:count]).astype(jnp.bfloat16)
-
-
-def expert_kernel(count, *refs):
-    blocks, (w_in, w_out), outs = refs[:count], refs[count : count + 2], refs[count + 2 :]
-    rows = stack(blocks).astype(jnp.bfloat16)
-    gate = jnp.dot(rows, w_in[0], preferred_element_type=jnp.float32)
-    upper = jnp.dot(rows, w_in[1], preferred_element_type=jnp.float32)
+    value, out = stack(refs[:count]).astype(jnp.bfloat16), refs[-1]
+    rows = value.shape[0]
+    for start in range(0, out.shape[0], rows):
+        out[pl.ds(start, rows), :] = value
+
+
+def expert_kernel(rows, w_in, w_out, out):
+    gate = jnp.dot(rows[...], w_in[0], preferred_element_type=jnp.float32)
+    upper = jnp.dot(rows[...], w_in[1], preferred_element_type=jnp.float32)
     hidden = (gate / (1.0 + jnp.exp(-gate)) * upper).astype(jnp.bfloat16)
-    unstack(jnp.dot(hidden, w_out[...], preferred_element_type=jnp.float32), outs)
-
-
-def sum_kernel(count, *refs):
-    total = refs[0][...].astype(jnp.float32)
-    for r in refs[1:count]:
-        total = total + r[...].astype(jnp.float32)
-    unstack(total, refs[count:])
+    out[...] = jnp.dot(hidden, w_out[...], preferred_element_type=jnp.float32).astype(jnp.bfloat16)
+
+
+def sum_kernel(values, *outs):
+    rows = len(outs) * outs[0].shape[0]
+    total = values[pl.ds(0, rows), :].astype(jnp.float32)
+    for start in range(rows, values.shape[0], rows):
+        total = total + values[pl.ds(start, rows), :].astype(jnp.float32)
+    unstack(total, outs)
 
 
 def combine_kernel(terms, *refs):
@@ -157,10 +164,13 @@
     slots = slot_count * capacity
     bf16 = jnp.bfloat16
     chunk = jax.ShapeDtypeStruct((capacity, width), bf16)
-    block = jax.ShapeDtypeStruct((slots, width), bf16)
 
     def swap(value, offset):
         return lax.ppermute(value, "expert", [(e, e ^ offset) for e in range(n_devices)])
+
+    def exchange(value):
+        groups = [list(range(e, e + group_size)) for e in range(0, n_devices, group_size)]
+        return lax.all_to_all(value, "expert", 0, 0, axis_index_groups=groups, tiled=True)
 
     def local(kernel, inputs, outs, limit=16 * MIB):
         return call(kernel, inputs, [VMEM] * len(inputs), outs, limit)
@@ -190,19 +200,13 @@
             jax.ShapeDtypeStruct((3 * tok_count, slots), bf16),
         ],
         16 * MIB,
-        [pltpu.SemaphoreType.DMA((2,))],
+        [pltpu.SemaphoreType.DMA((5,))],
         2 * (w_in.size + w_out.size),
     )
-    own = local(functools.partial(stack_kernel, slot_count), chunks + [terms], block)
-    held = [own if q == 0 else swap(own, q) for q in range(group_size)]
-    result = local(
-        functools.partial(expert_kernel, group_size),
-        held + [w_in, w_out],
-        [block] * group_size,
-        40 * MIB,
-    )
-    result = [v if q == 0 else swap(v, q) for q, v in enumerate(result)]
-    summed = local(functools.partial(sum_kernel, group_size), result, [chunk] * slot_count)
+    everyone = jax.ShapeDtypeStruct((group_size * slots, width), bf16)
+    own = local(functools.partial(stack_kernel, slot_count), chunks + [terms], everyone)
+    result = local(expert_kernel, [exchange(own), w_in, w_out], everyone, 40 * MIB)
+    summed = local(sum_kernel, [exchange(result)], [chunk] * slot_count)
     returned = [v if d == 0 else swap(v, d * group_size) for d, v in enumerate(summed)]
     return local(
         combine_kernel, [terms] + returned, jax.ShapeDtypeStruct((tok_count, width), bf16)

time: 47.9 us -> 50 us (1.044)
  blocking collectives: 0 us -> 26.9 us
  waiting for transfers between devices: 24.6 us -> 6.83 us
  starting transfers between devices: 17.2 us -> 10.1 us
    all_to_all x0 -> x2, blocking collectives: none -> 26.9 us  [exchange(): lax.all_to_all(value, 'expert', 0, 0, axis_index_groups=groups, tiled=True)]
    ppermute x12 -> x6, waiting for transfers between devices: 24.6 us -> 6.83 us  [swap(): lax.ppermute(value, 'expert', [(e, e ^ offset) for e in range(n_devices)])]
    ppermute x12 -> x6, starting transfers between devices: 17.2 us -> 10.1 us  [swap(): lax.ppermute(value, 'expert', [(e, e ^ offset) for e in range(n_devices)])]
  transfers between devices with their start and end apart: 12 -> 6, of which waited for: 9 -> 4; matrix products, arithmetic and copies ran while one was open for 0% -> 0% of each run, Pallas kernels for 5% -> 5%
where the time goes in v6:
time: 50 us; the launch traced here: 49.8 us
  blocking collectives  26.9 us (54%)
  starting transfers between devices  10.1 us (20%)
  waiting for transfers between devices  6.83 us (14%)
  Pallas kernels  5.92 us (12%)
    all_to_all x2, blocking collectives, exchange(): lax.all_to_all(value, 'expert', 0, 0, axis_index_groups=groups, tiled=True)  26.9 us
    ppermute x6, starting transfers between devices, swap(): lax.ppermute(value, 'expert', [(e, e ^ offset) for e in range(n_devices)])  10.1 us
    ppermute x6, waiting for transfers between devices, swap(): lax.ppermute(value, 'expert', [(e, e ^ offset) for e in range(n_devices)])  6.83 us
    pallas_call x6, Pallas kernels, call(): pl.pallas_call(kernel, out_shape=outs, in_specs=in_specs, out_specs=jax.t...  5.92 us
  transfers between devices with their start and end apart: 6, of which 4 were waited for; matrix products, arithmetic and copies ran while one was open for 0% of the time, Pallas kernels for 5%

profile of v6, /device:TPU:0, one launch (start us, length us, event | category | flops | bytes accessed | tf_op | source)
XLA Modules:
  0.0 49.8 jit_solution(10844127333946323716)
XLA Ops:
  0.0 1.2 %shard_map.73 = (bf16[8,3584]{1,0:T(8,128)(2,1)S(1)}, bf16[8,3584]{1,0:T(8,128)(2,1)S(1)}, bf16[8,3584]{1,0:T(8,128)(2,1)S(1)}, bf16[8,3584]{1,0:T(8,128)(2,1)S(1)}, f32[32,16]{1,0:T(8,128)S(1)}) custom-call(s32[4]{0:T(128)} %refs_0_.1, s32[2,16]{1,0:T(2,128)} %bitcast.11, s32[2,16]{1,0:T(2,128)} %bitcast.12, f32[2,16]{1,0:T(2,128)} %bitcast.13, ...), custom_call_target="tpu_custom_call" | custom-call | tf_op jit(solution)/shard_map/pallas_call | solution.py:145
  1.2 3.1 %collective-permute-start = (bf16[8,3584]{1,0:T(8,128)(2,1)S(1)}, bf16[8,3584]{1,0:T(8,128)(2,1)S(1)}, u32[]{:S(2)}, u32[]{:S(2)}) collective-permute-start(bf16[8,3584]{1,0:T(8,128)(2,1)S(1)} %get-tuple-element.20), channel_id=1, source_target_pairs={{0,8},{2,10},{4,12},{6,14},{8,0},{10,2},{12,4},{14,6},{16,24},{18,... | collective-permute-start | bytes 172040 | tf_op jit(solution)/shard_map/ppermute | solution.py:169
  4.3 2.6 %collective-permute-start.1 = (bf16[8,3584]{1,0:T(8,128)(2,1)S(1)}, bf16[8,3584]{1,0:T(8,128)(2,1)S(1)}, u32[]{:S(2)}, u32[]{:S(2)}) collective-permute-start(bf16[8,3584]{1,0:T(8,128)(2,1)S(1)} %get-tuple-element.21), channel_id=1, source_target_pairs={{0,16},{2,18},{4,20},{6,22},{8,24},{10,26},{12,28},{14,30},{16,0},... | collective-permute-start | bytes 172040 | tf_op jit(solution)/shard_map/ppermute | solution.py:169
  6.9 0.0 collective-permute-start.2
  6.9 2.7 %shard_map.74 = (bf16[2,3584,256]{2,1,0:T(8,128)(2,1)S(1)}, bf16[256,3584]{1,0:T(8,128)(2,1)S(1)}, bf16[48,32]{1,0:T(8,128)(2,1)S(1)}) custom-call(bf16[2,3584,256]{2,1,0:T(8,128)(2,1)} %w_in.1, bf16[256,3584]{1,0:T(8,128)(2,1)} %w_out.1, f32[32,16]{1,0:T(8,128)S(1)} %get-tuple-element.17.combine), custom_call_target="tpu_custom_call" | custom-call | bytes 5505024 | tf_op jit(solution)/shard_map/pallas_call | solution.py:145
  9.5 0.0 collective-permute-done.refs_1_
  9.5 0.9 %collective-permute-done.1.refs_2_ = bf16[8,3584]{1,0:T(8,128)(2,1)S(1)} collective-permute-done((bf16[8,3584]{1,0:T(8,128)(2,1)S(1)}, bf16[8,3584]{1,0:T(8,128)(2,1)S(1)}, u32[]{:S(2)}, u32[]{:S(2)}) %collective-permute-start.1) | collective-permute-done | bytes 57376 | tf_op jit(solution)/shard_map/ppermute | solution.py:169
  10.5 2.4 %collective-permute-done.2.refs_3_ = bf16[8,3584]{1,0:T(8,128)(2,1)S(1)} collective-permute-done((bf16[8,3584]{1,0:T(8,128)(2,1)S(1)}, bf16[8,3584]{1,0:T(8,128)(2,1)S(1)}, u32[]{:S(2)}, u32[]{:S(2)}) %collective-permute-start.2) | collective-permute-done | bytes 57376 | tf_op jit(solution)/shard_map/ppermute | solution.py:169
  12.8 0.1 shard_map.75
  12.9 14.7 %all_to_all.22 = bf16[4,32,3584]{2,1,0:T(8,128)(2,1)S(1)} all-to-all(bf16[4,32,3584]{2,1,0:T(8,128)(2,1)S(1)} %bitcast.10), channel_id=1, replica_groups={{0,2,4,6},{8,10,12,14},{16,18,20,22},{24,26,28,30},{1,3,5,7},{9,11,13,1..., dimensions={0} | all-to-all | bytes 1835008 | tf_op jit(solution)/shard_map/all_to_all | solution.py:173
  27.6 1.0 %shard_map.76 = bf16[128,3584]{1,0:T(8,128)(2,1)S(1)} custom-call(bf16[128,3584]{1,0:T(8,128)(2,1)S(1)} %bitcast.7, bf16[2,3584,256]{2,1,0:T(8,128)(2,1)S(1)} %get-tuple-element.23.w_in, bf16[256,3584]{1,0:T(8,128)(2,1)S(1)} %get-tuple-element.24.w_out), custom_call_target="tpu_custom_call" | custom-call | tf_op jit(solution)/shard_map/pallas_call | solution.py:145
  28.6 12.3 %all_to_all.23 = bf16[4,32,3584]{2,1,0:T(8,128)(2,1)S(1)} all-to-all(bf16[4,32,3584]{2,1,0:T(8,128)(2,1)S(1)} %bitcast.8), channel_id=1, replica_groups={{0,2,4,6},{8,10,12,14},{16,18,20,22},{24,26,28,30},{1,3,5,7},{9,11,13,1..., dimensions={0} | all-to-all | bytes 1835008 | tf_op jit(solution)/shard_map/all_to_all | solution.py:173
  40.8 0.1 shard_map.77
  41.0 0.1 collective-permute-start.3
  41.0 1.9 %collective-permute-start.4 = (bf16[8,3584]{1,0:T(8,128)(2,1)S(1)}, bf16[8,3584]{1,0:T(8,128)(2,1)S(1)}, u32[]{:S(2)}, u32[]{:S(2)}) collective-permute-start(bf16[8,3584]{1,0:T(8,128)(2,1)S(1)} %get-tuple-element.27), channel_id=1, source_target_pairs={{0,16},{2,18},{4,20},{6,22},{8,24},{10,26},{12,28},{14,30},{16,0},... | collective-permute-start | bytes 172040 | tf_op jit(solution)/shard_map/ppermute | solution.py:169
  43.0 2.4 %collective-permute-start.5 = (bf16[8,3584]{1,0:T(8,128)(2,1)S(1)}, bf16[8,3584]{1,0:T(8,128)(2,1)S(1)}, u32[]{:S(2)}, u32[]{:S(2)}) collective-permute-start(bf16[8,3584]{1,0:T(8,128)(2,1)S(1)} %get-tuple-element.28), channel_id=1, source_target_pairs={{0,24},{2,26},{4,28},{6,30},{8,16},{10,18},{12,20},{14,22},{16,8},... | collective-permute-start | bytes 172040 | tf_op jit(solution)/shard_map/ppermute | solution.py:169
  45.4 0.0 collective-permute-done.3.refs_1_
  45.4 0.8 %collective-permute-done.4.refs_2_ = bf16[8,3584]{1,0:T(8,128)(2,1)S(1)} collective-permute-done((bf16[8,3584]{1,0:T(8,128)(2,1)S(1)}, bf16[8,3584]{1,0:T(8,128)(2,1)S(1)}, u32[]{:S(2)}, u32[]{:S(2)}) %collective-permute-start.4) | collective-permute-done | bytes 57376 | tf_op jit(solution)/shard_map/ppermute | solution.py:169
  46.2 2.8 %collective-permute-done.5.refs_3_ = bf16[8,3584]{1,0:T(8,128)(2,1)S(1)} collective-permute-done((bf16[8,3584]{1,0:T(8,128)(2,1)S(1)}, bf16[8,3584]{1,0:T(8,128)(2,1)S(1)}, u32[]{:S(2)}, u32[]{:S(2)}) %collective-permute-start.5) | collective-permute-done | bytes 57376 | tf_op jit(solution)/shard_map/ppermute | solution.py:169
  48.9 0.9 %shard_map.78 = bf16[16,3584]{1,0:T(8,128)(2,1)} custom-call(bf16[48,32]{1,0:T(8,128)(2,1)S(1)} %get-tuple-element.18.refs_4_.terms, bf16[8,3584]{1,0:T(8,128)(2,1)S(1)} %get-tuple-element.25.refs_0_, bf16[8,3584]{1,0:T(8,128)(2,1)S(1)} %collective-permute-done.3.refs_1_, bf16[8,3584]{1,0:T(8,128)(2,1)S(1)} %collective-permute-done.4.refs_2_, ...), custom_call_target="tpu_custom_call" | custom-call | tf_op jit(solution)/shard_map/pallas_call | solution.py:145
Async XLA Ops:
  1.2 8.3 %collective-permute-start = (bf16[8,3584]{1,0:T(8,128)(2,1)S(1)}, bf16[8,3584]{1,0:T(8,128)(2,1)S(1)}, u32[]{:S(2)}, u32[]{:S(2)}) collective-permute-start(bf16[8,3584]{1,0:T(8,128)(2,1)S(1)} %get-tuple-element.20), channel_id=1, source_target_pairs={{0,8},{2,10},{4,12},{6,14},{8,0},{10,2},{12,4},{14,6},{16,24},{18,... | collective-permute-start | bytes 172040 | tf_op jit(solution)/shard_map/ppermute | solution.py:169
  4.3 6.2 %collective-permute-start.1 = (bf16[8,3584]{1,0:T(8,128)(2,1)S(1)}, bf16[8,3584]{1,0:T(8,128)(2,1)S(1)}, u32[]{:S(2)}, u32[]{:S(2)}) collective-permute-start(bf16[8,3584]{1,0:T(8,128)(2,1)S(1)} %get-tuple-element.21), channel_id=1, source_target_pairs={{0,16},{2,18},{4,20},{6,22},{8,24},{10,26},{12,28},{14,30},{16,0},... | collective-permute-start | bytes 172040 | tf_op jit(solution)/shard_map/ppermute | solution.py:169
  6.9 6.0 %collective-permute-start.2 = (bf16[8,3584]{1,0:T(8,128)(2,1)S(1)}, bf16[8,3584]{1,0:T(8,128)(2,1)S(1)}, u32[]{:S(2)}, u32[]{:S(2)}) collective-permute-start(bf16[8,3584]{1,0:T(8,128)(2,1)S(1)} %get-tuple-element.22), channel_id=1, source_target_pairs={{0,24},{2,26},{4,28},{6,30},{8,16},{10,18},{12,20},{14,22},{16,8},... | collective-permute-start | bytes 172040 | tf_op jit(solution)/shard_map/ppermute | solution.py:169
  41.0 4.5 %collective-permute-start.3 = (bf16[8,3584]{1,0:T(8,128)(2,1)S(1)}, bf16[8,3584]{1,0:T(8,128)(2,1)S(1)}, u32[]{:S(2)}, u32[]{:S(2)}) collective-permute-start(bf16[8,3584]{1,0:T(8,128)(2,1)S(1)} %get-tuple-element.26), channel_id=1, source_target_pairs={{0,8},{2,10},{4,12},{6,14},{8,0},{10,2},{12,4},{14,6},{16,24},{18,... | collective-permute-start | bytes 172040 | tf_op jit(solution)/shard_map/ppermute | solution.py:169
  41.0 5.1 %collective-permute-start.4 = (bf16[8,3584]{1,0:T(8,128)(2,1)S(1)}, bf16[8,3584]{1,0:T(8,128)(2,1)S(1)}, u32[]{:S(2)}, u32[]{:S(2)}) collective-permute-start(bf16[8,3584]{1,0:T(8,128)(2,1)S(1)} %get-tuple-element.27), channel_id=1, source_target_pairs={{0,16},{2,18},{4,20},{6,22},{8,24},{10,26},{12,28},{14,30},{16,0},... | collective-permute-start | bytes 172040 | tf_op jit(solution)/shard_map/ppermute | solution.py:169
  43.0 6.0 %collective-permute-start.5 = (bf16[8,3584]{1,0:T(8,128)(2,1)S(1)}, bf16[8,3584]{1,0:T(8,128)(2,1)S(1)}, u32[]{:S(2)}, u32[]{:S(2)}) collective-permute-start(bf16[8,3584]{1,0:T(8,128)(2,1)S(1)} %get-tuple-element.28), channel_id=1, source_target_pairs={{0,24},{2,26},{4,28},{6,30},{8,16},{10,18},{12,20},{14,22},{16,8},... | collective-permute-start | bytes 172040 | tf_op jit(solution)/shard_map/ppermute | solution.py:169

commit v7 on v4

--- a/solution.py
+++ b/solution.py
@@ -49,7 +49,8 @@
     for p in range(slot_count):
         here = copy_row == p
         named = jnp.where(here, placement[p], named)
-        relative = jnp.where(here, lax.bitwise_xor(own, p), relative)
+        d = lax.bitwise_xor(own, p)
+        relative = jnp.where(here, d // 2 + d % 2 * (slot_count // 2), relative)
         seen = jnp.int32(0)
         for q in range(p):
             seen = seen + (placement[q] == placement[p]).astype(jnp.int32)
@@ -83,26 +84,32 @@
     unstack(rows, row_outs)
 
 
-def prepare_kernel(w_in, w_out, combine, w_in_held, w_out_held, terms_out, sems):
-    first = pltpu.make_async_copy(w_in, w_in_held, sems.at[0])
-    second = pltpu.make_async_copy(w_out, w_out_held, sems.at[1])
-    first.start()
-    second.start()
-    rest = combine[...]
-    slots = rest.shape[0]
+def prepare_kernel(w_in, w_out, combine, w_in_held, w_out_held, near_terms, far_terms, sems):
+    half = w_in.shape[1] // 2
+    rows = [pl.ds(0, half), pl.ds(half, half)]
+    copies = [
+        pltpu.make_async_copy(w_in.at[i, r], w_in_held.at[i, r], sems.at[2 * i + j])
+        for i in range(2)
+        for j, r in enumerate(rows)
+    ] + [pltpu.make_async_copy(w_out, w_out_held, sems.at[4])]
+    for c in copies:
+        c.start()
+    slots = combine.shape[0] // 2
     same = (iota((slots, slots), 0) == iota((slots, slots), 1)).astype(jnp.float32)
-    terms = []
-    for _ in range(3):
-        term = rest.astype(jnp.bfloat16).astype(jnp.float32)
-        rest = rest - term
-        terms.append(
-            lax.dot_general(
-                term, same, (((0,), (0,)), ((), ())), preferred_element_type=jnp.float32
+    for start, out in ((0, near_terms), (slots, far_terms)):
+        rest = combine[pl.ds(start, slots), :]
+        terms = []
+        for _ in range(3):
+            term = rest.astype(jnp.bfloat16).astype(jnp.float32)
+            rest = rest - term
+            terms.append(
+                lax.dot_general(
+                    term, same, (((0,), (0,)), ((), ())), preferred_element_type=jnp.float32
+                )
             )
-        )
-    terms_out[...] = jnp.concatenate(terms, axis=0).astype(jnp.bfloat16)
-    first.wait()
-    second.wait()
+        out[...] = jnp.concatenate(terms, axis=0).astype(jnp.bfloat16)
+    for c in copies:
+        c.wait()
 
 
 def stack_kernel(count, *refs):
@@ -125,13 +132,19 @@
     unstack(total, refs[count:])
 
 
-def combine_kernel(terms, *refs):
-    parts, out = refs[:-1], refs[-1]
+def combined(terms, parts, rows):
     values = stack(parts).astype(jnp.bfloat16)
     product = jnp.dot(terms[...], values, preferred_element_type=jnp.float32)
-    rows = out.shape[0]
-    total = product[2 * rows :] + product[rows : 2 * rows] + product[:rows]
-    out[...] = total.astype(jnp.bfloat16)
+    return product[2 * rows :] + product[rows : 2 * rows] + product[:rows]
+
+
+def near_kernel(terms, *refs):
+    refs[-1][...] = combined(terms, refs[:-1], refs[-1].shape[0])
+
+
+def far_kernel(terms, near, *refs):
+    total = near[...] + combined(terms, refs[:-1], refs[-1].shape[0])
+    refs[-1][...] = total.astype(jnp.bfloat16)
 
 
 def call(kernel, inputs, in_specs, outs, limit, scratch=(), moved=0):
@@ -155,9 +168,10 @@
     tok_count, width = tokens.shape
     capacity = tok_count * expert_ids.shape[1] // slot_count
     slots = slot_count * capacity
+    offsets = [*range(0, slot_count, 2), *range(1, slot_count, 2)]
     bf16 = jnp.bfloat16
     chunk = jax.ShapeDtypeStruct((capacity, width), bf16)
-    block = jax.ShapeDtypeStruct((slots, width), bf16)
+    half = jax.ShapeDtypeStruct((slots // 2, width), bf16)
 
     def swap(value, offset):
         return lax.ppermute(value, "expert", [(e, e ^ offset) for e in range(n_devices)])
@@ -179,33 +193,59 @@
         + [pltpu.VMEM(s.shape, s.dtype) for s in sources[1:]]
         + [pltpu.SemaphoreType.DMA((5,))],
     )
-    chunks = [c if d == 0 else swap(c, d * group_size) for d, c in enumerate(chunks)]
-    w_in, w_out, terms = call(
+    chunks = [swap(c, d * group_size) if d else c for d, c in zip(offsets, chunks)]
+    terms = jax.ShapeDtypeStruct((3 * tok_count, slots // 2), bf16)
+    w_in, w_out, *terms = call(
         prepare_kernel,
         (*in_hbm(w_in, w_out), combine),
         [HBM] * 2 + [VMEM],
-        [
-            jax.ShapeDtypeStruct(w_in.shape, bf16),
-            jax.ShapeDtypeStruct(w_out.shape, bf16),
-            jax.ShapeDtypeStruct((3 * tok_count, slots), bf16),
-        ],
+        [*(jax.ShapeDtypeStruct(w.shape, bf16) for w in (w_in, w_out)), terms, terms],
         16 * MIB,
-        [pltpu.SemaphoreType.DMA((2,))],
+        [pltpu.SemaphoreType.DMA((5,))],
         2 * (w_in.size + w_out.size),
     )
-    own = local(functools.partial(stack_kernel, slot_count), chunks + [terms], block)
-    held = [own if q == 0 else swap(own, q) for q in range(group_size)]
-    result = local(
-        functools.partial(expert_kernel, group_size),
-        held + [w_in, w_out],
-        [block] * group_size,
-        40 * MIB,
-    )
-    result = [v if q == 0 else swap(v, q) for q, v in enumerate(result)]
-    summed = local(functools.partial(sum_kernel, group_size), result, [chunk] * slot_count)
-    returned = [v if d == 0 else swap(v, d * group_size) for d, v in enumerate(summed)]
+
+    square = group_size == 4
+    count = slot_count // 2
+    sides = ((1, 2), (2, 1))
+    earlier = []
+    summed = []
+    for h in range(2):
+        a, b = sides[h]
+        own = local(
+            functools.partial(stack_kernel, count), chunks[h * count :][:count] + earlier, half
+        )
+        if square:
+            held = {a: swap(own, a), b: swap(own, b)}
+            held = [own, held[a], held[b], swap(held[a], b)]
+        else:
+            held = [swap(own, q) if q else own for q in range(group_size)]
+        earlier = [held[1]]
+        result = local(
+            functools.partial(expert_kernel, group_size),
+            held + [w_in, w_out],
+            [half] * group_size,
+            40 * MIB,
+        )
+        if square:
+            mine, first, second, cross = result
+            cross = swap(cross, a)
+            first = swap(first, a)
+            second = local(functools.partial(sum_kernel, 2), [second, cross], [half])[0]
+            result = [mine, first, swap(second, b)]
+        else:
+            result = [swap(v, q) if q else v for q, v in enumerate(result)]
+        summed += local(functools.partial(sum_kernel, len(result)), result, [chunk] * count)
+    summed = [swap(v, d * group_size) if d else v for d, v in zip(offsets, summed)]
+    near = local(
+        near_kernel,
+        [terms[0]] + summed[:count],
+        jax.ShapeDtypeStruct((tok_count, width), jnp.float32),
+    )
     return local(
-        combine_kernel, [terms] + returned, jax.ShapeDtypeStruct((tok_count, width), bf16)
+        far_kernel,
+        [terms[1], near] + summed[count:],
+        jax.ShapeDtypeStruct((tok_count, width), bf16),
     )
 
 

time: 47.9 us -> 46.8 us (0.977)
  waiting for transfers between devices: 24.6 us -> 12.4 us
  starting transfers between devices: 17.2 us -> 26.7 us
  Pallas kernels: 5.84 us -> 7.42 us
    ppermute x12 -> x18, waiting for transfers between devices: 24.6 us -> 12.4 us  [swap(): lax.ppermute(value, 'expert', [(e, e ^ offset) for e in range(n_devices)])]
    ppermute x12 -> x18, starting transfers between devices: 17.2 us -> 26.7 us  [swap(): lax.ppermute(value, 'expert', [(e, e ^ offset) for e in range(n_devices)])]
    pallas_call x6 -> x12, Pallas kernels: 5.84 us -> 7.42 us  [call(): pl.pallas_call(kernel, out_shape=outs, in_specs=in_specs, out_specs=jax.t...]
  transfers between devices with their start and end apart: 12 -> 18, of which waited for: 9 -> 11; matrix products, arithmetic and copies ran while one was open for 0% -> 0% of each run, Pallas kernels for 5% -> 11%
where the time goes in v7:
time: 46.8 us; the launch traced here: 46.7 us
  starting transfers between devices  26.7 us (57%)
  waiting for transfers between devices  12.4 us (26%)
  Pallas kernels  7.42 us (16%)
    ppermute x18, starting transfers between devices, swap(): lax.ppermute(value, 'expert', [(e, e ^ offset) for e in range(n_devices)])  26.7 us
    ppermute x18, waiting for transfers between devices, swap(): lax.ppermute(value, 'expert', [(e, e ^ offset) for e in range(n_devices)])  12.4 us
    pallas_call x12, Pallas kernels, call(): pl.pallas_call(kernel, out_shape=outs, in_specs=in_specs, out_specs=jax.t...  7.42 us
  transfers between devices with their start and end apart: 18, of which 11 were waited for; matrix products, arithmetic and copies ran while one was open for 0% of the time, Pallas kernels for 11%

profile of v7, /device:TPU:0, one launch (start us, length us, event | category | flops | bytes accessed | tf_op | source)
XLA Modules:
  0.0 46.7 jit_solution(16427260045868910416)
XLA Ops:
  0.0 1.2 %shard_map.73 = (bf16[8,3584]{1,0:T(8,128)(2,1)S(1)}, bf16[8,3584]{1,0:T(8,128)(2,1)S(1)}, bf16[8,3584]{1,0:T(8,128)(2,1)S(1)}, bf16[8,3584]{1,0:T(8,128)(2,1)S(1)}, f32[32,16]{1,0:T(8,128)S(1)}) custom-call(s32[4]{0:T(128)} %refs_0_.1, s32[2,16]{1,0:T(2,128)} %bitcast.3, s32[2,16]{1,0:T(2,128)} %bitcast.4, f32[2,16]{1,0:T(2,128)} %bitcast.5, ...), custom_call_target="tpu_custom_call" | custom-call | tf_op jit(solution)/shard_map/pallas_call | solution.py:151
  1.2 4.1 %collective-permute-start = (bf16[8,3584]{1,0:T(8,128)(2,1)S(1)}, bf16[8,3584]{1,0:T(8,128)(2,1)S(1)}, u32[]{:S(2)}, u32[]{:S(2)}) collective-permute-start(bf16[8,3584]{1,0:T(8,128)(2,1)S(1)} %get-tuple-element.30), channel_id=1, source_target_pairs={{0,16},{2,18},{4,20},{6,22},{8,24},{10,26},{12,28},{14,30},{16,0},... | collective-permute-start | bytes 172040 | tf_op jit(solution)/shard_map/ppermute | solution.py:177
  5.3 2.8 %collective-permute-done.refs_1_ = bf16[8,3584]{1,0:T(8,128)(2,1)S(1)} collective-permute-done((bf16[8,3584]{1,0:T(8,128)(2,1)S(1)}, bf16[8,3584]{1,0:T(8,128)(2,1)S(1)}, u32[]{:S(2)}, u32[]{:S(2)}) %collective-permute-start) | collective-permute-done | bytes 57376 | tf_op jit(solution)/shard_map/ppermute | solution.py:177
  8.1 1.8 %collective-permute-start.1 = (bf16[16,3584]{1,0:T(8,128)(2,1)S(1)}, bf16[16,3584]{1,0:T(8,128)(2,1)S(1)}, u32[]{:S(2)}, u32[]{:S(2)}) collective-permute-start(bf16[16,3584]{1,0:T(8,128)(2,1)S(1)} %shard_map.75.refs_0_), channel_id=1, source_target_pairs={{0,2},{2,0},{4,6},{6,4},{8,10},{10,8},{12,14},{14,12},{16,18},{18,... | collective-permute-start | bytes 344072 | tf_op jit(solution)/shard_map/ppermute | solution.py:177
  9.9 1.2 %collective-permute-start.8 = (bf16[8,3584]{1,0:T(8,128)(2,1)S(1)}, bf16[8,3584]{1,0:T(8,128)(2,1)S(1)}, u32[]{:S(2)}, u32[]{:S(2)}) collective-permute-start(bf16[8,3584]{1,0:T(8,128)(2,1)S(1)} %get-tuple-element.39), channel_id=1, source_target_pairs={{0,8},{2,10},{4,12},{6,14},{8,0},{10,2},{12,4},{14,6},{16,24},{18,... | collective-permute-start | bytes 172040 | tf_op jit(solution)/shard_map/ppermute | solution.py:177
  11.0 2.5 %collective-permute-start.9 = (bf16[8,3584]{1,0:T(8,128)(2,1)S(1)}, bf16[8,3584]{1,0:T(8,128)(2,1)S(1)}, u32[]{:S(2)}, u32[]{:S(2)}) collective-permute-start(bf16[8,3584]{1,0:T(8,128)(2,1)S(1)} %get-tuple-element.40), channel_id=1, source_target_pairs={{0,24},{2,26},{4,28},{6,30},{8,16},{10,18},{12,20},{14,22},{16,8},... | collective-permute-start | bytes 172040 | tf_op jit(solution)/shard_map/ppermute | solution.py:177
  13.5 1.1 %collective-permute-done.8.refs_0_ = bf16[8,3584]{1,0:T(8,128)(2,1)S(1)} collective-permute-done((bf16[8,3584]{1,0:T(8,128)(2,1)S(1)}, bf16[8,3584]{1,0:T(8,128)(2,1)S(1)}, u32[]{:S(2)}, u32[]{:S(2)}) %collective-permute-start.8) | collective-permute-done | bytes 57376 | tf_op jit(solution)/shard_map/ppermute | solution.py:177
  14.6 2.4 %collective-permute-done.9.refs_1_ = bf16[8,3584]{1,0:T(8,128)(2,1)S(1)} collective-permute-done((bf16[8,3584]{1,0:T(8,128)(2,1)S(1)}, bf16[8,3584]{1,0:T(8,128)(2,1)S(1)}, u32[]{:S(2)}, u32[]{:S(2)}) %collective-permute-start.9) | collective-permute-done | bytes 57376 | tf_op jit(solution)/shard_map/ppermute | solution.py:177
  17.0 1.6 %collective-permute-start.10 = (bf16[16,3584]{1,0:T(8,128)(2,1)S(1)}, bf16[16,3584]{1,0:T(8,128)(2,1)S(1)}, u32[]{:S(2)}, u32[]{:S(2)}) collective-permute-start(bf16[16,3584]{1,0:T(8,128)(2,1)S(1)} %shard_map.80.refs_0_), channel_id=1, source_target_pairs={{0,4},{2,6},{4,0},{6,2},{8,12},{10,14},{12,8},{14,10},{16,20},{18,... | collective-permute-start | bytes 344072 | tf_op jit(solution)/shard_map/ppermute | solution.py:177
  18.6 0.5 %collective-permute-start.2 = (bf16[16,3584]{1,0:T(8,128)(2,1)S(1)}, bf16[16,3584]{1,0:T(8,128)(2,1)S(1)}, u32[]{:S(2)}, u32[]{:S(2)}) collective-permute-start(bf16[16,3584]{1,0:T(8,128)(2,1)S(1)} %shard_map.75.refs_0_), channel_id=1, source_target_pairs={{0,4},{2,6},{4,0},{6,2},{8,12},{10,14},{12,8},{14,10},{16,20},{18,... | collective-permute-start | bytes 344072 | tf_op jit(solution)/shard_map/ppermute | solution.py:177
  19.1 1.5 %collective-permute-start.3 = (bf16[16,3584]{1,0:T(8,128)(2,1)S(1)}, bf16[16,3584]{1,0:T(8,128)(2,1)S(1)}, u32[]{:S(2)}, u32[]{:S(2)}) collective-permute-start(bf16[16,3584]{1,0:T(8,128)(2,1)S(1)} %collective-permute-done.1.refs_1_.refs_2_), channel_id=1, source_target_pairs={{0,4},{2,6},{4,0},{6,2},{8,12},{10,14},{12,8},{14,10},{16,20},{18,... | collective-permute-start | bytes 344072 | tf_op jit(solution)/shard_map/ppermute | solution.py:177
  20.6 0.5 %collective-permute-start.11 = (bf16[16,3584]{1,0:T(8,128)(2,1)S(1)}, bf16[16,3584]{1,0:T(8,128)(2,1)S(1)}, u32[]{:S(2)}, u32[]{:S(2)}) collective-permute-start(bf16[16,3584]{1,0:T(8,128)(2,1)S(1)} %shard_map.80.refs_0_), channel_id=1, source_target_pairs={{0,2},{2,0},{4,6},{6,4},{8,10},{10,8},{12,14},{14,12},{16,18},{18,... | collective-permute-start | bytes 344072 | tf_op jit(solution)/shard_map/ppermute | solution.py:177
  21.2 0.7 %collective-permute-done.10.refs_1_ = bf16[16,3584]{1,0:T(8,128)(2,1)S(1)} collective-permute-done((bf16[16,3584]{1,0:T(8,128)(2,1)S(1)}, bf16[16,3584]{1,0:T(8,128)(2,1)S(1)}, u32[]{:S(2)}, u32[]{:S(2)}) %collective-permute-start.10) | collective-permute-done | bytes 114720 | tf_op jit(solution)/shard_map/ppermute | solution.py:177
  21.9 0.8 %collective-permute-start.12 = (bf16[16,3584]{1,0:T(8,128)(2,1)S(1)}, bf16[16,3584]{1,0:T(8,128)(2,1)S(1)}, u32[]{:S(2)}, u32[]{:S(2)}) collective-permute-start(bf16[16,3584]{1,0:T(8,128)(2,1)S(1)} %collective-permute-done.10.refs_1_), channel_id=1, source_target_pairs={{0,2},{2,0},{4,6},{6,4},{8,10},{10,8},{12,14},{14,12},{16,18},{18,... | collective-permute-start | bytes 344072 | tf_op jit(solution)/shard_map/ppermute | solution.py:177
  22.7 2.7 %shard_map.74 = (bf16[2,3584,256]{2,1,0:T(8,128)(2,1)S(1)}, bf16[256,3584]{1,0:T(8,128)(2,1)S(1)}, bf16[48,16]{1,0:T(8,128)(2,1)S(1)}, bf16[48,16]{1,0:T(8,128)(2,1)S(1)}) custom-call(bf16[2,3584,256]{2,1,0:T(8,128)(2,1)} %w_in.1, bf16[256,3584]{1,0:T(8,128)(2,1)} %w_out.1, f32[32,16]{1,0:T(8,128)S(1)} %get-tuple-element.26.combine), custom_call_target="tpu_custom_call" | custom-call | bytes 5505024 | tf_op jit(solution)/shard_map/pallas_call | solution.py:151
  25.3 1.2 %shard_map.76 = (bf16[16,3584]{1,0:T(8,128)(2,1)S(1)}, bf16[16,3584]{1,0:T(8,128)(2,1)S(1)}, bf16[16,3584]{1,0:T(8,128)(2,1)S(1)}, bf16[16,3584]{1,0:T(8,128)(2,1)S(1)}) custom-call(bf16[16,3584]{1,0:T(8,128)(2,1)S(1)} %shard_map.75.refs_0_, bf16[16,3584]{1,0:T(8,128)(2,1)S(1)} %collective-permute-done.1.refs_1_.refs_2_, ...), custom_call_target="tpu_custom_call" | custom-call | tf_op jit(solution)/shard_map/pallas_call | solution.py:151
  26.5 1.3 %collective-permute-start.5 = (bf16[16,3584]{1,0:T(8,128)(2,1)S(1)}, bf16[16,3584]{1,0:T(8,128)(2,1)S(1)}, u32[]{:S(2)}, u32[]{:S(2)}) collective-permute-start(bf16[16,3584]{1,0:T(8,128)(2,1)S(1)} %get-tuple-element.36), channel_id=1, source_target_pairs={{0,2},{2,0},{4,6},{6,4},{8,10},{10,8},{12,14},{14,12},{16,18},{18,... | collective-permute-start | bytes 344072 | tf_op jit(solution)/shard_map/ppermute | solution.py:177
  27.9 1.2 %shard_map.81 = (bf16[16,3584]{1,0:T(8,128)(2,1)S(1)}, bf16[16,3584]{1,0:T(8,128)(2,1)S(1)}, bf16[16,3584]{1,0:T(8,128)(2,1)S(1)}, bf16[16,3584]{1,0:T(8,128)(2,1)S(1)}) custom-call(bf16[16,3584]{1,0:T(8,128)(2,1)S(1)} %shard_map.80.refs_0_, bf16[16,3584]{1,0:T(8,128)(2,1)S(1)} %collective-permute-done.10.refs_1_, ...), custom_call_target="tpu_custom_call" | custom-call | tf_op jit(solution)/shard_map/pallas_call | solution.py:151
  29.0 1.5 %collective-permute-start.14 = (bf16[16,3584]{1,0:T(8,128)(2,1)S(1)}, bf16[16,3584]{1,0:T(8,128)(2,1)S(1)}, u32[]{:S(2)}, u32[]{:S(2)}) collective-permute-start(bf16[16,3584]{1,0:T(8,128)(2,1)S(1)} %get-tuple-element.44), channel_id=1, source_target_pairs={{0,4},{2,6},{4,0},{6,2},{8,12},{10,14},{12,8},{14,10},{16,20},{18,... | collective-permute-start | bytes 344072 | tf_op jit(solution)/shard_map/ppermute | solution.py:177
  30.6 0.5 %collective-permute-start.4 = (bf16[16,3584]{1,0:T(8,128)(2,1)S(1)}, bf16[16,3584]{1,0:T(8,128)(2,1)S(1)}, u32[]{:S(2)}, u32[]{:S(2)}) collective-permute-start(bf16[16,3584]{1,0:T(8,128)(2,1)S(1)} %get-tuple-element.34), channel_id=1, source_target_pairs={{0,2},{2,0},{4,6},{6,4},{8,10},{10,8},{12,14},{14,12},{16,18},{18,... | collective-permute-start | bytes 344072 | tf_op jit(solution)/shard_map/ppermute | solution.py:177
  31.4 1.5 %collective-permute-start.6 = (bf16[16,3584]{1,0:T(8,128)(2,1)S(1)}, bf16[16,3584]{1,0:T(8,128)(2,1)S(1)}, u32[]{:S(2)}, u32[]{:S(2)}) collective-permute-start(bf16[16,3584]{1,0:T(8,128)(2,1)S(1)} %shard_map.77), channel_id=1, source_target_pairs={{0,4},{2,6},{4,0},{6,2},{8,12},{10,14},{12,8},{14,10},{16,20},{18,... | collective-permute-start | bytes 344072 | tf_op jit(solution)/shard_map/ppermute | solution.py:177
  32.9 0.6 %collective-permute-start.13 = (bf16[16,3584]{1,0:T(8,128)(2,1)S(1)}, bf16[16,3584]{1,0:T(8,128)(2,1)S(1)}, u32[]{:S(2)}, u32[]{:S(2)}) collective-permute-start(bf16[16,3584]{1,0:T(8,128)(2,1)S(1)} %get-tuple-element.42), channel_id=1, source_target_pairs={{0,4},{2,6},{4,0},{6,2},{8,12},{10,14},{12,8},{14,10},{16,20},{18,... | collective-permute-start | bytes 344072 | tf_op jit(solution)/shard_map/ppermute | solution.py:177
  33.5 0.4 collective-permute-done.14.refs_1_
  33.9 1.0 %collective-permute-start.15 = (bf16[16,3584]{1,0:T(8,128)(2,1)S(1)}, bf16[16,3584]{1,0:T(8,128)(2,1)S(1)}, u32[]{:S(2)}, u32[]{:S(2)}) collective-permute-start(bf16[16,3584]{1,0:T(8,128)(2,1)S(1)} %shard_map.82), channel_id=1, source_target_pairs={{0,2},{2,0},{4,6},{6,4},{8,10},{10,8},{12,14},{14,12},{16,18},{18,... | collective-permute-start | bytes 344072 | tf_op jit(solution)/shard_map/ppermute | solution.py:177
  35.0 0.4 collective-permute-done.4.refs_1_
  35.4 0.9 %collective-permute-done.6.refs_2_ = bf16[16,3584]{1,0:T(8,128)(2,1)S(1)} collective-permute-done((bf16[16,3584]{1,0:T(8,128)(2,1)S(1)}, bf16[16,3584]{1,0:T(8,128)(2,1)S(1)}, u32[]{:S(2)}, u32[]{:S(2)}) %collective-permute-start.6) | collective-permute-done | bytes 114720 | tf_op jit(solution)/shard_map/ppermute | solution.py:177
  36.3 2.2 %collective-permute-start.7 = (bf16[8,3584]{1,0:T(8,128)(2,1)S(1)}, bf16[8,3584]{1,0:T(8,128)(2,1)S(1)}, u32[]{:S(2)}, u32[]{:S(2)}) collective-permute-start(bf16[8,3584]{1,0:T(8,128)(2,1)S(1)} %get-tuple-element.38), channel_id=1, source_target_pairs={{0,16},{2,18},{4,20},{6,22},{8,24},{10,26},{12,28},{14,30},{16,0},... | collective-permute-start | bytes 172040 | tf_op jit(solution)/shard_map/ppermute | solution.py:177
  38.8 1.0 %collective-permute-start.16 = (bf16[8,3584]{1,0:T(8,128)(2,1)S(1)}, bf16[8,3584]{1,0:T(8,128)(2,1)S(1)}, u32[]{:S(2)}, u32[]{:S(2)}) collective-permute-start(bf16[8,3584]{1,0:T(8,128)(2,1)S(1)} %get-tuple-element.45), channel_id=1, source_target_pairs={{0,8},{2,10},{4,12},{6,14},{8,0},{10,2},{12,4},{14,6},{16,24},{18,... | collective-permute-start | bytes 172040 | tf_op jit(solution)/shard_map/ppermute | solution.py:177
  39.8 2.5 %collective-permute-start.17 = (bf16[8,3584]{1,0:T(8,128)(2,1)S(1)}, bf16[8,3584]{1,0:T(8,128)(2,1)S(1)}, u32[]{:S(2)}, u32[]{:S(2)}) collective-permute-start(bf16[8,3584]{1,0:T(8,128)(2,1)S(1)} %get-tuple-element.46), channel_id=1, source_target_pairs={{0,24},{2,26},{4,28},{6,30},{8,16},{10,18},{12,20},{14,22},{16,8},... | collective-permute-start | bytes 172040 | tf_op jit(solution)/shard_map/ppermute | solution.py:177
  42.6 0.5 %collective-permute-done.16.refs_0_ = bf16[8,3584]{1,0:T(8,128)(2,1)S(1)} collective-permute-done((bf16[8,3584]{1,0:T(8,128)(2,1)S(1)}, bf16[8,3584]{1,0:T(8,128)(2,1)S(1)}, u32[]{:S(2)}, u32[]{:S(2)}) %collective-permute-start.16) | collective-permute-done | bytes 57376 | tf_op jit(solution)/shard_map/ppermute | solution.py:177
  43.1 2.7 %collective-permute-done.17.refs_1_ = bf16[8,3584]{1,0:T(8,128)(2,1)S(1)} collective-permute-done((bf16[8,3584]{1,0:T(8,128)(2,1)S(1)}, bf16[8,3584]{1,0:T(8,128)(2,1)S(1)}, u32[]{:S(2)}, u32[]{:S(2)}) %collective-permute-start.17) | collective-permute-done | bytes 57376 | tf_op jit(solution)/shard_map/ppermute | solution.py:177
  45.8 0.9 %shard_map.84 = bf16[16,3584]{1,0:T(8,128)(2,1)} custom-call(bf16[48,16]{1,0:T(8,128)(2,1)S(1)} %get-tuple-element.27.terms, f32[16,3584]{1,0:T(8,128)S(1)} %shard_map.79.near, bf16[8,3584]{1,0:T(8,128)(2,1)S(1)} %collective-permute-done.16.refs_0_, bf16[8,3584]{1,0:T(8,128)(2,1)S(1)} %collective-permute-done.17.refs_1_), custom_call_target="tpu_custom_call" | custom-call | tf_op jit(solution)/shard_map/pallas_call | solution.py:151
  (16 shorter events, 1.0 us)
Async XLA Ops:
  1.2 6.9 %collective-permute-start = (bf16[8,3584]{1,0:T(8,128)(2,1)S(1)}, bf16[8,3584]{1,0:T(8,128)(2,1)S(1)}, u32[]{:S(2)}, u32[]{:S(2)}) collective-permute-start(bf16[8,3584]{1,0:T(8,128)(2,1)S(1)} %get-tuple-element.30), channel_id=1, source_target_pairs={{0,16},{2,18},{4,20},{6,22},{8,24},{10,26},{12,28},{14,30},{16,0},... | collective-permute-start | bytes 172040 | tf_op jit(solution)/shard_map/ppermute | solution.py:177
  8.1 8.9 %collective-permute-start.1 = (bf16[16,3584]{1,0:T(8,128)(2,1)S(1)}, bf16[16,3584]{1,0:T(8,128)(2,1)S(1)}, u32[]{:S(2)}, u32[]{:S(2)}) collective-permute-start(bf16[16,3584]{1,0:T(8,128)(2,1)S(1)} %shard_map.75.refs_0_), channel_id=1, source_target_pairs={{0,2},{2,0},{4,6},{6,4},{8,10},{10,8},{12,14},{14,12},{16,18},{18,... | collective-permute-start | bytes 344072 | tf_op jit(solution)/shard_map/ppermute | solution.py:177
  9.9 4.8 %collective-permute-start.8 = (bf16[8,3584]{1,0:T(8,128)(2,1)S(1)}, bf16[8,3584]{1,0:T(8,128)(2,1)S(1)}, u32[]{:S(2)}, u32[]{:S(2)}) collective-permute-start(bf16[8,3584]{1,0:T(8,128)(2,1)S(1)} %get-tuple-element.39), channel_id=1, source_target_pairs={{0,8},{2,10},{4,12},{6,14},{8,0},{10,2},{12,4},{14,6},{16,24},{18,... | collective-permute-start | bytes 172040 | tf_op jit(solution)/shard_map/ppermute | solution.py:177
  11.0 6.0 %collective-permute-start.9 = (bf16[8,3584]{1,0:T(8,128)(2,1)S(1)}, bf16[8,3584]{1,0:T(8,128)(2,1)S(1)}, u32[]{:S(2)}, u32[]{:S(2)}) collective-permute-start(bf16[8,3584]{1,0:T(8,128)(2,1)S(1)} %get-tuple-element.40), channel_id=1, source_target_pairs={{0,24},{2,26},{4,28},{6,30},{8,16},{10,18},{12,20},{14,22},{16,8},... | collective-permute-start | bytes 172040 | tf_op jit(solution)/shard_map/ppermute | solution.py:177
  17.0 4.9 %collective-permute-start.10 = (bf16[16,3584]{1,0:T(8,128)(2,1)S(1)}, bf16[16,3584]{1,0:T(8,128)(2,1)S(1)}, u32[]{:S(2)}, u32[]{:S(2)}) collective-permute-start(bf16[16,3584]{1,0:T(8,128)(2,1)S(1)} %shard_map.80.refs_0_), channel_id=1, source_target_pairs={{0,4},{2,6},{4,0},{6,2},{8,12},{10,14},{12,8},{14,10},{16,20},{18,... | collective-permute-start | bytes 344072 | tf_op jit(solution)/shard_map/ppermute | solution.py:177
  18.6 6.7 %collective-permute-start.2 = (bf16[16,3584]{1,0:T(8,128)(2,1)S(1)}, bf16[16,3584]{1,0:T(8,128)(2,1)S(1)}, u32[]{:S(2)}, u32[]{:S(2)}) collective-permute-start(bf16[16,3584]{1,0:T(8,128)(2,1)S(1)} %shard_map.75.refs_0_), channel_id=1, source_target_pairs={{0,4},{2,6},{4,0},{6,2},{8,12},{10,14},{12,8},{14,10},{16,20},{18,... | collective-permute-start | bytes 344072 | tf_op jit(solution)/shard_map/ppermute | solution.py:177
  19.1 6.2 %collective-permute-start.3 = (bf16[16,3584]{1,0:T(8,128)(2,1)S(1)}, bf16[16,3584]{1,0:T(8,128)(2,1)S(1)}, u32[]{:S(2)}, u32[]{:S(2)}) collective-permute-start(bf16[16,3584]{1,0:T(8,128)(2,1)S(1)} %collective-permute-done.1.refs_1_.refs_2_), channel_id=1, source_target_pairs={{0,4},{2,6},{4,0},{6,2},{8,12},{10,14},{12,8},{14,10},{16,20},{18,... | collective-permute-start | bytes 344072 | tf_op jit(solution)/shard_map/ppermute | solution.py:177
  20.6 7.2 %collective-permute-start.11 = (bf16[16,3584]{1,0:T(8,128)(2,1)S(1)}, bf16[16,3584]{1,0:T(8,128)(2,1)S(1)}, u32[]{:S(2)}, u32[]{:S(2)}) collective-permute-start(bf16[16,3584]{1,0:T(8,128)(2,1)S(1)} %shard_map.80.refs_0_), channel_id=1, source_target_pairs={{0,2},{2,0},{4,6},{6,4},{8,10},{10,8},{12,14},{14,12},{16,18},{18,... | collective-permute-start | bytes 344072 | tf_op jit(solution)/shard_map/ppermute | solution.py:177
  21.9 6.0 %collective-permute-start.12 = (bf16[16,3584]{1,0:T(8,128)(2,1)S(1)}, bf16[16,3584]{1,0:T(8,128)(2,1)S(1)}, u32[]{:S(2)}, u32[]{:S(2)}) collective-permute-start(bf16[16,3584]{1,0:T(8,128)(2,1)S(1)} %collective-permute-done.10.refs_1_), channel_id=1, source_target_pairs={{0,2},{2,0},{4,6},{6,4},{8,10},{10,8},{12,14},{14,12},{16,18},{18,... | collective-permute-start | bytes 344072 | tf_op jit(solution)/shard_map/ppermute | solution.py:177
  26.5 4.9 %collective-permute-start.5 = (bf16[16,3584]{1,0:T(8,128)(2,1)S(1)}, bf16[16,3584]{1,0:T(8,128)(2,1)S(1)}, u32[]{:S(2)}, u32[]{:S(2)}) collective-permute-start(bf16[16,3584]{1,0:T(8,128)(2,1)S(1)} %get-tuple-element.36), channel_id=1, source_target_pairs={{0,2},{2,0},{4,6},{6,4},{8,10},{10,8},{12,14},{14,12},{16,18},{18,... | collective-permute-start | bytes 344072 | tf_op jit(solution)/shard_map/ppermute | solution.py:177
  29.0 4.9 %collective-permute-start.14 = (bf16[16,3584]{1,0:T(8,128)(2,1)S(1)}, bf16[16,3584]{1,0:T(8,128)(2,1)S(1)}, u32[]{:S(2)}, u32[]{:S(2)}) collective-permute-start(bf16[16,3584]{1,0:T(8,128)(2,1)S(1)} %get-tuple-element.44), channel_id=1, source_target_pairs={{0,4},{2,6},{4,0},{6,2},{8,12},{10,14},{12,8},{14,10},{16,20},{18,... | collective-permute-start | bytes 344072 | tf_op jit(solution)/shard_map/ppermute | solution.py:177
  30.6 4.8 %collective-permute-start.4 = (bf16[16,3584]{1,0:T(8,128)(2,1)S(1)}, bf16[16,3584]{1,0:T(8,128)(2,1)S(1)}, u32[]{:S(2)}, u32[]{:S(2)}) collective-permute-start(bf16[16,3584]{1,0:T(8,128)(2,1)S(1)} %get-tuple-element.34), channel_id=1, source_target_pairs={{0,2},{2,0},{4,6},{6,4},{8,10},{10,8},{12,14},{14,12},{16,18},{18,... | collective-permute-start | bytes 344072 | tf_op jit(solution)/shard_map/ppermute | solution.py:177
  31.4 4.9 %collective-permute-start.6 = (bf16[16,3584]{1,0:T(8,128)(2,1)S(1)}, bf16[16,3584]{1,0:T(8,128)(2,1)S(1)}, u32[]{:S(2)}, u32[]{:S(2)}) collective-permute-start(bf16[16,3584]{1,0:T(8,128)(2,1)S(1)} %shard_map.77), channel_id=1, source_target_pairs={{0,4},{2,6},{4,0},{6,2},{8,12},{10,14},{12,8},{14,10},{16,20},{18,... | collective-permute-start | bytes 344072 | tf_op jit(solution)/shard_map/ppermute | solution.py:177
  32.9 5.6 %collective-permute-start.13 = (bf16[16,3584]{1,0:T(8,128)(2,1)S(1)}, bf16[16,3584]{1,0:T(8,128)(2,1)S(1)}, u32[]{:S(2)}, u32[]{:S(2)}) collective-permute-start(bf16[16,3584]{1,0:T(8,128)(2,1)S(1)} %get-tuple-element.42), channel_id=1, source_target_pairs={{0,4},{2,6},{4,0},{6,2},{8,12},{10,14},{12,8},{14,10},{16,20},{18,... | collective-permute-start | bytes 344072 | tf_op jit(solution)/shard_map/ppermute | solution.py:177
  33.9 4.9 %collective-permute-start.15 = (bf16[16,3584]{1,0:T(8,128)(2,1)S(1)}, bf16[16,3584]{1,0:T(8,128)(2,1)S(1)}, u32[]{:S(2)}, u32[]{:S(2)}) collective-permute-start(bf16[16,3584]{1,0:T(8,128)(2,1)S(1)} %shard_map.82), channel_id=1, source_target_pairs={{0,2},{2,0},{4,6},{6,4},{8,10},{10,8},{12,14},{14,12},{16,18},{18,... | collective-permute-start | bytes 344072 | tf_op jit(solution)/shard_map/ppermute | solution.py:177
  36.3 6.0 %collective-permute-start.7 = (bf16[8,3584]{1,0:T(8,128)(2,1)S(1)}, bf16[8,3584]{1,0:T(8,128)(2,1)S(1)}, u32[]{:S(2)}, u32[]{:S(2)}) collective-permute-start(bf16[8,3584]{1,0:T(8,128)(2,1)S(1)} %get-tuple-element.38), channel_id=1, source_target_pairs={{0,16},{2,18},{4,20},{6,22},{8,24},{10,26},{12,28},{14,30},{16,0},... | collective-permute-start | bytes 172040 | tf_op jit(solution)/shard_map/ppermute | solution.py:177
  38.8 4.2 %collective-permute-start.16 = (bf16[8,3584]{1,0:T(8,128)(2,1)S(1)}, bf16[8,3584]{1,0:T(8,128)(2,1)S(1)}, u32[]{:S(2)}, u32[]{:S(2)}) collective-permute-start(bf16[8,3584]{1,0:T(8,128)(2,1)S(1)} %get-tuple-element.45), channel_id=1, source_target_pairs={{0,8},{2,10},{4,12},{6,14},{8,0},{10,2},{12,4},{14,6},{16,24},{18,... | collective-permute-start | bytes 172040 | tf_op jit(solution)/shard_map/ppermute | solution.py:177
  39.8 6.0 %collective-permute-start.17 = (bf16[8,3584]{1,0:T(8,128)(2,1)S(1)}, bf16[8,3584]{1,0:T(8,128)(2,1)S(1)}, u32[]{:S(2)}, u32[]{:S(2)}) collective-permute-start(bf16[8,3584]{1,0:T(8,128)(2,1)S(1)} %get-tuple-element.46), channel_id=1, source_target_pairs={{0,24},{2,26},{4,28},{6,30},{8,16},{10,18},{12,20},{14,22},{16,8},... | collective-permute-start | bytes 172040 | tf_op jit(solution)/shard_map/ppermute | solution.py:177

commit v8 on v7

--- a/solution.py
+++ b/solution.py
@@ -84,16 +84,20 @@
     unstack(rows, row_outs)
 
 
-def prepare_kernel(w_in, w_out, combine, w_in_held, w_out_held, near_terms, far_terms, sems):
-    half = w_in.shape[1] // 2
-    rows = [pl.ds(0, half), pl.ds(half, half)]
+def fetch_kernel(*refs):
+    source, held, sems = refs[0], refs[-2], refs[-1]
+    rows = held.shape[0] // sems.shape[0]
     copies = [
-        pltpu.make_async_copy(w_in.at[i, r], w_in_held.at[i, r], sems.at[2 * i + j])
-        for i in range(2)
-        for j, r in enumerate(rows)
-    ] + [pltpu.make_async_copy(w_out, w_out_held, sems.at[4])]
+        pltpu.make_async_copy(source.at[pl.ds(i * rows, rows)], held.at[pl.ds(i * rows, rows)], sem)
+        for i, sem in enumerate(sems.at[j] for j in range(sems.shape[0]))
+    ]
     for c in copies:
         c.start()
+    for c in copies:
+        c.wait()
+
+
+def terms_kernel(combine, near_terms, far_terms):
     slots = combine.shape[0] // 2
     same = (iota((slots, slots), 0) == iota((slots, slots), 1)).astype(jnp.float32)
     for start, out in ((0, near_terms), (slots, far_terms)):
@@ -108,8 +112,6 @@
                 )
             )
         out[...] = jnp.concatenate(terms, axis=0).astype(jnp.bfloat16)
-    for c in copies:
-        c.wait()
 
 
 def stack_kernel(count, *refs):
@@ -195,20 +197,26 @@
     )
     chunks = [swap(c, d * group_size) if d else c for d, c in zip(offsets, chunks)]
     terms = jax.ShapeDtypeStruct((3 * tok_count, slots // 2), bf16)
-    w_in, w_out, *terms = call(
-        prepare_kernel,
-        (*in_hbm(w_in, w_out), combine),
-        [HBM] * 2 + [VMEM],
-        [*(jax.ShapeDtypeStruct(w.shape, bf16) for w in (w_in, w_out)), terms, terms],
-        16 * MIB,
-        [pltpu.SemaphoreType.DMA((5,))],
-        2 * (w_in.size + w_out.size),
-    )
+    terms = local(terms_kernel, [combine], [terms, terms])
+
+    def fetch(array, after):
+        return call(
+            fetch_kernel,
+            (*in_hbm(array), after),
+            [HBM, VMEM],
+            jax.ShapeDtypeStruct(array.shape, bf16),
+            16 * MIB,
+            [pltpu.SemaphoreType.DMA((2,))],
+            2 * array.size,
+        )
+
+    w_in = fetch(w_in, terms[0])
+    w_out = fetch(w_out, terms[1])
 
     square = group_size == 4
     count = slot_count // 2
     sides = ((1, 2), (2, 1))
-    earlier = []
+    earlier = chunks[count:] + [w_in]
     summed = []
     for h in range(2):
         a, b = sides[h]
@@ -220,7 +228,7 @@
             held = [own, held[a], held[b], swap(held[a], b)]
         else:
             held = [swap(own, q) if q else own for q in range(group_size)]
-        earlier = [held[1]]
+        earlier = []
         result = local(
             functools.partial(expert_kernel, group_size),
             held + [w_in, w_out],

time: 46.8 us -> 44.8 us (0.957)
  starting transfers between devices: 26.7 us -> 24 us
  Pallas kernels: 7.42 us -> 8.5 us
    ppermute x18, starting transfers between devices: 26.7 us -> 24 us  [swap(): lax.ppermute(value, 'expert', [(e, e ^ offset) for e in range(n_devices)])]
    pallas_call x12 -> x14, Pallas kernels: 7.42 us -> 8.5 us  [call(): pl.pallas_call(kernel, out_shape=outs, in_specs=in_specs, out_specs=jax.t...]
  transfers between devices with their start and end apart: 18 -> 18, of which waited for: 11 -> 11; matrix products, arithmetic and copies ran while one was open for 0% -> 0% of each run, Pallas kernels for 11% -> 14%
where the time goes in v8:
time: 44.8 us; the launch traced here: 44.6 us
  starting transfers between devices  24 us (54%)
  waiting for transfers between devices  12 us (27%)
  Pallas kernels  8.5 us (19%)
    ppermute x18, starting transfers between devices, swap(): lax.ppermute(value, 'expert', [(e, e ^ offset) for e in range(n_devices)])  24 us
    ppermute x18, waiting for transfers between devices, swap(): lax.ppermute(value, 'expert', [(e, e ^ offset) for e in range(n_devices)])  12 us
    pallas_call x14, Pallas kernels, call(): pl.pallas_call(kernel, out_shape=outs, in_specs=in_specs, out_specs=jax.t...  8.5 us
  transfers between devices with their start and end apart: 18, of which 11 were waited for; matrix products, arithmetic and copies ran while one was open for 0% of the time, Pallas kernels for 14%

profile of v8, /device:TPU:0, one launch (start us, length us, event | category | flops | bytes accessed | tf_op | source)
XLA Modules:
  0.0 44.6 jit_solution(6858531695645065645)
XLA Ops:
  0.0 1.2 %shard_map.73 = (bf16[8,3584]{1,0:T(8,128)(2,1)S(1)}, bf16[8,3584]{1,0:T(8,128)(2,1)S(1)}, bf16[8,3584]{1,0:T(8,128)(2,1)S(1)}, bf16[8,3584]{1,0:T(8,128)(2,1)S(1)}, f32[32,16]{1,0:T(8,128)S(1)}) custom-call(s32[4]{0:T(128)} %refs_0_.3, s32[2,16]{1,0:T(2,128)} %bitcast.3, s32[2,16]{1,0:T(2,128)} %bitcast.4, f32[2,16]{1,0:T(2,128)} %bitcast.5, ...), custom_call_target="tpu_custom_call" | custom-call | tf_op jit(solution)/shard_map/pallas_call | solution.py:153
  1.2 4.1 %collective-permute-start = (bf16[8,3584]{1,0:T(8,128)(2,1)S(1)}, bf16[8,3584]{1,0:T(8,128)(2,1)S(1)}, u32[]{:S(2)}, u32[]{:S(2)}) collective-permute-start(bf16[8,3584]{1,0:T(8,128)(2,1)S(1)} %get-tuple-element.28), channel_id=1, source_target_pairs={{0,16},{2,18},{4,20},{6,22},{8,24},{10,26},{12,28},{14,30},{16,0},... | collective-permute-start | bytes 172040 | tf_op jit(solution)/shard_map/ppermute | solution.py:179
  5.3 1.6 %collective-permute-start.1 = (bf16[8,3584]{1,0:T(8,128)(2,1)S(1)}, bf16[8,3584]{1,0:T(8,128)(2,1)S(1)}, u32[]{:S(2)}, u32[]{:S(2)}) collective-permute-start(bf16[8,3584]{1,0:T(8,128)(2,1)S(1)} %get-tuple-element.29), channel_id=1, source_target_pairs={{0,8},{2,10},{4,12},{6,14},{8,0},{10,2},{12,4},{14,6},{16,24},{18,... | collective-permute-start | bytes 172040 | tf_op jit(solution)/shard_map/ppermute | solution.py:179
  7.1 2.1 %shard_map.75.refs_4_ = bf16[2,3584,256]{2,1,0:T(8,128)(2,1)S(1)} custom-call(bf16[2,3584,256]{2,1,0:T(8,128)(2,1)} %refs_0_.4, bf16[48,16]{1,0:T(8,128)(2,1)S(1)} %get-tuple-element.26.refs_1_.terms), custom_call_target="tpu_custom_call" | custom-call | bytes 3670016 | tf_op jit(solution)/shard_map/pallas_call | solution.py:153
  9.5 3.4 %collective-permute-done.2.refs_3_.refs_1_ = bf16[8,3584]{1,0:T(8,128)(2,1)S(1)} collective-permute-done((bf16[8,3584]{1,0:T(8,128)(2,1)S(1)}, bf16[8,3584]{1,0:T(8,128)(2,1)S(1)}, u32[]{:S(2)}, u32[]{:S(2)}) %collective-permute-start.2) | collective-permute-done | bytes 57376 | tf_op jit(solution)/shard_map/ppermute | solution.py:179
  12.8 1.6 %collective-permute-start.3 = (bf16[16,3584]{1,0:T(8,128)(2,1)S(1)}, bf16[16,3584]{1,0:T(8,128)(2,1)S(1)}, u32[]{:S(2)}, u32[]{:S(2)}) collective-permute-start(bf16[16,3584]{1,0:T(8,128)(2,1)S(1)} %shard_map.76.refs_0_), channel_id=1, source_target_pairs={{0,2},{2,0},{4,6},{6,4},{8,10},{10,8},{12,14},{14,12},{16,18},{18,... | collective-permute-start | bytes 344072 | tf_op jit(solution)/shard_map/ppermute | solution.py:179
  14.4 1.6 %collective-permute-start.10 = (bf16[16,3584]{1,0:T(8,128)(2,1)S(1)}, bf16[16,3584]{1,0:T(8,128)(2,1)S(1)}, u32[]{:S(2)}, u32[]{:S(2)}) collective-permute-start(bf16[16,3584]{1,0:T(8,128)(2,1)S(1)} %shard_map.82.refs_0_), channel_id=1, source_target_pairs={{0,4},{2,6},{4,0},{6,2},{8,12},{10,14},{12,8},{14,10},{16,20},{18,... | collective-permute-start | bytes 344072 | tf_op jit(solution)/shard_map/ppermute | solution.py:179
  16.0 0.5 %collective-permute-start.4 = (bf16[16,3584]{1,0:T(8,128)(2,1)S(1)}, bf16[16,3584]{1,0:T(8,128)(2,1)S(1)}, u32[]{:S(2)}, u32[]{:S(2)}) collective-permute-start(bf16[16,3584]{1,0:T(8,128)(2,1)S(1)} %shard_map.76.refs_0_), channel_id=1, source_target_pairs={{0,4},{2,6},{4,0},{6,2},{8,12},{10,14},{12,8},{14,10},{16,20},{18,... | collective-permute-start | bytes 344072 | tf_op jit(solution)/shard_map/ppermute | solution.py:179
  16.5 1.2 %collective-permute-done.3.refs_1_ = bf16[16,3584]{1,0:T(8,128)(2,1)S(1)} collective-permute-done((bf16[16,3584]{1,0:T(8,128)(2,1)S(1)}, bf16[16,3584]{1,0:T(8,128)(2,1)S(1)}, u32[]{:S(2)}, u32[]{:S(2)}) %collective-permute-start.3) | collective-permute-done | bytes 114720 | tf_op jit(solution)/shard_map/ppermute | solution.py:179
  17.7 1.6 %collective-permute-start.5 = (bf16[16,3584]{1,0:T(8,128)(2,1)S(1)}, bf16[16,3584]{1,0:T(8,128)(2,1)S(1)}, u32[]{:S(2)}, u32[]{:S(2)}) collective-permute-start(bf16[16,3584]{1,0:T(8,128)(2,1)S(1)} %collective-permute-done.3.refs_1_), channel_id=1, source_target_pairs={{0,4},{2,6},{4,0},{6,2},{8,12},{10,14},{12,8},{14,10},{16,20},{18,... | collective-permute-start | bytes 344072 | tf_op jit(solution)/shard_map/ppermute | solution.py:179
  19.3 1.5 %collective-permute-start.11 = (bf16[16,3584]{1,0:T(8,128)(2,1)S(1)}, bf16[16,3584]{1,0:T(8,128)(2,1)S(1)}, u32[]{:S(2)}, u32[]{:S(2)}) collective-permute-start(bf16[16,3584]{1,0:T(8,128)(2,1)S(1)} %shard_map.82.refs_0_), channel_id=1, source_target_pairs={{0,2},{2,0},{4,6},{6,4},{8,10},{10,8},{12,14},{14,12},{16,18},{18,... | collective-permute-start | bytes 344072 | tf_op jit(solution)/shard_map/ppermute | solution.py:179
  20.8 0.5 %collective-permute-start.12 = (bf16[16,3584]{1,0:T(8,128)(2,1)S(1)}, bf16[16,3584]{1,0:T(8,128)(2,1)S(1)}, u32[]{:S(2)}, u32[]{:S(2)}) collective-permute-start(bf16[16,3584]{1,0:T(8,128)(2,1)S(1)} %collective-permute-done.10.refs_1_), channel_id=1, source_target_pairs={{0,2},{2,0},{4,6},{6,4},{8,10},{10,8},{12,14},{14,12},{16,18},{18,... | collective-permute-start | bytes 344072 | tf_op jit(solution)/shard_map/ppermute | solution.py:179
  21.3 1.5 %shard_map.77.refs_5_ = bf16[256,3584]{1,0:T(8,128)(2,1)S(1)} custom-call(bf16[256,3584]{1,0:T(8,128)(2,1)} %refs_0_.5, bf16[48,16]{1,0:T(8,128)(2,1)S(1)} %get-tuple-element.25.refs_1_.terms), custom_call_target="tpu_custom_call" | custom-call | bytes 1835008 | tf_op jit(solution)/shard_map/pallas_call | solution.py:153
  22.8 1.2 %shard_map.78 = (bf16[16,3584]{1,0:T(8,128)(2,1)S(1)}, bf16[16,3584]{1,0:T(8,128)(2,1)S(1)}, bf16[16,3584]{1,0:T(8,128)(2,1)S(1)}, bf16[16,3584]{1,0:T(8,128)(2,1)S(1)}) custom-call(bf16[16,3584]{1,0:T(8,128)(2,1)S(1)} %shard_map.76.refs_0_, bf16[16,3584]{1,0:T(8,128)(2,1)S(1)} %collective-permute-done.3.refs_1_, ...), custom_call_target="tpu_custom_call" | custom-call | tf_op jit(solution)/shard_map/pallas_call | solution.py:153
  24.0 1.6 %collective-permute-start.7 = (bf16[16,3584]{1,0:T(8,128)(2,1)S(1)}, bf16[16,3584]{1,0:T(8,128)(2,1)S(1)}, u32[]{:S(2)}, u32[]{:S(2)}) collective-permute-start(bf16[16,3584]{1,0:T(8,128)(2,1)S(1)} %get-tuple-element.34), channel_id=1, source_target_pairs={{0,2},{2,0},{4,6},{6,4},{8,10},{10,8},{12,14},{14,12},{16,18},{18,... | collective-permute-start | bytes 344072 | tf_op jit(solution)/shard_map/ppermute | solution.py:179
  25.6 1.0 %collective-permute-done.12.refs_3_ = bf16[16,3584]{1,0:T(8,128)(2,1)S(1)} collective-permute-done((bf16[16,3584]{1,0:T(8,128)(2,1)S(1)}, bf16[16,3584]{1,0:T(8,128)(2,1)S(1)}, u32[]{:S(2)}, u32[]{:S(2)}) %collective-permute-start.12) | collective-permute-done | bytes 114720 | tf_op jit(solution)/shard_map/ppermute | solution.py:179
  26.6 1.2 %shard_map.83 = (bf16[16,3584]{1,0:T(8,128)(2,1)S(1)}, bf16[16,3584]{1,0:T(8,128)(2,1)S(1)}, bf16[16,3584]{1,0:T(8,128)(2,1)S(1)}, bf16[16,3584]{1,0:T(8,128)(2,1)S(1)}) custom-call(bf16[16,3584]{1,0:T(8,128)(2,1)S(1)} %shard_map.82.refs_0_, bf16[16,3584]{1,0:T(8,128)(2,1)S(1)} %collective-permute-done.10.refs_1_, ...), custom_call_target="tpu_custom_call" | custom-call | tf_op jit(solution)/shard_map/pallas_call | solution.py:153
  27.7 1.0 %collective-permute-start.14 = (bf16[16,3584]{1,0:T(8,128)(2,1)S(1)}, bf16[16,3584]{1,0:T(8,128)(2,1)S(1)}, u32[]{:S(2)}, u32[]{:S(2)}) collective-permute-start(bf16[16,3584]{1,0:T(8,128)(2,1)S(1)} %get-tuple-element.40), channel_id=1, source_target_pairs={{0,4},{2,6},{4,0},{6,2},{8,12},{10,14},{12,8},{14,10},{16,20},{18,... | collective-permute-start | bytes 344072 | tf_op jit(solution)/shard_map/ppermute | solution.py:179
  28.7 0.9 %collective-permute-start.6 = (bf16[16,3584]{1,0:T(8,128)(2,1)S(1)}, bf16[16,3584]{1,0:T(8,128)(2,1)S(1)}, u32[]{:S(2)}, u32[]{:S(2)}) collective-permute-start(bf16[16,3584]{1,0:T(8,128)(2,1)S(1)} %get-tuple-element.32), channel_id=1, source_target_pairs={{0,2},{2,0},{4,6},{6,4},{8,10},{10,8},{12,14},{14,12},{16,18},{18,... | collective-permute-start | bytes 344072 | tf_op jit(solution)/shard_map/ppermute | solution.py:179
  29.6 0.3 collective-permute-done.7.refs_1_
  30.0 1.7 %collective-permute-start.8 = (bf16[16,3584]{1,0:T(8,128)(2,1)S(1)}, bf16[16,3584]{1,0:T(8,128)(2,1)S(1)}, u32[]{:S(2)}, u32[]{:S(2)}) collective-permute-start(bf16[16,3584]{1,0:T(8,128)(2,1)S(1)} %shard_map.79), channel_id=1, source_target_pairs={{0,4},{2,6},{4,0},{6,2},{8,12},{10,14},{12,8},{14,10},{16,20},{18,... | collective-permute-start | bytes 344072 | tf_op jit(solution)/shard_map/ppermute | solution.py:179
  31.6 0.4 collective-permute-start.13
  32.0 0.5 %collective-permute-done.14.refs_1_ = bf16[16,3584]{1,0:T(8,128)(2,1)S(1)} collective-permute-done((bf16[16,3584]{1,0:T(8,128)(2,1)S(1)}, bf16[16,3584]{1,0:T(8,128)(2,1)S(1)}, u32[]{:S(2)}, u32[]{:S(2)}) %collective-permute-start.14) | collective-permute-done | bytes 114720 | tf_op jit(solution)/shard_map/ppermute | solution.py:179
  32.6 1.8 %collective-permute-start.15 = (bf16[16,3584]{1,0:T(8,128)(2,1)S(1)}, bf16[16,3584]{1,0:T(8,128)(2,1)S(1)}, u32[]{:S(2)}, u32[]{:S(2)}) collective-permute-start(bf16[16,3584]{1,0:T(8,128)(2,1)S(1)} %shard_map.84), channel_id=1, source_target_pairs={{0,2},{2,0},{4,6},{6,4},{8,10},{10,8},{12,14},{14,12},{16,18},{18,... | collective-permute-start | bytes 344072 | tf_op jit(solution)/shard_map/ppermute | solution.py:179
  34.4 0.4 collective-permute-done.8.refs_2_
  34.9 1.2 %collective-permute-start.9 = (bf16[8,3584]{1,0:T(8,128)(2,1)S(1)}, bf16[8,3584]{1,0:T(8,128)(2,1)S(1)}, u32[]{:S(2)}, u32[]{:S(2)}) collective-permute-start(bf16[8,3584]{1,0:T(8,128)(2,1)S(1)} %get-tuple-element.36), channel_id=1, source_target_pairs={{0,16},{2,18},{4,20},{6,22},{8,24},{10,26},{12,28},{14,30},{16,0},... | collective-permute-start | bytes 172040 | tf_op jit(solution)/shard_map/ppermute | solution.py:179
  36.0 0.4 collective-permute-done.13.refs_1_
  36.4 1.0 %collective-permute-done.15.refs_2_ = bf16[16,3584]{1,0:T(8,128)(2,1)S(1)} collective-permute-done((bf16[16,3584]{1,0:T(8,128)(2,1)S(1)}, bf16[16,3584]{1,0:T(8,128)(2,1)S(1)}, u32[]{:S(2)}, u32[]{:S(2)}) %collective-permute-start.15) | collective-permute-done | bytes 114720 | tf_op jit(solution)/shard_map/ppermute | solution.py:179
  37.6 2.5 %collective-permute-start.17 = (bf16[8,3584]{1,0:T(8,128)(2,1)S(1)}, bf16[8,3584]{1,0:T(8,128)(2,1)S(1)}, u32[]{:S(2)}, u32[]{:S(2)}) collective-permute-start(bf16[8,3584]{1,0:T(8,128)(2,1)S(1)} %get-tuple-element.42), channel_id=1, source_target_pairs={{0,24},{2,26},{4,28},{6,30},{8,16},{10,18},{12,20},{14,22},{16,8},... | collective-permute-start | bytes 172040 | tf_op jit(solution)/shard_map/ppermute | solution.py:179
  40.3 1.4 %collective-permute-done.16.refs_0_ = bf16[8,3584]{1,0:T(8,128)(2,1)S(1)} collective-permute-done((bf16[8,3584]{1,0:T(8,128)(2,1)S(1)}, bf16[8,3584]{1,0:T(8,128)(2,1)S(1)}, u32[]{:S(2)}, u32[]{:S(2)}) %collective-permute-start.16) | collective-permute-done | bytes 57376 | tf_op jit(solution)/shard_map/ppermute | solution.py:179
  41.8 2.0 %collective-permute-done.17.refs_1_ = bf16[8,3584]{1,0:T(8,128)(2,1)S(1)} collective-permute-done((bf16[8,3584]{1,0:T(8,128)(2,1)S(1)}, bf16[8,3584]{1,0:T(8,128)(2,1)S(1)}, u32[]{:S(2)}, u32[]{:S(2)}) %collective-permute-start.17) | collective-permute-done | bytes 57376 | tf_op jit(solution)/shard_map/ppermute | solution.py:179
  43.7 0.9 %shard_map.86 = bf16[16,3584]{1,0:T(8,128)(2,1)} custom-call(bf16[48,16]{1,0:T(8,128)(2,1)S(1)} %get-tuple-element.25.refs_1_.terms, f32[16,3584]{1,0:T(8,128)S(1)} %shard_map.81.near, bf16[8,3584]{1,0:T(8,128)(2,1)S(1)} %collective-permute-done.16.refs_0_, bf16[8,3584]{1,0:T(8,128)(2,1)S(1)} %collective-permute-done.17.refs_1_), custom_call_target="tpu_custom_call" | custom-call | tf_op jit(solution)/shard_map/pallas_call | solution.py:153
  (18 shorter events, 1.0 us)
Async XLA Ops:
  1.2 8.0 %collective-permute-start = (bf16[8,3584]{1,0:T(8,128)(2,1)S(1)}, bf16[8,3584]{1,0:T(8,128)(2,1)S(1)}, u32[]{:S(2)}, u32[]{:S(2)}) collective-permute-start(bf16[8,3584]{1,0:T(8,128)(2,1)S(1)} %get-tuple-element.28), channel_id=1, source_target_pairs={{0,16},{2,18},{4,20},{6,22},{8,24},{10,26},{12,28},{14,30},{16,0},... | collective-permute-start | bytes 172040 | tf_op jit(solution)/shard_map/ppermute | solution.py:179
  5.3 4.2 %collective-permute-start.1 = (bf16[8,3584]{1,0:T(8,128)(2,1)S(1)}, bf16[8,3584]{1,0:T(8,128)(2,1)S(1)}, u32[]{:S(2)}, u32[]{:S(2)}) collective-permute-start(bf16[8,3584]{1,0:T(8,128)(2,1)S(1)} %get-tuple-element.29), channel_id=1, source_target_pairs={{0,8},{2,10},{4,12},{6,14},{8,0},{10,2},{12,4},{14,6},{16,24},{18,... | collective-permute-start | bytes 172040 | tf_op jit(solution)/shard_map/ppermute | solution.py:179
  6.9 6.0 %collective-permute-start.2 = (bf16[8,3584]{1,0:T(8,128)(2,1)S(1)}, bf16[8,3584]{1,0:T(8,128)(2,1)S(1)}, u32[]{:S(2)}, u32[]{:S(2)}) collective-permute-start(bf16[8,3584]{1,0:T(8,128)(2,1)S(1)} %get-tuple-element.30), channel_id=1, source_target_pairs={{0,24},{2,26},{4,28},{6,30},{8,16},{10,18},{12,20},{14,22},{16,8},... | collective-permute-start | bytes 172040 | tf_op jit(solution)/shard_map/ppermute | solution.py:179
  12.8 4.9 %collective-permute-start.3 = (bf16[16,3584]{1,0:T(8,128)(2,1)S(1)}, bf16[16,3584]{1,0:T(8,128)(2,1)S(1)}, u32[]{:S(2)}, u32[]{:S(2)}) collective-permute-start(bf16[16,3584]{1,0:T(8,128)(2,1)S(1)} %shard_map.76.refs_0_), channel_id=1, source_target_pairs={{0,2},{2,0},{4,6},{6,4},{8,10},{10,8},{12,14},{14,12},{16,18},{18,... | collective-permute-start | bytes 344072 | tf_op jit(solution)/shard_map/ppermute | solution.py:179
  14.4 6.4 %collective-permute-start.10 = (bf16[16,3584]{1,0:T(8,128)(2,1)S(1)}, bf16[16,3584]{1,0:T(8,128)(2,1)S(1)}, u32[]{:S(2)}, u32[]{:S(2)}) collective-permute-start(bf16[16,3584]{1,0:T(8,128)(2,1)S(1)} %shard_map.82.refs_0_), channel_id=1, source_target_pairs={{0,4},{2,6},{4,0},{6,2},{8,12},{10,14},{12,8},{14,10},{16,20},{18,... | collective-permute-start | bytes 344072 | tf_op jit(solution)/shard_map/ppermute | solution.py:179
  16.0 6.8 %collective-permute-start.4 = (bf16[16,3584]{1,0:T(8,128)(2,1)S(1)}, bf16[16,3584]{1,0:T(8,128)(2,1)S(1)}, u32[]{:S(2)}, u32[]{:S(2)}) collective-permute-start(bf16[16,3584]{1,0:T(8,128)(2,1)S(1)} %shard_map.76.refs_0_), channel_id=1, source_target_pairs={{0,4},{2,6},{4,0},{6,2},{8,12},{10,14},{12,8},{14,10},{16,20},{18,... | collective-permute-start | bytes 344072 | tf_op jit(solution)/shard_map/ppermute | solution.py:179
  17.7 5.1 %collective-permute-start.5 = (bf16[16,3584]{1,0:T(8,128)(2,1)S(1)}, bf16[16,3584]{1,0:T(8,128)(2,1)S(1)}, u32[]{:S(2)}, u32[]{:S(2)}) collective-permute-start(bf16[16,3584]{1,0:T(8,128)(2,1)S(1)} %collective-permute-done.3.refs_1_), channel_id=1, source_target_pairs={{0,4},{2,6},{4,0},{6,2},{8,12},{10,14},{12,8},{14,10},{16,20},{18,... | collective-permute-start | bytes 344072 | tf_op jit(solution)/shard_map/ppermute | solution.py:179
  19.3 6.3 %collective-permute-start.11 = (bf16[16,3584]{1,0:T(8,128)(2,1)S(1)}, bf16[16,3584]{1,0:T(8,128)(2,1)S(1)}, u32[]{:S(2)}, u32[]{:S(2)}) collective-permute-start(bf16[16,3584]{1,0:T(8,128)(2,1)S(1)} %shard_map.82.refs_0_), channel_id=1, source_target_pairs={{0,2},{2,0},{4,6},{6,4},{8,10},{10,8},{12,14},{14,12},{16,18},{18,... | collective-permute-start | bytes 344072 | tf_op jit(solution)/shard_map/ppermute | solution.py:179
  20.8 5.8 %collective-permute-start.12 = (bf16[16,3584]{1,0:T(8,128)(2,1)S(1)}, bf16[16,3584]{1,0:T(8,128)(2,1)S(1)}, u32[]{:S(2)}, u32[]{:S(2)}) collective-permute-start(bf16[16,3584]{1,0:T(8,128)(2,1)S(1)} %collective-permute-done.10.refs_1_), channel_id=1, source_target_pairs={{0,2},{2,0},{4,6},{6,4},{8,10},{10,8},{12,14},{14,12},{16,18},{18,... | collective-permute-start | bytes 344072 | tf_op jit(solution)/shard_map/ppermute | solution.py:179
  24.0 5.9 %collective-permute-start.7 = (bf16[16,3584]{1,0:T(8,128)(2,1)S(1)}, bf16[16,3584]{1,0:T(8,128)(2,1)S(1)}, u32[]{:S(2)}, u32[]{:S(2)}) collective-permute-start(bf16[16,3584]{1,0:T(8,128)(2,1)S(1)} %get-tuple-element.34), channel_id=1, source_target_pairs={{0,2},{2,0},{4,6},{6,4},{8,10},{10,8},{12,14},{14,12},{16,18},{18,... | collective-permute-start | bytes 344072 | tf_op jit(solution)/shard_map/ppermute | solution.py:179
  27.7 4.9 %collective-permute-start.14 = (bf16[16,3584]{1,0:T(8,128)(2,1)S(1)}, bf16[16,3584]{1,0:T(8,128)(2,1)S(1)}, u32[]{:S(2)}, u32[]{:S(2)}) collective-permute-start(bf16[16,3584]{1,0:T(8,128)(2,1)S(1)} %get-tuple-element.40), channel_id=1, source_target_pairs={{0,4},{2,6},{4,0},{6,2},{8,12},{10,14},{12,8},{14,10},{16,20},{18,... | collective-permute-start | bytes 344072 | tf_op jit(solution)/shard_map/ppermute | solution.py:179
  28.7 5.7 %collective-permute-start.6 = (bf16[16,3584]{1,0:T(8,128)(2,1)S(1)}, bf16[16,3584]{1,0:T(8,128)(2,1)S(1)}, u32[]{:S(2)}, u32[]{:S(2)}) collective-permute-start(bf16[16,3584]{1,0:T(8,128)(2,1)S(1)} %get-tuple-element.32), channel_id=1, source_target_pairs={{0,2},{2,0},{4,6},{6,4},{8,10},{10,8},{12,14},{14,12},{16,18},{18,... | collective-permute-start | bytes 344072 | tf_op jit(solution)/shard_map/ppermute | solution.py:179
  30.0 4.9 %collective-permute-start.8 = (bf16[16,3584]{1,0:T(8,128)(2,1)S(1)}, bf16[16,3584]{1,0:T(8,128)(2,1)S(1)}, u32[]{:S(2)}, u32[]{:S(2)}) collective-permute-start(bf16[16,3584]{1,0:T(8,128)(2,1)S(1)} %shard_map.79), channel_id=1, source_target_pairs={{0,4},{2,6},{4,0},{6,2},{8,12},{10,14},{12,8},{14,10},{16,20},{18,... | collective-permute-start | bytes 344072 | tf_op jit(solution)/shard_map/ppermute | solution.py:179
  31.6 4.8 %collective-permute-start.13 = (bf16[16,3584]{1,0:T(8,128)(2,1)S(1)}, bf16[16,3584]{1,0:T(8,128)(2,1)S(1)}, u32[]{:S(2)}, u32[]{:S(2)}) collective-permute-start(bf16[16,3584]{1,0:T(8,128)(2,1)S(1)} %get-tuple-element.38), channel_id=1, source_target_pairs={{0,4},{2,6},{4,0},{6,2},{8,12},{10,14},{12,8},{14,10},{16,20},{18,... | collective-permute-start | bytes 344072 | tf_op jit(solution)/shard_map/ppermute | solution.py:179
  32.6 4.9 %collective-permute-start.15 = (bf16[16,3584]{1,0:T(8,128)(2,1)S(1)}, bf16[16,3584]{1,0:T(8,128)(2,1)S(1)}, u32[]{:S(2)}, u32[]{:S(2)}) collective-permute-start(bf16[16,3584]{1,0:T(8,128)(2,1)S(1)} %shard_map.84), channel_id=1, source_target_pairs={{0,2},{2,0},{4,6},{6,4},{8,10},{10,8},{12,14},{14,12},{16,18},{18,... | collective-permute-start | bytes 344072 | tf_op jit(solution)/shard_map/ppermute | solution.py:179
  34.9 5.3 %collective-permute-start.9 = (bf16[8,3584]{1,0:T(8,128)(2,1)S(1)}, bf16[8,3584]{1,0:T(8,128)(2,1)S(1)}, u32[]{:S(2)}, u32[]{:S(2)}) collective-permute-start(bf16[8,3584]{1,0:T(8,128)(2,1)S(1)} %get-tuple-element.36), channel_id=1, source_target_pairs={{0,16},{2,18},{4,20},{6,22},{8,24},{10,26},{12,28},{14,30},{16,0},... | collective-permute-start | bytes 172040 | tf_op jit(solution)/shard_map/ppermute | solution.py:179
  37.5 4.2 %collective-permute-start.16 = (bf16[8,3584]{1,0:T(8,128)(2,1)S(1)}, bf16[8,3584]{1,0:T(8,128)(2,1)S(1)}, u32[]{:S(2)}, u32[]{:S(2)}) collective-permute-start(bf16[8,3584]{1,0:T(8,128)(2,1)S(1)} %get-tuple-element.41), channel_id=1, source_target_pairs={{0,8},{2,10},{4,12},{6,14},{8,0},{10,2},{12,4},{14,6},{16,24},{18,... | collective-permute-start | bytes 172040 | tf_op jit(solution)/shard_map/ppermute | solution.py:179
  37.6 6.1 %collective-permute-start.17 = (bf16[8,3584]{1,0:T(8,128)(2,1)S(1)}, bf16[8,3584]{1,0:T(8,128)(2,1)S(1)}, u32[]{:S(2)}, u32[]{:S(2)}) collective-permute-start(bf16[8,3584]{1,0:T(8,128)(2,1)S(1)} %get-tuple-element.42), channel_id=1, source_target_pairs={{0,24},{2,26},{4,28},{6,30},{8,16},{10,18},{12,20},{14,22},{16,8},... | collective-permute-start | bytes 172040 | tf_op jit(solution)/shard_map/ppermute | solution.py:179

commit v9 on v8

--- a/solution.py
+++ b/solution.py
@@ -28,8 +28,9 @@
 
 
 def route_kernel(group_size, slot_count, *refs):
+    chain = slot_count // 2
     sources, refs = refs[:5], refs[5:]
-    row_outs, combine_out, refs = refs[:slot_count], refs[slot_count], refs[slot_count + 1 :]
+    row_outs, combine_out, refs = refs[: chain + 1], refs[chain + 1], refs[chain + 2 :]
     scratch, sems = refs[:5], refs[5]
     copies_in = [
         pltpu.make_async_copy(s, t, sems.at[i]) for i, (s, t) in enumerate(zip(sources, scratch))
@@ -40,6 +41,7 @@
     capacity = row_outs[0].shape[0]
     top_count, tok_count = expert_ids.shape
     own = lax.axis_index("expert") // group_size
+    core = lax.axis_index("dp") % 2
     copy_row = iota((slot_count, tok_count), 0)
     named = jnp.zeros_like(copy_row)
     before = jnp.zeros_like(copy_row)
@@ -50,7 +52,8 @@
         here = copy_row == p
         named = jnp.where(here, placement[p], named)
         d = lax.bitwise_xor(own, p)
-        relative = jnp.where(here, d // 2 + d % 2 * (slot_count // 2), relative)
+        step = jnp.where(d % 2 == 0, (d // 2 + chain - 1) % chain, d // 2)
+        relative = jnp.where(here, step + jnp.where(d % 2 == core, 0, chain), relative)
         seen = jnp.int32(0)
         for q in range(p):
             seen = seen + (placement[q] == placement[p]).astype(jnp.int32)
@@ -114,8 +117,33 @@
         out[...] = jnp.concatenate(terms, axis=0).astype(jnp.bfloat16)
 
 
-def stack_kernel(count, *refs):
-    refs[-1][...] = stack(refs[:count]).astype(jnp.bfloat16)
+def message_kernel(chain, *refs):
+    own, other, outs = refs[:chain], refs[chain][...].astype(jnp.float32), refs[chain + 1 :]
+    capacity = own[0].shape[0]
+    for j, out in enumerate(outs):
+        rows = other[j * capacity : (j + 1) * capacity]
+        out[...] = jnp.concatenate([own[j][...].astype(jnp.float32), rows], axis=0).astype(
+            jnp.bfloat16
+        )
+
+
+def arrived(refs, kept):
+    core = lax.axis_index("dp") % 2
+    values = [r[...].astype(jnp.float32) for r in refs]
+    values[-1] = jnp.where(core == 0, kept[...].astype(jnp.float32), values[-1])
+    return values
+
+
+def block_kernel(chain, *refs):
+    values = arrived(refs[:chain], refs[chain])
+    refs[-1][...] = jnp.concatenate(values, axis=0).astype(jnp.bfloat16)
+
+
+def split_kernel(chain, *refs):
+    values = arrived(refs[:chain], refs[chain])
+    half = values[0].shape[0] // 2
+    refs[-2][...] = jnp.concatenate([v[:half] for v in values], axis=0).astype(jnp.bfloat16)
+    refs[-1][...] = jnp.concatenate([v[half:] for v in values], axis=0).astype(jnp.bfloat16)
 
 
 def expert_kernel(count, *refs):
@@ -170,13 +198,32 @@
     tok_count, width = tokens.shape
     capacity = tok_count * expert_ids.shape[1] // slot_count
     slots = slot_count * capacity
-    offsets = [*range(0, slot_count, 2), *range(1, slot_count, 2)]
     bf16 = jnp.bfloat16
+    chain = slot_count // 2
     chunk = jax.ShapeDtypeStruct((capacity, width), bf16)
-    half = jax.ShapeDtypeStruct((slots // 2, width), bf16)
-
-    def swap(value, offset):
-        return lax.ppermute(value, "expert", [(e, e ^ offset) for e in range(n_devices)])
+    pair = jax.ShapeDtypeStruct((2 * capacity, width), bf16)
+    half = jax.ShapeDtypeStruct((chain * capacity, width), bf16)
+    block = jax.ShapeDtypeStruct((slots, width), bf16)
+    parts = lax.axis_size("dp")
+
+    def move(value, even, odd):
+        pairs = [
+            (e * parts + part, (e ^ offset) * parts + part)
+            for e in range(n_devices)
+            for part in range(parts)
+            for offset in [odd if part % 2 else even]
+            if offset
+        ]
+        return lax.ppermute(value, ("expert", "dp"), pairs)
+
+    def cross_cores(value):
+        return lax.ppermute(value, "dp", [(part, part ^ 1) for part in range(parts)])
+
+    def steps(values):
+        even = [*range(2, slot_count, 2), 0]
+        return [
+            move(v, even[j] * group_size, (2 * j + 1) * group_size) for j, v in enumerate(values)
+        ]
 
     def local(kernel, inputs, outs, limit=16 * MIB):
         return call(kernel, inputs, [VMEM] * len(inputs), outs, limit)
@@ -185,17 +232,19 @@
         return [pltpu.with_memory_space_constraint(a, pltpu.HBM) for a in arrays]
 
     sources = in_hbm(placement, expert_ids.T, replica_pick.T, gate_weights.T, tokens)
-    *chunks, combine = call(
+    *chunks, other, combine = call(
         functools.partial(route_kernel, group_size, slot_count),
         sources,
         [HBM] * 5,
-        [chunk] * slot_count + [jax.ShapeDtypeStruct((slots, tok_count), jnp.float32)],
+        [chunk] * chain + [half, jax.ShapeDtypeStruct((slots, tok_count), jnp.float32)],
         16 * MIB,
         [pltpu.SMEM(placement.shape, jnp.int32)]
         + [pltpu.VMEM(s.shape, s.dtype) for s in sources[1:]]
         + [pltpu.SemaphoreType.DMA((5,))],
     )
-    chunks = [swap(c, d * group_size) if d else c for d, c in zip(offsets, chunks)]
+    messages = local(
+        functools.partial(message_kernel, chain), chunks + [cross_cores(other)], [pair] * chain
+    )
     terms = jax.ShapeDtypeStruct((3 * tok_count, slots // 2), bf16)
     terms = local(terms_kernel, [combine], [terms, terms])
 
@@ -213,47 +262,39 @@
     w_in = fetch(w_in, terms[0])
     w_out = fetch(w_out, terms[1])
 
+    own = local(
+        functools.partial(block_kernel, chain), steps(messages) + [messages[-1], w_in], block
+    )
     square = group_size == 4
-    count = slot_count // 2
-    sides = ((1, 2), (2, 1))
-    earlier = chunks[count:] + [w_in]
-    summed = []
-    for h in range(2):
-        a, b = sides[h]
-        own = local(
-            functools.partial(stack_kernel, count), chunks[h * count :][:count] + earlier, half
-        )
-        if square:
-            held = {a: swap(own, a), b: swap(own, b)}
-            held = [own, held[a], held[b], swap(held[a], b)]
-        else:
-            held = [swap(own, q) if q else own for q in range(group_size)]
-        earlier = []
-        result = local(
-            functools.partial(expert_kernel, group_size),
-            held + [w_in, w_out],
-            [half] * group_size,
-            40 * MIB,
-        )
-        if square:
-            mine, first, second, cross = result
-            cross = swap(cross, a)
-            first = swap(first, a)
-            second = local(functools.partial(sum_kernel, 2), [second, cross], [half])[0]
-            result = [mine, first, swap(second, b)]
-        else:
-            result = [swap(v, q) if q else v for q, v in enumerate(result)]
-        summed += local(functools.partial(sum_kernel, len(result)), result, [chunk] * count)
-    summed = [swap(v, d * group_size) if d else v for d, v in zip(offsets, summed)]
+    if square:
+        first = move(own, 1, 2)
+        held = [own, first, move(own, 2, 1), move(first, 2, 1)]
+    else:
+        held = [move(own, q, q) if q else own for q in range(group_size)]
+    result = local(
+        functools.partial(expert_kernel, group_size),
+        held + [w_in, w_out],
+        [block] * group_size,
+        40 * MIB,
+    )
+    if square:
+        mine, first, second, cross = result
+        cross = move(cross, 1, 2)
+        first = move(first, 1, 2)
+        second = local(functools.partial(sum_kernel, 2), [second, cross], [block])[0]
+        result = [mine, first, move(second, 2, 1)]
+    else:
+        result = [move(v, q, q) if q else v for q, v in enumerate(result)]
+    summed = local(functools.partial(sum_kernel, len(result)), result, [pair] * chain)
+    mine, other = local(
+        functools.partial(split_kernel, chain), steps(summed) + [summed[-1]], [half, half]
+    )
+    other = cross_cores(other)
     near = local(
-        near_kernel,
-        [terms[0]] + summed[:count],
-        jax.ShapeDtypeStruct((tok_count, width), jnp.float32),
+        near_kernel, [terms[0], mine], jax.ShapeDtypeStruct((tok_count, width), jnp.float32)
     )
     return local(
-        far_kernel,
-        [terms[1], near] + summed[count:],
-        jax.ShapeDtypeStruct((tok_count, width), bf16),
+        far_kernel, [terms[1], near, other], jax.ShapeDtypeStruct((tok_count, width), bf16)
     )
 
 

time: 44.8 us -> 51 us (1.14)
  the two profiles are of different devices: /device:TPU:0 before, /device:TPU:25 now
where the time goes in v9:
time: 51 us; the launch traced here: 50.8 us
  waiting for transfers between devices  23.7 us (46%)
  starting transfers between devices  19.7 us (39%)
  Pallas kernels  7.26 us (14%)
    ppermute x10, waiting for transfers between devices, move(): return lax.ppermute(value, ('expert', 'dp'), pairs)  22 us
    ppermute x10, starting transfers between devices, move(): return lax.ppermute(value, ('expert', 'dp'), pairs)  13.6 us
    pallas_call x12, Pallas kernels, call(): pl.pallas_call(kernel, out_shape=outs, in_specs=in_specs, out_specs=jax.t...  7.26 us
    ppermute x2, starting transfers between devices, cross_cores(): lax.ppermute(value, 'dp', [(part, part ^ 1) for part in range(parts)])  6.06 us
    ppermute x2, waiting for transfers between devices, cross_cores(): lax.ppermute(value, 'dp', [(part, part ^ 1) for part in range(parts)])  1.73 us
  transfers between devices with their start and end apart: 12, of which 9 were waited for; matrix products, arithmetic and copies ran while one was open for 0% of the time, Pallas kernels for 8%

profile of v9, /device:TPU:25, one launch (start us, length us, event | category | flops | bytes accessed | tf_op | source)
XLA Modules:
  0.0 50.8 jit_solution(14683099946591974423)
XLA Ops:
  0.0 1.2 %shard_map.73 = (bf16[8,3584]{1,0:T(8,128)(2,1)S(1)}, bf16[8,3584]{1,0:T(8,128)(2,1)S(1)}, bf16[16,3584]{1,0:T(8,128)(2,1)S(1)}, f32[32,16]{1,0:T(8,128)S(1)}) custom-call(s32[4]{0:T(128)} %refs_0_.3, s32[2,16]{1,0:T(2,128)} %bitcast.3, s32[2,16]{1,0:T(2,128)} %bitcast.4, f32[2,16]{1,0:T(2,128)} %bitcast.5, bf16[16,3584]{1,0:T(8,128)(2,1)} %refs_4_.1), custom_call_target="tpu_custom_call" | custom-call | tf_op jit(solution)/shard_map/pallas_call | solution.py:181
  1.2 0.7 %collective-permute-start = (bf16[16,3584]{1,0:T(8,128)(2,1)S(1)}, bf16[16,3584]{1,0:T(8,128)(2,1)S(1)}, u32[]{:S(2)}, u32[]{:S(2)}) collective-permute-start(bf16[16,3584]{1,0:T(8,128)(2,1)S(1)} %get-tuple-element.26), channel_id=1, source_target_pairs={{0,1},{1,0},{2,3},{3,2},{4,5},{5,4},{6,7},{7,6},{8,9},{9,8},{10,11... | collective-permute-start | bytes 344072 | tf_op jit(solution)/shard_map/ppermute | solution.py:220
  1.9 1.0 %collective-permute-done.refs_2_ = bf16[16,3584]{1,0:T(8,128)(2,1)S(1)} collective-permute-done((bf16[16,3584]{1,0:T(8,128)(2,1)S(1)}, bf16[16,3584]{1,0:T(8,128)(2,1)S(1)}, u32[]{:S(2)}, u32[]{:S(2)}) %collective-permute-start) | collective-permute-done | bytes 114720 | tf_op jit(solution)/shard_map/ppermute | solution.py:220
  2.9 0.2 collective-permute-start.1
  3.1 3.0 %collective-permute-start.2 = (bf16[16,3584]{1,0:T(8,128)(2,1)S(1)}, bf16[16,3584]{1,0:T(8,128)(2,1)S(1)}, u32[]{:S(2)}, u32[]{:S(2)}) collective-permute-start(bf16[16,3584]{1,0:T(8,128)(2,1)S(1)} %get-tuple-element.28.refs_2_), channel_id=1, source_target_pairs={{1,25},{3,27},{5,29},{7,31},{9,17},{11,19},{13,21},{15,23},{17,9},... | collective-permute-start | bytes 344072 | tf_op jit(solution)/shard_map/ppermute | solution.py:217
  6.1 0.2 shard_map.74
  6.3 2.1 %shard_map.76.refs_3_.refs_4_ = bf16[2,3584,256]{2,1,0:T(8,128)(2,1)S(1)} custom-call(bf16[2,3584,256]{2,1,0:T(8,128)(2,1)} %refs_0_.4, bf16[48,16]{1,0:T(8,128)(2,1)S(1)} %get-tuple-element.23.refs_1_.terms), custom_call_target="tpu_custom_call" | custom-call | bytes 3670016 | tf_op jit(solution)/shard_map/pallas_call | solution.py:181
  8.4 0.0 collective-permute-done.1.refs_0_
  8.4 2.2 %collective-permute-done.2.refs_1_ = bf16[16,3584]{1,0:T(8,128)(2,1)S(1)} collective-permute-done((bf16[16,3584]{1,0:T(8,128)(2,1)S(1)}, bf16[16,3584]{1,0:T(8,128)(2,1)S(1)}, u32[]{:S(2)}, u32[]{:S(2)}) %collective-permute-start.2) | collective-permute-done | bytes 114720 | tf_op jit(solution)/shard_map/ppermute | solution.py:217
  10.6 1.3 %collective-permute-start.3 = (bf16[32,3584]{1,0:T(8,128)(2,1)S(1)}, bf16[32,3584]{1,0:T(8,128)(2,1)S(1)}, u32[]{:S(2)}, u32[]{:S(2)}) collective-permute-start(bf16[32,3584]{1,0:T(8,128)(2,1)S(1)} %shard_map.77.refs_0_), channel_id=1, source_target_pairs={{0,2},{1,5},{2,0},{3,7},{4,6},{5,1},{6,4},{7,3},{8,10},{9,13},{10,... | collective-permute-start | bytes 688136 | tf_op jit(solution)/shard_map/ppermute | solution.py:217
  11.9 1.2 %collective-permute-start.4 = (bf16[32,3584]{1,0:T(8,128)(2,1)S(1)}, bf16[32,3584]{1,0:T(8,128)(2,1)S(1)}, u32[]{:S(2)}, u32[]{:S(2)}) collective-permute-start(bf16[32,3584]{1,0:T(8,128)(2,1)S(1)} %shard_map.77.refs_0_), channel_id=1, source_target_pairs={{0,4},{1,3},{2,6},{3,1},{4,0},{5,7},{6,2},{7,5},{8,12},{9,11},{10,... | collective-permute-start | bytes 688136 | tf_op jit(solution)/shard_map/ppermute | solution.py:217
  13.1 2.7 %collective-permute-done.3.refs_1_ = bf16[32,3584]{1,0:T(8,128)(2,1)S(1)} collective-permute-done((bf16[32,3584]{1,0:T(8,128)(2,1)S(1)}, bf16[32,3584]{1,0:T(8,128)(2,1)S(1)}, u32[]{:S(2)}, u32[]{:S(2)}) %collective-permute-start.3) | collective-permute-done | bytes 229408 | tf_op jit(solution)/shard_map/ppermute | solution.py:217
  15.8 1.2 %collective-permute-start.5 = (bf16[32,3584]{1,0:T(8,128)(2,1)S(1)}, bf16[32,3584]{1,0:T(8,128)(2,1)S(1)}, u32[]{:S(2)}, u32[]{:S(2)}) collective-permute-start(bf16[32,3584]{1,0:T(8,128)(2,1)S(1)} %collective-permute-done.3.refs_1_), channel_id=1, source_target_pairs={{0,4},{1,3},{2,6},{3,1},{4,0},{5,7},{6,2},{7,5},{8,12},{9,11},{10,... | collective-permute-start | bytes 688136 | tf_op jit(solution)/shard_map/ppermute | solution.py:217
  17.1 1.5 %shard_map.78.refs_5_ = bf16[256,3584]{1,0:T(8,128)(2,1)S(1)} custom-call(bf16[256,3584]{1,0:T(8,128)(2,1)} %refs_0_.5, bf16[48,16]{1,0:T(8,128)(2,1)S(1)} %get-tuple-element.22.refs_1_.terms), custom_call_target="tpu_custom_call" | custom-call | bytes 1835008 | tf_op jit(solution)/shard_map/pallas_call | solution.py:181
  18.5 0.0 collective-permute-done.4.refs_2_
  18.6 3.2 %collective-permute-done.5.refs_3_ = bf16[32,3584]{1,0:T(8,128)(2,1)S(1)} collective-permute-done((bf16[32,3584]{1,0:T(8,128)(2,1)S(1)}, bf16[32,3584]{1,0:T(8,128)(2,1)S(1)}, u32[]{:S(2)}, u32[]{:S(2)}) %collective-permute-start.5) | collective-permute-done | bytes 229408 | tf_op jit(solution)/shard_map/ppermute | solution.py:217
  21.7 1.0 %shard_map.79 = (bf16[32,3584]{1,0:T(8,128)(2,1)S(1)}, bf16[32,3584]{1,0:T(8,128)(2,1)S(1)}, bf16[32,3584]{1,0:T(8,128)(2,1)S(1)}, bf16[32,3584]{1,0:T(8,128)(2,1)S(1)}) custom-call(bf16[32,3584]{1,0:T(8,128)(2,1)S(1)} %shard_map.77.refs_0_, bf16[32,3584]{1,0:T(8,128)(2,1)S(1)} %collective-permute-done.3.refs_1_, ...), custom_call_target="tpu_custom_call" | custom-call | tf_op jit(solution)/shard_map/pallas_call | solution.py:181
  22.7 0.3 collective-permute-start.7
  23.0 1.2 %collective-permute-start.6 = (bf16[32,3584]{1,0:T(8,128)(2,1)S(1)}, bf16[32,3584]{1,0:T(8,128)(2,1)S(1)}, u32[]{:S(2)}, u32[]{:S(2)}) collective-permute-start(bf16[32,3584]{1,0:T(8,128)(2,1)S(1)} %get-tuple-element.30), channel_id=1, source_target_pairs={{0,2},{1,5},{2,0},{3,7},{4,6},{5,1},{6,4},{7,3},{8,10},{9,13},{10,... | collective-permute-start | bytes 688136 | tf_op jit(solution)/shard_map/ppermute | solution.py:217
  24.3 4.4 %collective-permute-done.7.refs_1_ = bf16[32,3584]{1,0:T(8,128)(2,1)S(1)} collective-permute-done((bf16[32,3584]{1,0:T(8,128)(2,1)S(1)}, bf16[32,3584]{1,0:T(8,128)(2,1)S(1)}, u32[]{:S(2)}, u32[]{:S(2)}) %collective-permute-start.7) | collective-permute-done | bytes 229408 | tf_op jit(solution)/shard_map/ppermute | solution.py:217
  28.7 0.1 shard_map.80
  28.7 1.3 %collective-permute-start.8 = (bf16[32,3584]{1,0:T(8,128)(2,1)S(1)}, bf16[32,3584]{1,0:T(8,128)(2,1)S(1)}, u32[]{:S(2)}, u32[]{:S(2)}) collective-permute-start(bf16[32,3584]{1,0:T(8,128)(2,1)S(1)} %shard_map.80), channel_id=1, source_target_pairs={{0,4},{1,3},{2,6},{3,1},{4,0},{5,7},{6,2},{7,5},{8,12},{9,11},{10,... | collective-permute-start | bytes 688136 | tf_op jit(solution)/shard_map/ppermute | solution.py:217
  30.0 1.1 %collective-permute-done.6.refs_1_ = bf16[32,3584]{1,0:T(8,128)(2,1)S(1)} collective-permute-done((bf16[32,3584]{1,0:T(8,128)(2,1)S(1)}, bf16[32,3584]{1,0:T(8,128)(2,1)S(1)}, u32[]{:S(2)}, u32[]{:S(2)}) %collective-permute-start.6) | collective-permute-done | bytes 229408 | tf_op jit(solution)/shard_map/ppermute | solution.py:217
  31.1 4.8 %collective-permute-done.8.refs_2_ = bf16[32,3584]{1,0:T(8,128)(2,1)S(1)} collective-permute-done((bf16[32,3584]{1,0:T(8,128)(2,1)S(1)}, bf16[32,3584]{1,0:T(8,128)(2,1)S(1)}, u32[]{:S(2)}, u32[]{:S(2)}) %collective-permute-start.8) | collective-permute-done | bytes 229408 | tf_op jit(solution)/shard_map/ppermute | solution.py:217
  36.0 0.1 shard_map.81
  36.0 0.1 collective-permute-start.9
  36.1 3.8 %collective-permute-start.10 = (bf16[16,3584]{1,0:T(8,128)(2,1)S(1)}, bf16[16,3584]{1,0:T(8,128)(2,1)S(1)}, u32[]{:S(2)}, u32[]{:S(2)}) collective-permute-start(bf16[16,3584]{1,0:T(8,128)(2,1)S(1)} %get-tuple-element.34.refs_2_), channel_id=1, source_target_pairs={{1,25},{3,27},{5,29},{7,31},{9,17},{11,19},{13,21},{15,23},{17,9},... | collective-permute-start | bytes 344072 | tf_op jit(solution)/shard_map/ppermute | solution.py:217
  40.0 3.6 %collective-permute-done.10.refs_1_ = bf16[16,3584]{1,0:T(8,128)(2,1)S(1)} collective-permute-done((bf16[16,3584]{1,0:T(8,128)(2,1)S(1)}, bf16[16,3584]{1,0:T(8,128)(2,1)S(1)}, u32[]{:S(2)}, u32[]{:S(2)}) %collective-permute-start.10) | collective-permute-done | bytes 114720 | tf_op jit(solution)/shard_map/ppermute | solution.py:217
  43.6 5.3 %collective-permute-start.11 = (bf16[16,3584]{1,0:T(8,128)(2,1)S(1)}, bf16[16,3584]{1,0:T(8,128)(2,1)S(1)}, u32[]{:S(2)}, u32[]{:S(2)}) collective-permute-start(bf16[16,3584]{1,0:T(8,128)(2,1)S(1)} %get-tuple-element.36), channel_id=1, source_target_pairs={{0,1},{1,0},{2,3},{3,2},{4,5},{5,4},{6,7},{7,6},{8,9},{9,8},{10,11... | collective-permute-start | bytes 344072 | tf_op jit(solution)/shard_map/ppermute | solution.py:220
  48.9 0.2 shard_map.83.near
  49.1 0.8 %collective-permute-done.11.refs_0_ = bf16[16,3584]{1,0:T(8,128)(2,1)S(1)} collective-permute-done((bf16[16,3584]{1,0:T(8,128)(2,1)S(1)}, bf16[16,3584]{1,0:T(8,128)(2,1)S(1)}, u32[]{:S(2)}, u32[]{:S(2)}) %collective-permute-start.11) | collective-permute-done | bytes 114720 | tf_op jit(solution)/shard_map/ppermute | solution.py:220
  49.9 0.9 %shard_map.84 = bf16[16,3584]{1,0:T(8,128)(2,1)} custom-call(bf16[48,16]{1,0:T(8,128)(2,1)S(1)} %get-tuple-element.22.refs_1_.terms, f32[16,3584]{1,0:T(8,128)S(1)} %shard_map.83.near, bf16[16,3584]{1,0:T(8,128)(2,1)S(1)} %collective-permute-done.11.refs_0_), custom_call_target="tpu_custom_call" | custom-call | tf_op jit(solution)/shard_map/pallas_call | solution.py:181
  (4 shorter events, 0.1 us)
Async XLA Ops:
  1.2 1.7 %collective-permute-start = (bf16[16,3584]{1,0:T(8,128)(2,1)S(1)}, bf16[16,3584]{1,0:T(8,128)(2,1)S(1)}, u32[]{:S(2)}, u32[]{:S(2)}) collective-permute-start(bf16[16,3584]{1,0:T(8,128)(2,1)S(1)} %get-tuple-element.26), channel_id=1, source_target_pairs={{0,1},{1,0},{2,3},{3,2},{4,5},{5,4},{6,7},{7,6},{8,9},{9,8},{10,11... | collective-permute-start | bytes 344072 | tf_op jit(solution)/shard_map/ppermute | solution.py:220
  2.9 5.5 %collective-permute-start.1 = (bf16[16,3584]{1,0:T(8,128)(2,1)S(1)}, bf16[16,3584]{1,0:T(8,128)(2,1)S(1)}, u32[]{:S(2)}, u32[]{:S(2)}) collective-permute-start(bf16[16,3584]{1,0:T(8,128)(2,1)S(1)} %get-tuple-element.27), channel_id=1, source_target_pairs={{0,16},{1,9},{2,18},{3,11},{4,20},{5,13},{6,22},{7,15},{8,24},{9,1... | collective-permute-start | bytes 344072 | tf_op jit(solution)/shard_map/ppermute | solution.py:217
  3.1 7.4 %collective-permute-start.2 = (bf16[16,3584]{1,0:T(8,128)(2,1)S(1)}, bf16[16,3584]{1,0:T(8,128)(2,1)S(1)}, u32[]{:S(2)}, u32[]{:S(2)}) collective-permute-start(bf16[16,3584]{1,0:T(8,128)(2,1)S(1)} %get-tuple-element.28.refs_2_), channel_id=1, source_target_pairs={{1,25},{3,27},{5,29},{7,31},{9,17},{11,19},{13,21},{15,23},{17,9},... | collective-permute-start | bytes 344072 | tf_op jit(solution)/shard_map/ppermute | solution.py:217
  10.6 5.2 %collective-permute-start.3 = (bf16[32,3584]{1,0:T(8,128)(2,1)S(1)}, bf16[32,3584]{1,0:T(8,128)(2,1)S(1)}, u32[]{:S(2)}, u32[]{:S(2)}) collective-permute-start(bf16[32,3584]{1,0:T(8,128)(2,1)S(1)} %shard_map.77.refs_0_), channel_id=1, source_target_pairs={{0,2},{1,5},{2,0},{3,7},{4,6},{5,1},{6,4},{7,3},{8,10},{9,13},{10,... | collective-permute-start | bytes 688136 | tf_op jit(solution)/shard_map/ppermute | solution.py:217
  11.9 6.6 %collective-permute-start.4 = (bf16[32,3584]{1,0:T(8,128)(2,1)S(1)}, bf16[32,3584]{1,0:T(8,128)(2,1)S(1)}, u32[]{:S(2)}, u32[]{:S(2)}) collective-permute-start(bf16[32,3584]{1,0:T(8,128)(2,1)S(1)} %shard_map.77.refs_0_), channel_id=1, source_target_pairs={{0,4},{1,3},{2,6},{3,1},{4,0},{5,7},{6,2},{7,5},{8,12},{9,11},{10,... | collective-permute-start | bytes 688136 | tf_op jit(solution)/shard_map/ppermute | solution.py:217
  15.8 5.9 %collective-permute-start.5 = (bf16[32,3584]{1,0:T(8,128)(2,1)S(1)}, bf16[32,3584]{1,0:T(8,128)(2,1)S(1)}, u32[]{:S(2)}, u32[]{:S(2)}) collective-permute-start(bf16[32,3584]{1,0:T(8,128)(2,1)S(1)} %collective-permute-done.3.refs_1_), channel_id=1, source_target_pairs={{0,4},{1,3},{2,6},{3,1},{4,0},{5,7},{6,2},{7,5},{8,12},{9,11},{10,... | collective-permute-start | bytes 688136 | tf_op jit(solution)/shard_map/ppermute | solution.py:217
  22.7 5.9 %collective-permute-start.7 = (bf16[32,3584]{1,0:T(8,128)(2,1)S(1)}, bf16[32,3584]{1,0:T(8,128)(2,1)S(1)}, u32[]{:S(2)}, u32[]{:S(2)}) collective-permute-start(bf16[32,3584]{1,0:T(8,128)(2,1)S(1)} %get-tuple-element.32), channel_id=1, source_target_pairs={{0,2},{1,5},{2,0},{3,7},{4,6},{5,1},{6,4},{7,3},{8,10},{9,13},{10,... | collective-permute-start | bytes 688136 | tf_op jit(solution)/shard_map/ppermute | solution.py:217
  23.0 8.1 %collective-permute-start.6 = (bf16[32,3584]{1,0:T(8,128)(2,1)S(1)}, bf16[32,3584]{1,0:T(8,128)(2,1)S(1)}, u32[]{:S(2)}, u32[]{:S(2)}) collective-permute-start(bf16[32,3584]{1,0:T(8,128)(2,1)S(1)} %get-tuple-element.30), channel_id=1, source_target_pairs={{0,2},{1,5},{2,0},{3,7},{4,6},{5,1},{6,4},{7,3},{8,10},{9,13},{10,... | collective-permute-start | bytes 688136 | tf_op jit(solution)/shard_map/ppermute | solution.py:217
  28.7 7.2 %collective-permute-start.8 = (bf16[32,3584]{1,0:T(8,128)(2,1)S(1)}, bf16[32,3584]{1,0:T(8,128)(2,1)S(1)}, u32[]{:S(2)}, u32[]{:S(2)}) collective-permute-start(bf16[32,3584]{1,0:T(8,128)(2,1)S(1)} %shard_map.80), channel_id=1, source_target_pairs={{0,4},{1,3},{2,6},{3,1},{4,0},{5,7},{6,2},{7,5},{8,12},{9,11},{10,... | collective-permute-start | bytes 688136 | tf_op jit(solution)/shard_map/ppermute | solution.py:217
  36.0 3.9 %collective-permute-start.9 = (bf16[16,3584]{1,0:T(8,128)(2,1)S(1)}, bf16[16,3584]{1,0:T(8,128)(2,1)S(1)}, u32[]{:S(2)}, u32[]{:S(2)}) collective-permute-start(bf16[16,3584]{1,0:T(8,128)(2,1)S(1)} %get-tuple-element.33), channel_id=1, source_target_pairs={{0,16},{1,9},{2,18},{3,11},{4,20},{5,13},{6,22},{7,15},{8,24},{9,1... | collective-permute-start | bytes 344072 | tf_op jit(solution)/shard_map/ppermute | solution.py:217
  36.1 7.4 %collective-permute-start.10 = (bf16[16,3584]{1,0:T(8,128)(2,1)S(1)}, bf16[16,3584]{1,0:T(8,128)(2,1)S(1)}, u32[]{:S(2)}, u32[]{:S(2)}) collective-permute-start(bf16[16,3584]{1,0:T(8,128)(2,1)S(1)} %get-tuple-element.34.refs_2_), channel_id=1, source_target_pairs={{1,25},{3,27},{5,29},{7,31},{9,17},{11,19},{13,21},{15,23},{17,9},... | collective-permute-start | bytes 344072 | tf_op jit(solution)/shard_map/ppermute | solution.py:217
  43.6 6.3 %collective-permute-start.11 = (bf16[16,3584]{1,0:T(8,128)(2,1)S(1)}, bf16[16,3584]{1,0:T(8,128)(2,1)S(1)}, u32[]{:S(2)}, u32[]{:S(2)}) collective-permute-start(bf16[16,3584]{1,0:T(8,128)(2,1)S(1)} %get-tuple-element.36), channel_id=1, source_target_pairs={{0,1},{1,0},{2,3},{3,2},{4,5},{5,4},{6,7},{7,6},{8,9},{9,8},{10,11... | collective-permute-start | bytes 344072 | tf_op jit(solution)/shard_map/ppermute | solution.py:220

commit v10 on v8

--- a/solution.py
+++ b/solution.py
@@ -216,7 +216,7 @@
     square = group_size == 4
     count = slot_count // 2
     sides = ((1, 2), (2, 1))
-    earlier = chunks[count:] + [w_in]
+    earlier = []
     summed = []
     for h in range(2):
         a, b = sides[h]
@@ -228,7 +228,7 @@
             held = [own, held[a], held[b], swap(held[a], b)]
         else:
             held = [swap(own, q) if q else own for q in range(group_size)]
-        earlier = []
+        earlier = [w_in]
         result = local(
             functools.partial(expert_kernel, group_size),
             held + [w_in, w_out],

time: 44.8 us -> 45.2 us (level)
  starting transfers between devices: 24 us -> 25.9 us
  waiting for transfers between devices: 12 us -> 10.6 us
    ppermute x18, starting transfers between devices: 24 us -> 25.9 us  [swap(): lax.ppermute(value, 'expert', [(e, e ^ offset) for e in range(n_devices)])]
    ppermute x18, waiting for transfers between devices: 12 us -> 10.6 us  [swap(): lax.ppermute(value, 'expert', [(e, e ^ offset) for e in range(n_devices)])]
  transfers between devices with their start and end apart: 18 -> 18, of which waited for: 11 -> 10; matrix products, arithmetic and copies ran while one was open for 0% -> 0% of each run, Pallas kernels for 14% -> 14%
where the time goes in v10:
time: 45.2 us; the launch traced here: 45.1 us
  starting transfers between devices  25.9 us (57%)
  waiting for transfers between devices  10.6 us (23%)
  Pallas kernels  8.49 us (19%)
    ppermute x18, starting transfers between devices, swap(): lax.ppermute(value, 'expert', [(e, e ^ offset) for e in range(n_devices)])  25.9 us
    ppermute x18, waiting for transfers between devices, swap(): lax.ppermute(value, 'expert', [(e, e ^ offset) for e in range(n_devices)])  10.6 us
    pallas_call x14, Pallas kernels, call(): pl.pallas_call(kernel, out_shape=outs, in_specs=in_specs, out_specs=jax.t...  8.49 us
  transfers between devices with their start and end apart: 18, of which 10 were waited for; matrix products, arithmetic and copies ran while one was open for 0% of the time, Pallas kernels for 14%

profile of v10, /device:TPU:0, one launch (start us, length us, event | category | flops | bytes accessed | tf_op | source)
XLA Modules:
  0.0 45.1 jit_solution(1436780358582015727)
XLA Ops:
  0.0 1.2 %shard_map.73 = (bf16[8,3584]{1,0:T(8,128)(2,1)S(1)}, bf16[8,3584]{1,0:T(8,128)(2,1)S(1)}, bf16[8,3584]{1,0:T(8,128)(2,1)S(1)}, bf16[8,3584]{1,0:T(8,128)(2,1)S(1)}, f32[32,16]{1,0:T(8,128)S(1)}) custom-call(s32[4]{0:T(128)} %refs_0_.3, s32[2,16]{1,0:T(2,128)} %bitcast.3, s32[2,16]{1,0:T(2,128)} %bitcast.4, f32[2,16]{1,0:T(2,128)} %bitcast.5, ...), custom_call_target="tpu_custom_call" | custom-call | tf_op jit(solution)/shard_map/pallas_call | solution.py:153
  1.2 4.1 %collective-permute-start = (bf16[8,3584]{1,0:T(8,128)(2,1)S(1)}, bf16[8,3584]{1,0:T(8,128)(2,1)S(1)}, u32[]{:S(2)}, u32[]{:S(2)}) collective-permute-start(bf16[8,3584]{1,0:T(8,128)(2,1)S(1)} %get-tuple-element.28), channel_id=1, source_target_pairs={{0,16},{2,18},{4,20},{6,22},{8,24},{10,26},{12,28},{14,30},{16,0},... | collective-permute-start | bytes 172040 | tf_op jit(solution)/shard_map/ppermute | solution.py:179
  5.3 1.6 %collective-permute-start.8 = (bf16[8,3584]{1,0:T(8,128)(2,1)S(1)}, bf16[8,3584]{1,0:T(8,128)(2,1)S(1)}, u32[]{:S(2)}, u32[]{:S(2)}) collective-permute-start(bf16[8,3584]{1,0:T(8,128)(2,1)S(1)} %get-tuple-element.35), channel_id=1, source_target_pairs={{0,8},{2,10},{4,12},{6,14},{8,0},{10,2},{12,4},{14,6},{16,24},{18,... | collective-permute-start | bytes 172040 | tf_op jit(solution)/shard_map/ppermute | solution.py:179
  7.1 1.1 %collective-permute-done.refs_1_ = bf16[8,3584]{1,0:T(8,128)(2,1)S(1)} collective-permute-done((bf16[8,3584]{1,0:T(8,128)(2,1)S(1)}, bf16[8,3584]{1,0:T(8,128)(2,1)S(1)}, u32[]{:S(2)}, u32[]{:S(2)}) %collective-permute-start) | collective-permute-done | bytes 57376 | tf_op jit(solution)/shard_map/ppermute | solution.py:179
  8.2 1.8 %collective-permute-start.1 = (bf16[16,3584]{1,0:T(8,128)(2,1)S(1)}, bf16[16,3584]{1,0:T(8,128)(2,1)S(1)}, u32[]{:S(2)}, u32[]{:S(2)}) collective-permute-start(bf16[16,3584]{1,0:T(8,128)(2,1)S(1)} %shard_map.75.refs_0_), channel_id=1, source_target_pairs={{0,2},{2,0},{4,6},{6,4},{8,10},{10,8},{12,14},{14,12},{16,18},{18,... | collective-permute-start | bytes 344072 | tf_op jit(solution)/shard_map/ppermute | solution.py:179
  9.9 2.1 %shard_map.76.refs_4_.refs_2_ = bf16[2,3584,256]{2,1,0:T(8,128)(2,1)S(1)} custom-call(bf16[2,3584,256]{2,1,0:T(8,128)(2,1)} %refs_0_.4, bf16[48,16]{1,0:T(8,128)(2,1)S(1)} %get-tuple-element.26.refs_1_.terms), custom_call_target="tpu_custom_call" | custom-call | bytes 3670016 | tf_op jit(solution)/shard_map/pallas_call | solution.py:153
  12.0 0.8 %collective-permute-done.9.refs_1_ = bf16[8,3584]{1,0:T(8,128)(2,1)S(1)} collective-permute-done((bf16[8,3584]{1,0:T(8,128)(2,1)S(1)}, bf16[8,3584]{1,0:T(8,128)(2,1)S(1)}, u32[]{:S(2)}, u32[]{:S(2)}) %collective-permute-start.9) | collective-permute-done | bytes 57376 | tf_op jit(solution)/shard_map/ppermute | solution.py:179
  12.8 1.6 %collective-permute-start.10 = (bf16[16,3584]{1,0:T(8,128)(2,1)S(1)}, bf16[16,3584]{1,0:T(8,128)(2,1)S(1)}, u32[]{:S(2)}, u32[]{:S(2)}) collective-permute-start(bf16[16,3584]{1,0:T(8,128)(2,1)S(1)} %shard_map.82.refs_0_), channel_id=1, source_target_pairs={{0,4},{2,6},{4,0},{6,2},{8,12},{10,14},{12,8},{14,10},{16,20},{18,... | collective-permute-start | bytes 344072 | tf_op jit(solution)/shard_map/ppermute | solution.py:179
  14.4 0.5 %collective-permute-start.2 = (bf16[16,3584]{1,0:T(8,128)(2,1)S(1)}, bf16[16,3584]{1,0:T(8,128)(2,1)S(1)}, u32[]{:S(2)}, u32[]{:S(2)}) collective-permute-start(bf16[16,3584]{1,0:T(8,128)(2,1)S(1)} %shard_map.75.refs_0_), channel_id=1, source_target_pairs={{0,4},{2,6},{4,0},{6,2},{8,12},{10,14},{12,8},{14,10},{16,20},{18,... | collective-permute-start | bytes 344072 | tf_op jit(solution)/shard_map/ppermute | solution.py:179
  14.9 1.5 %collective-permute-start.3 = (bf16[16,3584]{1,0:T(8,128)(2,1)S(1)}, bf16[16,3584]{1,0:T(8,128)(2,1)S(1)}, u32[]{:S(2)}, u32[]{:S(2)}) collective-permute-start(bf16[16,3584]{1,0:T(8,128)(2,1)S(1)} %collective-permute-done.1.refs_1_), channel_id=1, source_target_pairs={{0,4},{2,6},{4,0},{6,2},{8,12},{10,14},{12,8},{14,10},{16,20},{18,... | collective-permute-start | bytes 344072 | tf_op jit(solution)/shard_map/ppermute | solution.py:179
  16.5 1.5 %collective-permute-start.11 = (bf16[16,3584]{1,0:T(8,128)(2,1)S(1)}, bf16[16,3584]{1,0:T(8,128)(2,1)S(1)}, u32[]{:S(2)}, u32[]{:S(2)}) collective-permute-start(bf16[16,3584]{1,0:T(8,128)(2,1)S(1)} %shard_map.82.refs_0_), channel_id=1, source_target_pairs={{0,2},{2,0},{4,6},{6,4},{8,10},{10,8},{12,14},{14,12},{16,18},{18,... | collective-permute-start | bytes 344072 | tf_op jit(solution)/shard_map/ppermute | solution.py:179
  18.0 0.7 %collective-permute-done.10.refs_1_ = bf16[16,3584]{1,0:T(8,128)(2,1)S(1)} collective-permute-done((bf16[16,3584]{1,0:T(8,128)(2,1)S(1)}, bf16[16,3584]{1,0:T(8,128)(2,1)S(1)}, u32[]{:S(2)}, u32[]{:S(2)}) %collective-permute-start.10) | collective-permute-done | bytes 114720 | tf_op jit(solution)/shard_map/ppermute | solution.py:179
  18.7 1.5 %collective-permute-start.12 = (bf16[16,3584]{1,0:T(8,128)(2,1)S(1)}, bf16[16,3584]{1,0:T(8,128)(2,1)S(1)}, u32[]{:S(2)}, u32[]{:S(2)}) collective-permute-start(bf16[16,3584]{1,0:T(8,128)(2,1)S(1)} %collective-permute-done.10.refs_1_), channel_id=1, source_target_pairs={{0,2},{2,0},{4,6},{6,4},{8,10},{10,8},{12,14},{14,12},{16,18},{18,... | collective-permute-start | bytes 344072 | tf_op jit(solution)/shard_map/ppermute | solution.py:179
  20.2 1.5 %shard_map.77.refs_5_ = bf16[256,3584]{1,0:T(8,128)(2,1)S(1)} custom-call(bf16[256,3584]{1,0:T(8,128)(2,1)} %refs_0_.5, bf16[48,16]{1,0:T(8,128)(2,1)S(1)} %get-tuple-element.25.refs_1_.terms), custom_call_target="tpu_custom_call" | custom-call | bytes 1835008 | tf_op jit(solution)/shard_map/pallas_call | solution.py:153
  21.7 1.2 %shard_map.78 = (bf16[16,3584]{1,0:T(8,128)(2,1)S(1)}, bf16[16,3584]{1,0:T(8,128)(2,1)S(1)}, bf16[16,3584]{1,0:T(8,128)(2,1)S(1)}, bf16[16,3584]{1,0:T(8,128)(2,1)S(1)}) custom-call(bf16[16,3584]{1,0:T(8,128)(2,1)S(1)} %shard_map.75.refs_0_, bf16[16,3584]{1,0:T(8,128)(2,1)S(1)} %collective-permute-done.1.refs_1_, ...), custom_call_target="tpu_custom_call" | custom-call | tf_op jit(solution)/shard_map/pallas_call | solution.py:153
  22.8 1.0 %collective-permute-start.5 = (bf16[16,3584]{1,0:T(8,128)(2,1)S(1)}, bf16[16,3584]{1,0:T(8,128)(2,1)S(1)}, u32[]{:S(2)}, u32[]{:S(2)}) collective-permute-start(bf16[16,3584]{1,0:T(8,128)(2,1)S(1)} %get-tuple-element.32), channel_id=1, source_target_pairs={{0,2},{2,0},{4,6},{6,4},{8,10},{10,8},{12,14},{14,12},{16,18},{18,... | collective-permute-start | bytes 344072 | tf_op jit(solution)/shard_map/ppermute | solution.py:179
  23.8 0.8 %collective-permute-done.12.refs_3_ = bf16[16,3584]{1,0:T(8,128)(2,1)S(1)} collective-permute-done((bf16[16,3584]{1,0:T(8,128)(2,1)S(1)}, bf16[16,3584]{1,0:T(8,128)(2,1)S(1)}, u32[]{:S(2)}, u32[]{:S(2)}) %collective-permute-start.12) | collective-permute-done | bytes 114720 | tf_op jit(solution)/shard_map/ppermute | solution.py:179
  24.7 1.2 %shard_map.83 = (bf16[16,3584]{1,0:T(8,128)(2,1)S(1)}, bf16[16,3584]{1,0:T(8,128)(2,1)S(1)}, bf16[16,3584]{1,0:T(8,128)(2,1)S(1)}, bf16[16,3584]{1,0:T(8,128)(2,1)S(1)}) custom-call(bf16[16,3584]{1,0:T(8,128)(2,1)S(1)} %shard_map.82.refs_0_, bf16[16,3584]{1,0:T(8,128)(2,1)S(1)} %collective-permute-done.10.refs_1_, ...), custom_call_target="tpu_custom_call" | custom-call | tf_op jit(solution)/shard_map/pallas_call | solution.py:153
  25.8 1.6 %collective-permute-start.14 = (bf16[16,3584]{1,0:T(8,128)(2,1)S(1)}, bf16[16,3584]{1,0:T(8,128)(2,1)S(1)}, u32[]{:S(2)}, u32[]{:S(2)}) collective-permute-start(bf16[16,3584]{1,0:T(8,128)(2,1)S(1)} %get-tuple-element.40), channel_id=1, source_target_pairs={{0,4},{2,6},{4,0},{6,2},{8,12},{10,14},{12,8},{14,10},{16,20},{18,... | collective-permute-start | bytes 344072 | tf_op jit(solution)/shard_map/ppermute | solution.py:179
  27.4 1.5 %collective-permute-start.4 = (bf16[16,3584]{1,0:T(8,128)(2,1)S(1)}, bf16[16,3584]{1,0:T(8,128)(2,1)S(1)}, u32[]{:S(2)}, u32[]{:S(2)}) collective-permute-start(bf16[16,3584]{1,0:T(8,128)(2,1)S(1)} %get-tuple-element.30), channel_id=1, source_target_pairs={{0,2},{2,0},{4,6},{6,4},{8,10},{10,8},{12,14},{14,12},{16,18},{18,... | collective-permute-start | bytes 344072 | tf_op jit(solution)/shard_map/ppermute | solution.py:179
  28.9 0.6 %collective-permute-start.6 = (bf16[16,3584]{1,0:T(8,128)(2,1)S(1)}, bf16[16,3584]{1,0:T(8,128)(2,1)S(1)}, u32[]{:S(2)}, u32[]{:S(2)}) collective-permute-start(bf16[16,3584]{1,0:T(8,128)(2,1)S(1)} %shard_map.79), channel_id=1, source_target_pairs={{0,4},{2,6},{4,0},{6,2},{8,12},{10,14},{12,8},{14,10},{16,20},{18,... | collective-permute-start | bytes 344072 | tf_op jit(solution)/shard_map/ppermute | solution.py:179
  29.5 1.5 %collective-permute-start.13 = (bf16[16,3584]{1,0:T(8,128)(2,1)S(1)}, bf16[16,3584]{1,0:T(8,128)(2,1)S(1)}, u32[]{:S(2)}, u32[]{:S(2)}) collective-permute-start(bf16[16,3584]{1,0:T(8,128)(2,1)S(1)} %get-tuple-element.38), channel_id=1, source_target_pairs={{0,4},{2,6},{4,0},{6,2},{8,12},{10,14},{12,8},{14,10},{16,20},{18,... | collective-permute-start | bytes 344072 | tf_op jit(solution)/shard_map/ppermute | solution.py:179
  31.2 1.6 %collective-permute-start.15 = (bf16[16,3584]{1,0:T(8,128)(2,1)S(1)}, bf16[16,3584]{1,0:T(8,128)(2,1)S(1)}, u32[]{:S(2)}, u32[]{:S(2)}) collective-permute-start(bf16[16,3584]{1,0:T(8,128)(2,1)S(1)} %shard_map.84), channel_id=1, source_target_pairs={{0,2},{2,0},{4,6},{6,4},{8,10},{10,8},{12,14},{14,12},{16,18},{18,... | collective-permute-start | bytes 344072 | tf_op jit(solution)/shard_map/ppermute | solution.py:179
  32.8 1.0 %collective-permute-done.6.refs_2_ = bf16[16,3584]{1,0:T(8,128)(2,1)S(1)} collective-permute-done((bf16[16,3584]{1,0:T(8,128)(2,1)S(1)}, bf16[16,3584]{1,0:T(8,128)(2,1)S(1)}, u32[]{:S(2)}, u32[]{:S(2)}) %collective-permute-start.6) | collective-permute-done | bytes 114720 | tf_op jit(solution)/shard_map/ppermute | solution.py:179
  33.8 0.5 %collective-permute-start.7 = (bf16[8,3584]{1,0:T(8,128)(2,1)S(1)}, bf16[8,3584]{1,0:T(8,128)(2,1)S(1)}, u32[]{:S(2)}, u32[]{:S(2)}) collective-permute-start(bf16[8,3584]{1,0:T(8,128)(2,1)S(1)} %get-tuple-element.34), channel_id=1, source_target_pairs={{0,16},{2,18},{4,20},{6,22},{8,24},{10,26},{12,28},{14,30},{16,0},... | collective-permute-start | bytes 172040 | tf_op jit(solution)/shard_map/ppermute | solution.py:179
  34.3 0.7 %collective-permute-done.13.refs_1_ = bf16[16,3584]{1,0:T(8,128)(2,1)S(1)} collective-permute-done((bf16[16,3584]{1,0:T(8,128)(2,1)S(1)}, bf16[16,3584]{1,0:T(8,128)(2,1)S(1)}, u32[]{:S(2)}, u32[]{:S(2)}) %collective-permute-start.13) | collective-permute-done | bytes 114720 | tf_op jit(solution)/shard_map/ppermute | solution.py:179
  35.0 1.0 %collective-permute-done.15.refs_2_ = bf16[16,3584]{1,0:T(8,128)(2,1)S(1)} collective-permute-done((bf16[16,3584]{1,0:T(8,128)(2,1)S(1)}, bf16[16,3584]{1,0:T(8,128)(2,1)S(1)}, u32[]{:S(2)}, u32[]{:S(2)}) %collective-permute-start.15) | collective-permute-done | bytes 114720 | tf_op jit(solution)/shard_map/ppermute | solution.py:179
  36.1 2.1 %collective-permute-start.16 = (bf16[8,3584]{1,0:T(8,128)(2,1)S(1)}, bf16[8,3584]{1,0:T(8,128)(2,1)S(1)}, u32[]{:S(2)}, u32[]{:S(2)}) collective-permute-start(bf16[8,3584]{1,0:T(8,128)(2,1)S(1)} %get-tuple-element.41), channel_id=1, source_target_pairs={{0,8},{2,10},{4,12},{6,14},{8,0},{10,2},{12,4},{14,6},{16,24},{18,... | collective-permute-start | bytes 172040 | tf_op jit(solution)/shard_map/ppermute | solution.py:179
  38.2 1.5 %collective-permute-start.17 = (bf16[8,3584]{1,0:T(8,128)(2,1)S(1)}, bf16[8,3584]{1,0:T(8,128)(2,1)S(1)}, u32[]{:S(2)}, u32[]{:S(2)}) collective-permute-start(bf16[8,3584]{1,0:T(8,128)(2,1)S(1)} %get-tuple-element.42), channel_id=1, source_target_pairs={{0,24},{2,26},{4,28},{6,30},{8,16},{10,18},{12,20},{14,22},{16,8},... | collective-permute-start | bytes 172040 | tf_op jit(solution)/shard_map/ppermute | solution.py:179
  39.9 0.4 collective-permute-done.16.refs_0_
  40.4 3.8 %collective-permute-done.17.refs_1_ = bf16[8,3584]{1,0:T(8,128)(2,1)S(1)} collective-permute-done((bf16[8,3584]{1,0:T(8,128)(2,1)S(1)}, bf16[8,3584]{1,0:T(8,128)(2,1)S(1)}, u32[]{:S(2)}, u32[]{:S(2)}) %collective-permute-start.17) | collective-permute-done | bytes 57376 | tf_op jit(solution)/shard_map/ppermute | solution.py:179
  44.2 0.9 %shard_map.86 = bf16[16,3584]{1,0:T(8,128)(2,1)} custom-call(bf16[48,16]{1,0:T(8,128)(2,1)S(1)} %get-tuple-element.25.refs_1_.terms, f32[16,3584]{1,0:T(8,128)S(1)} %shard_map.81.near, bf16[8,3584]{1,0:T(8,128)(2,1)S(1)} %collective-permute-done.16.refs_0_, bf16[8,3584]{1,0:T(8,128)(2,1)S(1)} %collective-permute-done.17.refs_1_), custom_call_target="tpu_custom_call" | custom-call | tf_op jit(solution)/shard_map/pallas_call | solution.py:153
  (18 shorter events, 0.7 us)
Async XLA Ops:
  1.2 7.0 %collective-permute-start = (bf16[8,3584]{1,0:T(8,128)(2,1)S(1)}, bf16[8,3584]{1,0:T(8,128)(2,1)S(1)}, u32[]{:S(2)}, u32[]{:S(2)}) collective-permute-start(bf16[8,3584]{1,0:T(8,128)(2,1)S(1)} %get-tuple-element.28), channel_id=1, source_target_pairs={{0,16},{2,18},{4,20},{6,22},{8,24},{10,26},{12,28},{14,30},{16,0},... | collective-permute-start | bytes 172040 | tf_op jit(solution)/shard_map/ppermute | solution.py:179
  5.3 6.7 %collective-permute-start.8 = (bf16[8,3584]{1,0:T(8,128)(2,1)S(1)}, bf16[8,3584]{1,0:T(8,128)(2,1)S(1)}, u32[]{:S(2)}, u32[]{:S(2)}) collective-permute-start(bf16[8,3584]{1,0:T(8,128)(2,1)S(1)} %get-tuple-element.35), channel_id=1, source_target_pairs={{0,8},{2,10},{4,12},{6,14},{8,0},{10,2},{12,4},{14,6},{16,24},{18,... | collective-permute-start | bytes 172040 | tf_op jit(solution)/shard_map/ppermute | solution.py:179
  6.9 6.0 %collective-permute-start.9 = (bf16[8,3584]{1,0:T(8,128)(2,1)S(1)}, bf16[8,3584]{1,0:T(8,128)(2,1)S(1)}, u32[]{:S(2)}, u32[]{:S(2)}) collective-permute-start(bf16[8,3584]{1,0:T(8,128)(2,1)S(1)} %get-tuple-element.36), channel_id=1, source_target_pairs={{0,24},{2,26},{4,28},{6,30},{8,16},{10,18},{12,20},{14,22},{16,8},... | collective-permute-start | bytes 172040 | tf_op jit(solution)/shard_map/ppermute | solution.py:179
  8.2 6.8 %collective-permute-start.1 = (bf16[16,3584]{1,0:T(8,128)(2,1)S(1)}, bf16[16,3584]{1,0:T(8,128)(2,1)S(1)}, u32[]{:S(2)}, u32[]{:S(2)}) collective-permute-start(bf16[16,3584]{1,0:T(8,128)(2,1)S(1)} %shard_map.75.refs_0_), channel_id=1, source_target_pairs={{0,2},{2,0},{4,6},{6,4},{8,10},{10,8},{12,14},{14,12},{16,18},{18,... | collective-permute-start | bytes 344072 | tf_op jit(solution)/shard_map/ppermute | solution.py:179
  12.8 5.8 %collective-permute-start.10 = (bf16[16,3584]{1,0:T(8,128)(2,1)S(1)}, bf16[16,3584]{1,0:T(8,128)(2,1)S(1)}, u32[]{:S(2)}, u32[]{:S(2)}) collective-permute-start(bf16[16,3584]{1,0:T(8,128)(2,1)S(1)} %shard_map.82.refs_0_), channel_id=1, source_target_pairs={{0,4},{2,6},{4,0},{6,2},{8,12},{10,14},{12,8},{14,10},{16,20},{18,... | collective-permute-start | bytes 344072 | tf_op jit(solution)/shard_map/ppermute | solution.py:179
  14.4 7.2 %collective-permute-start.2 = (bf16[16,3584]{1,0:T(8,128)(2,1)S(1)}, bf16[16,3584]{1,0:T(8,128)(2,1)S(1)}, u32[]{:S(2)}, u32[]{:S(2)}) collective-permute-start(bf16[16,3584]{1,0:T(8,128)(2,1)S(1)} %shard_map.75.refs_0_), channel_id=1, source_target_pairs={{0,4},{2,6},{4,0},{6,2},{8,12},{10,14},{12,8},{14,10},{16,20},{18,... | collective-permute-start | bytes 344072 | tf_op jit(solution)/shard_map/ppermute | solution.py:179
  14.9 6.7 %collective-permute-start.3 = (bf16[16,3584]{1,0:T(8,128)(2,1)S(1)}, bf16[16,3584]{1,0:T(8,128)(2,1)S(1)}, u32[]{:S(2)}, u32[]{:S(2)}) collective-permute-start(bf16[16,3584]{1,0:T(8,128)(2,1)S(1)} %collective-permute-done.1.refs_1_), channel_id=1, source_target_pairs={{0,4},{2,6},{4,0},{6,2},{8,12},{10,14},{12,8},{14,10},{16,20},{18,... | collective-permute-start | bytes 344072 | tf_op jit(solution)/shard_map/ppermute | solution.py:179
  16.5 7.4 %collective-permute-start.11 = (bf16[16,3584]{1,0:T(8,128)(2,1)S(1)}, bf16[16,3584]{1,0:T(8,128)(2,1)S(1)}, u32[]{:S(2)}, u32[]{:S(2)}) collective-permute-start(bf16[16,3584]{1,0:T(8,128)(2,1)S(1)} %shard_map.82.refs_0_), channel_id=1, source_target_pairs={{0,2},{2,0},{4,6},{6,4},{8,10},{10,8},{12,14},{14,12},{16,18},{18,... | collective-permute-start | bytes 344072 | tf_op jit(solution)/shard_map/ppermute | solution.py:179
  18.7 6.0 %collective-permute-start.12 = (bf16[16,3584]{1,0:T(8,128)(2,1)S(1)}, bf16[16,3584]{1,0:T(8,128)(2,1)S(1)}, u32[]{:S(2)}, u32[]{:S(2)}) collective-permute-start(bf16[16,3584]{1,0:T(8,128)(2,1)S(1)} %collective-permute-done.10.refs_1_), channel_id=1, source_target_pairs={{0,2},{2,0},{4,6},{6,4},{8,10},{10,8},{12,14},{14,12},{16,18},{18,... | collective-permute-start | bytes 344072 | tf_op jit(solution)/shard_map/ppermute | solution.py:179
  22.8 6.1 %collective-permute-start.5 = (bf16[16,3584]{1,0:T(8,128)(2,1)S(1)}, bf16[16,3584]{1,0:T(8,128)(2,1)S(1)}, u32[]{:S(2)}, u32[]{:S(2)}) collective-permute-start(bf16[16,3584]{1,0:T(8,128)(2,1)S(1)} %get-tuple-element.32), channel_id=1, source_target_pairs={{0,2},{2,0},{4,6},{6,4},{8,10},{10,8},{12,14},{14,12},{16,18},{18,... | collective-permute-start | bytes 344072 | tf_op jit(solution)/shard_map/ppermute | solution.py:179
  25.8 5.3 %collective-permute-start.14 = (bf16[16,3584]{1,0:T(8,128)(2,1)S(1)}, bf16[16,3584]{1,0:T(8,128)(2,1)S(1)}, u32[]{:S(2)}, u32[]{:S(2)}) collective-permute-start(bf16[16,3584]{1,0:T(8,128)(2,1)S(1)} %get-tuple-element.40), channel_id=1, source_target_pairs={{0,4},{2,6},{4,0},{6,2},{8,12},{10,14},{12,8},{14,10},{16,20},{18,... | collective-permute-start | bytes 344072 | tf_op jit(solution)/shard_map/ppermute | solution.py:179
  27.4 5.4 %collective-permute-start.4 = (bf16[16,3584]{1,0:T(8,128)(2,1)S(1)}, bf16[16,3584]{1,0:T(8,128)(2,1)S(1)}, u32[]{:S(2)}, u32[]{:S(2)}) collective-permute-start(bf16[16,3584]{1,0:T(8,128)(2,1)S(1)} %get-tuple-element.30), channel_id=1, source_target_pairs={{0,2},{2,0},{4,6},{6,4},{8,10},{10,8},{12,14},{14,12},{16,18},{18,... | collective-permute-start | bytes 344072 | tf_op jit(solution)/shard_map/ppermute | solution.py:179
  28.9 4.9 %collective-permute-start.6 = (bf16[16,3584]{1,0:T(8,128)(2,1)S(1)}, bf16[16,3584]{1,0:T(8,128)(2,1)S(1)}, u32[]{:S(2)}, u32[]{:S(2)}) collective-permute-start(bf16[16,3584]{1,0:T(8,128)(2,1)S(1)} %shard_map.79), channel_id=1, source_target_pairs={{0,4},{2,6},{4,0},{6,2},{8,12},{10,14},{12,8},{14,10},{16,20},{18,... | collective-permute-start | bytes 344072 | tf_op jit(solution)/shard_map/ppermute | solution.py:179
  29.5 5.5 %collective-permute-start.13 = (bf16[16,3584]{1,0:T(8,128)(2,1)S(1)}, bf16[16,3584]{1,0:T(8,128)(2,1)S(1)}, u32[]{:S(2)}, u32[]{:S(2)}) collective-permute-start(bf16[16,3584]{1,0:T(8,128)(2,1)S(1)} %get-tuple-element.38), channel_id=1, source_target_pairs={{0,4},{2,6},{4,0},{6,2},{8,12},{10,14},{12,8},{14,10},{16,20},{18,... | collective-permute-start | bytes 344072 | tf_op jit(solution)/shard_map/ppermute | solution.py:179
  31.2 4.9 %collective-permute-start.15 = (bf16[16,3584]{1,0:T(8,128)(2,1)S(1)}, bf16[16,3584]{1,0:T(8,128)(2,1)S(1)}, u32[]{:S(2)}, u32[]{:S(2)}) collective-permute-start(bf16[16,3584]{1,0:T(8,128)(2,1)S(1)} %shard_map.84), channel_id=1, source_target_pairs={{0,2},{2,0},{4,6},{6,4},{8,10},{10,8},{12,14},{14,12},{16,18},{18,... | collective-permute-start | bytes 344072 | tf_op jit(solution)/shard_map/ppermute | solution.py:179
  33.8 5.9 %collective-permute-start.7 = (bf16[8,3584]{1,0:T(8,128)(2,1)S(1)}, bf16[8,3584]{1,0:T(8,128)(2,1)S(1)}, u32[]{:S(2)}, u32[]{:S(2)}) collective-permute-start(bf16[8,3584]{1,0:T(8,128)(2,1)S(1)} %get-tuple-element.34), channel_id=1, source_target_pairs={{0,16},{2,18},{4,20},{6,22},{8,24},{10,26},{12,28},{14,30},{16,0},... | collective-permute-start | bytes 172040 | tf_op jit(solution)/shard_map/ppermute | solution.py:179
  36.1 4.3 %collective-permute-start.16 = (bf16[8,3584]{1,0:T(8,128)(2,1)S(1)}, bf16[8,3584]{1,0:T(8,128)(2,1)S(1)}, u32[]{:S(2)}, u32[]{:S(2)}) collective-permute-start(bf16[8,3584]{1,0:T(8,128)(2,1)S(1)} %get-tuple-element.41), channel_id=1, source_target_pairs={{0,8},{2,10},{4,12},{6,14},{8,0},{10,2},{12,4},{14,6},{16,24},{18,... | collective-permute-start | bytes 172040 | tf_op jit(solution)/shard_map/ppermute | solution.py:179
  38.2 6.0 %collective-permute-start.17 = (bf16[8,3584]{1,0:T(8,128)(2,1)S(1)}, bf16[8,3584]{1,0:T(8,128)(2,1)S(1)}, u32[]{:S(2)}, u32[]{:S(2)}) collective-permute-start(bf16[8,3584]{1,0:T(8,128)(2,1)S(1)} %get-tuple-element.42), channel_id=1, source_target_pairs={{0,24},{2,26},{4,28},{6,30},{8,16},{10,18},{12,20},{14,22},{16,8},... | collective-permute-start | bytes 172040 | tf_op jit(solution)/shard_map/ppermute | solution.py:179

commit v11 on v10

--- a/solution.py
+++ b/solution.py
@@ -50,7 +50,7 @@
         here = copy_row == p
         named = jnp.where(here, placement[p], named)
         d = lax.bitwise_xor(own, p)
-        relative = jnp.where(here, d // 2 + d % 2 * (slot_count // 2), relative)
+        relative = jnp.where(here, d, relative)
         seen = jnp.int32(0)
         for q in range(p):
             seen = seen + (placement[q] == placement[p]).astype(jnp.int32)
@@ -67,6 +67,7 @@
     earlier = jnp.dot(
         total.astype(jnp.bfloat16), ahead, preferred_element_type=jnp.float32
     ).astype(jnp.int32)
+    half = slot_count * capacity // 2
     slot_row = iota((slot_count * capacity, tok_count), 0)
     pick_rows = jnp.zeros((slot_count * capacity, tok_count), jnp.float32)
     combine = jnp.zeros((slot_count * capacity, tok_count), jnp.float32)
@@ -76,7 +77,9 @@
         slot = jnp.where(rank < capacity, place * capacity + rank, -1)
         hot = slot_row == slot
         pick_rows = pick_rows + hot.astype(jnp.float32)
-        combine = combine + jnp.where(hot, gate_weights[pl.ds(k, 1), :], 0.0)
+        turned = jnp.where(slot < half, slot + half, slot - half)
+        turned = slot_row == jnp.where(slot < 0, -1, turned)
+        combine = combine + jnp.where(turned, gate_weights[pl.ds(k, 1), :], 0.0)
         earlier = earlier + chosen[k]
     combine_out[...] = combine
     copies_in[4].wait()
@@ -119,8 +122,14 @@
 
 
 def expert_kernel(count, *refs):
-    blocks, (w_in, w_out), outs = refs[:count], refs[count : count + 2], refs[count + 2 :]
-    rows = stack(blocks).astype(jnp.bfloat16)
+    rests, firsts = refs[:count], refs[count : 2 * count]
+    (w_in, w_out), outs = refs[2 * count : 2 * count + 2], refs[2 * count + 2 :]
+    rests = [r[...].astype(jnp.float32) for r in rests]
+    cut = rests[0].shape[0] - outs[0].shape[0]
+    rows = [r[cut:] for r in rests]
+    for first, rest in zip(firsts, rests):
+        rows += [first[...].astype(jnp.float32), rest[:cut]]
+    rows = jnp.concatenate(rows, axis=0).astype(jnp.bfloat16)
     gate = jnp.dot(rows, w_in[0], preferred_element_type=jnp.float32)
     upper = jnp.dot(rows, w_in[1], preferred_element_type=jnp.float32)
     hidden = (gate / (1.0 + jnp.exp(-gate)) * upper).astype(jnp.bfloat16)
@@ -170,13 +179,21 @@
     tok_count, width = tokens.shape
     capacity = tok_count * expert_ids.shape[1] // slot_count
     slots = slot_count * capacity
-    offsets = [*range(0, slot_count, 2), *range(1, slot_count, 2)]
     bf16 = jnp.bfloat16
     chunk = jax.ShapeDtypeStruct((capacity, width), bf16)
     half = jax.ShapeDtypeStruct((slots // 2, width), bf16)
 
     def swap(value, offset):
         return lax.ppermute(value, "expert", [(e, e ^ offset) for e in range(n_devices)])
+
+    def turn(value, even, odd):
+        parts = lax.axis_size("dp")
+        pairs = [
+            (e * parts + part, (e ^ (odd if part % 2 else even)) * parts + part)
+            for e in range(n_devices)
+            for part in range(parts)
+        ]
+        return lax.ppermute(value, ("expert", "dp"), pairs)
 
     def local(kernel, inputs, outs, limit=16 * MIB):
         return call(kernel, inputs, [VMEM] * len(inputs), outs, limit)
@@ -195,7 +212,7 @@
         + [pltpu.VMEM(s.shape, s.dtype) for s in sources[1:]]
         + [pltpu.SemaphoreType.DMA((5,))],
     )
-    chunks = [swap(c, d * group_size) if d else c for d, c in zip(offsets, chunks)]
+    chunks = [swap(c, d * group_size) if d else c for d, c in enumerate(chunks)]
     terms = jax.ShapeDtypeStruct((3 * tok_count, slots // 2), bf16)
     terms = local(terms_kernel, [combine], [terms, terms])
 
@@ -207,43 +224,48 @@
             jax.ShapeDtypeStruct(array.shape, bf16),
             16 * MIB,
             [pltpu.SemaphoreType.DMA((2,))],
-            2 * array.size,
+            4 * array.size,
         )
 
     w_in = fetch(w_in, terms[0])
     w_out = fetch(w_out, terms[1])
 
     square = group_size == 4
+
+    def spread(own):
+        if not square:
+            return [swap(own, q) if q else own for q in range(group_size)]
+        return [own, turn(own, 1, 2), turn(own, 2, 1)]
+
+    firsts = spread(chunks[0])
+    rest = jax.ShapeDtypeStruct((slots - capacity, width), bf16)
+    rest = local(
+        functools.partial(stack_kernel, slot_count - 1), chunks[1:] + [w_in] + firsts[1:], rest
+    )
+    rests = spread(rest)
+    if square:
+        firsts.append(turn(firsts[1], 2, 1))
+        rests.append(turn(rests[1], 2, 1))
+    result = local(
+        functools.partial(expert_kernel, group_size),
+        rests + firsts + [w_in, w_out],
+        [half] * (2 * group_size),
+        40 * MIB,
+    )
     count = slot_count // 2
-    sides = ((1, 2), (2, 1))
-    earlier = []
+    offsets = [*range(count, slot_count), *range(count)]
     summed = []
-    for h in range(2):
-        a, b = sides[h]
-        own = local(
-            functools.partial(stack_kernel, count), chunks[h * count :][:count] + earlier, half
-        )
+    for h, (a, b) in enumerate(((1, 2), (2, 1))):
+        part = result[h * group_size : (h + 1) * group_size]
         if square:
-            held = {a: swap(own, a), b: swap(own, b)}
-            held = [own, held[a], held[b], swap(held[a], b)]
+            mine, first, second, cross = part if h == 0 else [part[i] for i in (0, 2, 1, 3)]
+            cross = turn(cross, a, b)
+            first = turn(first, a, b)
+            second = local(functools.partial(sum_kernel, 2), [second, cross], [half])[0]
+            part = [mine, first, turn(second, b, a)]
         else:
-            held = [swap(own, q) if q else own for q in range(group_size)]
-        earlier = [w_in]
-        result = local(
-            functools.partial(expert_kernel, group_size),
-            held + [w_in, w_out],
-            [half] * group_size,
-            40 * MIB,
-        )
-        if square:
-            mine, first, second, cross = result
-            cross = swap(cross, a)
-            first = swap(first, a)
-            second = local(functools.partial(sum_kernel, 2), [second, cross], [half])[0]
-            result = [mine, first, swap(second, b)]
-        else:
-            result = [swap(v, q) if q else v for q, v in enumerate(result)]
-        summed += local(functools.partial(sum_kernel, len(result)), result, [chunk] * count)
+            part = [swap(v, q) if q else v for q, v in enumerate(part)]
+        summed += local(functools.partial(sum_kernel, len(part)), part, [chunk] * count)
     summed = [swap(v, d * group_size) if d else v for d, v in zip(offsets, summed)]
     near = local(
         near_kernel,

time: 45.2 us -> 47.2 us (1.044)
  waiting for transfers between devices: 10.6 us -> 14.7 us
  Pallas kernels: 8.49 us -> 7.19 us
  starting transfers between devices: 25.9 us -> 25 us
    ppermute x18 -> x6, starting transfers between devices: 25.9 us -> 10.4 us  [swap(): lax.ppermute(value, 'expert', [(e, e ^ offset) for e in range(n_devices)])]
    ppermute x0 -> x12, starting transfers between devices: none -> 14.6 us  [turn(): return lax.ppermute(value, ('expert', 'dp'), pairs)]
    ppermute x0 -> x12, waiting for transfers between devices: none -> 10.8 us  [turn(): return lax.ppermute(value, ('expert', 'dp'), pairs)]
    ppermute x18 -> x6, waiting for transfers between devices: 10.6 us -> 3.93 us  [swap(): lax.ppermute(value, 'expert', [(e, e ^ offset) for e in range(n_devices)])]
    pallas_call x14 -> x12, Pallas kernels: 8.49 us -> 7.19 us  [call(): pl.pallas_call(kernel, out_shape=outs, in_specs=in_specs, out_specs=jax.t...]
  transfers between devices with their start and end apart: 18 -> 18, of which waited for: 10 -> 8; matrix products, arithmetic and copies ran while one was open for 0% -> 0% of each run, Pallas kernels for 14% -> 9%
where the time goes in v11:
time: 47.2 us; the launch traced here: 47 us
  starting transfers between devices  25 us (53%)
  waiting for transfers between devices  14.7 us (31%)
  Pallas kernels  7.19 us (15%)
    ppermute x12, starting transfers between devices, turn(): return lax.ppermute(value, ('expert', 'dp'), pairs)  14.6 us
    ppermute x12, waiting for transfers between devices, turn(): return lax.ppermute(value, ('expert', 'dp'), pairs)  10.8 us
    ppermute x6, starting transfers between devices, swap(): lax.ppermute(value, 'expert', [(e, e ^ offset) for e in range(n_devices)])  10.4 us
    pallas_call x12, Pallas kernels, call(): pl.pallas_call(kernel, out_shape=outs, in_specs=in_specs, out_specs=jax.t...  7.19 us
    ppermute x6, waiting for transfers between devices, swap(): lax.ppermute(value, 'expert', [(e, e ^ offset) for e in range(n_devices)])  3.93 us
  transfers between devices with their start and end apart: 18, of which 8 were waited for; matrix products, arithmetic and copies ran while one was open for 0% of the time, Pallas kernels for 9%

profile of v11, /device:TPU:0, one launch (start us, length us, event | category | flops | bytes accessed | tf_op | source)
XLA Modules:
  0.0 47.0 jit_solution(11774180317961006094)
XLA Ops:
  0.0 1.2 %shard_map.73 = (bf16[8,3584]{1,0:T(8,128)(2,1)S(1)}, bf16[8,3584]{1,0:T(8,128)(2,1)S(1)}, bf16[8,3584]{1,0:T(8,128)(2,1)S(1)}, bf16[8,3584]{1,0:T(8,128)(2,1)S(1)}, f32[32,16]{1,0:T(8,128)S(1)}) custom-call(s32[4]{0:T(128)} %refs_0_.3, s32[2,16]{1,0:T(2,128)} %bitcast.3, s32[2,16]{1,0:T(2,128)} %bitcast.4, f32[2,16]{1,0:T(2,128)} %bitcast.5, ...), custom_call_target="tpu_custom_call" | custom-call | tf_op jit(solution)/shard_map/pallas_call | solution.py:162
  1.2 3.1 %collective-permute-start = (bf16[8,3584]{1,0:T(8,128)(2,1)S(1)}, bf16[8,3584]{1,0:T(8,128)(2,1)S(1)}, u32[]{:S(2)}, u32[]{:S(2)}) collective-permute-start(bf16[8,3584]{1,0:T(8,128)(2,1)S(1)} %get-tuple-element.27), channel_id=1, source_target_pairs={{0,8},{2,10},{4,12},{6,14},{8,0},{10,2},{12,4},{14,6},{16,24},{18,... | collective-permute-start | bytes 172040 | tf_op jit(solution)/shard_map/ppermute | solution.py:187
  4.3 2.6 %collective-permute-start.1 = (bf16[8,3584]{1,0:T(8,128)(2,1)S(1)}, bf16[8,3584]{1,0:T(8,128)(2,1)S(1)}, u32[]{:S(2)}, u32[]{:S(2)}) collective-permute-start(bf16[8,3584]{1,0:T(8,128)(2,1)S(1)} %get-tuple-element.28), channel_id=1, source_target_pairs={{0,16},{2,18},{4,20},{6,22},{8,24},{10,26},{12,28},{14,30},{16,0},... | collective-permute-start | bytes 172040 | tf_op jit(solution)/shard_map/ppermute | solution.py:187
  6.9 1.7 %collective-permute-start.4 = (bf16[8,3584]{1,0:T(8,128)(2,1)S(1)}, bf16[8,3584]{1,0:T(8,128)(2,1)S(1)}, u32[]{:S(2)}, u32[]{:S(2)}) collective-permute-start(bf16[8,3584]{1,0:T(8,128)(2,1)S(1)} %get-tuple-element.30.refs_4_), channel_id=1, source_target_pairs={{0,4},{1,3},{2,6},{3,1},{4,0},{5,7},{6,2},{7,5},{8,12},{9,11},{10,... | collective-permute-start | bytes 172040 | tf_op jit(solution)/shard_map/ppermute | solution.py:196
  8.6 1.5 %collective-permute-start.3 = (bf16[8,3584]{1,0:T(8,128)(2,1)S(1)}, bf16[8,3584]{1,0:T(8,128)(2,1)S(1)}, u32[]{:S(2)}, u32[]{:S(2)}) collective-permute-start(bf16[8,3584]{1,0:T(8,128)(2,1)S(1)} %get-tuple-element.30.refs_4_), channel_id=1, source_target_pairs={{0,2},{1,5},{2,0},{3,7},{4,6},{5,1},{6,4},{7,3},{8,10},{9,13},{10,... | collective-permute-start | bytes 172040 | tf_op jit(solution)/shard_map/ppermute | solution.py:196
  10.1 0.2 shard_map.74
  10.3 2.1 %shard_map.75.refs_3_.refs_8_ = bf16[2,3584,256]{2,1,0:T(8,128)(2,1)S(1)} custom-call(bf16[2,3584,256]{2,1,0:T(8,128)(2,1)} %refs_0_.4, bf16[48,16]{1,0:T(8,128)(2,1)S(1)} %get-tuple-element.26.refs_1_.terms), custom_call_target="tpu_custom_call" | custom-call | bytes 7340032 | tf_op jit(solution)/shard_map/pallas_call | solution.py:162
  12.4 0.4 collective-permute-done.2.refs_2_
  12.9 1.6 %collective-permute-start.5 = (bf16[24,3584]{1,0:T(8,128)(2,1)S(1)}, bf16[24,3584]{1,0:T(8,128)(2,1)S(1)}, u32[]{:S(2)}, u32[]{:S(2)}) collective-permute-start(bf16[24,3584]{1,0:T(8,128)(2,1)S(1)} %shard_map.76.refs_0_), channel_id=1, source_target_pairs={{0,2},{1,5},{2,0},{3,7},{4,6},{5,1},{6,4},{7,3},{8,10},{9,13},{10,... | collective-permute-start | bytes 516104 | tf_op jit(solution)/shard_map/ppermute | solution.py:196
  14.4 1.5 %collective-permute-start.6 = (bf16[24,3584]{1,0:T(8,128)(2,1)S(1)}, bf16[24,3584]{1,0:T(8,128)(2,1)S(1)}, u32[]{:S(2)}, u32[]{:S(2)}) collective-permute-start(bf16[24,3584]{1,0:T(8,128)(2,1)S(1)} %shard_map.76.refs_0_), channel_id=1, source_target_pairs={{0,4},{1,3},{2,6},{3,1},{4,0},{5,7},{6,2},{7,5},{8,12},{9,11},{10,... | collective-permute-start | bytes 516104 | tf_op jit(solution)/shard_map/ppermute | solution.py:196
  15.9 3.3 %collective-permute-done.5.refs_1_ = bf16[24,3584]{1,0:T(8,128)(2,1)S(1)} collective-permute-done((bf16[24,3584]{1,0:T(8,128)(2,1)S(1)}, bf16[24,3584]{1,0:T(8,128)(2,1)S(1)}, u32[]{:S(2)}, u32[]{:S(2)}) %collective-permute-start.5) | collective-permute-done | bytes 172064 | tf_op jit(solution)/shard_map/ppermute | solution.py:196
  19.3 0.8 %collective-permute-start.7 = (bf16[24,3584]{1,0:T(8,128)(2,1)S(1)}, bf16[24,3584]{1,0:T(8,128)(2,1)S(1)}, u32[]{:S(2)}, u32[]{:S(2)}) collective-permute-start(bf16[24,3584]{1,0:T(8,128)(2,1)S(1)} %collective-permute-done.5.refs_1_), channel_id=1, source_target_pairs={{0,4},{1,3},{2,6},{3,1},{4,0},{5,7},{6,2},{7,5},{8,12},{9,11},{10,... | collective-permute-start | bytes 516104 | tf_op jit(solution)/shard_map/ppermute | solution.py:196
  20.1 1.2 %collective-permute-start.8 = (bf16[8,3584]{1,0:T(8,128)(2,1)S(1)}, bf16[8,3584]{1,0:T(8,128)(2,1)S(1)}, u32[]{:S(2)}, u32[]{:S(2)}) collective-permute-start(bf16[8,3584]{1,0:T(8,128)(2,1)S(1)} %collective-permute-done.3.refs_4_.refs_5_), channel_id=1, source_target_pairs={{0,4},{1,3},{2,6},{3,1},{4,0},{5,7},{6,2},{7,5},{8,12},{9,11},{10,... | collective-permute-start | bytes 172040 | tf_op jit(solution)/shard_map/ppermute | solution.py:196
  21.3 1.5 %shard_map.77.refs_9_ = bf16[256,3584]{1,0:T(8,128)(2,1)S(1)} custom-call(bf16[256,3584]{1,0:T(8,128)(2,1)} %refs_0_.5, bf16[48,16]{1,0:T(8,128)(2,1)S(1)} %get-tuple-element.25.refs_1_.terms), custom_call_target="tpu_custom_call" | custom-call | bytes 3670016 | tf_op jit(solution)/shard_map/pallas_call | solution.py:162
  22.8 3.1 %collective-permute-done.8.refs_7_ = bf16[8,3584]{1,0:T(8,128)(2,1)S(1)} collective-permute-done((bf16[8,3584]{1,0:T(8,128)(2,1)S(1)}, bf16[8,3584]{1,0:T(8,128)(2,1)S(1)}, u32[]{:S(2)}, u32[]{:S(2)}) %collective-permute-start.8) | collective-permute-done | bytes 57376 | tf_op jit(solution)/shard_map/ppermute | solution.py:196
  25.9 1.0 %shard_map.78 = (bf16[16,3584]{1,0:T(8,128)(2,1)S(1)}, bf16[16,3584]{1,0:T(8,128)(2,1)S(1)}, bf16[16,3584]{1,0:T(8,128)(2,1)S(1)}, bf16[16,3584]{1,0:T(8,128)(2,...) custom-call(bf16[24,3584]{1,0:T(8,128)(2,1)S(1)} %shard_map.76.refs_, ...), custom_call_target="tpu_custom_call" | custom-call | tf_op jit(solution)/shard_map/pallas_call | solution.py:162
  26.9 1.6 %collective-permute-start.10 = (bf16[16,3584]{1,0:T(8,128)(2,1)S(1)}, bf16[16,3584]{1,0:T(8,128)(2,1)S(1)}, u32[]{:S(2)}, u32[]{:S(2)}) collective-permute-start(bf16[16,3584]{1,0:T(8,128)(2,1)S(1)} %get-tuple-element.34), channel_id=1, source_target_pairs={{0,2},{1,5},{2,0},{3,7},{4,6},{5,1},{6,4},{7,3},{8,10},{9,13},{10,... | collective-permute-start | bytes 344072 | tf_op jit(solution)/shard_map/ppermute | solution.py:196
  28.5 0.5 %collective-permute-start.15 = (bf16[16,3584]{1,0:T(8,128)(2,1)S(1)}, bf16[16,3584]{1,0:T(8,128)(2,1)S(1)}, u32[]{:S(2)}, u32[]{:S(2)}) collective-permute-start(bf16[16,3584]{1,0:T(8,128)(2,1)S(1)} %get-tuple-element.40), channel_id=1, source_target_pairs={{0,4},{1,3},{2,6},{3,1},{4,0},{5,7},{6,2},{7,5},{8,12},{9,11},{10,... | collective-permute-start | bytes 344072 | tf_op jit(solution)/shard_map/ppermute | solution.py:196
  29.0 0.5 %collective-permute-start.9 = (bf16[16,3584]{1,0:T(8,128)(2,1)S(1)}, bf16[16,3584]{1,0:T(8,128)(2,1)S(1)}, u32[]{:S(2)}, u32[]{:S(2)}) collective-permute-start(bf16[16,3584]{1,0:T(8,128)(2,1)S(1)} %get-tuple-element.32), channel_id=1, source_target_pairs={{0,2},{1,5},{2,0},{3,7},{4,6},{5,1},{6,4},{7,3},{8,10},{9,13},{10,... | collective-permute-start | bytes 344072 | tf_op jit(solution)/shard_map/ppermute | solution.py:196
  29.5 3.2 %collective-permute-done.10.refs_1_ = bf16[16,3584]{1,0:T(8,128)(2,1)S(1)} collective-permute-done((bf16[16,3584]{1,0:T(8,128)(2,1)S(1)}, bf16[16,3584]{1,0:T(8,128)(2,1)S(1)}, u32[]{:S(2)}, u32[]{:S(2)}) %collective-permute-start.10) | collective-permute-done | bytes 114720 | tf_op jit(solution)/shard_map/ppermute | solution.py:196
  32.8 0.9 %collective-permute-start.11 = (bf16[16,3584]{1,0:T(8,128)(2,1)S(1)}, bf16[16,3584]{1,0:T(8,128)(2,1)S(1)}, u32[]{:S(2)}, u32[]{:S(2)}) collective-permute-start(bf16[16,3584]{1,0:T(8,128)(2,1)S(1)} %shard_map.79), channel_id=1, source_target_pairs={{0,4},{1,3},{2,6},{3,1},{4,0},{5,7},{6,2},{7,5},{8,12},{9,11},{10,... | collective-permute-start | bytes 344072 | tf_op jit(solution)/shard_map/ppermute | solution.py:196
  33.6 1.2 %collective-permute-start.14 = (bf16[16,3584]{1,0:T(8,128)(2,1)S(1)}, bf16[16,3584]{1,0:T(8,128)(2,1)S(1)}, u32[]{:S(2)}, u32[]{:S(2)}) collective-permute-start(bf16[16,3584]{1,0:T(8,128)(2,1)S(1)} %get-tuple-element.38), channel_id=1, source_target_pairs={{0,4},{1,3},{2,6},{3,1},{4,0},{5,7},{6,2},{7,5},{8,12},{9,11},{10,... | collective-permute-start | bytes 344072 | tf_op jit(solution)/shard_map/ppermute | solution.py:196
  34.9 1.6 %collective-permute-start.16 = (bf16[16,3584]{1,0:T(8,128)(2,1)S(1)}, bf16[16,3584]{1,0:T(8,128)(2,1)S(1)}, u32[]{:S(2)}, u32[]{:S(2)}) collective-permute-start(bf16[16,3584]{1,0:T(8,128)(2,1)S(1)} %shard_map.82), channel_id=1, source_target_pairs={{0,2},{1,5},{2,0},{3,7},{4,6},{5,1},{6,4},{7,3},{8,10},{9,13},{10,... | collective-permute-start | bytes 344072 | tf_op jit(solution)/shard_map/ppermute | solution.py:196
  36.4 1.2 %collective-permute-done.11.refs_2_ = bf16[16,3584]{1,0:T(8,128)(2,1)S(1)} collective-permute-done((bf16[16,3584]{1,0:T(8,128)(2,1)S(1)}, bf16[16,3584]{1,0:T(8,128)(2,1)S(1)}, u32[]{:S(2)}, u32[]{:S(2)}) %collective-permute-start.11) | collective-permute-done | bytes 114720 | tf_op jit(solution)/shard_map/ppermute | solution.py:196
  37.7 1.8 %collective-permute-start.12 = (bf16[8,3584]{1,0:T(8,128)(2,1)S(1)}, bf16[8,3584]{1,0:T(8,128)(2,1)S(1)}, u32[]{:S(2)}, u32[]{:S(2)}) collective-permute-start(bf16[8,3584]{1,0:T(8,128)(2,1)S(1)} %get-tuple-element.35), channel_id=1, source_target_pairs={{0,16},{2,18},{4,20},{6,22},{8,24},{10,26},{12,28},{14,30},{16,0},... | collective-permute-start | bytes 172040 | tf_op jit(solution)/shard_map/ppermute | solution.py:187
  39.4 2.4 %collective-permute-start.13 = (bf16[8,3584]{1,0:T(8,128)(2,1)S(1)}, bf16[8,3584]{1,0:T(8,128)(2,1)S(1)}, u32[]{:S(2)}, u32[]{:S(2)}) collective-permute-start(bf16[8,3584]{1,0:T(8,128)(2,1)S(1)} %get-tuple-element.36), channel_id=1, source_target_pairs={{0,24},{2,26},{4,28},{6,30},{8,16},{10,18},{12,20},{14,22},{16,8},... | collective-permute-start | bytes 172040 | tf_op jit(solution)/shard_map/ppermute | solution.py:187
  41.9 0.6 %collective-permute-start.17 = (bf16[8,3584]{1,0:T(8,128)(2,1)S(1)}, bf16[8,3584]{1,0:T(8,128)(2,1)S(1)}, u32[]{:S(2)}, u32[]{:S(2)}) collective-permute-start(bf16[8,3584]{1,0:T(8,128)(2,1)S(1)} %get-tuple-element.42), channel_id=1, source_target_pairs={{0,8},{2,10},{4,12},{6,14},{8,0},{10,2},{12,4},{14,6},{16,24},{18,... | collective-permute-start | bytes 172040 | tf_op jit(solution)/shard_map/ppermute | solution.py:187
  42.5 0.3 collective-permute-done.12.refs_0_
  42.8 2.6 %collective-permute-done.13.refs_1_ = bf16[8,3584]{1,0:T(8,128)(2,1)S(1)} collective-permute-done((bf16[8,3584]{1,0:T(8,128)(2,1)S(1)}, bf16[8,3584]{1,0:T(8,128)(2,1)S(1)}, u32[]{:S(2)}, u32[]{:S(2)}) %collective-permute-start.13) | collective-permute-done | bytes 57376 | tf_op jit(solution)/shard_map/ppermute | solution.py:187
  45.4 0.2 shard_map.81.near
  45.6 0.5 %collective-permute-done.17.refs_1_ = bf16[8,3584]{1,0:T(8,128)(2,1)S(1)} collective-permute-done((bf16[8,3584]{1,0:T(8,128)(2,1)S(1)}, bf16[8,3584]{1,0:T(8,128)(2,1)S(1)}, u32[]{:S(2)}, u32[]{:S(2)}) %collective-permute-start.17) | collective-permute-done | bytes 57376 | tf_op jit(solution)/shard_map/ppermute | solution.py:187
  46.1 0.9 %shard_map.84 = bf16[16,3584]{1,0:T(8,128)(2,1)} custom-call(bf16[48,16]{1,0:T(8,128)(2,1)S(1)} %get-tuple-element.25.refs_1_.terms, f32[16,3584]{1,0:T(8,128)S(1)} %shard_map.81.near, bf16[8,3584]{1,0:T(8,128)(2,1)S(1)} %get-tuple-element.41.refs_0_, bf16[8,3584]{1,0:T(8,128)(2,1)S(1)} %collective-permute-done.17.refs_1_), custom_call_target="tpu_custom_call" | custom-call | tf_op jit(solution)/shard_map/pallas_call | solution.py:162
  (16 shorter events, 0.2 us)
Async XLA Ops:
  1.2 11.2 %collective-permute-start = (bf16[8,3584]{1,0:T(8,128)(2,1)S(1)}, bf16[8,3584]{1,0:T(8,128)(2,1)S(1)}, u32[]{:S(2)}, u32[]{:S(2)}) collective-permute-start(bf16[8,3584]{1,0:T(8,128)(2,1)S(1)} %get-tuple-element.27), channel_id=1, source_target_pairs={{0,8},{2,10},{4,12},{6,14},{8,0},{10,2},{12,4},{14,6},{16,24},{18,... | collective-permute-start | bytes 172040 | tf_op jit(solution)/shard_map/ppermute | solution.py:187
  4.3 8.1 %collective-permute-start.1 = (bf16[8,3584]{1,0:T(8,128)(2,1)S(1)}, bf16[8,3584]{1,0:T(8,128)(2,1)S(1)}, u32[]{:S(2)}, u32[]{:S(2)}) collective-permute-start(bf16[8,3584]{1,0:T(8,128)(2,1)S(1)} %get-tuple-element.28), channel_id=1, source_target_pairs={{0,16},{2,18},{4,20},{6,22},{8,24},{10,26},{12,28},{14,30},{16,0},... | collective-permute-start | bytes 172040 | tf_op jit(solution)/shard_map/ppermute | solution.py:187
  6.9 6.0 %collective-permute-start.2 = (bf16[8,3584]{1,0:T(8,128)(2,1)S(1)}, bf16[8,3584]{1,0:T(8,128)(2,1)S(1)}, u32[]{:S(2)}, u32[]{:S(2)}) collective-permute-start(bf16[8,3584]{1,0:T(8,128)(2,1)S(1)} %get-tuple-element.29), channel_id=1, source_target_pairs={{0,24},{2,26},{4,28},{6,30},{8,16},{10,18},{12,20},{14,22},{16,8},... | collective-permute-start | bytes 172040 | tf_op jit(solution)/shard_map/ppermute | solution.py:187
  6.9 6.0 %collective-permute-start.4 = (bf16[8,3584]{1,0:T(8,128)(2,1)S(1)}, bf16[8,3584]{1,0:T(8,128)(2,1)S(1)}, u32[]{:S(2)}, u32[]{:S(2)}) collective-permute-start(bf16[8,3584]{1,0:T(8,128)(2,1)S(1)} %get-tuple-element.30.refs_4_), channel_id=1, source_target_pairs={{0,4},{1,3},{2,6},{3,1},{4,0},{5,7},{6,2},{7,5},{8,12},{9,11},{10,... | collective-permute-start | bytes 172040 | tf_op jit(solution)/shard_map/ppermute | solution.py:196
  8.6 4.2 %collective-permute-start.3 = (bf16[8,3584]{1,0:T(8,128)(2,1)S(1)}, bf16[8,3584]{1,0:T(8,128)(2,1)S(1)}, u32[]{:S(2)}, u32[]{:S(2)}) collective-permute-start(bf16[8,3584]{1,0:T(8,128)(2,1)S(1)} %get-tuple-element.30.refs_4_), channel_id=1, source_target_pairs={{0,2},{1,5},{2,0},{3,7},{4,6},{5,1},{6,4},{7,3},{8,10},{9,13},{10,... | collective-permute-start | bytes 172040 | tf_op jit(solution)/shard_map/ppermute | solution.py:196
  12.9 6.4 %collective-permute-start.5 = (bf16[24,3584]{1,0:T(8,128)(2,1)S(1)}, bf16[24,3584]{1,0:T(8,128)(2,1)S(1)}, u32[]{:S(2)}, u32[]{:S(2)}) collective-permute-start(bf16[24,3584]{1,0:T(8,128)(2,1)S(1)} %shard_map.76.refs_0_), channel_id=1, source_target_pairs={{0,2},{1,5},{2,0},{3,7},{4,6},{5,1},{6,4},{7,3},{8,10},{9,13},{10,... | collective-permute-start | bytes 516104 | tf_op jit(solution)/shard_map/ppermute | solution.py:196
  14.4 11.5 %collective-permute-start.6 = (bf16[24,3584]{1,0:T(8,128)(2,1)S(1)}, bf16[24,3584]{1,0:T(8,128)(2,1)S(1)}, u32[]{:S(2)}, u32[]{:S(2)}) collective-permute-start(bf16[24,3584]{1,0:T(8,128)(2,1)S(1)} %shard_map.76.refs_0_), channel_id=1, source_target_pairs={{0,4},{1,3},{2,6},{3,1},{4,0},{5,7},{6,2},{7,5},{8,12},{9,11},{10,... | collective-permute-start | bytes 516104 | tf_op jit(solution)/shard_map/ppermute | solution.py:196
  19.3 6.6 %collective-permute-start.7 = (bf16[24,3584]{1,0:T(8,128)(2,1)S(1)}, bf16[24,3584]{1,0:T(8,128)(2,1)S(1)}, u32[]{:S(2)}, u32[]{:S(2)}) collective-permute-start(bf16[24,3584]{1,0:T(8,128)(2,1)S(1)} %collective-permute-done.5.refs_1_), channel_id=1, source_target_pairs={{0,4},{1,3},{2,6},{3,1},{4,0},{5,7},{6,2},{7,5},{8,12},{9,11},{10,... | collective-permute-start | bytes 516104 | tf_op jit(solution)/shard_map/ppermute | solution.py:196
  20.1 5.8 %collective-permute-start.8 = (bf16[8,3584]{1,0:T(8,128)(2,1)S(1)}, bf16[8,3584]{1,0:T(8,128)(2,1)S(1)}, u32[]{:S(2)}, u32[]{:S(2)}) collective-permute-start(bf16[8,3584]{1,0:T(8,128)(2,1)S(1)} %collective-permute-done.3.refs_4_.refs_5_), channel_id=1, source_target_pairs={{0,4},{1,3},{2,6},{3,1},{4,0},{5,7},{6,2},{7,5},{8,12},{9,11},{10,... | collective-permute-start | bytes 172040 | tf_op jit(solution)/shard_map/ppermute | solution.py:196
  26.9 5.8 %collective-permute-start.10 = (bf16[16,3584]{1,0:T(8,128)(2,1)S(1)}, bf16[16,3584]{1,0:T(8,128)(2,1)S(1)}, u32[]{:S(2)}, u32[]{:S(2)}) collective-permute-start(bf16[16,3584]{1,0:T(8,128)(2,1)S(1)} %get-tuple-element.34), channel_id=1, source_target_pairs={{0,2},{1,5},{2,0},{3,7},{4,6},{5,1},{6,4},{7,3},{8,10},{9,13},{10,... | collective-permute-start | bytes 344072 | tf_op jit(solution)/shard_map/ppermute | solution.py:196
  28.5 6.4 %collective-permute-start.15 = (bf16[16,3584]{1,0:T(8,128)(2,1)S(1)}, bf16[16,3584]{1,0:T(8,128)(2,1)S(1)}, u32[]{:S(2)}, u32[]{:S(2)}) collective-permute-start(bf16[16,3584]{1,0:T(8,128)(2,1)S(1)} %get-tuple-element.40), channel_id=1, source_target_pairs={{0,4},{1,3},{2,6},{3,1},{4,0},{5,7},{6,2},{7,5},{8,12},{9,11},{10,... | collective-permute-start | bytes 344072 | tf_op jit(solution)/shard_map/ppermute | solution.py:196
  29.0 7.5 %collective-permute-start.9 = (bf16[16,3584]{1,0:T(8,128)(2,1)S(1)}, bf16[16,3584]{1,0:T(8,128)(2,1)S(1)}, u32[]{:S(2)}, u32[]{:S(2)}) collective-permute-start(bf16[16,3584]{1,0:T(8,128)(2,1)S(1)} %get-tuple-element.32), channel_id=1, source_target_pairs={{0,2},{1,5},{2,0},{3,7},{4,6},{5,1},{6,4},{7,3},{8,10},{9,13},{10,... | collective-permute-start | bytes 344072 | tf_op jit(solution)/shard_map/ppermute | solution.py:196
  32.8 4.9 %collective-permute-start.11 = (bf16[16,3584]{1,0:T(8,128)(2,1)S(1)}, bf16[16,3584]{1,0:T(8,128)(2,1)S(1)}, u32[]{:S(2)}, u32[]{:S(2)}) collective-permute-start(bf16[16,3584]{1,0:T(8,128)(2,1)S(1)} %shard_map.79), channel_id=1, source_target_pairs={{0,4},{1,3},{2,6},{3,1},{4,0},{5,7},{6,2},{7,5},{8,12},{9,11},{10,... | collective-permute-start | bytes 344072 | tf_op jit(solution)/shard_map/ppermute | solution.py:196
  33.6 8.2 %collective-permute-start.14 = (bf16[16,3584]{1,0:T(8,128)(2,1)S(1)}, bf16[16,3584]{1,0:T(8,128)(2,1)S(1)}, u32[]{:S(2)}, u32[]{:S(2)}) collective-permute-start(bf16[16,3584]{1,0:T(8,128)(2,1)S(1)} %get-tuple-element.38), channel_id=1, source_target_pairs={{0,4},{1,3},{2,6},{3,1},{4,0},{5,7},{6,2},{7,5},{8,12},{9,11},{10,... | collective-permute-start | bytes 344072 | tf_op jit(solution)/shard_map/ppermute | solution.py:196
  34.9 7.0 %collective-permute-start.16 = (bf16[16,3584]{1,0:T(8,128)(2,1)S(1)}, bf16[16,3584]{1,0:T(8,128)(2,1)S(1)}, u32[]{:S(2)}, u32[]{:S(2)}) collective-permute-start(bf16[16,3584]{1,0:T(8,128)(2,1)S(1)} %shard_map.82), channel_id=1, source_target_pairs={{0,2},{1,5},{2,0},{3,7},{4,6},{5,1},{6,4},{7,3},{8,10},{9,13},{10,... | collective-permute-start | bytes 344072 | tf_op jit(solution)/shard_map/ppermute | solution.py:196
  37.7 5.1 %collective-permute-start.12 = (bf16[8,3584]{1,0:T(8,128)(2,1)S(1)}, bf16[8,3584]{1,0:T(8,128)(2,1)S(1)}, u32[]{:S(2)}, u32[]{:S(2)}) collective-permute-start(bf16[8,3584]{1,0:T(8,128)(2,1)S(1)} %get-tuple-element.35), channel_id=1, source_target_pairs={{0,16},{2,18},{4,20},{6,22},{8,24},{10,26},{12,28},{14,30},{16,0},... | collective-permute-start | bytes 172040 | tf_op jit(solution)/shard_map/ppermute | solution.py:187
  39.4 6.0 %collective-permute-start.13 = (bf16[8,3584]{1,0:T(8,128)(2,1)S(1)}, bf16[8,3584]{1,0:T(8,128)(2,1)S(1)}, u32[]{:S(2)}, u32[]{:S(2)}) collective-permute-start(bf16[8,3584]{1,0:T(8,128)(2,1)S(1)} %get-tuple-element.36), channel_id=1, source_target_pairs={{0,24},{2,26},{4,28},{6,30},{8,16},{10,18},{12,20},{14,22},{16,8},... | collective-permute-start | bytes 172040 | tf_op jit(solution)/shard_map/ppermute | solution.py:187
  41.9 4.2 %collective-permute-start.17 = (bf16[8,3584]{1,0:T(8,128)(2,1)S(1)}, bf16[8,3584]{1,0:T(8,128)(2,1)S(1)}, u32[]{:S(2)}, u32[]{:S(2)}) collective-permute-start(bf16[8,3584]{1,0:T(8,128)(2,1)S(1)} %get-tuple-element.42), channel_id=1, source_target_pairs={{0,8},{2,10},{4,12},{6,14},{8,0},{10,2},{12,4},{14,6},{16,24},{18,... | collective-permute-start | bytes 172040 | tf_op jit(solution)/shard_map/ppermute | solution.py:187

commit v12 on v10

--- a/solution.py
+++ b/solution.py
@@ -50,7 +50,7 @@
         here = copy_row == p
         named = jnp.where(here, placement[p], named)
         d = lax.bitwise_xor(own, p)
-        relative = jnp.where(here, d // 2 + d % 2 * (slot_count // 2), relative)
+        relative = jnp.where(here, (d + slot_count - 1) % slot_count, relative)
         seen = jnp.int32(0)
         for q in range(p):
             seen = seen + (placement[q] == placement[p]).astype(jnp.int32)
@@ -170,7 +170,7 @@
     tok_count, width = tokens.shape
     capacity = tok_count * expert_ids.shape[1] // slot_count
     slots = slot_count * capacity
-    offsets = [*range(0, slot_count, 2), *range(1, slot_count, 2)]
+    offsets = [*range(1, slot_count), 0]
     bf16 = jnp.bfloat16
     chunk = jax.ShapeDtypeStruct((capacity, width), bf16)
     half = jax.ShapeDtypeStruct((slots // 2, width), bf16)
@@ -216,7 +216,7 @@
     square = group_size == 4
     count = slot_count // 2
     sides = ((1, 2), (2, 1))
-    earlier = []
+    earlier = [w_in]
     summed = []
     for h in range(2):
         a, b = sides[h]
@@ -228,7 +228,7 @@
             held = [own, held[a], held[b], swap(held[a], b)]
         else:
             held = [swap(own, q) if q else own for q in range(group_size)]
-        earlier = [w_in]
+        earlier = [w_out]
         result = local(
             functools.partial(expert_kernel, group_size),
             held + [w_in, w_out],

time: 45.2 us -> 43.8 us (0.969)
  waiting for transfers between devices: 10.6 us -> 7.98 us
  starting transfers between devices: 25.9 us -> 27.1 us
    ppermute x18, waiting for transfers between devices: 10.6 us -> 7.98 us  [swap(): lax.ppermute(value, 'expert', [(e, e ^ offset) for e in range(n_devices)])]
    ppermute x18, starting transfers between devices: 25.9 us -> 27.1 us  [swap(): lax.ppermute(value, 'expert', [(e, e ^ offset) for e in range(n_devices)])]
  transfers between devices with their start and end apart: 18 -> 18, of which waited for: 10 -> 6; matrix products, arithmetic and copies ran while one was open for 0% -> 0% of each run, Pallas kernels for 14% -> 15%
where the time goes in v12:
time: 43.8 us; the launch traced here: 43.6 us
  starting transfers between devices  27.1 us (62%)
  Pallas kernels  8.5 us (19%)
  waiting for transfers between devices  7.98 us (18%)
    ppermute x18, starting transfers between devices, swap(): lax.ppermute(value, 'expert', [(e, e ^ offset) for e in range(n_devices)])  27.1 us
    pallas_call x14, Pallas kernels, call(): pl.pallas_call(kernel, out_shape=outs, in_specs=in_specs, out_specs=jax.t...  8.5 us
    ppermute x18, waiting for transfers between devices, swap(): lax.ppermute(value, 'expert', [(e, e ^ offset) for e in range(n_devices)])  7.98 us
  transfers between devices with their start and end apart: 18, of which 6 were waited for; matrix products, arithmetic and copies ran while one was open for 0% of the time, Pallas kernels for 15%

profile of v12, /device:TPU:0, one launch (start us, length us, event | category | flops | bytes accessed | tf_op | source)
XLA Modules:
  0.0 43.6 jit_solution(175383888431450822)
XLA Ops:
  0.0 1.2 %shard_map.73 = (bf16[8,3584]{1,0:T(8,128)(2,1)S(1)}, bf16[8,3584]{1,0:T(8,128)(2,1)S(1)}, bf16[8,3584]{1,0:T(8,128)(2,1)S(1)}, bf16[8,3584]{1,0:T(8,128)(2,1)S(1)}, f32[32,16]{1,0:T(8,128)S(1)}) custom-call(s32[4]{0:T(128)} %refs_0_.3, s32[2,16]{1,0:T(2,128)} %bitcast.3, s32[2,16]{1,0:T(2,128)} %bitcast.4, f32[2,16]{1,0:T(2,128)} %bitcast.5, ...), custom_call_target="tpu_custom_call" | custom-call | tf_op jit(solution)/shard_map/pallas_call | solution.py:153
  1.2 3.1 %collective-permute-start = (bf16[8,3584]{1,0:T(8,128)(2,1)S(1)}, bf16[8,3584]{1,0:T(8,128)(2,1)S(1)}, u32[]{:S(2)}, u32[]{:S(2)}) collective-permute-start(bf16[8,3584]{1,0:T(8,128)(2,1)S(1)} %get-tuple-element.27), channel_id=1, source_target_pairs={{0,8},{2,10},{4,12},{6,14},{8,0},{10,2},{12,4},{14,6},{16,24},{18,... | collective-permute-start | bytes 172040 | tf_op jit(solution)/shard_map/ppermute | solution.py:179
  4.3 2.6 %collective-permute-start.1 = (bf16[8,3584]{1,0:T(8,128)(2,1)S(1)}, bf16[8,3584]{1,0:T(8,128)(2,1)S(1)}, u32[]{:S(2)}, u32[]{:S(2)}) collective-permute-start(bf16[8,3584]{1,0:T(8,128)(2,1)S(1)} %get-tuple-element.28), channel_id=1, source_target_pairs={{0,16},{2,18},{4,20},{6,22},{8,24},{10,26},{12,28},{14,30},{16,0},... | collective-permute-start | bytes 172040 | tf_op jit(solution)/shard_map/ppermute | solution.py:179
  6.9 0.0 collective-permute-start.10
  6.9 0.2 shard_map.74
  7.1 2.1 %shard_map.75.refs_2_.refs_4_ = bf16[2,3584,256]{2,1,0:T(8,128)(2,1)S(1)} custom-call(bf16[2,3584,256]{2,1,0:T(8,128)(2,1)} %refs_0_.4, bf16[48,16]{1,0:T(8,128)(2,1)S(1)} %get-tuple-element.26.refs_1_.terms), custom_call_target="tpu_custom_call" | custom-call | bytes 3670016 | tf_op jit(solution)/shard_map/pallas_call | solution.py:153
  9.1 1.3 %collective-permute-done.1.refs_1_ = bf16[8,3584]{1,0:T(8,128)(2,1)S(1)} collective-permute-done((bf16[8,3584]{1,0:T(8,128)(2,1)S(1)}, bf16[8,3584]{1,0:T(8,128)(2,1)S(1)}, u32[]{:S(2)}, u32[]{:S(2)}) %collective-permute-start.1) | collective-permute-done | bytes 57376 | tf_op jit(solution)/shard_map/ppermute | solution.py:179
  10.5 1.6 %collective-permute-start.2 = (bf16[16,3584]{1,0:T(8,128)(2,1)S(1)}, bf16[16,3584]{1,0:T(8,128)(2,1)S(1)}, u32[]{:S(2)}, u32[]{:S(2)}) collective-permute-start(bf16[16,3584]{1,0:T(8,128)(2,1)S(1)} %shard_map.76.refs_0_), channel_id=1, source_target_pairs={{0,2},{2,0},{4,6},{6,4},{8,10},{10,8},{12,14},{14,12},{16,18},{18,... | collective-permute-start | bytes 344072 | tf_op jit(solution)/shard_map/ppermute | solution.py:179
  12.0 1.5 %shard_map.77.refs_5_.refs_2_ = bf16[256,3584]{1,0:T(8,128)(2,1)S(1)} custom-call(bf16[256,3584]{1,0:T(8,128)(2,1)} %refs_0_.5, bf16[48,16]{1,0:T(8,128)(2,1)S(1)} %get-tuple-element.25.refs_1_.terms), custom_call_target="tpu_custom_call" | custom-call | bytes 1835008 | tf_op jit(solution)/shard_map/pallas_call | solution.py:153
  13.5 1.6 %collective-permute-start.11 = (bf16[16,3584]{1,0:T(8,128)(2,1)S(1)}, bf16[16,3584]{1,0:T(8,128)(2,1)S(1)}, u32[]{:S(2)}, u32[]{:S(2)}) collective-permute-start(bf16[16,3584]{1,0:T(8,128)(2,1)S(1)} %shard_map.82.refs_0_), channel_id=1, source_target_pairs={{0,4},{2,6},{4,0},{6,2},{8,12},{10,14},{12,8},{14,10},{16,20},{18,... | collective-permute-start | bytes 344072 | tf_op jit(solution)/shard_map/ppermute | solution.py:179
  15.1 0.5 %collective-permute-start.3 = (bf16[16,3584]{1,0:T(8,128)(2,1)S(1)}, bf16[16,3584]{1,0:T(8,128)(2,1)S(1)}, u32[]{:S(2)}, u32[]{:S(2)}) collective-permute-start(bf16[16,3584]{1,0:T(8,128)(2,1)S(1)} %shard_map.76.refs_0_), channel_id=1, source_target_pairs={{0,4},{2,6},{4,0},{6,2},{8,12},{10,14},{12,8},{14,10},{16,20},{18,... | collective-permute-start | bytes 344072 | tf_op jit(solution)/shard_map/ppermute | solution.py:179
  15.6 1.5 %collective-permute-start.4 = (bf16[16,3584]{1,0:T(8,128)(2,1)S(1)}, bf16[16,3584]{1,0:T(8,128)(2,1)S(1)}, u32[]{:S(2)}, u32[]{:S(2)}) collective-permute-start(bf16[16,3584]{1,0:T(8,128)(2,1)S(1)} %collective-permute-done.2.refs_1_), channel_id=1, source_target_pairs={{0,4},{2,6},{4,0},{6,2},{8,12},{10,14},{12,8},{14,10},{16,20},{18,... | collective-permute-start | bytes 344072 | tf_op jit(solution)/shard_map/ppermute | solution.py:179
  17.2 1.2 %collective-permute-start.12 = (bf16[16,3584]{1,0:T(8,128)(2,1)S(1)}, bf16[16,3584]{1,0:T(8,128)(2,1)S(1)}, u32[]{:S(2)}, u32[]{:S(2)}) collective-permute-start(bf16[16,3584]{1,0:T(8,128)(2,1)S(1)} %shard_map.82.refs_0_), channel_id=1, source_target_pairs={{0,2},{2,0},{4,6},{6,4},{8,10},{10,8},{12,14},{14,12},{16,18},{18,... | collective-permute-start | bytes 344072 | tf_op jit(solution)/shard_map/ppermute | solution.py:179
  18.3 0.5 %collective-permute-done.11.refs_1_ = bf16[16,3584]{1,0:T(8,128)(2,1)S(1)} collective-permute-done((bf16[16,3584]{1,0:T(8,128)(2,1)S(1)}, bf16[16,3584]{1,0:T(8,128)(2,1)S(1)}, u32[]{:S(2)}, u32[]{:S(2)}) %collective-permute-start.11) | collective-permute-done | bytes 114720 | tf_op jit(solution)/shard_map/ppermute | solution.py:179
  18.8 1.3 %collective-permute-start.13 = (bf16[16,3584]{1,0:T(8,128)(2,1)S(1)}, bf16[16,3584]{1,0:T(8,128)(2,1)S(1)}, u32[]{:S(2)}, u32[]{:S(2)}) collective-permute-start(bf16[16,3584]{1,0:T(8,128)(2,1)S(1)} %collective-permute-done.11.refs_1_), channel_id=1, source_target_pairs={{0,2},{2,0},{4,6},{6,4},{8,10},{10,8},{12,14},{14,12},{16,18},{18,... | collective-permute-start | bytes 344072 | tf_op jit(solution)/shard_map/ppermute | solution.py:179
  20.2 1.1 %collective-permute-done.4.refs_3_ = bf16[16,3584]{1,0:T(8,128)(2,1)S(1)} collective-permute-done((bf16[16,3584]{1,0:T(8,128)(2,1)S(1)}, bf16[16,3584]{1,0:T(8,128)(2,1)S(1)}, u32[]{:S(2)}, u32[]{:S(2)}) %collective-permute-start.4) | collective-permute-done | bytes 114720 | tf_op jit(solution)/shard_map/ppermute | solution.py:179
  21.3 1.2 %shard_map.78 = (bf16[16,3584]{1,0:T(8,128)(2,1)S(1)}, bf16[16,3584]{1,0:T(8,128)(2,1)S(1)}, bf16[16,3584]{1,0:T(8,128)(2,1)S(1)}, bf16[16,3584]{1,0:T(8,128)(2,1)S(1)}) custom-call(bf16[16,3584]{1,0:T(8,128)(2,1)S(1)} %shard_map.76.refs_0_, bf16[16,3584]{1,0:T(8,128)(2,1)S(1)} %collective-permute-done.2.refs_1_, ...), custom_call_target="tpu_custom_call" | custom-call | tf_op jit(solution)/shard_map/pallas_call | solution.py:153
  22.4 1.4 %collective-permute-start.6 = (bf16[16,3584]{1,0:T(8,128)(2,1)S(1)}, bf16[16,3584]{1,0:T(8,128)(2,1)S(1)}, u32[]{:S(2)}, u32[]{:S(2)}) collective-permute-start(bf16[16,3584]{1,0:T(8,128)(2,1)S(1)} %get-tuple-element.32), channel_id=1, source_target_pairs={{0,2},{2,0},{4,6},{6,4},{8,10},{10,8},{12,14},{14,12},{16,18},{18,... | collective-permute-start | bytes 344072 | tf_op jit(solution)/shard_map/ppermute | solution.py:179
  23.8 0.6 %collective-permute-done.13.refs_3_ = bf16[16,3584]{1,0:T(8,128)(2,1)S(1)} collective-permute-done((bf16[16,3584]{1,0:T(8,128)(2,1)S(1)}, bf16[16,3584]{1,0:T(8,128)(2,1)S(1)}, u32[]{:S(2)}, u32[]{:S(2)}) %collective-permute-start.13) | collective-permute-done | bytes 114720 | tf_op jit(solution)/shard_map/ppermute | solution.py:179
  24.5 1.2 %shard_map.83 = (bf16[16,3584]{1,0:T(8,128)(2,1)S(1)}, bf16[16,3584]{1,0:T(8,128)(2,1)S(1)}, bf16[16,3584]{1,0:T(8,128)(2,1)S(1)}, bf16[16,3584]{1,0:T(8,128)(2,1)S(1)}) custom-call(bf16[16,3584]{1,0:T(8,128)(2,1)S(1)} %shard_map.82.refs_0_, bf16[16,3584]{1,0:T(8,128)(2,1)S(1)} %collective-permute-done.11.refs_1_, ...), custom_call_target="tpu_custom_call" | custom-call | tf_op jit(solution)/shard_map/pallas_call | solution.py:153
  25.6 1.6 %collective-permute-start.15 = (bf16[16,3584]{1,0:T(8,128)(2,1)S(1)}, bf16[16,3584]{1,0:T(8,128)(2,1)S(1)}, u32[]{:S(2)}, u32[]{:S(2)}) collective-permute-start(bf16[16,3584]{1,0:T(8,128)(2,1)S(1)} %get-tuple-element.40), channel_id=1, source_target_pairs={{0,4},{2,6},{4,0},{6,2},{8,12},{10,14},{12,8},{14,10},{16,20},{18,... | collective-permute-start | bytes 344072 | tf_op jit(solution)/shard_map/ppermute | solution.py:179
  27.2 1.7 %collective-permute-start.5 = (bf16[16,3584]{1,0:T(8,128)(2,1)S(1)}, bf16[16,3584]{1,0:T(8,128)(2,1)S(1)}, u32[]{:S(2)}, u32[]{:S(2)}) collective-permute-start(bf16[16,3584]{1,0:T(8,128)(2,1)S(1)} %get-tuple-element.30), channel_id=1, source_target_pairs={{0,2},{2,0},{4,6},{6,4},{8,10},{10,8},{12,14},{14,12},{16,18},{18,... | collective-permute-start | bytes 344072 | tf_op jit(solution)/shard_map/ppermute | solution.py:179
  28.9 0.6 %collective-permute-start.7 = (bf16[16,3584]{1,0:T(8,128)(2,1)S(1)}, bf16[16,3584]{1,0:T(8,128)(2,1)S(1)}, u32[]{:S(2)}, u32[]{:S(2)}) collective-permute-start(bf16[16,3584]{1,0:T(8,128)(2,1)S(1)} %shard_map.79), channel_id=1, source_target_pairs={{0,4},{2,6},{4,0},{6,2},{8,12},{10,14},{12,8},{14,10},{16,20},{18,... | collective-permute-start | bytes 344072 | tf_op jit(solution)/shard_map/ppermute | solution.py:179
  29.5 1.5 %collective-permute-start.14 = (bf16[16,3584]{1,0:T(8,128)(2,1)S(1)}, bf16[16,3584]{1,0:T(8,128)(2,1)S(1)}, u32[]{:S(2)}, u32[]{:S(2)}) collective-permute-start(bf16[16,3584]{1,0:T(8,128)(2,1)S(1)} %get-tuple-element.38), channel_id=1, source_target_pairs={{0,4},{2,6},{4,0},{6,2},{8,12},{10,14},{12,8},{14,10},{16,20},{18,... | collective-permute-start | bytes 344072 | tf_op jit(solution)/shard_map/ppermute | solution.py:179
  31.1 1.7 %collective-permute-start.16 = (bf16[16,3584]{1,0:T(8,128)(2,1)S(1)}, bf16[16,3584]{1,0:T(8,128)(2,1)S(1)}, u32[]{:S(2)}, u32[]{:S(2)}) collective-permute-start(bf16[16,3584]{1,0:T(8,128)(2,1)S(1)} %shard_map.84), channel_id=1, source_target_pairs={{0,2},{2,0},{4,6},{6,4},{8,10},{10,8},{12,14},{14,12},{16,18},{18,... | collective-permute-start | bytes 344072 | tf_op jit(solution)/shard_map/ppermute | solution.py:179
  32.8 1.0 %collective-permute-done.7.refs_2_ = bf16[16,3584]{1,0:T(8,128)(2,1)S(1)} collective-permute-done((bf16[16,3584]{1,0:T(8,128)(2,1)S(1)}, bf16[16,3584]{1,0:T(8,128)(2,1)S(1)}, u32[]{:S(2)}, u32[]{:S(2)}) %collective-permute-start.7) | collective-permute-done | bytes 114720 | tf_op jit(solution)/shard_map/ppermute | solution.py:179
  33.8 0.1 collective-permute-start.8
  33.9 2.7 %collective-permute-start.9 = (bf16[8,3584]{1,0:T(8,128)(2,1)S(1)}, bf16[8,3584]{1,0:T(8,128)(2,1)S(1)}, u32[]{:S(2)}, u32[]{:S(2)}) collective-permute-start(bf16[8,3584]{1,0:T(8,128)(2,1)S(1)} %get-tuple-element.34), channel_id=1, source_target_pairs={{0,16},{2,18},{4,20},{6,22},{8,24},{10,26},{12,28},{14,30},{16,0},... | collective-permute-start | bytes 172040 | tf_op jit(solution)/shard_map/ppermute | solution.py:179
  36.7 2.4 %collective-permute-start.17 = (bf16[8,3584]{1,0:T(8,128)(2,1)S(1)}, bf16[8,3584]{1,0:T(8,128)(2,1)S(1)}, u32[]{:S(2)}, u32[]{:S(2)}) collective-permute-start(bf16[8,3584]{1,0:T(8,128)(2,1)S(1)} %get-tuple-element.41), channel_id=1, source_target_pairs={{0,24},{2,26},{4,28},{6,30},{8,16},{10,18},{12,20},{14,22},{16,8},... | collective-permute-start | bytes 172040 | tf_op jit(solution)/shard_map/ppermute | solution.py:179
  39.1 0.2 shard_map.81.near
  39.4 3.4 %collective-permute-done.17.refs_0_ = bf16[8,3584]{1,0:T(8,128)(2,1)S(1)} collective-permute-done((bf16[8,3584]{1,0:T(8,128)(2,1)S(1)}, bf16[8,3584]{1,0:T(8,128)(2,1)S(1)}, u32[]{:S(2)}, u32[]{:S(2)}) %collective-permute-start.17) | collective-permute-done | bytes 57376 | tf_op jit(solution)/shard_map/ppermute | solution.py:179
  42.8 0.9 %shard_map.86 = bf16[16,3584]{1,0:T(8,128)(2,1)} custom-call(bf16[48,16]{1,0:T(8,128)(2,1)S(1)} %get-tuple-element.25.refs_1_.terms, f32[16,3584]{1,0:T(8,128)S(1)} %shard_map.81.near, bf16[8,3584]{1,0:T(8,128)(2,1)S(1)} %collective-permute-done.17.refs_0_, bf16[8,3584]{1,0:T(8,128)(2,1)S(1)} %get-tuple-element.42.refs_1_), custom_call_target="tpu_custom_call" | custom-call | tf_op jit(solution)/shard_map/pallas_call | solution.py:153
  (18 shorter events, 0.2 us)
Async XLA Ops:
  1.2 8.0 %collective-permute-start = (bf16[8,3584]{1,0:T(8,128)(2,1)S(1)}, bf16[8,3584]{1,0:T(8,128)(2,1)S(1)}, u32[]{:S(2)}, u32[]{:S(2)}) collective-permute-start(bf16[8,3584]{1,0:T(8,128)(2,1)S(1)} %get-tuple-element.27), channel_id=1, source_target_pairs={{0,8},{2,10},{4,12},{6,14},{8,0},{10,2},{12,4},{14,6},{16,24},{18,... | collective-permute-start | bytes 172040 | tf_op jit(solution)/shard_map/ppermute | solution.py:179
  4.3 6.2 %collective-permute-start.1 = (bf16[8,3584]{1,0:T(8,128)(2,1)S(1)}, bf16[8,3584]{1,0:T(8,128)(2,1)S(1)}, u32[]{:S(2)}, u32[]{:S(2)}) collective-permute-start(bf16[8,3584]{1,0:T(8,128)(2,1)S(1)} %get-tuple-element.28), channel_id=1, source_target_pairs={{0,16},{2,18},{4,20},{6,22},{8,24},{10,26},{12,28},{14,30},{16,0},... | collective-permute-start | bytes 172040 | tf_op jit(solution)/shard_map/ppermute | solution.py:179
  6.9 6.7 %collective-permute-start.10 = (bf16[8,3584]{1,0:T(8,128)(2,1)S(1)}, bf16[8,3584]{1,0:T(8,128)(2,1)S(1)}, u32[]{:S(2)}, u32[]{:S(2)}) collective-permute-start(bf16[8,3584]{1,0:T(8,128)(2,1)S(1)} %get-tuple-element.35), channel_id=1, source_target_pairs={{0,24},{2,26},{4,28},{6,30},{8,16},{10,18},{12,20},{14,22},{16,8},... | collective-permute-start | bytes 172040 | tf_op jit(solution)/shard_map/ppermute | solution.py:179
  10.5 5.2 %collective-permute-start.2 = (bf16[16,3584]{1,0:T(8,128)(2,1)S(1)}, bf16[16,3584]{1,0:T(8,128)(2,1)S(1)}, u32[]{:S(2)}, u32[]{:S(2)}) collective-permute-start(bf16[16,3584]{1,0:T(8,128)(2,1)S(1)} %shard_map.76.refs_0_), channel_id=1, source_target_pairs={{0,2},{2,0},{4,6},{6,4},{8,10},{10,8},{12,14},{14,12},{16,18},{18,... | collective-permute-start | bytes 344072 | tf_op jit(solution)/shard_map/ppermute | solution.py:179
  13.5 5.3 %collective-permute-start.11 = (bf16[16,3584]{1,0:T(8,128)(2,1)S(1)}, bf16[16,3584]{1,0:T(8,128)(2,1)S(1)}, u32[]{:S(2)}, u32[]{:S(2)}) collective-permute-start(bf16[16,3584]{1,0:T(8,128)(2,1)S(1)} %shard_map.82.refs_0_), channel_id=1, source_target_pairs={{0,4},{2,6},{4,0},{6,2},{8,12},{10,14},{12,8},{14,10},{16,20},{18,... | collective-permute-start | bytes 344072 | tf_op jit(solution)/shard_map/ppermute | solution.py:179
  15.1 5.0 %collective-permute-start.3 = (bf16[16,3584]{1,0:T(8,128)(2,1)S(1)}, bf16[16,3584]{1,0:T(8,128)(2,1)S(1)}, u32[]{:S(2)}, u32[]{:S(2)}) collective-permute-start(bf16[16,3584]{1,0:T(8,128)(2,1)S(1)} %shard_map.76.refs_0_), channel_id=1, source_target_pairs={{0,4},{2,6},{4,0},{6,2},{8,12},{10,14},{12,8},{14,10},{16,20},{18,... | collective-permute-start | bytes 344072 | tf_op jit(solution)/shard_map/ppermute | solution.py:179
  15.6 5.6 %collective-permute-start.4 = (bf16[16,3584]{1,0:T(8,128)(2,1)S(1)}, bf16[16,3584]{1,0:T(8,128)(2,1)S(1)}, u32[]{:S(2)}, u32[]{:S(2)}) collective-permute-start(bf16[16,3584]{1,0:T(8,128)(2,1)S(1)} %collective-permute-done.2.refs_1_), channel_id=1, source_target_pairs={{0,4},{2,6},{4,0},{6,2},{8,12},{10,14},{12,8},{14,10},{16,20},{18,... | collective-permute-start | bytes 344072 | tf_op jit(solution)/shard_map/ppermute | solution.py:179
  17.2 6.7 %collective-permute-start.12 = (bf16[16,3584]{1,0:T(8,128)(2,1)S(1)}, bf16[16,3584]{1,0:T(8,128)(2,1)S(1)}, u32[]{:S(2)}, u32[]{:S(2)}) collective-permute-start(bf16[16,3584]{1,0:T(8,128)(2,1)S(1)} %shard_map.82.refs_0_), channel_id=1, source_target_pairs={{0,2},{2,0},{4,6},{6,4},{8,10},{10,8},{12,14},{14,12},{16,18},{18,... | collective-permute-start | bytes 344072 | tf_op jit(solution)/shard_map/ppermute | solution.py:179
  18.8 5.6 %collective-permute-start.13 = (bf16[16,3584]{1,0:T(8,128)(2,1)S(1)}, bf16[16,3584]{1,0:T(8,128)(2,1)S(1)}, u32[]{:S(2)}, u32[]{:S(2)}) collective-permute-start(bf16[16,3584]{1,0:T(8,128)(2,1)S(1)} %collective-permute-done.11.refs_1_), channel_id=1, source_target_pairs={{0,2},{2,0},{4,6},{6,4},{8,10},{10,8},{12,14},{14,12},{16,18},{18,... | collective-permute-start | bytes 344072 | tf_op jit(solution)/shard_map/ppermute | solution.py:179
  22.4 6.5 %collective-permute-start.6 = (bf16[16,3584]{1,0:T(8,128)(2,1)S(1)}, bf16[16,3584]{1,0:T(8,128)(2,1)S(1)}, u32[]{:S(2)}, u32[]{:S(2)}) collective-permute-start(bf16[16,3584]{1,0:T(8,128)(2,1)S(1)} %get-tuple-element.32), channel_id=1, source_target_pairs={{0,2},{2,0},{4,6},{6,4},{8,10},{10,8},{12,14},{14,12},{16,18},{18,... | collective-permute-start | bytes 344072 | tf_op jit(solution)/shard_map/ppermute | solution.py:179
  25.6 5.4 %collective-permute-start.15 = (bf16[16,3584]{1,0:T(8,128)(2,1)S(1)}, bf16[16,3584]{1,0:T(8,128)(2,1)S(1)}, u32[]{:S(2)}, u32[]{:S(2)}) collective-permute-start(bf16[16,3584]{1,0:T(8,128)(2,1)S(1)} %get-tuple-element.40), channel_id=1, source_target_pairs={{0,4},{2,6},{4,0},{6,2},{8,12},{10,14},{12,8},{14,10},{16,20},{18,... | collective-permute-start | bytes 344072 | tf_op jit(solution)/shard_map/ppermute | solution.py:179
  27.2 5.6 %collective-permute-start.5 = (bf16[16,3584]{1,0:T(8,128)(2,1)S(1)}, bf16[16,3584]{1,0:T(8,128)(2,1)S(1)}, u32[]{:S(2)}, u32[]{:S(2)}) collective-permute-start(bf16[16,3584]{1,0:T(8,128)(2,1)S(1)} %get-tuple-element.30), channel_id=1, source_target_pairs={{0,2},{2,0},{4,6},{6,4},{8,10},{10,8},{12,14},{14,12},{16,18},{18,... | collective-permute-start | bytes 344072 | tf_op jit(solution)/shard_map/ppermute | solution.py:179
  28.9 4.9 %collective-permute-start.7 = (bf16[16,3584]{1,0:T(8,128)(2,1)S(1)}, bf16[16,3584]{1,0:T(8,128)(2,1)S(1)}, u32[]{:S(2)}, u32[]{:S(2)}) collective-permute-start(bf16[16,3584]{1,0:T(8,128)(2,1)S(1)} %shard_map.79), channel_id=1, source_target_pairs={{0,4},{2,6},{4,0},{6,2},{8,12},{10,14},{12,8},{14,10},{16,20},{18,... | collective-permute-start | bytes 344072 | tf_op jit(solution)/shard_map/ppermute | solution.py:179
  29.5 7.2 %collective-permute-start.14 = (bf16[16,3584]{1,0:T(8,128)(2,1)S(1)}, bf16[16,3584]{1,0:T(8,128)(2,1)S(1)}, u32[]{:S(2)}, u32[]{:S(2)}) collective-permute-start(bf16[16,3584]{1,0:T(8,128)(2,1)S(1)} %get-tuple-element.38), channel_id=1, source_target_pairs={{0,4},{2,6},{4,0},{6,2},{8,12},{10,14},{12,8},{14,10},{16,20},{18,... | collective-permute-start | bytes 344072 | tf_op jit(solution)/shard_map/ppermute | solution.py:179
  31.1 5.6 %collective-permute-start.16 = (bf16[16,3584]{1,0:T(8,128)(2,1)S(1)}, bf16[16,3584]{1,0:T(8,128)(2,1)S(1)}, u32[]{:S(2)}, u32[]{:S(2)}) collective-permute-start(bf16[16,3584]{1,0:T(8,128)(2,1)S(1)} %shard_map.84), channel_id=1, source_target_pairs={{0,2},{2,0},{4,6},{6,4},{8,10},{10,8},{12,14},{14,12},{16,18},{18,... | collective-permute-start | bytes 344072 | tf_op jit(solution)/shard_map/ppermute | solution.py:179
  33.8 5.3 %collective-permute-start.8 = (bf16[8,3584]{1,0:T(8,128)(2,1)S(1)}, bf16[8,3584]{1,0:T(8,128)(2,1)S(1)}, u32[]{:S(2)}, u32[]{:S(2)}) collective-permute-start(bf16[8,3584]{1,0:T(8,128)(2,1)S(1)} %get-tuple-element.33), channel_id=1, source_target_pairs={{0,8},{2,10},{4,12},{6,14},{8,0},{10,2},{12,4},{14,6},{16,24},{18,... | collective-permute-start | bytes 172040 | tf_op jit(solution)/shard_map/ppermute | solution.py:179
  33.9 5.2 %collective-permute-start.9 = (bf16[8,3584]{1,0:T(8,128)(2,1)S(1)}, bf16[8,3584]{1,0:T(8,128)(2,1)S(1)}, u32[]{:S(2)}, u32[]{:S(2)}) collective-permute-start(bf16[8,3584]{1,0:T(8,128)(2,1)S(1)} %get-tuple-element.34), channel_id=1, source_target_pairs={{0,16},{2,18},{4,20},{6,22},{8,24},{10,26},{12,28},{14,30},{16,0},... | collective-permute-start | bytes 172040 | tf_op jit(solution)/shard_map/ppermute | solution.py:179
  36.7 6.0 %collective-permute-start.17 = (bf16[8,3584]{1,0:T(8,128)(2,1)S(1)}, bf16[8,3584]{1,0:T(8,128)(2,1)S(1)}, u32[]{:S(2)}, u32[]{:S(2)}) collective-permute-start(bf16[8,3584]{1,0:T(8,128)(2,1)S(1)} %get-tuple-element.41), channel_id=1, source_target_pairs={{0,24},{2,26},{4,28},{6,30},{8,16},{10,18},{12,20},{14,22},{16,8},... | collective-permute-start | bytes 172040 | tf_op jit(solution)/shard_map/ppermute | solution.py:179

commit v13 on v12

--- a/solution.py
+++ b/solution.py
@@ -50,7 +50,9 @@
         here = copy_row == p
         named = jnp.where(here, placement[p], named)
         d = lax.bitwise_xor(own, p)
-        relative = jnp.where(here, (d + slot_count - 1) % slot_count, relative)
+        near = jnp.where(d == 0, slot_count - 1, d + slot_count // 2 - 1)
+        place = jnp.where(d < slot_count // 2, near, d - slot_count // 2)
+        relative = jnp.where(here, place, relative)
         seen = jnp.int32(0)
         for q in range(p):
             seen = seen + (placement[q] == placement[p]).astype(jnp.int32)
@@ -170,7 +172,7 @@
     tok_count, width = tokens.shape
     capacity = tok_count * expert_ids.shape[1] // slot_count
     slots = slot_count * capacity
-    offsets = [*range(1, slot_count), 0]
+    offsets = [*range(slot_count // 2, slot_count), *range(1, slot_count // 2), 0]
     bf16 = jnp.bfloat16
     chunk = jax.ShapeDtypeStruct((capacity, width), bf16)
     half = jax.ShapeDtypeStruct((slots // 2, width), bf16)
@@ -228,7 +230,7 @@
             held = [own, held[a], held[b], swap(held[a], b)]
         else:
             held = [swap(own, q) if q else own for q in range(group_size)]
-        earlier = [w_out]
+        earlier = []
         result = local(
             functools.partial(expert_kernel, group_size),
             held + [w_in, w_out],

time: 43.8 us -> 43.7 us (level)
  starting transfers between devices: 27.1 us -> 23.9 us
  waiting for transfers between devices: 7.98 us -> 11 us
    ppermute x18, starting transfers between devices: 27.1 us -> 23.9 us  [swap(): lax.ppermute(value, 'expert', [(e, e ^ offset) for e in range(n_devices)])]
    ppermute x18, waiting for transfers between devices: 7.98 us -> 11 us  [swap(): lax.ppermute(value, 'expert', [(e, e ^ offset) for e in range(n_devices)])]
  transfers between devices with their start and end apart: 18 -> 18, of which waited for: 6 -> 8; matrix products, arithmetic and copies ran while one was open for 0% -> 0% of each run, Pallas kernels for 15% -> 15%
where the time goes in v13:
time: 43.7 us; the launch traced here: 43.5 us
  starting transfers between devices  23.9 us (55%)
  waiting for transfers between devices  11 us (25%)
  Pallas kernels  8.52 us (19%)
    ppermute x18, starting transfers between devices, swap(): lax.ppermute(value, 'expert', [(e, e ^ offset) for e in range(n_devices)])  23.9 us
    ppermute x18, waiting for transfers between devices, swap(): lax.ppermute(value, 'expert', [(e, e ^ offset) for e in range(n_devices)])  11 us
    pallas_call x14, Pallas kernels, call(): pl.pallas_call(kernel, out_shape=outs, in_specs=in_specs, out_specs=jax.t...  8.52 us
  transfers between devices with their start and end apart: 18, of which 8 were waited for; matrix products, arithmetic and copies ran while one was open for 0% of the time, Pallas kernels for 15%

profile of v13, /device:TPU:0, one launch (start us, length us, event | category | flops | bytes accessed | tf_op | source)
XLA Modules:
  0.0 43.5 jit_solution(15443417816768422867)
XLA Ops:
  0.0 1.2 %shard_map.73 = (bf16[8,3584]{1,0:T(8,128)(2,1)S(1)}, bf16[8,3584]{1,0:T(8,128)(2,1)S(1)}, bf16[8,3584]{1,0:T(8,128)(2,1)S(1)}, bf16[8,3584]{1,0:T(8,128)(2,1)S(1)}, f32[32,16]{1,0:T(8,128)S(1)}) custom-call(s32[4]{0:T(128)} %refs_0_.3, s32[2,16]{1,0:T(2,128)} %bitcast.3, s32[2,16]{1,0:T(2,128)} %bitcast.4, f32[2,16]{1,0:T(2,128)} %bitcast.5, ...), custom_call_target="tpu_custom_call" | custom-call | tf_op jit(solution)/shard_map/pallas_call | solution.py:155
  1.2 4.1 %collective-permute-start = (bf16[8,3584]{1,0:T(8,128)(2,1)S(1)}, bf16[8,3584]{1,0:T(8,128)(2,1)S(1)}, u32[]{:S(2)}, u32[]{:S(2)}) collective-permute-start(bf16[8,3584]{1,0:T(8,128)(2,1)S(1)} %get-tuple-element.27), channel_id=1, source_target_pairs={{0,16},{2,18},{4,20},{6,22},{8,24},{10,26},{12,28},{14,30},{16,0},... | collective-permute-start | bytes 172040 | tf_op jit(solution)/shard_map/ppermute | solution.py:181
  5.3 1.4 %collective-permute-start.1 = (bf16[8,3584]{1,0:T(8,128)(2,1)S(1)}, bf16[8,3584]{1,0:T(8,128)(2,1)S(1)}, u32[]{:S(2)}, u32[]{:S(2)}) collective-permute-start(bf16[8,3584]{1,0:T(8,128)(2,1)S(1)} %get-tuple-element.28), channel_id=1, source_target_pairs={{0,24},{2,26},{4,28},{6,30},{8,16},{10,18},{12,20},{14,22},{16,8},... | collective-permute-start | bytes 172040 | tf_op jit(solution)/shard_map/ppermute | solution.py:181
  6.6 0.2 collective-permute-start.10
  7.1 2.1 %shard_map.75.refs_2_.refs_4_ = bf16[2,3584,256]{2,1,0:T(8,128)(2,1)S(1)} custom-call(bf16[2,3584,256]{2,1,0:T(8,128)(2,1)} %refs_0_.4, bf16[48,16]{1,0:T(8,128)(2,1)S(1)} %get-tuple-element.26.refs_1_.terms), custom_call_target="tpu_custom_call" | custom-call | bytes 3670016 | tf_op jit(solution)/shard_map/pallas_call | solution.py:155
  9.1 2.2 %collective-permute-done.1.refs_1_ = bf16[8,3584]{1,0:T(8,128)(2,1)S(1)} collective-permute-done((bf16[8,3584]{1,0:T(8,128)(2,1)S(1)}, bf16[8,3584]{1,0:T(8,128)(2,1)S(1)}, u32[]{:S(2)}, u32[]{:S(2)}) %collective-permute-start.1) | collective-permute-done | bytes 57376 | tf_op jit(solution)/shard_map/ppermute | solution.py:181
  11.4 1.6 %collective-permute-start.2 = (bf16[16,3584]{1,0:T(8,128)(2,1)S(1)}, bf16[16,3584]{1,0:T(8,128)(2,1)S(1)}, u32[]{:S(2)}, u32[]{:S(2)}) collective-permute-start(bf16[16,3584]{1,0:T(8,128)(2,1)S(1)} %shard_map.76.refs_0_), channel_id=1, source_target_pairs={{0,2},{2,0},{4,6},{6,4},{8,10},{10,8},{12,14},{14,12},{16,18},{18,... | collective-permute-start | bytes 344072 | tf_op jit(solution)/shard_map/ppermute | solution.py:181
  13.0 1.6 %collective-permute-start.11 = (bf16[16,3584]{1,0:T(8,128)(2,1)S(1)}, bf16[16,3584]{1,0:T(8,128)(2,1)S(1)}, u32[]{:S(2)}, u32[]{:S(2)}) collective-permute-start(bf16[16,3584]{1,0:T(8,128)(2,1)S(1)} %shard_map.82.refs_0_), channel_id=1, source_target_pairs={{0,4},{2,6},{4,0},{6,2},{8,12},{10,14},{12,8},{14,10},{16,20},{18,... | collective-permute-start | bytes 344072 | tf_op jit(solution)/shard_map/ppermute | solution.py:181
  14.6 0.5 %collective-permute-start.3 = (bf16[16,3584]{1,0:T(8,128)(2,1)S(1)}, bf16[16,3584]{1,0:T(8,128)(2,1)S(1)}, u32[]{:S(2)}, u32[]{:S(2)}) collective-permute-start(bf16[16,3584]{1,0:T(8,128)(2,1)S(1)} %shard_map.76.refs_0_), channel_id=1, source_target_pairs={{0,4},{2,6},{4,0},{6,2},{8,12},{10,14},{12,8},{14,10},{16,20},{18,... | collective-permute-start | bytes 344072 | tf_op jit(solution)/shard_map/ppermute | solution.py:181
  15.1 1.1 %collective-permute-done.2.refs_1_ = bf16[16,3584]{1,0:T(8,128)(2,1)S(1)} collective-permute-done((bf16[16,3584]{1,0:T(8,128)(2,1)S(1)}, bf16[16,3584]{1,0:T(8,128)(2,1)S(1)}, u32[]{:S(2)}, u32[]{:S(2)}) %collective-permute-start.2) | collective-permute-done | bytes 114720 | tf_op jit(solution)/shard_map/ppermute | solution.py:181
  16.2 1.5 %collective-permute-start.4 = (bf16[16,3584]{1,0:T(8,128)(2,1)S(1)}, bf16[16,3584]{1,0:T(8,128)(2,1)S(1)}, u32[]{:S(2)}, u32[]{:S(2)}) collective-permute-start(bf16[16,3584]{1,0:T(8,128)(2,1)S(1)} %collective-permute-done.2.refs_1_), channel_id=1, source_target_pairs={{0,4},{2,6},{4,0},{6,2},{8,12},{10,14},{12,8},{14,10},{16,20},{18,... | collective-permute-start | bytes 344072 | tf_op jit(solution)/shard_map/ppermute | solution.py:181
  17.8 1.5 %collective-permute-start.12 = (bf16[16,3584]{1,0:T(8,128)(2,1)S(1)}, bf16[16,3584]{1,0:T(8,128)(2,1)S(1)}, u32[]{:S(2)}, u32[]{:S(2)}) collective-permute-start(bf16[16,3584]{1,0:T(8,128)(2,1)S(1)} %shard_map.82.refs_0_), channel_id=1, source_target_pairs={{0,2},{2,0},{4,6},{6,4},{8,10},{10,8},{12,14},{14,12},{16,18},{18,... | collective-permute-start | bytes 344072 | tf_op jit(solution)/shard_map/ppermute | solution.py:181
  19.3 0.5 %collective-permute-start.13 = (bf16[16,3584]{1,0:T(8,128)(2,1)S(1)}, bf16[16,3584]{1,0:T(8,128)(2,1)S(1)}, u32[]{:S(2)}, u32[]{:S(2)}) collective-permute-start(bf16[16,3584]{1,0:T(8,128)(2,1)S(1)} %collective-permute-done.11.refs_1_), channel_id=1, source_target_pairs={{0,2},{2,0},{4,6},{6,4},{8,10},{10,8},{12,14},{14,12},{16,18},{18,... | collective-permute-start | bytes 344072 | tf_op jit(solution)/shard_map/ppermute | solution.py:181
  19.8 1.5 %shard_map.77.refs_5_ = bf16[256,3584]{1,0:T(8,128)(2,1)S(1)} custom-call(bf16[256,3584]{1,0:T(8,128)(2,1)} %refs_0_.5, bf16[48,16]{1,0:T(8,128)(2,1)S(1)} %get-tuple-element.25.refs_1_.terms), custom_call_target="tpu_custom_call" | custom-call | bytes 1835008 | tf_op jit(solution)/shard_map/pallas_call | solution.py:155
  21.3 1.2 %shard_map.78 = (bf16[16,3584]{1,0:T(8,128)(2,1)S(1)}, bf16[16,3584]{1,0:T(8,128)(2,1)S(1)}, bf16[16,3584]{1,0:T(8,128)(2,1)S(1)}, bf16[16,3584]{1,0:T(8,128)(2,1)S(1)}) custom-call(bf16[16,3584]{1,0:T(8,128)(2,1)S(1)} %shard_map.76.refs_0_, bf16[16,3584]{1,0:T(8,128)(2,1)S(1)} %collective-permute-done.2.refs_1_, ...), custom_call_target="tpu_custom_call" | custom-call | tf_op jit(solution)/shard_map/pallas_call | solution.py:155
  22.5 1.6 %collective-permute-start.6 = (bf16[16,3584]{1,0:T(8,128)(2,1)S(1)}, bf16[16,3584]{1,0:T(8,128)(2,1)S(1)}, u32[]{:S(2)}, u32[]{:S(2)}) collective-permute-start(bf16[16,3584]{1,0:T(8,128)(2,1)S(1)} %get-tuple-element.32), channel_id=1, source_target_pairs={{0,2},{2,0},{4,6},{6,4},{8,10},{10,8},{12,14},{14,12},{16,18},{18,... | collective-permute-start | bytes 344072 | tf_op jit(solution)/shard_map/ppermute | solution.py:181
  24.0 1.0 %collective-permute-done.13.refs_3_ = bf16[16,3584]{1,0:T(8,128)(2,1)S(1)} collective-permute-done((bf16[16,3584]{1,0:T(8,128)(2,1)S(1)}, bf16[16,3584]{1,0:T(8,128)(2,1)S(1)}, u32[]{:S(2)}, u32[]{:S(2)}) %collective-permute-start.13) | collective-permute-done | bytes 114720 | tf_op jit(solution)/shard_map/ppermute | solution.py:181
  25.0 1.2 %shard_map.83 = (bf16[16,3584]{1,0:T(8,128)(2,1)S(1)}, bf16[16,3584]{1,0:T(8,128)(2,1)S(1)}, bf16[16,3584]{1,0:T(8,128)(2,1)S(1)}, bf16[16,3584]{1,0:T(8,128)(2,1)S(1)}) custom-call(bf16[16,3584]{1,0:T(8,128)(2,1)S(1)} %shard_map.82.refs_0_, bf16[16,3584]{1,0:T(8,128)(2,1)S(1)} %collective-permute-done.11.refs_1_, ...), custom_call_target="tpu_custom_call" | custom-call | tf_op jit(solution)/shard_map/pallas_call | solution.py:155
  26.2 1.1 %collective-permute-start.15 = (bf16[16,3584]{1,0:T(8,128)(2,1)S(1)}, bf16[16,3584]{1,0:T(8,128)(2,1)S(1)}, u32[]{:S(2)}, u32[]{:S(2)}) collective-permute-start(bf16[16,3584]{1,0:T(8,128)(2,1)S(1)} %get-tuple-element.40), channel_id=1, source_target_pairs={{0,4},{2,6},{4,0},{6,2},{8,12},{10,14},{12,8},{14,10},{16,20},{18,... | collective-permute-start | bytes 344072 | tf_op jit(solution)/shard_map/ppermute | solution.py:181
  27.3 0.7 %collective-permute-start.5 = (bf16[16,3584]{1,0:T(8,128)(2,1)S(1)}, bf16[16,3584]{1,0:T(8,128)(2,1)S(1)}, u32[]{:S(2)}, u32[]{:S(2)}) collective-permute-start(bf16[16,3584]{1,0:T(8,128)(2,1)S(1)} %get-tuple-element.30), channel_id=1, source_target_pairs={{0,2},{2,0},{4,6},{6,4},{8,10},{10,8},{12,14},{14,12},{16,18},{18,... | collective-permute-start | bytes 344072 | tf_op jit(solution)/shard_map/ppermute | solution.py:181
  28.0 0.5 %collective-permute-done.6.refs_1_ = bf16[16,3584]{1,0:T(8,128)(2,1)S(1)} collective-permute-done((bf16[16,3584]{1,0:T(8,128)(2,1)S(1)}, bf16[16,3584]{1,0:T(8,128)(2,1)S(1)}, u32[]{:S(2)}, u32[]{:S(2)}) %collective-permute-start.6) | collective-permute-done | bytes 114720 | tf_op jit(solution)/shard_map/ppermute | solution.py:181
  28.5 1.5 %collective-permute-start.7 = (bf16[16,3584]{1,0:T(8,128)(2,1)S(1)}, bf16[16,3584]{1,0:T(8,128)(2,1)S(1)}, u32[]{:S(2)}, u32[]{:S(2)}) collective-permute-start(bf16[16,3584]{1,0:T(8,128)(2,1)S(1)} %shard_map.79), channel_id=1, source_target_pairs={{0,4},{2,6},{4,0},{6,2},{8,12},{10,14},{12,8},{14,10},{16,20},{18,... | collective-permute-start | bytes 344072 | tf_op jit(solution)/shard_map/ppermute | solution.py:181
  30.0 0.6 %collective-permute-start.14 = (bf16[16,3584]{1,0:T(8,128)(2,1)S(1)}, bf16[16,3584]{1,0:T(8,128)(2,1)S(1)}, u32[]{:S(2)}, u32[]{:S(2)}) collective-permute-start(bf16[16,3584]{1,0:T(8,128)(2,1)S(1)} %get-tuple-element.38), channel_id=1, source_target_pairs={{0,4},{2,6},{4,0},{6,2},{8,12},{10,14},{12,8},{14,10},{16,20},{18,... | collective-permute-start | bytes 344072 | tf_op jit(solution)/shard_map/ppermute | solution.py:181
  30.6 0.4 %collective-permute-done.15.refs_1_ = bf16[16,3584]{1,0:T(8,128)(2,1)S(1)} collective-permute-done((bf16[16,3584]{1,0:T(8,128)(2,1)S(1)}, bf16[16,3584]{1,0:T(8,128)(2,1)S(1)}, u32[]{:S(2)}, u32[]{:S(2)}) %collective-permute-start.15) | collective-permute-done | bytes 114720 | tf_op jit(solution)/shard_map/ppermute | solution.py:181
  31.1 1.8 %collective-permute-start.16 = (bf16[16,3584]{1,0:T(8,128)(2,1)S(1)}, bf16[16,3584]{1,0:T(8,128)(2,1)S(1)}, u32[]{:S(2)}, u32[]{:S(2)}) collective-permute-start(bf16[16,3584]{1,0:T(8,128)(2,1)S(1)} %shard_map.84), channel_id=1, source_target_pairs={{0,2},{2,0},{4,6},{6,4},{8,10},{10,8},{12,14},{14,12},{16,18},{18,... | collective-permute-start | bytes 344072 | tf_op jit(solution)/shard_map/ppermute | solution.py:181
  32.9 0.5 %collective-permute-done.7.refs_2_ = bf16[16,3584]{1,0:T(8,128)(2,1)S(1)} collective-permute-done((bf16[16,3584]{1,0:T(8,128)(2,1)S(1)}, bf16[16,3584]{1,0:T(8,128)(2,1)S(1)}, u32[]{:S(2)}, u32[]{:S(2)}) %collective-permute-start.7) | collective-permute-done | bytes 114720 | tf_op jit(solution)/shard_map/ppermute | solution.py:181
  33.4 3.0 %collective-permute-start.8 = (bf16[8,3584]{1,0:T(8,128)(2,1)S(1)}, bf16[8,3584]{1,0:T(8,128)(2,1)S(1)}, u32[]{:S(2)}, u32[]{:S(2)}) collective-permute-start(bf16[8,3584]{1,0:T(8,128)(2,1)S(1)} %get-tuple-element.33), channel_id=1, source_target_pairs={{0,16},{2,18},{4,20},{6,22},{8,24},{10,26},{12,28},{14,30},{16,0},... | collective-permute-start | bytes 172040 | tf_op jit(solution)/shard_map/ppermute | solution.py:181
  36.4 0.4 %collective-permute-start.9 = (bf16[8,3584]{1,0:T(8,128)(2,1)S(1)}, bf16[8,3584]{1,0:T(8,128)(2,1)S(1)}, u32[]{:S(2)}, u32[]{:S(2)}) collective-permute-start(bf16[8,3584]{1,0:T(8,128)(2,1)S(1)} %get-tuple-element.34), channel_id=1, source_target_pairs={{0,24},{2,26},{4,28},{6,30},{8,16},{10,18},{12,20},{14,22},{16,8},... | collective-permute-start | bytes 172040 | tf_op jit(solution)/shard_map/ppermute | solution.py:181
  36.9 0.3 collective-permute-start.17
  37.2 1.5 %collective-permute-done.8.refs_0_ = bf16[8,3584]{1,0:T(8,128)(2,1)S(1)} collective-permute-done((bf16[8,3584]{1,0:T(8,128)(2,1)S(1)}, bf16[8,3584]{1,0:T(8,128)(2,1)S(1)}, u32[]{:S(2)}, u32[]{:S(2)}) %collective-permute-start.8) | collective-permute-done | bytes 57376 | tf_op jit(solution)/shard_map/ppermute | solution.py:181
  38.7 3.7 %collective-permute-done.9.refs_1_ = bf16[8,3584]{1,0:T(8,128)(2,1)S(1)} collective-permute-done((bf16[8,3584]{1,0:T(8,128)(2,1)S(1)}, bf16[8,3584]{1,0:T(8,128)(2,1)S(1)}, u32[]{:S(2)}, u32[]{:S(2)}) %collective-permute-start.9) | collective-permute-done | bytes 57376 | tf_op jit(solution)/shard_map/ppermute | solution.py:181
  42.6 0.9 %shard_map.86 = bf16[16,3584]{1,0:T(8,128)(2,1)} custom-call(bf16[48,16]{1,0:T(8,128)(2,1)S(1)} %get-tuple-element.25.refs_1_.terms, f32[16,3584]{1,0:T(8,128)S(1)} %shard_map.81.near, bf16[8,3584]{1,0:T(8,128)(2,1)S(1)} %collective-permute-done.17.refs_0_, bf16[8,3584]{1,0:T(8,128)(2,1)S(1)} %get-tuple-element.42.refs_1_), custom_call_target="tpu_custom_call" | custom-call | tf_op jit(solution)/shard_map/pallas_call | solution.py:155
  (18 shorter events, 0.6 us)
Async XLA Ops:
  1.2 8.0 %collective-permute-start = (bf16[8,3584]{1,0:T(8,128)(2,1)S(1)}, bf16[8,3584]{1,0:T(8,128)(2,1)S(1)}, u32[]{:S(2)}, u32[]{:S(2)}) collective-permute-start(bf16[8,3584]{1,0:T(8,128)(2,1)S(1)} %get-tuple-element.27), channel_id=1, source_target_pairs={{0,16},{2,18},{4,20},{6,22},{8,24},{10,26},{12,28},{14,30},{16,0},... | collective-permute-start | bytes 172040 | tf_op jit(solution)/shard_map/ppermute | solution.py:181
  5.3 6.1 %collective-permute-start.1 = (bf16[8,3584]{1,0:T(8,128)(2,1)S(1)}, bf16[8,3584]{1,0:T(8,128)(2,1)S(1)}, u32[]{:S(2)}, u32[]{:S(2)}) collective-permute-start(bf16[8,3584]{1,0:T(8,128)(2,1)S(1)} %get-tuple-element.28), channel_id=1, source_target_pairs={{0,24},{2,26},{4,28},{6,30},{8,16},{10,18},{12,20},{14,22},{16,8},... | collective-permute-start | bytes 172040 | tf_op jit(solution)/shard_map/ppermute | solution.py:181
  6.6 6.3 %collective-permute-start.10 = (bf16[8,3584]{1,0:T(8,128)(2,1)S(1)}, bf16[8,3584]{1,0:T(8,128)(2,1)S(1)}, u32[]{:S(2)}, u32[]{:S(2)}) collective-permute-start(bf16[8,3584]{1,0:T(8,128)(2,1)S(1)} %get-tuple-element.35), channel_id=1, source_target_pairs={{0,8},{2,10},{4,12},{6,14},{8,0},{10,2},{12,4},{14,6},{16,24},{18,... | collective-permute-start | bytes 172040 | tf_op jit(solution)/shard_map/ppermute | solution.py:181
  11.4 4.9 %collective-permute-start.2 = (bf16[16,3584]{1,0:T(8,128)(2,1)S(1)}, bf16[16,3584]{1,0:T(8,128)(2,1)S(1)}, u32[]{:S(2)}, u32[]{:S(2)}) collective-permute-start(bf16[16,3584]{1,0:T(8,128)(2,1)S(1)} %shard_map.76.refs_0_), channel_id=1, source_target_pairs={{0,2},{2,0},{4,6},{6,4},{8,10},{10,8},{12,14},{14,12},{16,18},{18,... | collective-permute-start | bytes 344072 | tf_op jit(solution)/shard_map/ppermute | solution.py:181
  13.0 6.3 %collective-permute-start.11 = (bf16[16,3584]{1,0:T(8,128)(2,1)S(1)}, bf16[16,3584]{1,0:T(8,128)(2,1)S(1)}, u32[]{:S(2)}, u32[]{:S(2)}) collective-permute-start(bf16[16,3584]{1,0:T(8,128)(2,1)S(1)} %shard_map.82.refs_0_), channel_id=1, source_target_pairs={{0,4},{2,6},{4,0},{6,2},{8,12},{10,14},{12,8},{14,10},{16,20},{18,... | collective-permute-start | bytes 344072 | tf_op jit(solution)/shard_map/ppermute | solution.py:181
  14.6 6.7 %collective-permute-start.3 = (bf16[16,3584]{1,0:T(8,128)(2,1)S(1)}, bf16[16,3584]{1,0:T(8,128)(2,1)S(1)}, u32[]{:S(2)}, u32[]{:S(2)}) collective-permute-start(bf16[16,3584]{1,0:T(8,128)(2,1)S(1)} %shard_map.76.refs_0_), channel_id=1, source_target_pairs={{0,4},{2,6},{4,0},{6,2},{8,12},{10,14},{12,8},{14,10},{16,20},{18,... | collective-permute-start | bytes 344072 | tf_op jit(solution)/shard_map/ppermute | solution.py:181
  16.2 5.1 %collective-permute-start.4 = (bf16[16,3584]{1,0:T(8,128)(2,1)S(1)}, bf16[16,3584]{1,0:T(8,128)(2,1)S(1)}, u32[]{:S(2)}, u32[]{:S(2)}) collective-permute-start(bf16[16,3584]{1,0:T(8,128)(2,1)S(1)} %collective-permute-done.2.refs_1_), channel_id=1, source_target_pairs={{0,4},{2,6},{4,0},{6,2},{8,12},{10,14},{12,8},{14,10},{16,20},{18,... | collective-permute-start | bytes 344072 | tf_op jit(solution)/shard_map/ppermute | solution.py:181
  17.8 6.3 %collective-permute-start.12 = (bf16[16,3584]{1,0:T(8,128)(2,1)S(1)}, bf16[16,3584]{1,0:T(8,128)(2,1)S(1)}, u32[]{:S(2)}, u32[]{:S(2)}) collective-permute-start(bf16[16,3584]{1,0:T(8,128)(2,1)S(1)} %shard_map.82.refs_0_), channel_id=1, source_target_pairs={{0,2},{2,0},{4,6},{6,4},{8,10},{10,8},{12,14},{14,12},{16,18},{18,... | collective-permute-start | bytes 344072 | tf_op jit(solution)/shard_map/ppermute | solution.py:181
  19.3 5.8 %collective-permute-start.13 = (bf16[16,3584]{1,0:T(8,128)(2,1)S(1)}, bf16[16,3584]{1,0:T(8,128)(2,1)S(1)}, u32[]{:S(2)}, u32[]{:S(2)}) collective-permute-start(bf16[16,3584]{1,0:T(8,128)(2,1)S(1)} %collective-permute-done.11.refs_1_), channel_id=1, source_target_pairs={{0,2},{2,0},{4,6},{6,4},{8,10},{10,8},{12,14},{14,12},{16,18},{18,... | collective-permute-start | bytes 344072 | tf_op jit(solution)/shard_map/ppermute | solution.py:181
  22.5 6.0 %collective-permute-start.6 = (bf16[16,3584]{1,0:T(8,128)(2,1)S(1)}, bf16[16,3584]{1,0:T(8,128)(2,1)S(1)}, u32[]{:S(2)}, u32[]{:S(2)}) collective-permute-start(bf16[16,3584]{1,0:T(8,128)(2,1)S(1)} %get-tuple-element.32), channel_id=1, source_target_pairs={{0,2},{2,0},{4,6},{6,4},{8,10},{10,8},{12,14},{14,12},{16,18},{18,... | collective-permute-start | bytes 344072 | tf_op jit(solution)/shard_map/ppermute | solution.py:181
  26.2 4.9 %collective-permute-start.15 = (bf16[16,3584]{1,0:T(8,128)(2,1)S(1)}, bf16[16,3584]{1,0:T(8,128)(2,1)S(1)}, u32[]{:S(2)}, u32[]{:S(2)}) collective-permute-start(bf16[16,3584]{1,0:T(8,128)(2,1)S(1)} %get-tuple-element.40), channel_id=1, source_target_pairs={{0,4},{2,6},{4,0},{6,2},{8,12},{10,14},{12,8},{14,10},{16,20},{18,... | collective-permute-start | bytes 344072 | tf_op jit(solution)/shard_map/ppermute | solution.py:181
  27.3 5.6 %collective-permute-start.5 = (bf16[16,3584]{1,0:T(8,128)(2,1)S(1)}, bf16[16,3584]{1,0:T(8,128)(2,1)S(1)}, u32[]{:S(2)}, u32[]{:S(2)}) collective-permute-start(bf16[16,3584]{1,0:T(8,128)(2,1)S(1)} %get-tuple-element.30), channel_id=1, source_target_pairs={{0,2},{2,0},{4,6},{6,4},{8,10},{10,8},{12,14},{14,12},{16,18},{18,... | collective-permute-start | bytes 344072 | tf_op jit(solution)/shard_map/ppermute | solution.py:181
  28.5 4.9 %collective-permute-start.7 = (bf16[16,3584]{1,0:T(8,128)(2,1)S(1)}, bf16[16,3584]{1,0:T(8,128)(2,1)S(1)}, u32[]{:S(2)}, u32[]{:S(2)}) collective-permute-start(bf16[16,3584]{1,0:T(8,128)(2,1)S(1)} %shard_map.79), channel_id=1, source_target_pairs={{0,4},{2,6},{4,0},{6,2},{8,12},{10,14},{12,8},{14,10},{16,20},{18,... | collective-permute-start | bytes 344072 | tf_op jit(solution)/shard_map/ppermute | solution.py:181
  30.0 6.9 %collective-permute-start.14 = (bf16[16,3584]{1,0:T(8,128)(2,1)S(1)}, bf16[16,3584]{1,0:T(8,128)(2,1)S(1)}, u32[]{:S(2)}, u32[]{:S(2)}) collective-permute-start(bf16[16,3584]{1,0:T(8,128)(2,1)S(1)} %get-tuple-element.38), channel_id=1, source_target_pairs={{0,4},{2,6},{4,0},{6,2},{8,12},{10,14},{12,8},{14,10},{16,20},{18,... | collective-permute-start | bytes 344072 | tf_op jit(solution)/shard_map/ppermute | solution.py:181
  31.1 5.8 %collective-permute-start.16 = (bf16[16,3584]{1,0:T(8,128)(2,1)S(1)}, bf16[16,3584]{1,0:T(8,128)(2,1)S(1)}, u32[]{:S(2)}, u32[]{:S(2)}) collective-permute-start(bf16[16,3584]{1,0:T(8,128)(2,1)S(1)} %shard_map.84), channel_id=1, source_target_pairs={{0,2},{2,0},{4,6},{6,4},{8,10},{10,8},{12,14},{14,12},{16,18},{18,... | collective-permute-start | bytes 344072 | tf_op jit(solution)/shard_map/ppermute | solution.py:181
  33.4 5.3 %collective-permute-start.8 = (bf16[8,3584]{1,0:T(8,128)(2,1)S(1)}, bf16[8,3584]{1,0:T(8,128)(2,1)S(1)}, u32[]{:S(2)}, u32[]{:S(2)}) collective-permute-start(bf16[8,3584]{1,0:T(8,128)(2,1)S(1)} %get-tuple-element.33), channel_id=1, source_target_pairs={{0,16},{2,18},{4,20},{6,22},{8,24},{10,26},{12,28},{14,30},{16,0},... | collective-permute-start | bytes 172040 | tf_op jit(solution)/shard_map/ppermute | solution.py:181
  36.4 6.0 %collective-permute-start.9 = (bf16[8,3584]{1,0:T(8,128)(2,1)S(1)}, bf16[8,3584]{1,0:T(8,128)(2,1)S(1)}, u32[]{:S(2)}, u32[]{:S(2)}) collective-permute-start(bf16[8,3584]{1,0:T(8,128)(2,1)S(1)} %get-tuple-element.34), channel_id=1, source_target_pairs={{0,24},{2,26},{4,28},{6,30},{8,16},{10,18},{12,20},{14,22},{16,8},... | collective-permute-start | bytes 172040 | tf_op jit(solution)/shard_map/ppermute | solution.py:181
  36.9 5.7 %collective-permute-start.17 = (bf16[8,3584]{1,0:T(8,128)(2,1)S(1)}, bf16[8,3584]{1,0:T(8,128)(2,1)S(1)}, u32[]{:S(2)}, u32[]{:S(2)}) collective-permute-start(bf16[8,3584]{1,0:T(8,128)(2,1)S(1)} %get-tuple-element.41), channel_id=1, source_target_pairs={{0,8},{2,10},{4,12},{6,14},{8,0},{10,2},{12,4},{14,6},{16,24},{18,... | collective-permute-start | bytes 172040 | tf_op jit(solution)/shard_map/ppermute | solution.py:181

commit v14 on v13

--- a/solution.py
+++ b/solution.py
@@ -180,6 +180,15 @@
     def swap(value, offset):
         return lax.ppermute(value, "expert", [(e, e ^ offset) for e in range(n_devices)])
 
+    def turn(value, even, odd):
+        parts = lax.axis_size("dp")
+        pairs = [
+            (e * parts + part, (e ^ (odd if part % 2 else even)) * parts + part)
+            for e in range(n_devices)
+            for part in range(parts)
+        ]
+        return lax.ppermute(value, ("expert", "dp"), pairs)
+
     def local(kernel, inputs, outs, limit=16 * MIB):
         return call(kernel, inputs, [VMEM] * len(inputs), outs, limit)
 
@@ -226,8 +235,8 @@
             functools.partial(stack_kernel, count), chunks[h * count :][:count] + earlier, half
         )
         if square:
-            held = {a: swap(own, a), b: swap(own, b)}
-            held = [own, held[a], held[b], swap(held[a], b)]
+            first = turn(own, a, b)
+            held = [own, first, turn(own, b, a), turn(first, b, a)]
         else:
             held = [swap(own, q) if q else own for q in range(group_size)]
         earlier = []
@@ -239,10 +248,10 @@
         )
         if square:
             mine, first, second, cross = result
-            cross = swap(cross, a)
-            first = swap(first, a)
+            cross = turn(cross, a, b)
+            first = turn(first, a, b)
             second = local(functools.partial(sum_kernel, 2), [second, cross], [half])[0]
-            result = [mine, first, swap(second, b)]
+            result = [mine, first, turn(second, b, a)]
         else:
             result = [swap(v, q) if q else v for q, v in enumerate(result)]
         summed += local(functools.partial(sum_kernel, len(result)), result, [chunk] * count)

time: 43.7 us -> 44.7 us (1.023)
  waiting for transfers between devices: 11 us -> 12.9 us
  starting transfers between devices: 23.9 us -> 23 us
    ppermute x18 -> x6, starting transfers between devices: 23.9 us -> 9.29 us  [swap(): lax.ppermute(value, 'expert', [(e, e ^ offset) for e in range(n_devices)])]
    ppermute x0 -> x12, starting transfers between devices: none -> 13.7 us  [turn(): return lax.ppermute(value, ('expert', 'dp'), pairs)]
    ppermute x0 -> x12, waiting for transfers between devices: none -> 6.1 us  [turn(): return lax.ppermute(value, ('expert', 'dp'), pairs)]
    ppermute x18 -> x6, waiting for transfers between devices: 11 us -> 6.77 us  [swap(): lax.ppermute(value, 'expert', [(e, e ^ offset) for e in range(n_devices)])]
  transfers between devices with their start and end apart: 18 -> 18, of which waited for: 8 -> 7; matrix products, arithmetic and copies ran while one was open for 0% -> 0% of each run, Pallas kernels for 15% -> 14%
where the time goes in v14:
time: 44.7 us; the launch traced here: 44.5 us
  starting transfers between devices  23 us (51%)
  waiting for transfers between devices  12.9 us (29%)
  Pallas kernels  8.52 us (19%)
    ppermute x12, starting transfers between devices, turn(): return lax.ppermute(value, ('expert', 'dp'), pairs)  13.7 us
    ppermute x6, starting transfers between devices, swap(): lax.ppermute(value, 'expert', [(e, e ^ offset) for e in range(n_devices)])  9.29 us
    pallas_call x14, Pallas kernels, call(): pl.pallas_call(kernel, out_shape=outs, in_specs=in_specs, out_specs=jax.t...  8.52 us
    ppermute x6, waiting for transfers between devices, swap(): lax.ppermute(value, 'expert', [(e, e ^ offset) for e in range(n_devices)])  6.77 us
    ppermute x12, waiting for transfers between devices, turn(): return lax.ppermute(value, ('expert', 'dp'), pairs)  6.1 us
  transfers between devices with their start and end apart: 18, of which 7 were waited for; matrix products, arithmetic and copies ran while one was open for 0% of the time, Pallas kernels for 14%

profile of v14, /device:TPU:0, one launch (start us, length us, event | category | flops | bytes accessed | tf_op | source)
XLA Modules:
  0.0 44.5 jit_solution(1224489571323685323)
XLA Ops:
  0.0 1.2 %shard_map.73 = (bf16[8,3584]{1,0:T(8,128)(2,1)S(1)}, bf16[8,3584]{1,0:T(8,128)(2,1)S(1)}, bf16[8,3584]{1,0:T(8,128)(2,1)S(1)}, bf16[8,3584]{1,0:T(8,128)(2,1)S(1)}, f32[32,16]{1,0:T(8,128)S(1)}) custom-call(s32[4]{0:T(128)} %refs_0_.3, s32[2,16]{1,0:T(2,128)} %bitcast.3, s32[2,16]{1,0:T(2,128)} %bitcast.4, f32[2,16]{1,0:T(2,128)} %bitcast.5, ...), custom_call_target="tpu_custom_call" | custom-call | tf_op jit(solution)/shard_map/pallas_call | solution.py:155
  1.2 4.1 %collective-permute-start = (bf16[8,3584]{1,0:T(8,128)(2,1)S(1)}, bf16[8,3584]{1,0:T(8,128)(2,1)S(1)}, u32[]{:S(2)}, u32[]{:S(2)}) collective-permute-start(bf16[8,3584]{1,0:T(8,128)(2,1)S(1)} %get-tuple-element.27), channel_id=1, source_target_pairs={{0,16},{2,18},{4,20},{6,22},{8,24},{10,26},{12,28},{14,30},{16,0},... | collective-permute-start | bytes 172040 | tf_op jit(solution)/shard_map/ppermute | solution.py:181
  5.3 1.4 %collective-permute-start.1 = (bf16[8,3584]{1,0:T(8,128)(2,1)S(1)}, bf16[8,3584]{1,0:T(8,128)(2,1)S(1)}, u32[]{:S(2)}, u32[]{:S(2)}) collective-permute-start(bf16[8,3584]{1,0:T(8,128)(2,1)S(1)} %get-tuple-element.28), channel_id=1, source_target_pairs={{0,24},{2,26},{4,28},{6,30},{8,16},{10,18},{12,20},{14,22},{16,8},... | collective-permute-start | bytes 172040 | tf_op jit(solution)/shard_map/ppermute | solution.py:181
  6.6 0.2 collective-permute-start.10
  6.9 0.2 shard_map.74
  7.1 2.1 %shard_map.75.refs_2_.refs_4_ = bf16[2,3584,256]{2,1,0:T(8,128)(2,1)S(1)} custom-call(bf16[2,3584,256]{2,1,0:T(8,128)(2,1)} %refs_0_.4, bf16[48,16]{1,0:T(8,128)(2,1)S(1)} %get-tuple-element.26.refs_1_.terms), custom_call_target="tpu_custom_call" | custom-call | bytes 3670016 | tf_op jit(solution)/shard_map/pallas_call | solution.py:155
  9.1 2.2 %collective-permute-done.1.refs_1_ = bf16[8,3584]{1,0:T(8,128)(2,1)S(1)} collective-permute-done((bf16[8,3584]{1,0:T(8,128)(2,1)S(1)}, bf16[8,3584]{1,0:T(8,128)(2,1)S(1)}, u32[]{:S(2)}, u32[]{:S(2)}) %collective-permute-start.1) | collective-permute-done | bytes 57376 | tf_op jit(solution)/shard_map/ppermute | solution.py:181
  11.4 1.6 %collective-permute-start.2 = (bf16[16,3584]{1,0:T(8,128)(2,1)S(1)}, bf16[16,3584]{1,0:T(8,128)(2,1)S(1)}, u32[]{:S(2)}, u32[]{:S(2)}) collective-permute-start(bf16[16,3584]{1,0:T(8,128)(2,1)S(1)} %shard_map.76.refs_0_), channel_id=1, source_target_pairs={{0,2},{1,5},{2,0},{3,7},{4,6},{5,1},{6,4},{7,3},{8,10},{9,13},{10,... | collective-permute-start | bytes 344072 | tf_op jit(solution)/shard_map/ppermute | solution.py:190
  13.0 1.6 %collective-permute-start.11 = (bf16[16,3584]{1,0:T(8,128)(2,1)S(1)}, bf16[16,3584]{1,0:T(8,128)(2,1)S(1)}, u32[]{:S(2)}, u32[]{:S(2)}) collective-permute-start(bf16[16,3584]{1,0:T(8,128)(2,1)S(1)} %shard_map.82.refs_0_), channel_id=1, source_target_pairs={{0,4},{1,3},{2,6},{3,1},{4,0},{5,7},{6,2},{7,5},{8,12},{9,11},{10,... | collective-permute-start | bytes 344072 | tf_op jit(solution)/shard_map/ppermute | solution.py:190
  14.6 0.5 %collective-permute-start.3 = (bf16[16,3584]{1,0:T(8,128)(2,1)S(1)}, bf16[16,3584]{1,0:T(8,128)(2,1)S(1)}, u32[]{:S(2)}, u32[]{:S(2)}) collective-permute-start(bf16[16,3584]{1,0:T(8,128)(2,1)S(1)} %shard_map.76.refs_0_), channel_id=1, source_target_pairs={{0,4},{1,3},{2,6},{3,1},{4,0},{5,7},{6,2},{7,5},{8,12},{9,11},{10,... | collective-permute-start | bytes 344072 | tf_op jit(solution)/shard_map/ppermute | solution.py:190
  15.1 2.4 %collective-permute-done.2.refs_1_ = bf16[16,3584]{1,0:T(8,128)(2,1)S(1)} collective-permute-done((bf16[16,3584]{1,0:T(8,128)(2,1)S(1)}, bf16[16,3584]{1,0:T(8,128)(2,1)S(1)}, u32[]{:S(2)}, u32[]{:S(2)}) %collective-permute-start.2) | collective-permute-done | bytes 114720 | tf_op jit(solution)/shard_map/ppermute | solution.py:190
  17.5 0.7 %collective-permute-start.4 = (bf16[16,3584]{1,0:T(8,128)(2,1)S(1)}, bf16[16,3584]{1,0:T(8,128)(2,1)S(1)}, u32[]{:S(2)}, u32[]{:S(2)}) collective-permute-start(bf16[16,3584]{1,0:T(8,128)(2,1)S(1)} %collective-permute-done.2.refs_1_), channel_id=1, source_target_pairs={{0,4},{1,3},{2,6},{3,1},{4,0},{5,7},{6,2},{7,5},{8,12},{9,11},{10,... | collective-permute-start | bytes 344072 | tf_op jit(solution)/shard_map/ppermute | solution.py:190
  18.3 1.5 %collective-permute-start.12 = (bf16[16,3584]{1,0:T(8,128)(2,1)S(1)}, bf16[16,3584]{1,0:T(8,128)(2,1)S(1)}, u32[]{:S(2)}, u32[]{:S(2)}) collective-permute-start(bf16[16,3584]{1,0:T(8,128)(2,1)S(1)} %shard_map.82.refs_0_), channel_id=1, source_target_pairs={{0,2},{1,5},{2,0},{3,7},{4,6},{5,1},{6,4},{7,3},{8,10},{9,13},{10,... | collective-permute-start | bytes 344072 | tf_op jit(solution)/shard_map/ppermute | solution.py:190
  19.8 0.5 %collective-permute-start.13 = (bf16[16,3584]{1,0:T(8,128)(2,1)S(1)}, bf16[16,3584]{1,0:T(8,128)(2,1)S(1)}, u32[]{:S(2)}, u32[]{:S(2)}) collective-permute-start(bf16[16,3584]{1,0:T(8,128)(2,1)S(1)} %collective-permute-done.11.refs_1_), channel_id=1, source_target_pairs={{0,2},{1,5},{2,0},{3,7},{4,6},{5,1},{6,4},{7,3},{8,10},{9,13},{10,... | collective-permute-start | bytes 344072 | tf_op jit(solution)/shard_map/ppermute | solution.py:190
  20.3 1.5 %shard_map.77.refs_5_ = bf16[256,3584]{1,0:T(8,128)(2,1)S(1)} custom-call(bf16[256,3584]{1,0:T(8,128)(2,1)} %refs_0_.5, bf16[48,16]{1,0:T(8,128)(2,1)S(1)} %get-tuple-element.25.refs_1_.terms), custom_call_target="tpu_custom_call" | custom-call | bytes 1835008 | tf_op jit(solution)/shard_map/pallas_call | solution.py:155
  21.8 1.1 %collective-permute-done.4.refs_3_ = bf16[16,3584]{1,0:T(8,128)(2,1)S(1)} collective-permute-done((bf16[16,3584]{1,0:T(8,128)(2,1)S(1)}, bf16[16,3584]{1,0:T(8,128)(2,1)S(1)}, u32[]{:S(2)}, u32[]{:S(2)}) %collective-permute-start.4) | collective-permute-done | bytes 114720 | tf_op jit(solution)/shard_map/ppermute | solution.py:190
  22.9 1.2 %shard_map.78 = (bf16[16,3584]{1,0:T(8,128)(2,1)S(1)}, bf16[16,3584]{1,0:T(8,128)(2,1)S(1)}, bf16[16,3584]{1,0:T(8,128)(2,1)S(1)}, bf16[16,3584]{1,0:T(8,128)(2,1)S(1)}) custom-call(bf16[16,3584]{1,0:T(8,128)(2,1)S(1)} %shard_map.76.refs_0_, bf16[16,3584]{1,0:T(8,128)(2,1)S(1)} %collective-permute-done.2.refs_1_, ...), custom_call_target="tpu_custom_call" | custom-call | tf_op jit(solution)/shard_map/pallas_call | solution.py:155
  24.0 1.0 %collective-permute-start.6 = (bf16[16,3584]{1,0:T(8,128)(2,1)S(1)}, bf16[16,3584]{1,0:T(8,128)(2,1)S(1)}, u32[]{:S(2)}, u32[]{:S(2)}) collective-permute-start(bf16[16,3584]{1,0:T(8,128)(2,1)S(1)} %get-tuple-element.32), channel_id=1, source_target_pairs={{0,2},{1,5},{2,0},{3,7},{4,6},{5,1},{6,4},{7,3},{8,10},{9,13},{10,... | collective-permute-start | bytes 344072 | tf_op jit(solution)/shard_map/ppermute | solution.py:190
  25.1 1.2 %shard_map.83 = (bf16[16,3584]{1,0:T(8,128)(2,1)S(1)}, bf16[16,3584]{1,0:T(8,128)(2,1)S(1)}, bf16[16,3584]{1,0:T(8,128)(2,1)S(1)}, bf16[16,3584]{1,0:T(8,128)(2,1)S(1)}) custom-call(bf16[16,3584]{1,0:T(8,128)(2,1)S(1)} %shard_map.82.refs_0_, bf16[16,3584]{1,0:T(8,128)(2,1)S(1)} %collective-permute-done.11.refs_1_, ...), custom_call_target="tpu_custom_call" | custom-call | tf_op jit(solution)/shard_map/pallas_call | solution.py:155
  26.2 1.3 %collective-permute-start.15 = (bf16[16,3584]{1,0:T(8,128)(2,1)S(1)}, bf16[16,3584]{1,0:T(8,128)(2,1)S(1)}, u32[]{:S(2)}, u32[]{:S(2)}) collective-permute-start(bf16[16,3584]{1,0:T(8,128)(2,1)S(1)} %get-tuple-element.40), channel_id=1, source_target_pairs={{0,4},{1,3},{2,6},{3,1},{4,0},{5,7},{6,2},{7,5},{8,12},{9,11},{10,... | collective-permute-start | bytes 344072 | tf_op jit(solution)/shard_map/ppermute | solution.py:190
  27.5 1.9 %collective-permute-start.5 = (bf16[16,3584]{1,0:T(8,128)(2,1)S(1)}, bf16[16,3584]{1,0:T(8,128)(2,1)S(1)}, u32[]{:S(2)}, u32[]{:S(2)}) collective-permute-start(bf16[16,3584]{1,0:T(8,128)(2,1)S(1)} %get-tuple-element.30), channel_id=1, source_target_pairs={{0,2},{1,5},{2,0},{3,7},{4,6},{5,1},{6,4},{7,3},{8,10},{9,13},{10,... | collective-permute-start | bytes 344072 | tf_op jit(solution)/shard_map/ppermute | solution.py:190
  29.4 0.7 %collective-permute-done.6.refs_1_ = bf16[16,3584]{1,0:T(8,128)(2,1)S(1)} collective-permute-done((bf16[16,3584]{1,0:T(8,128)(2,1)S(1)}, bf16[16,3584]{1,0:T(8,128)(2,1)S(1)}, u32[]{:S(2)}, u32[]{:S(2)}) %collective-permute-start.6) | collective-permute-done | bytes 114720 | tf_op jit(solution)/shard_map/ppermute | solution.py:190
  30.2 2.2 %collective-permute-start.7 = (bf16[16,3584]{1,0:T(8,128)(2,1)S(1)}, bf16[16,3584]{1,0:T(8,128)(2,1)S(1)}, u32[]{:S(2)}, u32[]{:S(2)}) collective-permute-start(bf16[16,3584]{1,0:T(8,128)(2,1)S(1)} %shard_map.79), channel_id=1, source_target_pairs={{0,4},{1,3},{2,6},{3,1},{4,0},{5,7},{6,2},{7,5},{8,12},{9,11},{10,... | collective-permute-start | bytes 344072 | tf_op jit(solution)/shard_map/ppermute | solution.py:190
  32.4 0.8 %collective-permute-start.16 = (bf16[16,3584]{1,0:T(8,128)(2,1)S(1)}, bf16[16,3584]{1,0:T(8,128)(2,1)S(1)}, u32[]{:S(2)}, u32[]{:S(2)}) collective-permute-start(bf16[16,3584]{1,0:T(8,128)(2,1)S(1)} %shard_map.84), channel_id=1, source_target_pairs={{0,2},{1,5},{2,0},{3,7},{4,6},{5,1},{6,4},{7,3},{8,10},{9,13},{10,... | collective-permute-start | bytes 344072 | tf_op jit(solution)/shard_map/ppermute | solution.py:190
  33.3 1.8 %collective-permute-done.7.refs_2_ = bf16[16,3584]{1,0:T(8,128)(2,1)S(1)} collective-permute-done((bf16[16,3584]{1,0:T(8,128)(2,1)S(1)}, bf16[16,3584]{1,0:T(8,128)(2,1)S(1)}, u32[]{:S(2)}, u32[]{:S(2)}) %collective-permute-start.7) | collective-permute-done | bytes 114720 | tf_op jit(solution)/shard_map/ppermute | solution.py:190
  35.1 2.2 %collective-permute-start.8 = (bf16[8,3584]{1,0:T(8,128)(2,1)S(1)}, bf16[8,3584]{1,0:T(8,128)(2,1)S(1)}, u32[]{:S(2)}, u32[]{:S(2)}) collective-permute-start(bf16[8,3584]{1,0:T(8,128)(2,1)S(1)} %get-tuple-element.33), channel_id=1, source_target_pairs={{0,16},{2,18},{4,20},{6,22},{8,24},{10,26},{12,28},{14,30},{16,0},... | collective-permute-start | bytes 172040 | tf_op jit(solution)/shard_map/ppermute | solution.py:181
  37.4 0.4 collective-permute-start.9
  37.9 0.9 %collective-permute-start.17 = (bf16[8,3584]{1,0:T(8,128)(2,1)S(1)}, bf16[8,3584]{1,0:T(8,128)(2,1)S(1)}, u32[]{:S(2)}, u32[]{:S(2)}) collective-permute-start(bf16[8,3584]{1,0:T(8,128)(2,1)S(1)} %get-tuple-element.41), channel_id=1, source_target_pairs={{0,8},{2,10},{4,12},{6,14},{8,0},{10,2},{12,4},{14,6},{16,24},{18,... | collective-permute-start | bytes 172040 | tf_op jit(solution)/shard_map/ppermute | solution.py:181
  38.8 1.8 %collective-permute-done.8.refs_0_ = bf16[8,3584]{1,0:T(8,128)(2,1)S(1)} collective-permute-done((bf16[8,3584]{1,0:T(8,128)(2,1)S(1)}, bf16[8,3584]{1,0:T(8,128)(2,1)S(1)}, u32[]{:S(2)}, u32[]{:S(2)}) %collective-permute-start.8) | collective-permute-done | bytes 57376 | tf_op jit(solution)/shard_map/ppermute | solution.py:181
  40.6 2.8 %collective-permute-done.9.refs_1_ = bf16[8,3584]{1,0:T(8,128)(2,1)S(1)} collective-permute-done((bf16[8,3584]{1,0:T(8,128)(2,1)S(1)}, bf16[8,3584]{1,0:T(8,128)(2,1)S(1)}, u32[]{:S(2)}, u32[]{:S(2)}) %collective-permute-start.9) | collective-permute-done | bytes 57376 | tf_op jit(solution)/shard_map/ppermute | solution.py:181
  43.3 0.2 shard_map.81.near
  43.6 0.9 %shard_map.86 = bf16[16,3584]{1,0:T(8,128)(2,1)} custom-call(bf16[48,16]{1,0:T(8,128)(2,1)S(1)} %get-tuple-element.25.refs_1_.terms, f32[16,3584]{1,0:T(8,128)S(1)} %shard_map.81.near, bf16[8,3584]{1,0:T(8,128)(2,1)S(1)} %collective-permute-done.17.refs_0_, bf16[8,3584]{1,0:T(8,128)(2,1)S(1)} %get-tuple-element.42.refs_1_), custom_call_target="tpu_custom_call" | custom-call | tf_op jit(solution)/shard_map/pallas_call | solution.py:155
  (18 shorter events, 0.3 us)
Async XLA Ops:
  1.2 8.0 %collective-permute-start = (bf16[8,3584]{1,0:T(8,128)(2,1)S(1)}, bf16[8,3584]{1,0:T(8,128)(2,1)S(1)}, u32[]{:S(2)}, u32[]{:S(2)}) collective-permute-start(bf16[8,3584]{1,0:T(8,128)(2,1)S(1)} %get-tuple-element.27), channel_id=1, source_target_pairs={{0,16},{2,18},{4,20},{6,22},{8,24},{10,26},{12,28},{14,30},{16,0},... | collective-permute-start | bytes 172040 | tf_op jit(solution)/shard_map/ppermute | solution.py:181
  5.3 6.1 %collective-permute-start.1 = (bf16[8,3584]{1,0:T(8,128)(2,1)S(1)}, bf16[8,3584]{1,0:T(8,128)(2,1)S(1)}, u32[]{:S(2)}, u32[]{:S(2)}) collective-permute-start(bf16[8,3584]{1,0:T(8,128)(2,1)S(1)} %get-tuple-element.28), channel_id=1, source_target_pairs={{0,24},{2,26},{4,28},{6,30},{8,16},{10,18},{12,20},{14,22},{16,8},... | collective-permute-start | bytes 172040 | tf_op jit(solution)/shard_map/ppermute | solution.py:181
  6.6 6.3 %collective-permute-start.10 = (bf16[8,3584]{1,0:T(8,128)(2,1)S(1)}, bf16[8,3584]{1,0:T(8,128)(2,1)S(1)}, u32[]{:S(2)}, u32[]{:S(2)}) collective-permute-start(bf16[8,3584]{1,0:T(8,128)(2,1)S(1)} %get-tuple-element.35), channel_id=1, source_target_pairs={{0,8},{2,10},{4,12},{6,14},{8,0},{10,2},{12,4},{14,6},{16,24},{18,... | collective-permute-start | bytes 172040 | tf_op jit(solution)/shard_map/ppermute | solution.py:181
  11.4 6.1 %collective-permute-start.2 = (bf16[16,3584]{1,0:T(8,128)(2,1)S(1)}, bf16[16,3584]{1,0:T(8,128)(2,1)S(1)}, u32[]{:S(2)}, u32[]{:S(2)}) collective-permute-start(bf16[16,3584]{1,0:T(8,128)(2,1)S(1)} %shard_map.76.refs_0_), channel_id=1, source_target_pairs={{0,2},{1,5},{2,0},{3,7},{4,6},{5,1},{6,4},{7,3},{8,10},{9,13},{10,... | collective-permute-start | bytes 344072 | tf_op jit(solution)/shard_map/ppermute | solution.py:190
  13.0 6.8 %collective-permute-start.11 = (bf16[16,3584]{1,0:T(8,128)(2,1)S(1)}, bf16[16,3584]{1,0:T(8,128)(2,1)S(1)}, u32[]{:S(2)}, u32[]{:S(2)}) collective-permute-start(bf16[16,3584]{1,0:T(8,128)(2,1)S(1)} %shard_map.82.refs_0_), channel_id=1, source_target_pairs={{0,4},{1,3},{2,6},{3,1},{4,0},{5,7},{6,2},{7,5},{8,12},{9,11},{10,... | collective-permute-start | bytes 344072 | tf_op jit(solution)/shard_map/ppermute | solution.py:190
  14.6 7.2 %collective-permute-start.3 = (bf16[16,3584]{1,0:T(8,128)(2,1)S(1)}, bf16[16,3584]{1,0:T(8,128)(2,1)S(1)}, u32[]{:S(2)}, u32[]{:S(2)}) collective-permute-start(bf16[16,3584]{1,0:T(8,128)(2,1)S(1)} %shard_map.76.refs_0_), channel_id=1, source_target_pairs={{0,4},{1,3},{2,6},{3,1},{4,0},{5,7},{6,2},{7,5},{8,12},{9,11},{10,... | collective-permute-start | bytes 344072 | tf_op jit(solution)/shard_map/ppermute | solution.py:190
  17.5 5.4 %collective-permute-start.4 = (bf16[16,3584]{1,0:T(8,128)(2,1)S(1)}, bf16[16,3584]{1,0:T(8,128)(2,1)S(1)}, u32[]{:S(2)}, u32[]{:S(2)}) collective-permute-start(bf16[16,3584]{1,0:T(8,128)(2,1)S(1)} %collective-permute-done.2.refs_1_), channel_id=1, source_target_pairs={{0,4},{1,3},{2,6},{3,1},{4,0},{5,7},{6,2},{7,5},{8,12},{9,11},{10,... | collective-permute-start | bytes 344072 | tf_op jit(solution)/shard_map/ppermute | solution.py:190
  18.3 6.8 %collective-permute-start.12 = (bf16[16,3584]{1,0:T(8,128)(2,1)S(1)}, bf16[16,3584]{1,0:T(8,128)(2,1)S(1)}, u32[]{:S(2)}, u32[]{:S(2)}) collective-permute-start(bf16[16,3584]{1,0:T(8,128)(2,1)S(1)} %shard_map.82.refs_0_), channel_id=1, source_target_pairs={{0,2},{1,5},{2,0},{3,7},{4,6},{5,1},{6,4},{7,3},{8,10},{9,13},{10,... | collective-permute-start | bytes 344072 | tf_op jit(solution)/shard_map/ppermute | solution.py:190
  19.8 5.3 %collective-permute-start.13 = (bf16[16,3584]{1,0:T(8,128)(2,1)S(1)}, bf16[16,3584]{1,0:T(8,128)(2,1)S(1)}, u32[]{:S(2)}, u32[]{:S(2)}) collective-permute-start(bf16[16,3584]{1,0:T(8,128)(2,1)S(1)} %collective-permute-done.11.refs_1_), channel_id=1, source_target_pairs={{0,2},{1,5},{2,0},{3,7},{4,6},{5,1},{6,4},{7,3},{8,10},{9,13},{10,... | collective-permute-start | bytes 344072 | tf_op jit(solution)/shard_map/ppermute | solution.py:190
  24.0 6.1 %collective-permute-start.6 = (bf16[16,3584]{1,0:T(8,128)(2,1)S(1)}, bf16[16,3584]{1,0:T(8,128)(2,1)S(1)}, u32[]{:S(2)}, u32[]{:S(2)}) collective-permute-start(bf16[16,3584]{1,0:T(8,128)(2,1)S(1)} %get-tuple-element.32), channel_id=1, source_target_pairs={{0,2},{1,5},{2,0},{3,7},{4,6},{5,1},{6,4},{7,3},{8,10},{9,13},{10,... | collective-permute-start | bytes 344072 | tf_op jit(solution)/shard_map/ppermute | solution.py:190
  26.2 6.2 %collective-permute-start.15 = (bf16[16,3584]{1,0:T(8,128)(2,1)S(1)}, bf16[16,3584]{1,0:T(8,128)(2,1)S(1)}, u32[]{:S(2)}, u32[]{:S(2)}) collective-permute-start(bf16[16,3584]{1,0:T(8,128)(2,1)S(1)} %get-tuple-element.40), channel_id=1, source_target_pairs={{0,4},{1,3},{2,6},{3,1},{4,0},{5,7},{6,2},{7,5},{8,12},{9,11},{10,... | collective-permute-start | bytes 344072 | tf_op jit(solution)/shard_map/ppermute | solution.py:190
  27.5 5.8 %collective-permute-start.5 = (bf16[16,3584]{1,0:T(8,128)(2,1)S(1)}, bf16[16,3584]{1,0:T(8,128)(2,1)S(1)}, u32[]{:S(2)}, u32[]{:S(2)}) collective-permute-start(bf16[16,3584]{1,0:T(8,128)(2,1)S(1)} %get-tuple-element.30), channel_id=1, source_target_pairs={{0,2},{1,5},{2,0},{3,7},{4,6},{5,1},{6,4},{7,3},{8,10},{9,13},{10,... | collective-permute-start | bytes 344072 | tf_op jit(solution)/shard_map/ppermute | solution.py:190
  30.2 4.9 %collective-permute-start.7 = (bf16[16,3584]{1,0:T(8,128)(2,1)S(1)}, bf16[16,3584]{1,0:T(8,128)(2,1)S(1)}, u32[]{:S(2)}, u32[]{:S(2)}) collective-permute-start(bf16[16,3584]{1,0:T(8,128)(2,1)S(1)} %shard_map.79), channel_id=1, source_target_pairs={{0,4},{1,3},{2,6},{3,1},{4,0},{5,7},{6,2},{7,5},{8,12},{9,11},{10,... | collective-permute-start | bytes 344072 | tf_op jit(solution)/shard_map/ppermute | solution.py:190
  32.3 5.5 %collective-permute-start.14 = (bf16[16,3584]{1,0:T(8,128)(2,1)S(1)}, bf16[16,3584]{1,0:T(8,128)(2,1)S(1)}, u32[]{:S(2)}, u32[]{:S(2)}) collective-permute-start(bf16[16,3584]{1,0:T(8,128)(2,1)S(1)} %get-tuple-element.38), channel_id=1, source_target_pairs={{0,4},{1,3},{2,6},{3,1},{4,0},{5,7},{6,2},{7,5},{8,12},{9,11},{10,... | collective-permute-start | bytes 344072 | tf_op jit(solution)/shard_map/ppermute | solution.py:190
  32.4 5.4 %collective-permute-start.16 = (bf16[16,3584]{1,0:T(8,128)(2,1)S(1)}, bf16[16,3584]{1,0:T(8,128)(2,1)S(1)}, u32[]{:S(2)}, u32[]{:S(2)}) collective-permute-start(bf16[16,3584]{1,0:T(8,128)(2,1)S(1)} %shard_map.84), channel_id=1, source_target_pairs={{0,2},{1,5},{2,0},{3,7},{4,6},{5,1},{6,4},{7,3},{8,10},{9,13},{10,... | collective-permute-start | bytes 344072 | tf_op jit(solution)/shard_map/ppermute | solution.py:190
  35.1 5.4 %collective-permute-start.8 = (bf16[8,3584]{1,0:T(8,128)(2,1)S(1)}, bf16[8,3584]{1,0:T(8,128)(2,1)S(1)}, u32[]{:S(2)}, u32[]{:S(2)}) collective-permute-start(bf16[8,3584]{1,0:T(8,128)(2,1)S(1)} %get-tuple-element.33), channel_id=1, source_target_pairs={{0,16},{2,18},{4,20},{6,22},{8,24},{10,26},{12,28},{14,30},{16,0},... | collective-permute-start | bytes 172040 | tf_op jit(solution)/shard_map/ppermute | solution.py:181
  37.4 6.0 %collective-permute-start.9 = (bf16[8,3584]{1,0:T(8,128)(2,1)S(1)}, bf16[8,3584]{1,0:T(8,128)(2,1)S(1)}, u32[]{:S(2)}, u32[]{:S(2)}) collective-permute-start(bf16[8,3584]{1,0:T(8,128)(2,1)S(1)} %get-tuple-element.34), channel_id=1, source_target_pairs={{0,24},{2,26},{4,28},{6,30},{8,16},{10,18},{12,20},{14,22},{16,8},... | collective-permute-start | bytes 172040 | tf_op jit(solution)/shard_map/ppermute | solution.py:181
  37.9 5.7 %collective-permute-start.17 = (bf16[8,3584]{1,0:T(8,128)(2,1)S(1)}, bf16[8,3584]{1,0:T(8,128)(2,1)S(1)}, u32[]{:S(2)}, u32[]{:S(2)}) collective-permute-start(bf16[8,3584]{1,0:T(8,128)(2,1)S(1)} %get-tuple-element.41), channel_id=1, source_target_pairs={{0,8},{2,10},{4,12},{6,14},{8,0},{10,2},{12,4},{14,6},{16,24},{18,... | collective-permute-start | bytes 172040 | tf_op jit(solution)/shard_map/ppermute | solution.py:181

commit v15 on v13

--- a/solution.py
+++ b/solution.py
@@ -50,9 +50,7 @@
         here = copy_row == p
         named = jnp.where(here, placement[p], named)
         d = lax.bitwise_xor(own, p)
-        near = jnp.where(d == 0, slot_count - 1, d + slot_count // 2 - 1)
-        place = jnp.where(d < slot_count // 2, near, d - slot_count // 2)
-        relative = jnp.where(here, place, relative)
+        relative = jnp.where(here, slot_count - 1 - d, relative)
         seen = jnp.int32(0)
         for q in range(p):
             seen = seen + (placement[q] == placement[p]).astype(jnp.int32)
@@ -172,7 +170,7 @@
     tok_count, width = tokens.shape
     capacity = tok_count * expert_ids.shape[1] // slot_count
     slots = slot_count * capacity
-    offsets = [*range(slot_count // 2, slot_count), *range(1, slot_count // 2), 0]
+    offsets = range(slot_count - 1, -1, -1)
     bf16 = jnp.bfloat16
     chunk = jax.ShapeDtypeStruct((capacity, width), bf16)
     half = jax.ShapeDtypeStruct((slots // 2, width), bf16)

time: 43.7 us -> 42.5 us (0.973)
  waiting for transfers between devices: 11 us -> 9.78 us
    ppermute x18, waiting for transfers between devices: 11 us -> 9.78 us  [swap(): lax.ppermute(value, 'expert', [(e, e ^ offset) for e in range(n_devices)])]
  transfers between devices with their start and end apart: 18 -> 18, of which waited for: 8 -> 10; matrix products, arithmetic and copies ran while one was open for 0% -> 0% of each run, Pallas kernels for 15% -> 15%
where the time goes in v15:
time: 42.5 us; the launch traced here: 42.4 us
  starting transfers between devices  24 us (56%)
  waiting for transfers between devices  9.78 us (23%)
  Pallas kernels  8.52 us (20%)
    ppermute x18, starting transfers between devices, swap(): lax.ppermute(value, 'expert', [(e, e ^ offset) for e in range(n_devices)])  24 us
    ppermute x18, waiting for transfers between devices, swap(): lax.ppermute(value, 'expert', [(e, e ^ offset) for e in range(n_devices)])  9.78 us
    pallas_call x14, Pallas kernels, call(): pl.pallas_call(kernel, out_shape=outs, in_specs=in_specs, out_specs=jax.t...  8.52 us
  transfers between devices with their start and end apart: 18, of which 10 were waited for; matrix products, arithmetic and copies ran while one was open for 0% of the time, Pallas kernels for 15%

profile of v15, /device:TPU:0, one launch (start us, length us, event | category | flops | bytes accessed | tf_op | source)
XLA Modules:
  0.0 42.4 jit_solution(3435077865656489012)
XLA Ops:
  0.0 1.2 %shard_map.73 = (bf16[8,3584]{1,0:T(8,128)(2,1)S(1)}, bf16[8,3584]{1,0:T(8,128)(2,1)S(1)}, bf16[8,3584]{1,0:T(8,128)(2,1)S(1)}, bf16[8,3584]{1,0:T(8,128)(2,1)S(1)}, f32[32,16]{1,0:T(8,128)S(1)}) custom-call(s32[4]{0:T(128)} %refs_0_.3, s32[2,16]{1,0:T(2,128)} %bitcast.3, s32[2,16]{1,0:T(2,128)} %bitcast.4, f32[2,16]{1,0:T(2,128)} %bitcast.5, ...), custom_call_target="tpu_custom_call" | custom-call | tf_op jit(solution)/shard_map/pallas_call | solution.py:153
  1.2 5.1 %collective-permute-start = (bf16[8,3584]{1,0:T(8,128)(2,1)S(1)}, bf16[8,3584]{1,0:T(8,128)(2,1)S(1)}, u32[]{:S(2)}, u32[]{:S(2)}) collective-permute-start(bf16[8,3584]{1,0:T(8,128)(2,1)S(1)} %get-tuple-element.27), channel_id=1, source_target_pairs={{0,24},{2,26},{4,28},{6,30},{8,16},{10,18},{12,20},{14,22},{16,8},... | collective-permute-start | bytes 172040 | tf_op jit(solution)/shard_map/ppermute | solution.py:179
  6.3 0.6 %collective-permute-start.10 = (bf16[8,3584]{1,0:T(8,128)(2,1)S(1)}, bf16[8,3584]{1,0:T(8,128)(2,1)S(1)}, u32[]{:S(2)}, u32[]{:S(2)}) collective-permute-start(bf16[8,3584]{1,0:T(8,128)(2,1)S(1)} %get-tuple-element.35), channel_id=1, source_target_pairs={{0,8},{2,10},{4,12},{6,14},{8,0},{10,2},{12,4},{14,6},{16,24},{18,... | collective-permute-start | bytes 172040 | tf_op jit(solution)/shard_map/ppermute | solution.py:179
  7.1 2.1 %shard_map.75.refs_2_.refs_4_ = bf16[2,3584,256]{2,1,0:T(8,128)(2,1)S(1)} custom-call(bf16[2,3584,256]{2,1,0:T(8,128)(2,1)} %refs_0_.4, bf16[48,16]{1,0:T(8,128)(2,1)S(1)} %get-tuple-element.26.refs_1_.terms), custom_call_target="tpu_custom_call" | custom-call | bytes 3670016 | tf_op jit(solution)/shard_map/pallas_call | solution.py:153
  9.2 2.2 %collective-permute-done.1.refs_1_ = bf16[8,3584]{1,0:T(8,128)(2,1)S(1)} collective-permute-done((bf16[8,3584]{1,0:T(8,128)(2,1)S(1)}, bf16[8,3584]{1,0:T(8,128)(2,1)S(1)}, u32[]{:S(2)}, u32[]{:S(2)}) %collective-permute-start.1) | collective-permute-done | bytes 57376 | tf_op jit(solution)/shard_map/ppermute | solution.py:179
  11.4 1.6 %collective-permute-start.2 = (bf16[16,3584]{1,0:T(8,128)(2,1)S(1)}, bf16[16,3584]{1,0:T(8,128)(2,1)S(1)}, u32[]{:S(2)}, u32[]{:S(2)}) collective-permute-start(bf16[16,3584]{1,0:T(8,128)(2,1)S(1)} %shard_map.76.refs_0_), channel_id=1, source_target_pairs={{0,2},{2,0},{4,6},{6,4},{8,10},{10,8},{12,14},{14,12},{16,18},{18,... | collective-permute-start | bytes 344072 | tf_op jit(solution)/shard_map/ppermute | solution.py:179
  13.0 1.6 %collective-permute-start.11 = (bf16[16,3584]{1,0:T(8,128)(2,1)S(1)}, bf16[16,3584]{1,0:T(8,128)(2,1)S(1)}, u32[]{:S(2)}, u32[]{:S(2)}) collective-permute-start(bf16[16,3584]{1,0:T(8,128)(2,1)S(1)} %shard_map.82.refs_0_), channel_id=1, source_target_pairs={{0,4},{2,6},{4,0},{6,2},{8,12},{10,14},{12,8},{14,10},{16,20},{18,... | collective-permute-start | bytes 344072 | tf_op jit(solution)/shard_map/ppermute | solution.py:179
  14.6 0.5 %collective-permute-start.3 = (bf16[16,3584]{1,0:T(8,128)(2,1)S(1)}, bf16[16,3584]{1,0:T(8,128)(2,1)S(1)}, u32[]{:S(2)}, u32[]{:S(2)}) collective-permute-start(bf16[16,3584]{1,0:T(8,128)(2,1)S(1)} %shard_map.76.refs_0_), channel_id=1, source_target_pairs={{0,4},{2,6},{4,0},{6,2},{8,12},{10,14},{12,8},{14,10},{16,20},{18,... | collective-permute-start | bytes 344072 | tf_op jit(solution)/shard_map/ppermute | solution.py:179
  15.1 1.2 %collective-permute-done.2.refs_1_ = bf16[16,3584]{1,0:T(8,128)(2,1)S(1)} collective-permute-done((bf16[16,3584]{1,0:T(8,128)(2,1)S(1)}, bf16[16,3584]{1,0:T(8,128)(2,1)S(1)}, u32[]{:S(2)}, u32[]{:S(2)}) %collective-permute-start.2) | collective-permute-done | bytes 114720 | tf_op jit(solution)/shard_map/ppermute | solution.py:179
  16.2 1.5 %collective-permute-start.4 = (bf16[16,3584]{1,0:T(8,128)(2,1)S(1)}, bf16[16,3584]{1,0:T(8,128)(2,1)S(1)}, u32[]{:S(2)}, u32[]{:S(2)}) collective-permute-start(bf16[16,3584]{1,0:T(8,128)(2,1)S(1)} %collective-permute-done.2.refs_1_), channel_id=1, source_target_pairs={{0,4},{2,6},{4,0},{6,2},{8,12},{10,14},{12,8},{14,10},{16,20},{18,... | collective-permute-start | bytes 344072 | tf_op jit(solution)/shard_map/ppermute | solution.py:179
  17.8 1.5 %collective-permute-start.12 = (bf16[16,3584]{1,0:T(8,128)(2,1)S(1)}, bf16[16,3584]{1,0:T(8,128)(2,1)S(1)}, u32[]{:S(2)}, u32[]{:S(2)}) collective-permute-start(bf16[16,3584]{1,0:T(8,128)(2,1)S(1)} %shard_map.82.refs_0_), channel_id=1, source_target_pairs={{0,2},{2,0},{4,6},{6,4},{8,10},{10,8},{12,14},{14,12},{16,18},{18,... | collective-permute-start | bytes 344072 | tf_op jit(solution)/shard_map/ppermute | solution.py:179
  19.3 0.5 %collective-permute-start.13 = (bf16[16,3584]{1,0:T(8,128)(2,1)S(1)}, bf16[16,3584]{1,0:T(8,128)(2,1)S(1)}, u32[]{:S(2)}, u32[]{:S(2)}) collective-permute-start(bf16[16,3584]{1,0:T(8,128)(2,1)S(1)} %collective-permute-done.11.refs_1_), channel_id=1, source_target_pairs={{0,2},{2,0},{4,6},{6,4},{8,10},{10,8},{12,14},{14,12},{16,18},{18,... | collective-permute-start | bytes 344072 | tf_op jit(solution)/shard_map/ppermute | solution.py:179
  19.8 1.5 %shard_map.77.refs_5_ = bf16[256,3584]{1,0:T(8,128)(2,1)S(1)} custom-call(bf16[256,3584]{1,0:T(8,128)(2,1)} %refs_0_.5, bf16[48,16]{1,0:T(8,128)(2,1)S(1)} %get-tuple-element.25.refs_1_.terms), custom_call_target="tpu_custom_call" | custom-call | bytes 1835008 | tf_op jit(solution)/shard_map/pallas_call | solution.py:153
  21.3 0.6 %collective-permute-done.4.refs_3_ = bf16[16,3584]{1,0:T(8,128)(2,1)S(1)} collective-permute-done((bf16[16,3584]{1,0:T(8,128)(2,1)S(1)}, bf16[16,3584]{1,0:T(8,128)(2,1)S(1)}, u32[]{:S(2)}, u32[]{:S(2)}) %collective-permute-start.4) | collective-permute-done | bytes 114720 | tf_op jit(solution)/shard_map/ppermute | solution.py:179
  22.0 1.2 %shard_map.78 = (bf16[16,3584]{1,0:T(8,128)(2,1)S(1)}, bf16[16,3584]{1,0:T(8,128)(2,1)S(1)}, bf16[16,3584]{1,0:T(8,128)(2,1)S(1)}, bf16[16,3584]{1,0:T(8,128)(2,1)S(1)}) custom-call(bf16[16,3584]{1,0:T(8,128)(2,1)S(1)} %shard_map.76.refs_0_, bf16[16,3584]{1,0:T(8,128)(2,1)S(1)} %collective-permute-done.2.refs_1_, ...), custom_call_target="tpu_custom_call" | custom-call | tf_op jit(solution)/shard_map/pallas_call | solution.py:153
  23.1 0.9 %collective-permute-start.6 = (bf16[16,3584]{1,0:T(8,128)(2,1)S(1)}, bf16[16,3584]{1,0:T(8,128)(2,1)S(1)}, u32[]{:S(2)}, u32[]{:S(2)}) collective-permute-start(bf16[16,3584]{1,0:T(8,128)(2,1)S(1)} %get-tuple-element.32), channel_id=1, source_target_pairs={{0,2},{2,0},{4,6},{6,4},{8,10},{10,8},{12,14},{14,12},{16,18},{18,... | collective-permute-start | bytes 344072 | tf_op jit(solution)/shard_map/ppermute | solution.py:179
  24.0 0.2 collective-permute-done.13.refs_3_
  24.3 1.2 %shard_map.83 = (bf16[16,3584]{1,0:T(8,128)(2,1)S(1)}, bf16[16,3584]{1,0:T(8,128)(2,1)S(1)}, bf16[16,3584]{1,0:T(8,128)(2,1)S(1)}, bf16[16,3584]{1,0:T(8,128)(2,1)S(1)}) custom-call(bf16[16,3584]{1,0:T(8,128)(2,1)S(1)} %shard_map.82.refs_0_, bf16[16,3584]{1,0:T(8,128)(2,1)S(1)} %collective-permute-done.11.refs_1_, ...), custom_call_target="tpu_custom_call" | custom-call | tf_op jit(solution)/shard_map/pallas_call | solution.py:153
  25.4 1.4 %collective-permute-start.15 = (bf16[16,3584]{1,0:T(8,128)(2,1)S(1)}, bf16[16,3584]{1,0:T(8,128)(2,1)S(1)}, u32[]{:S(2)}, u32[]{:S(2)}) collective-permute-start(bf16[16,3584]{1,0:T(8,128)(2,1)S(1)} %get-tuple-element.40), channel_id=1, source_target_pairs={{0,4},{2,6},{4,0},{6,2},{8,12},{10,14},{12,8},{14,10},{16,20},{18,... | collective-permute-start | bytes 344072 | tf_op jit(solution)/shard_map/ppermute | solution.py:179
  26.8 1.1 %collective-permute-start.5 = (bf16[16,3584]{1,0:T(8,128)(2,1)S(1)}, bf16[16,3584]{1,0:T(8,128)(2,1)S(1)}, u32[]{:S(2)}, u32[]{:S(2)}) collective-permute-start(bf16[16,3584]{1,0:T(8,128)(2,1)S(1)} %get-tuple-element.30), channel_id=1, source_target_pairs={{0,2},{2,0},{4,6},{6,4},{8,10},{10,8},{12,14},{14,12},{16,18},{18,... | collective-permute-start | bytes 344072 | tf_op jit(solution)/shard_map/ppermute | solution.py:179
  27.9 1.0 %collective-permute-done.6.refs_1_ = bf16[16,3584]{1,0:T(8,128)(2,1)S(1)} collective-permute-done((bf16[16,3584]{1,0:T(8,128)(2,1)S(1)}, bf16[16,3584]{1,0:T(8,128)(2,1)S(1)}, u32[]{:S(2)}, u32[]{:S(2)}) %collective-permute-start.6) | collective-permute-done | bytes 114720 | tf_op jit(solution)/shard_map/ppermute | solution.py:179
  28.9 1.1 %collective-permute-start.7 = (bf16[16,3584]{1,0:T(8,128)(2,1)S(1)}, bf16[16,3584]{1,0:T(8,128)(2,1)S(1)}, u32[]{:S(2)}, u32[]{:S(2)}) collective-permute-start(bf16[16,3584]{1,0:T(8,128)(2,1)S(1)} %shard_map.79), channel_id=1, source_target_pairs={{0,4},{2,6},{4,0},{6,2},{8,12},{10,14},{12,8},{14,10},{16,20},{18,... | collective-permute-start | bytes 344072 | tf_op jit(solution)/shard_map/ppermute | solution.py:179
  30.1 0.9 %collective-permute-start.14 = (bf16[16,3584]{1,0:T(8,128)(2,1)S(1)}, bf16[16,3584]{1,0:T(8,128)(2,1)S(1)}, u32[]{:S(2)}, u32[]{:S(2)}) collective-permute-start(bf16[16,3584]{1,0:T(8,128)(2,1)S(1)} %get-tuple-element.38), channel_id=1, source_target_pairs={{0,4},{2,6},{4,0},{6,2},{8,12},{10,14},{12,8},{14,10},{16,20},{18,... | collective-permute-start | bytes 344072 | tf_op jit(solution)/shard_map/ppermute | solution.py:179
  31.0 0.5 %collective-permute-done.15.refs_1_ = bf16[16,3584]{1,0:T(8,128)(2,1)S(1)} collective-permute-done((bf16[16,3584]{1,0:T(8,128)(2,1)S(1)}, bf16[16,3584]{1,0:T(8,128)(2,1)S(1)}, u32[]{:S(2)}, u32[]{:S(2)}) %collective-permute-start.15) | collective-permute-done | bytes 114720 | tf_op jit(solution)/shard_map/ppermute | solution.py:179
  31.5 1.3 %collective-permute-start.16 = (bf16[16,3584]{1,0:T(8,128)(2,1)S(1)}, bf16[16,3584]{1,0:T(8,128)(2,1)S(1)}, u32[]{:S(2)}, u32[]{:S(2)}) collective-permute-start(bf16[16,3584]{1,0:T(8,128)(2,1)S(1)} %shard_map.84), channel_id=1, source_target_pairs={{0,2},{2,0},{4,6},{6,4},{8,10},{10,8},{12,14},{14,12},{16,18},{18,... | collective-permute-start | bytes 344072 | tf_op jit(solution)/shard_map/ppermute | solution.py:179
  32.8 1.0 %collective-permute-done.7.refs_2_ = bf16[16,3584]{1,0:T(8,128)(2,1)S(1)} collective-permute-done((bf16[16,3584]{1,0:T(8,128)(2,1)S(1)}, bf16[16,3584]{1,0:T(8,128)(2,1)S(1)}, u32[]{:S(2)}, u32[]{:S(2)}) %collective-permute-start.7) | collective-permute-done | bytes 114720 | tf_op jit(solution)/shard_map/ppermute | solution.py:179
  33.9 2.2 %collective-permute-start.8 = (bf16[8,3584]{1,0:T(8,128)(2,1)S(1)}, bf16[8,3584]{1,0:T(8,128)(2,1)S(1)}, u32[]{:S(2)}, u32[]{:S(2)}) collective-permute-start(bf16[8,3584]{1,0:T(8,128)(2,1)S(1)} %get-tuple-element.33), channel_id=1, source_target_pairs={{0,24},{2,26},{4,28},{6,30},{8,16},{10,18},{12,20},{14,22},{16,8},... | collective-permute-start | bytes 172040 | tf_op jit(solution)/shard_map/ppermute | solution.py:179
  36.1 0.3 collective-permute-done.16.refs_2_
  36.4 2.0 %collective-permute-start.17 = (bf16[8,3584]{1,0:T(8,128)(2,1)S(1)}, bf16[8,3584]{1,0:T(8,128)(2,1)S(1)}, u32[]{:S(2)}, u32[]{:S(2)}) collective-permute-start(bf16[8,3584]{1,0:T(8,128)(2,1)S(1)} %get-tuple-element.41), channel_id=1, source_target_pairs={{0,8},{2,10},{4,12},{6,14},{8,0},{10,2},{12,4},{14,6},{16,24},{18,... | collective-permute-start | bytes 172040 | tf_op jit(solution)/shard_map/ppermute | solution.py:179
  38.4 1.5 %collective-permute-done.8.refs_0_ = bf16[8,3584]{1,0:T(8,128)(2,1)S(1)} collective-permute-done((bf16[8,3584]{1,0:T(8,128)(2,1)S(1)}, bf16[8,3584]{1,0:T(8,128)(2,1)S(1)}, u32[]{:S(2)}, u32[]{:S(2)}) %collective-permute-start.8) | collective-permute-done | bytes 57376 | tf_op jit(solution)/shard_map/ppermute | solution.py:179
  39.9 1.3 %collective-permute-done.9.refs_1_ = bf16[8,3584]{1,0:T(8,128)(2,1)S(1)} collective-permute-done((bf16[8,3584]{1,0:T(8,128)(2,1)S(1)}, bf16[8,3584]{1,0:T(8,128)(2,1)S(1)}, u32[]{:S(2)}, u32[]{:S(2)}) %collective-permute-start.9) | collective-permute-done | bytes 57376 | tf_op jit(solution)/shard_map/ppermute | solution.py:179
  41.5 0.9 %shard_map.86 = bf16[16,3584]{1,0:T(8,128)(2,1)} custom-call(bf16[48,16]{1,0:T(8,128)(2,1)S(1)} %get-tuple-element.25.refs_1_.terms, f32[16,3584]{1,0:T(8,128)S(1)} %shard_map.81.near, bf16[8,3584]{1,0:T(8,128)(2,1)S(1)} %collective-permute-done.17.refs_0_, bf16[8,3584]{1,0:T(8,128)(2,1)S(1)} %get-tuple-element.42.refs_1_), custom_call_target="tpu_custom_call" | custom-call | tf_op jit(solution)/shard_map/pallas_call | solution.py:153
  (18 shorter events, 0.6 us)
Async XLA Ops:
  1.2 8.0 %collective-permute-start = (bf16[8,3584]{1,0:T(8,128)(2,1)S(1)}, bf16[8,3584]{1,0:T(8,128)(2,1)S(1)}, u32[]{:S(2)}, u32[]{:S(2)}) collective-permute-start(bf16[8,3584]{1,0:T(8,128)(2,1)S(1)} %get-tuple-element.27), channel_id=1, source_target_pairs={{0,24},{2,26},{4,28},{6,30},{8,16},{10,18},{12,20},{14,22},{16,8},... | collective-permute-start | bytes 172040 | tf_op jit(solution)/shard_map/ppermute | solution.py:179
  6.3 5.1 %collective-permute-start.1 = (bf16[8,3584]{1,0:T(8,128)(2,1)S(1)}, bf16[8,3584]{1,0:T(8,128)(2,1)S(1)}, u32[]{:S(2)}, u32[]{:S(2)}) collective-permute-start(bf16[8,3584]{1,0:T(8,128)(2,1)S(1)} %get-tuple-element.28), channel_id=1, source_target_pairs={{0,16},{2,18},{4,20},{6,22},{8,24},{10,26},{12,28},{14,30},{16,0},... | collective-permute-start | bytes 172040 | tf_op jit(solution)/shard_map/ppermute | solution.py:179
  6.3 6.7 %collective-permute-start.10 = (bf16[8,3584]{1,0:T(8,128)(2,1)S(1)}, bf16[8,3584]{1,0:T(8,128)(2,1)S(1)}, u32[]{:S(2)}, u32[]{:S(2)}) collective-permute-start(bf16[8,3584]{1,0:T(8,128)(2,1)S(1)} %get-tuple-element.35), channel_id=1, source_target_pairs={{0,8},{2,10},{4,12},{6,14},{8,0},{10,2},{12,4},{14,6},{16,24},{18,... | collective-permute-start | bytes 172040 | tf_op jit(solution)/shard_map/ppermute | solution.py:179
  11.4 4.9 %collective-permute-start.2 = (bf16[16,3584]{1,0:T(8,128)(2,1)S(1)}, bf16[16,3584]{1,0:T(8,128)(2,1)S(1)}, u32[]{:S(2)}, u32[]{:S(2)}) collective-permute-start(bf16[16,3584]{1,0:T(8,128)(2,1)S(1)} %shard_map.76.refs_0_), channel_id=1, source_target_pairs={{0,2},{2,0},{4,6},{6,4},{8,10},{10,8},{12,14},{14,12},{16,18},{18,... | collective-permute-start | bytes 344072 | tf_op jit(solution)/shard_map/ppermute | solution.py:179
  13.0 6.3 %collective-permute-start.11 = (bf16[16,3584]{1,0:T(8,128)(2,1)S(1)}, bf16[16,3584]{1,0:T(8,128)(2,1)S(1)}, u32[]{:S(2)}, u32[]{:S(2)}) collective-permute-start(bf16[16,3584]{1,0:T(8,128)(2,1)S(1)} %shard_map.82.refs_0_), channel_id=1, source_target_pairs={{0,4},{2,6},{4,0},{6,2},{8,12},{10,14},{12,8},{14,10},{16,20},{18,... | collective-permute-start | bytes 344072 | tf_op jit(solution)/shard_map/ppermute | solution.py:179
  14.6 6.7 %collective-permute-start.3 = (bf16[16,3584]{1,0:T(8,128)(2,1)S(1)}, bf16[16,3584]{1,0:T(8,128)(2,1)S(1)}, u32[]{:S(2)}, u32[]{:S(2)}) collective-permute-start(bf16[16,3584]{1,0:T(8,128)(2,1)S(1)} %shard_map.76.refs_0_), channel_id=1, source_target_pairs={{0,4},{2,6},{4,0},{6,2},{8,12},{10,14},{12,8},{14,10},{16,20},{18,... | collective-permute-start | bytes 344072 | tf_op jit(solution)/shard_map/ppermute | solution.py:179
  16.2 5.7 %collective-permute-start.4 = (bf16[16,3584]{1,0:T(8,128)(2,1)S(1)}, bf16[16,3584]{1,0:T(8,128)(2,1)S(1)}, u32[]{:S(2)}, u32[]{:S(2)}) collective-permute-start(bf16[16,3584]{1,0:T(8,128)(2,1)S(1)} %collective-permute-done.2.refs_1_), channel_id=1, source_target_pairs={{0,4},{2,6},{4,0},{6,2},{8,12},{10,14},{12,8},{14,10},{16,20},{18,... | collective-permute-start | bytes 344072 | tf_op jit(solution)/shard_map/ppermute | solution.py:179
  17.8 6.3 %collective-permute-start.12 = (bf16[16,3584]{1,0:T(8,128)(2,1)S(1)}, bf16[16,3584]{1,0:T(8,128)(2,1)S(1)}, u32[]{:S(2)}, u32[]{:S(2)}) collective-permute-start(bf16[16,3584]{1,0:T(8,128)(2,1)S(1)} %shard_map.82.refs_0_), channel_id=1, source_target_pairs={{0,2},{2,0},{4,6},{6,4},{8,10},{10,8},{12,14},{14,12},{16,18},{18,... | collective-permute-start | bytes 344072 | tf_op jit(solution)/shard_map/ppermute | solution.py:179
  19.3 5.0 %collective-permute-start.13 = (bf16[16,3584]{1,0:T(8,128)(2,1)S(1)}, bf16[16,3584]{1,0:T(8,128)(2,1)S(1)}, u32[]{:S(2)}, u32[]{:S(2)}) collective-permute-start(bf16[16,3584]{1,0:T(8,128)(2,1)S(1)} %collective-permute-done.11.refs_1_), channel_id=1, source_target_pairs={{0,2},{2,0},{4,6},{6,4},{8,10},{10,8},{12,14},{14,12},{16,18},{18,... | collective-permute-start | bytes 344072 | tf_op jit(solution)/shard_map/ppermute | solution.py:179
  23.1 5.8 %collective-permute-start.6 = (bf16[16,3584]{1,0:T(8,128)(2,1)S(1)}, bf16[16,3584]{1,0:T(8,128)(2,1)S(1)}, u32[]{:S(2)}, u32[]{:S(2)}) collective-permute-start(bf16[16,3584]{1,0:T(8,128)(2,1)S(1)} %get-tuple-element.32), channel_id=1, source_target_pairs={{0,2},{2,0},{4,6},{6,4},{8,10},{10,8},{12,14},{14,12},{16,18},{18,... | collective-permute-start | bytes 344072 | tf_op jit(solution)/shard_map/ppermute | solution.py:179
  25.4 6.1 %collective-permute-start.15 = (bf16[16,3584]{1,0:T(8,128)(2,1)S(1)}, bf16[16,3584]{1,0:T(8,128)(2,1)S(1)}, u32[]{:S(2)}, u32[]{:S(2)}) collective-permute-start(bf16[16,3584]{1,0:T(8,128)(2,1)S(1)} %get-tuple-element.40), channel_id=1, source_target_pairs={{0,4},{2,6},{4,0},{6,2},{8,12},{10,14},{12,8},{14,10},{16,20},{18,... | collective-permute-start | bytes 344072 | tf_op jit(solution)/shard_map/ppermute | solution.py:179
  26.8 6.0 %collective-permute-start.5 = (bf16[16,3584]{1,0:T(8,128)(2,1)S(1)}, bf16[16,3584]{1,0:T(8,128)(2,1)S(1)}, u32[]{:S(2)}, u32[]{:S(2)}) collective-permute-start(bf16[16,3584]{1,0:T(8,128)(2,1)S(1)} %get-tuple-element.30), channel_id=1, source_target_pairs={{0,2},{2,0},{4,6},{6,4},{8,10},{10,8},{12,14},{14,12},{16,18},{18,... | collective-permute-start | bytes 344072 | tf_op jit(solution)/shard_map/ppermute | solution.py:179
  28.9 4.9 %collective-permute-start.7 = (bf16[16,3584]{1,0:T(8,128)(2,1)S(1)}, bf16[16,3584]{1,0:T(8,128)(2,1)S(1)}, u32[]{:S(2)}, u32[]{:S(2)}) collective-permute-start(bf16[16,3584]{1,0:T(8,128)(2,1)S(1)} %shard_map.79), channel_id=1, source_target_pairs={{0,4},{2,6},{4,0},{6,2},{8,12},{10,14},{12,8},{14,10},{16,20},{18,... | collective-permute-start | bytes 344072 | tf_op jit(solution)/shard_map/ppermute | solution.py:179
  30.1 6.0 %collective-permute-start.14 = (bf16[16,3584]{1,0:T(8,128)(2,1)S(1)}, bf16[16,3584]{1,0:T(8,128)(2,1)S(1)}, u32[]{:S(2)}, u32[]{:S(2)}) collective-permute-start(bf16[16,3584]{1,0:T(8,128)(2,1)S(1)} %get-tuple-element.38), channel_id=1, source_target_pairs={{0,4},{2,6},{4,0},{6,2},{8,12},{10,14},{12,8},{14,10},{16,20},{18,... | collective-permute-start | bytes 344072 | tf_op jit(solution)/shard_map/ppermute | solution.py:179
  31.5 4.9 %collective-permute-start.16 = (bf16[16,3584]{1,0:T(8,128)(2,1)S(1)}, bf16[16,3584]{1,0:T(8,128)(2,1)S(1)}, u32[]{:S(2)}, u32[]{:S(2)}) collective-permute-start(bf16[16,3584]{1,0:T(8,128)(2,1)S(1)} %shard_map.84), channel_id=1, source_target_pairs={{0,2},{2,0},{4,6},{6,4},{8,10},{10,8},{12,14},{14,12},{16,18},{18,... | collective-permute-start | bytes 344072 | tf_op jit(solution)/shard_map/ppermute | solution.py:179
  33.9 6.0 %collective-permute-start.8 = (bf16[8,3584]{1,0:T(8,128)(2,1)S(1)}, bf16[8,3584]{1,0:T(8,128)(2,1)S(1)}, u32[]{:S(2)}, u32[]{:S(2)}) collective-permute-start(bf16[8,3584]{1,0:T(8,128)(2,1)S(1)} %get-tuple-element.33), channel_id=1, source_target_pairs={{0,24},{2,26},{4,28},{6,30},{8,16},{10,18},{12,20},{14,22},{16,8},... | collective-permute-start | bytes 172040 | tf_op jit(solution)/shard_map/ppermute | solution.py:179
  36.0 5.2 %collective-permute-start.9 = (bf16[8,3584]{1,0:T(8,128)(2,1)S(1)}, bf16[8,3584]{1,0:T(8,128)(2,1)S(1)}, u32[]{:S(2)}, u32[]{:S(2)}) collective-permute-start(bf16[8,3584]{1,0:T(8,128)(2,1)S(1)} %get-tuple-element.34), channel_id=1, source_target_pairs={{0,16},{2,18},{4,20},{6,22},{8,24},{10,26},{12,28},{14,30},{16,0},... | collective-permute-start | bytes 172040 | tf_op jit(solution)/shard_map/ppermute | solution.py:179
  36.4 5.0 %collective-permute-start.17 = (bf16[8,3584]{1,0:T(8,128)(2,1)S(1)}, bf16[8,3584]{1,0:T(8,128)(2,1)S(1)}, u32[]{:S(2)}, u32[]{:S(2)}) collective-permute-start(bf16[8,3584]{1,0:T(8,128)(2,1)S(1)} %get-tuple-element.41), channel_id=1, source_target_pairs={{0,8},{2,10},{4,12},{6,14},{8,0},{10,2},{12,4},{14,6},{16,24},{18,... | collective-permute-start | bytes 172040 | tf_op jit(solution)/shard_map/ppermute | solution.py:179

commit v16 on v15

--- a/solution.py
+++ b/solution.py
@@ -237,10 +237,10 @@
         )
         if square:
             mine, first, second, cross = result
-            cross = swap(cross, a)
-            first = swap(first, a)
-            second = local(functools.partial(sum_kernel, 2), [second, cross], [half])[0]
-            result = [mine, first, swap(second, b)]
+            cross = swap(cross, b)
+            second = swap(second, b)
+            first = local(functools.partial(sum_kernel, 2), [first, cross], [half])[0]
+            result = [mine, second, swap(first, a)]
         else:
             result = [swap(v, q) if q else v for q, v in enumerate(result)]
         summed += local(functools.partial(sum_kernel, len(result)), result, [chunk] * count)

time: 42.5 us -> 42.5 us (level)
  transfers between devices with their start and end apart: 18 -> 18, of which waited for: 10 -> 9; matrix products, arithmetic and copies ran while one was open for 0% -> 0% of each run, Pallas kernels for 15% -> 15%
where the time goes in v16:
time: 42.5 us; the launch traced here: 42.3 us
  starting transfers between devices  24 us (56%)
  waiting for transfers between devices  9.76 us (23%)
  Pallas kernels  8.53 us (20%)
    ppermute x18, starting transfers between devices, swap(): lax.ppermute(value, 'expert', [(e, e ^ offset) for e in range(n_devices)])  24 us
    ppermute x18, waiting for transfers between devices, swap(): lax.ppermute(value, 'expert', [(e, e ^ offset) for e in range(n_devices)])  9.76 us
    pallas_call x14, Pallas kernels, call(): pl.pallas_call(kernel, out_shape=outs, in_specs=in_specs, out_specs=jax.t...  8.53 us
  transfers between devices with their start and end apart: 18, of which 9 were waited for; matrix products, arithmetic and copies ran while one was open for 0% of the time, Pallas kernels for 15%

profile of v16, /device:TPU:0, one launch (start us, length us, event | category | flops | bytes accessed | tf_op | source)
XLA Modules:
  0.0 42.3 jit_solution(8066264026305695834)
XLA Ops:
  0.0 1.2 %shard_map.73 = (bf16[8,3584]{1,0:T(8,128)(2,1)S(1)}, bf16[8,3584]{1,0:T(8,128)(2,1)S(1)}, bf16[8,3584]{1,0:T(8,128)(2,1)S(1)}, bf16[8,3584]{1,0:T(8,128)(2,1)S(1)}, f32[32,16]{1,0:T(8,128)S(1)}) custom-call(s32[4]{0:T(128)} %refs_0_.3, s32[2,16]{1,0:T(2,128)} %bitcast.3, s32[2,16]{1,0:T(2,128)} %bitcast.4, f32[2,16]{1,0:T(2,128)} %bitcast.5, ...), custom_call_target="tpu_custom_call" | custom-call | tf_op jit(solution)/shard_map/pallas_call | solution.py:153
  1.2 5.1 %collective-permute-start = (bf16[8,3584]{1,0:T(8,128)(2,1)S(1)}, bf16[8,3584]{1,0:T(8,128)(2,1)S(1)}, u32[]{:S(2)}, u32[]{:S(2)}) collective-permute-start(bf16[8,3584]{1,0:T(8,128)(2,1)S(1)} %get-tuple-element.27), channel_id=1, source_target_pairs={{0,24},{2,26},{4,28},{6,30},{8,16},{10,18},{12,20},{14,22},{16,8},... | collective-permute-start | bytes 172040 | tf_op jit(solution)/shard_map/ppermute | solution.py:179
  6.3 0.6 %collective-permute-start.10 = (bf16[8,3584]{1,0:T(8,128)(2,1)S(1)}, bf16[8,3584]{1,0:T(8,128)(2,1)S(1)}, u32[]{:S(2)}, u32[]{:S(2)}) collective-permute-start(bf16[8,3584]{1,0:T(8,128)(2,1)S(1)} %get-tuple-element.35), channel_id=1, source_target_pairs={{0,8},{2,10},{4,12},{6,14},{8,0},{10,2},{12,4},{14,6},{16,24},{18,... | collective-permute-start | bytes 172040 | tf_op jit(solution)/shard_map/ppermute | solution.py:179
  6.9 0.2 shard_map.74
  7.1 2.1 %shard_map.75.refs_2_.refs_4_ = bf16[2,3584,256]{2,1,0:T(8,128)(2,1)S(1)} custom-call(bf16[2,3584,256]{2,1,0:T(8,128)(2,1)} %refs_0_.4, bf16[48,16]{1,0:T(8,128)(2,1)S(1)} %get-tuple-element.26.refs_1_.terms), custom_call_target="tpu_custom_call" | custom-call | bytes 3670016 | tf_op jit(solution)/shard_map/pallas_call | solution.py:153
  9.2 2.2 %collective-permute-done.1.refs_1_ = bf16[8,3584]{1,0:T(8,128)(2,1)S(1)} collective-permute-done((bf16[8,3584]{1,0:T(8,128)(2,1)S(1)}, bf16[8,3584]{1,0:T(8,128)(2,1)S(1)}, u32[]{:S(2)}, u32[]{:S(2)}) %collective-permute-start.1) | collective-permute-done | bytes 57376 | tf_op jit(solution)/shard_map/ppermute | solution.py:179
  11.4 1.6 %collective-permute-start.2 = (bf16[16,3584]{1,0:T(8,128)(2,1)S(1)}, bf16[16,3584]{1,0:T(8,128)(2,1)S(1)}, u32[]{:S(2)}, u32[]{:S(2)}) collective-permute-start(bf16[16,3584]{1,0:T(8,128)(2,1)S(1)} %shard_map.76.refs_0_), channel_id=1, source_target_pairs={{0,2},{2,0},{4,6},{6,4},{8,10},{10,8},{12,14},{14,12},{16,18},{18,... | collective-permute-start | bytes 344072 | tf_op jit(solution)/shard_map/ppermute | solution.py:179
  13.0 1.6 %collective-permute-start.11 = (bf16[16,3584]{1,0:T(8,128)(2,1)S(1)}, bf16[16,3584]{1,0:T(8,128)(2,1)S(1)}, u32[]{:S(2)}, u32[]{:S(2)}) collective-permute-start(bf16[16,3584]{1,0:T(8,128)(2,1)S(1)} %shard_map.82.refs_0_), channel_id=1, source_target_pairs={{0,4},{2,6},{4,0},{6,2},{8,12},{10,14},{12,8},{14,10},{16,20},{18,... | collective-permute-start | bytes 344072 | tf_op jit(solution)/shard_map/ppermute | solution.py:179
  14.6 0.5 %collective-permute-start.3 = (bf16[16,3584]{1,0:T(8,128)(2,1)S(1)}, bf16[16,3584]{1,0:T(8,128)(2,1)S(1)}, u32[]{:S(2)}, u32[]{:S(2)}) collective-permute-start(bf16[16,3584]{1,0:T(8,128)(2,1)S(1)} %shard_map.76.refs_0_), channel_id=1, source_target_pairs={{0,4},{2,6},{4,0},{6,2},{8,12},{10,14},{12,8},{14,10},{16,20},{18,... | collective-permute-start | bytes 344072 | tf_op jit(solution)/shard_map/ppermute | solution.py:179
  15.1 1.2 %collective-permute-done.2.refs_1_ = bf16[16,3584]{1,0:T(8,128)(2,1)S(1)} collective-permute-done((bf16[16,3584]{1,0:T(8,128)(2,1)S(1)}, bf16[16,3584]{1,0:T(8,128)(2,1)S(1)}, u32[]{:S(2)}, u32[]{:S(2)}) %collective-permute-start.2) | collective-permute-done | bytes 114720 | tf_op jit(solution)/shard_map/ppermute | solution.py:179
  16.2 1.5 %collective-permute-start.4 = (bf16[16,3584]{1,0:T(8,128)(2,1)S(1)}, bf16[16,3584]{1,0:T(8,128)(2,1)S(1)}, u32[]{:S(2)}, u32[]{:S(2)}) collective-permute-start(bf16[16,3584]{1,0:T(8,128)(2,1)S(1)} %collective-permute-done.2.refs_1_), channel_id=1, source_target_pairs={{0,4},{2,6},{4,0},{6,2},{8,12},{10,14},{12,8},{14,10},{16,20},{18,... | collective-permute-start | bytes 344072 | tf_op jit(solution)/shard_map/ppermute | solution.py:179
  17.8 1.5 %collective-permute-start.12 = (bf16[16,3584]{1,0:T(8,128)(2,1)S(1)}, bf16[16,3584]{1,0:T(8,128)(2,1)S(1)}, u32[]{:S(2)}, u32[]{:S(2)}) collective-permute-start(bf16[16,3584]{1,0:T(8,128)(2,1)S(1)} %shard_map.82.refs_0_), channel_id=1, source_target_pairs={{0,2},{2,0},{4,6},{6,4},{8,10},{10,8},{12,14},{14,12},{16,18},{18,... | collective-permute-start | bytes 344072 | tf_op jit(solution)/shard_map/ppermute | solution.py:179
  19.3 0.5 %collective-permute-start.13 = (bf16[16,3584]{1,0:T(8,128)(2,1)S(1)}, bf16[16,3584]{1,0:T(8,128)(2,1)S(1)}, u32[]{:S(2)}, u32[]{:S(2)}) collective-permute-start(bf16[16,3584]{1,0:T(8,128)(2,1)S(1)} %collective-permute-done.11.refs_1_), channel_id=1, source_target_pairs={{0,2},{2,0},{4,6},{6,4},{8,10},{10,8},{12,14},{14,12},{16,18},{18,... | collective-permute-start | bytes 344072 | tf_op jit(solution)/shard_map/ppermute | solution.py:179
  19.8 1.5 %shard_map.77.refs_5_ = bf16[256,3584]{1,0:T(8,128)(2,1)S(1)} custom-call(bf16[256,3584]{1,0:T(8,128)(2,1)} %refs_0_.5, bf16[48,16]{1,0:T(8,128)(2,1)S(1)} %get-tuple-element.25.refs_1_.terms), custom_call_target="tpu_custom_call" | custom-call | bytes 1835008 | tf_op jit(solution)/shard_map/pallas_call | solution.py:153
  21.3 0.6 %collective-permute-done.4.refs_3_ = bf16[16,3584]{1,0:T(8,128)(2,1)S(1)} collective-permute-done((bf16[16,3584]{1,0:T(8,128)(2,1)S(1)}, bf16[16,3584]{1,0:T(8,128)(2,1)S(1)}, u32[]{:S(2)}, u32[]{:S(2)}) %collective-permute-start.4) | collective-permute-done | bytes 114720 | tf_op jit(solution)/shard_map/ppermute | solution.py:179
  22.0 1.2 %shard_map.78 = (bf16[16,3584]{1,0:T(8,128)(2,1)S(1)}, bf16[16,3584]{1,0:T(8,128)(2,1)S(1)}, bf16[16,3584]{1,0:T(8,128)(2,1)S(1)}, bf16[16,3584]{1,0:T(8,128)(2,1)S(1)}) custom-call(bf16[16,3584]{1,0:T(8,128)(2,1)S(1)} %shard_map.76.refs_0_, bf16[16,3584]{1,0:T(8,128)(2,1)S(1)} %collective-permute-done.2.refs_1_, ...), custom_call_target="tpu_custom_call" | custom-call | tf_op jit(solution)/shard_map/pallas_call | solution.py:153
  23.1 1.6 %collective-permute-start.6 = (bf16[16,3584]{1,0:T(8,128)(2,1)S(1)}, bf16[16,3584]{1,0:T(8,128)(2,1)S(1)}, u32[]{:S(2)}, u32[]{:S(2)}) collective-permute-start(bf16[16,3584]{1,0:T(8,128)(2,1)S(1)} %get-tuple-element.32), channel_id=1, source_target_pairs={{0,4},{2,6},{4,0},{6,2},{8,12},{10,14},{12,8},{14,10},{16,20},{18,... | collective-permute-start | bytes 344072 | tf_op jit(solution)/shard_map/ppermute | solution.py:179
  24.7 1.2 %shard_map.83 = (bf16[16,3584]{1,0:T(8,128)(2,1)S(1)}, bf16[16,3584]{1,0:T(8,128)(2,1)S(1)}, bf16[16,3584]{1,0:T(8,128)(2,1)S(1)}, bf16[16,3584]{1,0:T(8,128)(2,1)S(1)}) custom-call(bf16[16,3584]{1,0:T(8,128)(2,1)S(1)} %shard_map.82.refs_0_, bf16[16,3584]{1,0:T(8,128)(2,1)S(1)} %collective-permute-done.11.refs_1_, ...), custom_call_target="tpu_custom_call" | custom-call | tf_op jit(solution)/shard_map/pallas_call | solution.py:153
  25.9 0.8 %collective-permute-start.15 = (bf16[16,3584]{1,0:T(8,128)(2,1)S(1)}, bf16[16,3584]{1,0:T(8,128)(2,1)S(1)}, u32[]{:S(2)}, u32[]{:S(2)}) collective-permute-start(bf16[16,3584]{1,0:T(8,128)(2,1)S(1)} %get-tuple-element.40), channel_id=1, source_target_pairs={{0,2},{2,0},{4,6},{6,4},{8,10},{10,8},{12,14},{14,12},{16,18},{18,... | collective-permute-start | bytes 344072 | tf_op jit(solution)/shard_map/ppermute | solution.py:179
  26.6 0.7 %collective-permute-start.5 = (bf16[16,3584]{1,0:T(8,128)(2,1)S(1)}, bf16[16,3584]{1,0:T(8,128)(2,1)S(1)}, u32[]{:S(2)}, u32[]{:S(2)}) collective-permute-start(bf16[16,3584]{1,0:T(8,128)(2,1)S(1)} %get-tuple-element.30), channel_id=1, source_target_pairs={{0,4},{2,6},{4,0},{6,2},{8,12},{10,14},{12,8},{14,10},{16,20},{18,... | collective-permute-start | bytes 344072 | tf_op jit(solution)/shard_map/ppermute | solution.py:179
  27.3 1.6 %collective-permute-done.6.refs_1_ = bf16[16,3584]{1,0:T(8,128)(2,1)S(1)} collective-permute-done((bf16[16,3584]{1,0:T(8,128)(2,1)S(1)}, bf16[16,3584]{1,0:T(8,128)(2,1)S(1)}, u32[]{:S(2)}, u32[]{:S(2)}) %collective-permute-start.6) | collective-permute-done | bytes 114720 | tf_op jit(solution)/shard_map/ppermute | solution.py:179
  28.9 0.9 %collective-permute-start.7 = (bf16[16,3584]{1,0:T(8,128)(2,1)S(1)}, bf16[16,3584]{1,0:T(8,128)(2,1)S(1)}, u32[]{:S(2)}, u32[]{:S(2)}) collective-permute-start(bf16[16,3584]{1,0:T(8,128)(2,1)S(1)} %shard_map.79), channel_id=1, source_target_pairs={{0,2},{2,0},{4,6},{6,4},{8,10},{10,8},{12,14},{14,12},{16,18},{18,... | collective-permute-start | bytes 344072 | tf_op jit(solution)/shard_map/ppermute | solution.py:179
  29.9 1.1 %collective-permute-start.14 = (bf16[16,3584]{1,0:T(8,128)(2,1)S(1)}, bf16[16,3584]{1,0:T(8,128)(2,1)S(1)}, u32[]{:S(2)}, u32[]{:S(2)}) collective-permute-start(bf16[16,3584]{1,0:T(8,128)(2,1)S(1)} %get-tuple-element.38), channel_id=1, source_target_pairs={{0,2},{2,0},{4,6},{6,4},{8,10},{10,8},{12,14},{14,12},{16,18},{18,... | collective-permute-start | bytes 344072 | tf_op jit(solution)/shard_map/ppermute | solution.py:179
  31.0 0.3 collective-permute-done.15.refs_1_
  31.3 1.5 %collective-permute-start.16 = (bf16[16,3584]{1,0:T(8,128)(2,1)S(1)}, bf16[16,3584]{1,0:T(8,128)(2,1)S(1)}, u32[]{:S(2)}, u32[]{:S(2)}) collective-permute-start(bf16[16,3584]{1,0:T(8,128)(2,1)S(1)} %shard_map.84), channel_id=1, source_target_pairs={{0,4},{2,6},{4,0},{6,2},{8,12},{10,14},{12,8},{14,10},{16,20},{18,... | collective-permute-start | bytes 344072 | tf_op jit(solution)/shard_map/ppermute | solution.py:179
  32.8 1.0 %collective-permute-done.7.refs_2_ = bf16[16,3584]{1,0:T(8,128)(2,1)S(1)} collective-permute-done((bf16[16,3584]{1,0:T(8,128)(2,1)S(1)}, bf16[16,3584]{1,0:T(8,128)(2,1)S(1)}, u32[]{:S(2)}, u32[]{:S(2)}) %collective-permute-start.7) | collective-permute-done | bytes 114720 | tf_op jit(solution)/shard_map/ppermute | solution.py:179
  33.9 2.2 %collective-permute-start.8 = (bf16[8,3584]{1,0:T(8,128)(2,1)S(1)}, bf16[8,3584]{1,0:T(8,128)(2,1)S(1)}, u32[]{:S(2)}, u32[]{:S(2)}) collective-permute-start(bf16[8,3584]{1,0:T(8,128)(2,1)S(1)} %get-tuple-element.33), channel_id=1, source_target_pairs={{0,24},{2,26},{4,28},{6,30},{8,16},{10,18},{12,20},{14,22},{16,8},... | collective-permute-start | bytes 172040 | tf_op jit(solution)/shard_map/ppermute | solution.py:179
  36.2 2.2 %collective-permute-start.17 = (bf16[8,3584]{1,0:T(8,128)(2,1)S(1)}, bf16[8,3584]{1,0:T(8,128)(2,1)S(1)}, u32[]{:S(2)}, u32[]{:S(2)}) collective-permute-start(bf16[8,3584]{1,0:T(8,128)(2,1)S(1)} %get-tuple-element.41), channel_id=1, source_target_pairs={{0,8},{2,10},{4,12},{6,14},{8,0},{10,2},{12,4},{14,6},{16,24},{18,... | collective-permute-start | bytes 172040 | tf_op jit(solution)/shard_map/ppermute | solution.py:179
  38.4 1.5 %collective-permute-done.8.refs_0_ = bf16[8,3584]{1,0:T(8,128)(2,1)S(1)} collective-permute-done((bf16[8,3584]{1,0:T(8,128)(2,1)S(1)}, bf16[8,3584]{1,0:T(8,128)(2,1)S(1)}, u32[]{:S(2)}, u32[]{:S(2)}) %collective-permute-start.8) | collective-permute-done | bytes 57376 | tf_op jit(solution)/shard_map/ppermute | solution.py:179
  39.9 1.3 %collective-permute-done.9.refs_1_ = bf16[8,3584]{1,0:T(8,128)(2,1)S(1)} collective-permute-done((bf16[8,3584]{1,0:T(8,128)(2,1)S(1)}, bf16[8,3584]{1,0:T(8,128)(2,1)S(1)}, u32[]{:S(2)}, u32[]{:S(2)}) %collective-permute-start.9) | collective-permute-done | bytes 57376 | tf_op jit(solution)/shard_map/ppermute | solution.py:179
  41.2 0.2 shard_map.81.near
  41.4 0.9 %shard_map.86 = bf16[16,3584]{1,0:T(8,128)(2,1)} custom-call(bf16[48,16]{1,0:T(8,128)(2,1)S(1)} %get-tuple-element.25.refs_1_.terms, f32[16,3584]{1,0:T(8,128)S(1)} %shard_map.81.near, bf16[8,3584]{1,0:T(8,128)(2,1)S(1)} %collective-permute-done.17.refs_0_, bf16[8,3584]{1,0:T(8,128)(2,1)S(1)} %get-tuple-element.42.refs_1_), custom_call_target="tpu_custom_call" | custom-call | tf_op jit(solution)/shard_map/pallas_call | solution.py:153
  (18 shorter events, 0.3 us)
Async XLA Ops:
  1.2 8.0 %collective-permute-start = (bf16[8,3584]{1,0:T(8,128)(2,1)S(1)}, bf16[8,3584]{1,0:T(8,128)(2,1)S(1)}, u32[]{:S(2)}, u32[]{:S(2)}) collective-permute-start(bf16[8,3584]{1,0:T(8,128)(2,1)S(1)} %get-tuple-element.27), channel_id=1, source_target_pairs={{0,24},{2,26},{4,28},{6,30},{8,16},{10,18},{12,20},{14,22},{16,8},... | collective-permute-start | bytes 172040 | tf_op jit(solution)/shard_map/ppermute | solution.py:179
  6.3 5.1 %collective-permute-start.1 = (bf16[8,3584]{1,0:T(8,128)(2,1)S(1)}, bf16[8,3584]{1,0:T(8,128)(2,1)S(1)}, u32[]{:S(2)}, u32[]{:S(2)}) collective-permute-start(bf16[8,3584]{1,0:T(8,128)(2,1)S(1)} %get-tuple-element.28), channel_id=1, source_target_pairs={{0,16},{2,18},{4,20},{6,22},{8,24},{10,26},{12,28},{14,30},{16,0},... | collective-permute-start | bytes 172040 | tf_op jit(solution)/shard_map/ppermute | solution.py:179
  6.3 6.7 %collective-permute-start.10 = (bf16[8,3584]{1,0:T(8,128)(2,1)S(1)}, bf16[8,3584]{1,0:T(8,128)(2,1)S(1)}, u32[]{:S(2)}, u32[]{:S(2)}) collective-permute-start(bf16[8,3584]{1,0:T(8,128)(2,1)S(1)} %get-tuple-element.35), channel_id=1, source_target_pairs={{0,8},{2,10},{4,12},{6,14},{8,0},{10,2},{12,4},{14,6},{16,24},{18,... | collective-permute-start | bytes 172040 | tf_op jit(solution)/shard_map/ppermute | solution.py:179
  11.4 4.9 %collective-permute-start.2 = (bf16[16,3584]{1,0:T(8,128)(2,1)S(1)}, bf16[16,3584]{1,0:T(8,128)(2,1)S(1)}, u32[]{:S(2)}, u32[]{:S(2)}) collective-permute-start(bf16[16,3584]{1,0:T(8,128)(2,1)S(1)} %shard_map.76.refs_0_), channel_id=1, source_target_pairs={{0,2},{2,0},{4,6},{6,4},{8,10},{10,8},{12,14},{14,12},{16,18},{18,... | collective-permute-start | bytes 344072 | tf_op jit(solution)/shard_map/ppermute | solution.py:179
  13.0 6.3 %collective-permute-start.11 = (bf16[16,3584]{1,0:T(8,128)(2,1)S(1)}, bf16[16,3584]{1,0:T(8,128)(2,1)S(1)}, u32[]{:S(2)}, u32[]{:S(2)}) collective-permute-start(bf16[16,3584]{1,0:T(8,128)(2,1)S(1)} %shard_map.82.refs_0_), channel_id=1, source_target_pairs={{0,4},{2,6},{4,0},{6,2},{8,12},{10,14},{12,8},{14,10},{16,20},{18,... | collective-permute-start | bytes 344072 | tf_op jit(solution)/shard_map/ppermute | solution.py:179
  14.6 6.7 %collective-permute-start.3 = (bf16[16,3584]{1,0:T(8,128)(2,1)S(1)}, bf16[16,3584]{1,0:T(8,128)(2,1)S(1)}, u32[]{:S(2)}, u32[]{:S(2)}) collective-permute-start(bf16[16,3584]{1,0:T(8,128)(2,1)S(1)} %shard_map.76.refs_0_), channel_id=1, source_target_pairs={{0,4},{2,6},{4,0},{6,2},{8,12},{10,14},{12,8},{14,10},{16,20},{18,... | collective-permute-start | bytes 344072 | tf_op jit(solution)/shard_map/ppermute | solution.py:179
  16.2 5.7 %collective-permute-start.4 = (bf16[16,3584]{1,0:T(8,128)(2,1)S(1)}, bf16[16,3584]{1,0:T(8,128)(2,1)S(1)}, u32[]{:S(2)}, u32[]{:S(2)}) collective-permute-start(bf16[16,3584]{1,0:T(8,128)(2,1)S(1)} %collective-permute-done.2.refs_1_), channel_id=1, source_target_pairs={{0,4},{2,6},{4,0},{6,2},{8,12},{10,14},{12,8},{14,10},{16,20},{18,... | collective-permute-start | bytes 344072 | tf_op jit(solution)/shard_map/ppermute | solution.py:179
  17.8 6.9 %collective-permute-start.12 = (bf16[16,3584]{1,0:T(8,128)(2,1)S(1)}, bf16[16,3584]{1,0:T(8,128)(2,1)S(1)}, u32[]{:S(2)}, u32[]{:S(2)}) collective-permute-start(bf16[16,3584]{1,0:T(8,128)(2,1)S(1)} %shard_map.82.refs_0_), channel_id=1, source_target_pairs={{0,2},{2,0},{4,6},{6,4},{8,10},{10,8},{12,14},{14,12},{16,18},{18,... | collective-permute-start | bytes 344072 | tf_op jit(solution)/shard_map/ppermute | solution.py:179
  19.3 5.4 %collective-permute-start.13 = (bf16[16,3584]{1,0:T(8,128)(2,1)S(1)}, bf16[16,3584]{1,0:T(8,128)(2,1)S(1)}, u32[]{:S(2)}, u32[]{:S(2)}) collective-permute-start(bf16[16,3584]{1,0:T(8,128)(2,1)S(1)} %collective-permute-done.11.refs_1_), channel_id=1, source_target_pairs={{0,2},{2,0},{4,6},{6,4},{8,10},{10,8},{12,14},{14,12},{16,18},{18,... | collective-permute-start | bytes 344072 | tf_op jit(solution)/shard_map/ppermute | solution.py:179
  23.1 5.8 %collective-permute-start.6 = (bf16[16,3584]{1,0:T(8,128)(2,1)S(1)}, bf16[16,3584]{1,0:T(8,128)(2,1)S(1)}, u32[]{:S(2)}, u32[]{:S(2)}) collective-permute-start(bf16[16,3584]{1,0:T(8,128)(2,1)S(1)} %get-tuple-element.32), channel_id=1, source_target_pairs={{0,4},{2,6},{4,0},{6,2},{8,12},{10,14},{12,8},{14,10},{16,20},{18,... | collective-permute-start | bytes 344072 | tf_op jit(solution)/shard_map/ppermute | solution.py:179
  25.9 5.4 %collective-permute-start.15 = (bf16[16,3584]{1,0:T(8,128)(2,1)S(1)}, bf16[16,3584]{1,0:T(8,128)(2,1)S(1)}, u32[]{:S(2)}, u32[]{:S(2)}) collective-permute-start(bf16[16,3584]{1,0:T(8,128)(2,1)S(1)} %get-tuple-element.40), channel_id=1, source_target_pairs={{0,2},{2,0},{4,6},{6,4},{8,10},{10,8},{12,14},{14,12},{16,18},{18,... | collective-permute-start | bytes 344072 | tf_op jit(solution)/shard_map/ppermute | solution.py:179
  26.6 6.2 %collective-permute-start.5 = (bf16[16,3584]{1,0:T(8,128)(2,1)S(1)}, bf16[16,3584]{1,0:T(8,128)(2,1)S(1)}, u32[]{:S(2)}, u32[]{:S(2)}) collective-permute-start(bf16[16,3584]{1,0:T(8,128)(2,1)S(1)} %get-tuple-element.30), channel_id=1, source_target_pairs={{0,4},{2,6},{4,0},{6,2},{8,12},{10,14},{12,8},{14,10},{16,20},{18,... | collective-permute-start | bytes 344072 | tf_op jit(solution)/shard_map/ppermute | solution.py:179
  28.9 4.9 %collective-permute-start.7 = (bf16[16,3584]{1,0:T(8,128)(2,1)S(1)}, bf16[16,3584]{1,0:T(8,128)(2,1)S(1)}, u32[]{:S(2)}, u32[]{:S(2)}) collective-permute-start(bf16[16,3584]{1,0:T(8,128)(2,1)S(1)} %shard_map.79), channel_id=1, source_target_pairs={{0,2},{2,0},{4,6},{6,4},{8,10},{10,8},{12,14},{14,12},{16,18},{18,... | collective-permute-start | bytes 344072 | tf_op jit(solution)/shard_map/ppermute | solution.py:179
  29.9 6.2 %collective-permute-start.14 = (bf16[16,3584]{1,0:T(8,128)(2,1)S(1)}, bf16[16,3584]{1,0:T(8,128)(2,1)S(1)}, u32[]{:S(2)}, u32[]{:S(2)}) collective-permute-start(bf16[16,3584]{1,0:T(8,128)(2,1)S(1)} %get-tuple-element.38), channel_id=1, source_target_pairs={{0,2},{2,0},{4,6},{6,4},{8,10},{10,8},{12,14},{14,12},{16,18},{18,... | collective-permute-start | bytes 344072 | tf_op jit(solution)/shard_map/ppermute | solution.py:179
  31.3 4.9 %collective-permute-start.16 = (bf16[16,3584]{1,0:T(8,128)(2,1)S(1)}, bf16[16,3584]{1,0:T(8,128)(2,1)S(1)}, u32[]{:S(2)}, u32[]{:S(2)}) collective-permute-start(bf16[16,3584]{1,0:T(8,128)(2,1)S(1)} %shard_map.84), channel_id=1, source_target_pairs={{0,4},{2,6},{4,0},{6,2},{8,12},{10,14},{12,8},{14,10},{16,20},{18,... | collective-permute-start | bytes 344072 | tf_op jit(solution)/shard_map/ppermute | solution.py:179
  33.9 6.0 %collective-permute-start.8 = (bf16[8,3584]{1,0:T(8,128)(2,1)S(1)}, bf16[8,3584]{1,0:T(8,128)(2,1)S(1)}, u32[]{:S(2)}, u32[]{:S(2)}) collective-permute-start(bf16[8,3584]{1,0:T(8,128)(2,1)S(1)} %get-tuple-element.33), channel_id=1, source_target_pairs={{0,24},{2,26},{4,28},{6,30},{8,16},{10,18},{12,20},{14,22},{16,8},... | collective-permute-start | bytes 172040 | tf_op jit(solution)/shard_map/ppermute | solution.py:179
  36.0 5.1 %collective-permute-start.9 = (bf16[8,3584]{1,0:T(8,128)(2,1)S(1)}, bf16[8,3584]{1,0:T(8,128)(2,1)S(1)}, u32[]{:S(2)}, u32[]{:S(2)}) collective-permute-start(bf16[8,3584]{1,0:T(8,128)(2,1)S(1)} %get-tuple-element.34), channel_id=1, source_target_pairs={{0,16},{2,18},{4,20},{6,22},{8,24},{10,26},{12,28},{14,30},{16,0},... | collective-permute-start | bytes 172040 | tf_op jit(solution)/shard_map/ppermute | solution.py:179
  36.2 5.2 %collective-permute-start.17 = (bf16[8,3584]{1,0:T(8,128)(2,1)S(1)}, bf16[8,3584]{1,0:T(8,128)(2,1)S(1)}, u32[]{:S(2)}, u32[]{:S(2)}) collective-permute-start(bf16[8,3584]{1,0:T(8,128)(2,1)S(1)} %get-tuple-element.41), channel_id=1, source_target_pairs={{0,8},{2,10},{4,12},{6,14},{8,0},{10,2},{12,4},{14,6},{16,24},{18,... | collective-permute-start | bytes 172040 | tf_op jit(solution)/shard_map/ppermute | solution.py:179

commit v17 on v16

--- a/solution.py
+++ b/solution.py
@@ -225,10 +225,11 @@
         )
         if square:
             held = {a: swap(own, a), b: swap(own, b)}
-            held = [own, held[a], held[b], swap(held[a], b)]
+            cross = swap(own, 3) if h == 0 else swap(held[a], b)
+            held = [own, held[a], held[b], cross]
         else:
             held = [swap(own, q) if q else own for q in range(group_size)]
-        earlier = []
+        earlier = [own]
         result = local(
             functools.partial(expert_kernel, group_size),
             held + [w_in, w_out],

time: 42.5 us -> 43.3 us (1.019)
  starting transfers between devices: 24 us -> 24.9 us
    ppermute x18, starting transfers between devices: 24 us -> 24.9 us  [swap(): lax.ppermute(value, 'expert', [(e, e ^ offset) for e in range(n_devices)])]
  transfers between devices with their start and end apart: 18 -> 18, of which waited for: 9 -> 8; matrix products, arithmetic and copies ran while one was open for 0% -> 0% of each run, Pallas kernels for 15% -> 15%
where the time goes in v17:
time: 43.3 us; the launch traced here: 43.1 us
  starting transfers between devices  24.9 us (58%)
  waiting for transfers between devices  9.65 us (22%)
  Pallas kernels  8.5 us (20%)
    ppermute x18, starting transfers between devices, swap(): lax.ppermute(value, 'expert', [(e, e ^ offset) for e in range(n_devices)])  24.9 us
    ppermute x18, waiting for transfers between devices, swap(): lax.ppermute(value, 'expert', [(e, e ^ offset) for e in range(n_devices)])  9.65 us
    pallas_call x14, Pallas kernels, call(): pl.pallas_call(kernel, out_shape=outs, in_specs=in_specs, out_specs=jax.t...  8.5 us
  transfers between devices with their start and end apart: 18, of which 8 were waited for; matrix products, arithmetic and copies ran while one was open for 0% of the time, Pallas kernels for 15%

profile of v17, /device:TPU:0, one launch (start us, length us, event | category | flops | bytes accessed | tf_op | source)
XLA Modules:
  0.0 43.1 jit_solution(10071212694945986831)
XLA Ops:
  0.0 1.2 %shard_map.73 = (bf16[8,3584]{1,0:T(8,128)(2,1)S(1)}, bf16[8,3584]{1,0:T(8,128)(2,1)S(1)}, bf16[8,3584]{1,0:T(8,128)(2,1)S(1)}, bf16[8,3584]{1,0:T(8,128)(2,1)S(1)}, f32[32,16]{1,0:T(8,128)S(1)}) custom-call(s32[4]{0:T(128)} %refs_0_.3, s32[2,16]{1,0:T(2,128)} %bitcast.3, s32[2,16]{1,0:T(2,128)} %bitcast.4, f32[2,16]{1,0:T(2,128)} %bitcast.5, ...), custom_call_target="tpu_custom_call" | custom-call | tf_op jit(solution)/shard_map/pallas_call | solution.py:153
  1.2 5.1 %collective-permute-start = (bf16[8,3584]{1,0:T(8,128)(2,1)S(1)}, bf16[8,3584]{1,0:T(8,128)(2,1)S(1)}, u32[]{:S(2)}, u32[]{:S(2)}) collective-permute-start(bf16[8,3584]{1,0:T(8,128)(2,1)S(1)} %get-tuple-element.27), channel_id=1, source_target_pairs={{0,24},{2,26},{4,28},{6,30},{8,16},{10,18},{12,20},{14,22},{16,8},... | collective-permute-start | bytes 172040 | tf_op jit(solution)/shard_map/ppermute | solution.py:179
  6.3 0.6 %collective-permute-start.10 = (bf16[8,3584]{1,0:T(8,128)(2,1)S(1)}, bf16[8,3584]{1,0:T(8,128)(2,1)S(1)}, u32[]{:S(2)}, u32[]{:S(2)}) collective-permute-start(bf16[8,3584]{1,0:T(8,128)(2,1)S(1)} %get-tuple-element.35), channel_id=1, source_target_pairs={{0,8},{2,10},{4,12},{6,14},{8,0},{10,2},{12,4},{14,6},{16,24},{18,... | collective-permute-start | bytes 172040 | tf_op jit(solution)/shard_map/ppermute | solution.py:179
  6.9 0.2 shard_map.74
  7.1 2.1 %shard_map.75.refs_2_.refs_4_ = bf16[2,3584,256]{2,1,0:T(8,128)(2,1)S(1)} custom-call(bf16[2,3584,256]{2,1,0:T(8,128)(2,1)} %refs_0_.4, bf16[48,16]{1,0:T(8,128)(2,1)S(1)} %get-tuple-element.26.refs_1_.terms), custom_call_target="tpu_custom_call" | custom-call | bytes 3670016 | tf_op jit(solution)/shard_map/pallas_call | solution.py:153
  9.2 2.2 %collective-permute-done.1.refs_1_ = bf16[8,3584]{1,0:T(8,128)(2,1)S(1)} collective-permute-done((bf16[8,3584]{1,0:T(8,128)(2,1)S(1)}, bf16[8,3584]{1,0:T(8,128)(2,1)S(1)}, u32[]{:S(2)}, u32[]{:S(2)}) %collective-permute-start.1) | collective-permute-done | bytes 57376 | tf_op jit(solution)/shard_map/ppermute | solution.py:179
  11.4 1.6 %collective-permute-start.11 = (bf16[16,3584]{1,0:T(8,128)(2,1)S(1)}, bf16[16,3584]{1,0:T(8,128)(2,1)S(1)}, u32[]{:S(2)}, u32[]{:S(2)}) collective-permute-start(bf16[16,3584]{1,0:T(8,128)(2,1)S(1)} %shard_map.82.refs_0_), channel_id=1, source_target_pairs={{0,4},{2,6},{4,0},{6,2},{8,12},{10,14},{12,8},{14,10},{16,20},{18,... | collective-permute-start | bytes 344072 | tf_op jit(solution)/shard_map/ppermute | solution.py:179
  13.0 1.4 %collective-permute-start.4 = (bf16[16,3584]{1,0:T(8,128)(2,1)S(1)}, bf16[16,3584]{1,0:T(8,128)(2,1)S(1)}, u32[]{:S(2)}, u32[]{:S(2)}) collective-permute-start(bf16[16,3584]{1,0:T(8,128)(2,1)S(1)} %shard_map.76.refs_0_.refs_2_), channel_id=1, source_target_pairs={{0,6},{2,4},{4,2},{6,0},{8,14},{10,12},{12,10},{14,8},{16,22},{18,... | collective-permute-start | bytes 344072 | tf_op jit(solution)/shard_map/ppermute | solution.py:179
  14.5 1.5 %collective-permute-start.3 = (bf16[16,3584]{1,0:T(8,128)(2,1)S(1)}, bf16[16,3584]{1,0:T(8,128)(2,1)S(1)}, u32[]{:S(2)}, u32[]{:S(2)}) collective-permute-start(bf16[16,3584]{1,0:T(8,128)(2,1)S(1)} %shard_map.76.refs_0_.refs_2_), channel_id=1, source_target_pairs={{0,4},{2,6},{4,0},{6,2},{8,12},{10,14},{12,8},{14,10},{16,20},{18,... | collective-permute-start | bytes 344072 | tf_op jit(solution)/shard_map/ppermute | solution.py:179
  16.0 0.5 %collective-permute-start.2 = (bf16[16,3584]{1,0:T(8,128)(2,1)S(1)}, bf16[16,3584]{1,0:T(8,128)(2,1)S(1)}, u32[]{:S(2)}, u32[]{:S(2)}) collective-permute-start(bf16[16,3584]{1,0:T(8,128)(2,1)S(1)} %shard_map.76.refs_0_.refs_2_), channel_id=1, source_target_pairs={{0,2},{2,0},{4,6},{6,4},{8,10},{10,8},{12,14},{14,12},{16,18},{18,... | collective-permute-start | bytes 344072 | tf_op jit(solution)/shard_map/ppermute | solution.py:179
  16.5 1.5 %collective-permute-start.12 = (bf16[16,3584]{1,0:T(8,128)(2,1)S(1)}, bf16[16,3584]{1,0:T(8,128)(2,1)S(1)}, u32[]{:S(2)}, u32[]{:S(2)}) collective-permute-start(bf16[16,3584]{1,0:T(8,128)(2,1)S(1)} %shard_map.82.refs_0_), channel_id=1, source_target_pairs={{0,2},{2,0},{4,6},{6,4},{8,10},{10,8},{12,14},{14,12},{16,18},{18,... | collective-permute-start | bytes 344072 | tf_op jit(solution)/shard_map/ppermute | solution.py:179
  18.0 1.1 %collective-permute-done.11.refs_1_ = bf16[16,3584]{1,0:T(8,128)(2,1)S(1)} collective-permute-done((bf16[16,3584]{1,0:T(8,128)(2,1)S(1)}, bf16[16,3584]{1,0:T(8,128)(2,1)S(1)}, u32[]{:S(2)}, u32[]{:S(2)}) %collective-permute-start.11) | collective-permute-done | bytes 114720 | tf_op jit(solution)/shard_map/ppermute | solution.py:179
  19.1 1.5 %collective-permute-start.13 = (bf16[16,3584]{1,0:T(8,128)(2,1)S(1)}, bf16[16,3584]{1,0:T(8,128)(2,1)S(1)}, u32[]{:S(2)}, u32[]{:S(2)}) collective-permute-start(bf16[16,3584]{1,0:T(8,128)(2,1)S(1)} %collective-permute-done.11.refs_1_), channel_id=1, source_target_pairs={{0,2},{2,0},{4,6},{6,4},{8,10},{10,8},{12,14},{14,12},{16,18},{18,... | collective-permute-start | bytes 344072 | tf_op jit(solution)/shard_map/ppermute | solution.py:179
  20.6 1.5 %shard_map.77.refs_5_ = bf16[256,3584]{1,0:T(8,128)(2,1)S(1)} custom-call(bf16[256,3584]{1,0:T(8,128)(2,1)} %refs_0_.5, bf16[48,16]{1,0:T(8,128)(2,1)S(1)} %get-tuple-element.25.refs_1_.terms), custom_call_target="tpu_custom_call" | custom-call | bytes 1835008 | tf_op jit(solution)/shard_map/pallas_call | solution.py:153
  22.1 1.2 %shard_map.78 = (bf16[16,3584]{1,0:T(8,128)(2,1)S(1)}, bf16[16,3584]{1,0:T(8,128)(2,1)S(1)}, bf16[16,3584]{1,0:T(8,128)(2,1)S(1)}, bf16[16,3584]{1,0:T(8,128)(2,1)S(1)}) custom-call(bf16[16,3584]{1,0:T(8,128)(2,1)S(1)} %shard_map.76.refs_0_.refs_2_, bf16[16,3584]{1,0:T(8,128)(2,1)S(1)} %collective-permute-done.2.refs_1_, ...), custom_call_target="tpu_custom_call" | custom-call | tf_op jit(solution)/shard_map/pallas_call | solution.py:153
  23.3 1.9 %collective-permute-start.6 = (bf16[16,3584]{1,0:T(8,128)(2,1)S(1)}, bf16[16,3584]{1,0:T(8,128)(2,1)S(1)}, u32[]{:S(2)}, u32[]{:S(2)}) collective-permute-start(bf16[16,3584]{1,0:T(8,128)(2,1)S(1)} %get-tuple-element.32), channel_id=1, source_target_pairs={{0,4},{2,6},{4,0},{6,2},{8,12},{10,14},{12,8},{14,10},{16,20},{18,... | collective-permute-start | bytes 344072 | tf_op jit(solution)/shard_map/ppermute | solution.py:179
  25.2 1.2 %shard_map.83 = (bf16[16,3584]{1,0:T(8,128)(2,1)S(1)}, bf16[16,3584]{1,0:T(8,128)(2,1)S(1)}, bf16[16,3584]{1,0:T(8,128)(2,1)S(1)}, bf16[16,3584]{1,0:T(8,128)(2,1)S(1)}) custom-call(bf16[16,3584]{1,0:T(8,128)(2,1)S(1)} %shard_map.82.refs_0_, bf16[16,3584]{1,0:T(8,128)(2,1)S(1)} %collective-permute-done.11.refs_1_, ...), custom_call_target="tpu_custom_call" | custom-call | tf_op jit(solution)/shard_map/pallas_call | solution.py:153
  26.4 0.9 %collective-permute-start.15 = (bf16[16,3584]{1,0:T(8,128)(2,1)S(1)}, bf16[16,3584]{1,0:T(8,128)(2,1)S(1)}, u32[]{:S(2)}, u32[]{:S(2)}) collective-permute-start(bf16[16,3584]{1,0:T(8,128)(2,1)S(1)} %get-tuple-element.40), channel_id=1, source_target_pairs={{0,2},{2,0},{4,6},{6,4},{8,10},{10,8},{12,14},{14,12},{16,18},{18,... | collective-permute-start | bytes 344072 | tf_op jit(solution)/shard_map/ppermute | solution.py:179
  27.3 1.3 %collective-permute-start.5 = (bf16[16,3584]{1,0:T(8,128)(2,1)S(1)}, bf16[16,3584]{1,0:T(8,128)(2,1)S(1)}, u32[]{:S(2)}, u32[]{:S(2)}) collective-permute-start(bf16[16,3584]{1,0:T(8,128)(2,1)S(1)} %get-tuple-element.30), channel_id=1, source_target_pairs={{0,4},{2,6},{4,0},{6,2},{8,12},{10,14},{12,8},{14,10},{16,20},{18,... | collective-permute-start | bytes 344072 | tf_op jit(solution)/shard_map/ppermute | solution.py:179
  28.6 0.8 %collective-permute-start.7 = (bf16[16,3584]{1,0:T(8,128)(2,1)S(1)}, bf16[16,3584]{1,0:T(8,128)(2,1)S(1)}, u32[]{:S(2)}, u32[]{:S(2)}) collective-permute-start(bf16[16,3584]{1,0:T(8,128)(2,1)S(1)} %shard_map.79), channel_id=1, source_target_pairs={{0,2},{2,0},{4,6},{6,4},{8,10},{10,8},{12,14},{14,12},{16,18},{18,... | collective-permute-start | bytes 344072 | tf_op jit(solution)/shard_map/ppermute | solution.py:179
  29.4 1.3 %collective-permute-start.14 = (bf16[16,3584]{1,0:T(8,128)(2,1)S(1)}, bf16[16,3584]{1,0:T(8,128)(2,1)S(1)}, u32[]{:S(2)}, u32[]{:S(2)}) collective-permute-start(bf16[16,3584]{1,0:T(8,128)(2,1)S(1)} %get-tuple-element.38), channel_id=1, source_target_pairs={{0,2},{2,0},{4,6},{6,4},{8,10},{10,8},{12,14},{14,12},{16,18},{18,... | collective-permute-start | bytes 344072 | tf_op jit(solution)/shard_map/ppermute | solution.py:179
  30.7 1.7 %collective-permute-done.15.refs_1_ = bf16[16,3584]{1,0:T(8,128)(2,1)S(1)} collective-permute-done((bf16[16,3584]{1,0:T(8,128)(2,1)S(1)}, bf16[16,3584]{1,0:T(8,128)(2,1)S(1)}, u32[]{:S(2)}, u32[]{:S(2)}) %collective-permute-start.15) | collective-permute-done | bytes 114720 | tf_op jit(solution)/shard_map/ppermute | solution.py:179
  32.5 0.9 %collective-permute-start.16 = (bf16[16,3584]{1,0:T(8,128)(2,1)S(1)}, bf16[16,3584]{1,0:T(8,128)(2,1)S(1)}, u32[]{:S(2)}, u32[]{:S(2)}) collective-permute-start(bf16[16,3584]{1,0:T(8,128)(2,1)S(1)} %shard_map.84), channel_id=1, source_target_pairs={{0,4},{2,6},{4,0},{6,2},{8,12},{10,14},{12,8},{14,10},{16,20},{18,... | collective-permute-start | bytes 344072 | tf_op jit(solution)/shard_map/ppermute | solution.py:179
  33.4 0.3 collective-permute-done.7.refs_2_
  33.7 3.0 %collective-permute-start.8 = (bf16[8,3584]{1,0:T(8,128)(2,1)S(1)}, bf16[8,3584]{1,0:T(8,128)(2,1)S(1)}, u32[]{:S(2)}, u32[]{:S(2)}) collective-permute-start(bf16[8,3584]{1,0:T(8,128)(2,1)S(1)} %get-tuple-element.33), channel_id=1, source_target_pairs={{0,24},{2,26},{4,28},{6,30},{8,16},{10,18},{12,20},{14,22},{16,8},... | collective-permute-start | bytes 172040 | tf_op jit(solution)/shard_map/ppermute | solution.py:179
  36.8 0.6 %collective-permute-done.16.refs_2_ = bf16[16,3584]{1,0:T(8,128)(2,1)S(1)} collective-permute-done((bf16[16,3584]{1,0:T(8,128)(2,1)S(1)}, bf16[16,3584]{1,0:T(8,128)(2,1)S(1)}, u32[]{:S(2)}, u32[]{:S(2)}) %collective-permute-start.16) | collective-permute-done | bytes 114720 | tf_op jit(solution)/shard_map/ppermute | solution.py:179
  37.4 0.9 %collective-permute-start.17 = (bf16[8,3584]{1,0:T(8,128)(2,1)S(1)}, bf16[8,3584]{1,0:T(8,128)(2,1)S(1)}, u32[]{:S(2)}, u32[]{:S(2)}) collective-permute-start(bf16[8,3584]{1,0:T(8,128)(2,1)S(1)} %get-tuple-element.41), channel_id=1, source_target_pairs={{0,8},{2,10},{4,12},{6,14},{8,0},{10,2},{12,4},{14,6},{16,24},{18,... | collective-permute-start | bytes 172040 | tf_op jit(solution)/shard_map/ppermute | solution.py:179
  38.3 1.5 %collective-permute-done.8.refs_0_ = bf16[8,3584]{1,0:T(8,128)(2,1)S(1)} collective-permute-done((bf16[8,3584]{1,0:T(8,128)(2,1)S(1)}, bf16[8,3584]{1,0:T(8,128)(2,1)S(1)}, u32[]{:S(2)}, u32[]{:S(2)}) %collective-permute-start.8) | collective-permute-done | bytes 57376 | tf_op jit(solution)/shard_map/ppermute | solution.py:179
  39.8 2.2 %collective-permute-done.9.refs_1_ = bf16[8,3584]{1,0:T(8,128)(2,1)S(1)} collective-permute-done((bf16[8,3584]{1,0:T(8,128)(2,1)S(1)}, bf16[8,3584]{1,0:T(8,128)(2,1)S(1)}, u32[]{:S(2)}, u32[]{:S(2)}) %collective-permute-start.9) | collective-permute-done | bytes 57376 | tf_op jit(solution)/shard_map/ppermute | solution.py:179
  41.9 0.2 shard_map.81.near
  42.2 0.1 collective-permute-done.17.refs_0_
  42.3 0.9 %shard_map.86 = bf16[16,3584]{1,0:T(8,128)(2,1)} custom-call(bf16[48,16]{1,0:T(8,128)(2,1)S(1)} %get-tuple-element.25.refs_1_.terms, f32[16,3584]{1,0:T(8,128)S(1)} %shard_map.81.near, bf16[8,3584]{1,0:T(8,128)(2,1)S(1)} %collective-permute-done.17.refs_0_, bf16[8,3584]{1,0:T(8,128)(2,1)S(1)} %get-tuple-element.42.refs_1_), custom_call_target="tpu_custom_call" | custom-call | tf_op jit(solution)/shard_map/pallas_call | solution.py:153
  (18 shorter events, 0.2 us)
Async XLA Ops:
  1.2 8.0 %collective-permute-start = (bf16[8,3584]{1,0:T(8,128)(2,1)S(1)}, bf16[8,3584]{1,0:T(8,128)(2,1)S(1)}, u32[]{:S(2)}, u32[]{:S(2)}) collective-permute-start(bf16[8,3584]{1,0:T(8,128)(2,1)S(1)} %get-tuple-element.27), channel_id=1, source_target_pairs={{0,24},{2,26},{4,28},{6,30},{8,16},{10,18},{12,20},{14,22},{16,8},... | collective-permute-start | bytes 172040 | tf_op jit(solution)/shard_map/ppermute | solution.py:179
  6.3 5.1 %collective-permute-start.1 = (bf16[8,3584]{1,0:T(8,128)(2,1)S(1)}, bf16[8,3584]{1,0:T(8,128)(2,1)S(1)}, u32[]{:S(2)}, u32[]{:S(2)}) collective-permute-start(bf16[8,3584]{1,0:T(8,128)(2,1)S(1)} %get-tuple-element.28), channel_id=1, source_target_pairs={{0,16},{2,18},{4,20},{6,22},{8,24},{10,26},{12,28},{14,30},{16,0},... | collective-permute-start | bytes 172040 | tf_op jit(solution)/shard_map/ppermute | solution.py:179
  6.3 5.1 %collective-permute-start.10 = (bf16[8,3584]{1,0:T(8,128)(2,1)S(1)}, bf16[8,3584]{1,0:T(8,128)(2,1)S(1)}, u32[]{:S(2)}, u32[]{:S(2)}) collective-permute-start(bf16[8,3584]{1,0:T(8,128)(2,1)S(1)} %get-tuple-element.35), channel_id=1, source_target_pairs={{0,8},{2,10},{4,12},{6,14},{8,0},{10,2},{12,4},{14,6},{16,24},{18,... | collective-permute-start | bytes 172040 | tf_op jit(solution)/shard_map/ppermute | solution.py:179
  11.4 7.7 %collective-permute-start.11 = (bf16[16,3584]{1,0:T(8,128)(2,1)S(1)}, bf16[16,3584]{1,0:T(8,128)(2,1)S(1)}, u32[]{:S(2)}, u32[]{:S(2)}) collective-permute-start(bf16[16,3584]{1,0:T(8,128)(2,1)S(1)} %shard_map.82.refs_0_), channel_id=1, source_target_pairs={{0,4},{2,6},{4,0},{6,2},{8,12},{10,14},{12,8},{14,10},{16,20},{18,... | collective-permute-start | bytes 344072 | tf_op jit(solution)/shard_map/ppermute | solution.py:179
  13.0 9.0 %collective-permute-start.4 = (bf16[16,3584]{1,0:T(8,128)(2,1)S(1)}, bf16[16,3584]{1,0:T(8,128)(2,1)S(1)}, u32[]{:S(2)}, u32[]{:S(2)}) collective-permute-start(bf16[16,3584]{1,0:T(8,128)(2,1)S(1)} %shard_map.76.refs_0_.refs_2_), channel_id=1, source_target_pairs={{0,6},{2,4},{4,2},{6,0},{8,14},{10,12},{12,10},{14,8},{16,22},{18,... | collective-permute-start | bytes 344072 | tf_op jit(solution)/shard_map/ppermute | solution.py:179
  14.5 7.6 %collective-permute-start.3 = (bf16[16,3584]{1,0:T(8,128)(2,1)S(1)}, bf16[16,3584]{1,0:T(8,128)(2,1)S(1)}, u32[]{:S(2)}, u32[]{:S(2)}) collective-permute-start(bf16[16,3584]{1,0:T(8,128)(2,1)S(1)} %shard_map.76.refs_0_.refs_2_), channel_id=1, source_target_pairs={{0,4},{2,6},{4,0},{6,2},{8,12},{10,14},{12,8},{14,10},{16,20},{18,... | collective-permute-start | bytes 344072 | tf_op jit(solution)/shard_map/ppermute | solution.py:179
  16.0 6.1 %collective-permute-start.2 = (bf16[16,3584]{1,0:T(8,128)(2,1)S(1)}, bf16[16,3584]{1,0:T(8,128)(2,1)S(1)}, u32[]{:S(2)}, u32[]{:S(2)}) collective-permute-start(bf16[16,3584]{1,0:T(8,128)(2,1)S(1)} %shard_map.76.refs_0_.refs_2_), channel_id=1, source_target_pairs={{0,2},{2,0},{4,6},{6,4},{8,10},{10,8},{12,14},{14,12},{16,18},{18,... | collective-permute-start | bytes 344072 | tf_op jit(solution)/shard_map/ppermute | solution.py:179
  16.5 8.7 %collective-permute-start.12 = (bf16[16,3584]{1,0:T(8,128)(2,1)S(1)}, bf16[16,3584]{1,0:T(8,128)(2,1)S(1)}, u32[]{:S(2)}, u32[]{:S(2)}) collective-permute-start(bf16[16,3584]{1,0:T(8,128)(2,1)S(1)} %shard_map.82.refs_0_), channel_id=1, source_target_pairs={{0,2},{2,0},{4,6},{6,4},{8,10},{10,8},{12,14},{14,12},{16,18},{18,... | collective-permute-start | bytes 344072 | tf_op jit(solution)/shard_map/ppermute | solution.py:179
  19.1 6.1 %collective-permute-start.13 = (bf16[16,3584]{1,0:T(8,128)(2,1)S(1)}, bf16[16,3584]{1,0:T(8,128)(2,1)S(1)}, u32[]{:S(2)}, u32[]{:S(2)}) collective-permute-start(bf16[16,3584]{1,0:T(8,128)(2,1)S(1)} %collective-permute-done.11.refs_1_), channel_id=1, source_target_pairs={{0,2},{2,0},{4,6},{6,4},{8,10},{10,8},{12,14},{14,12},{16,18},{18,... | collective-permute-start | bytes 344072 | tf_op jit(solution)/shard_map/ppermute | solution.py:179
  23.3 5.3 %collective-permute-start.6 = (bf16[16,3584]{1,0:T(8,128)(2,1)S(1)}, bf16[16,3584]{1,0:T(8,128)(2,1)S(1)}, u32[]{:S(2)}, u32[]{:S(2)}) collective-permute-start(bf16[16,3584]{1,0:T(8,128)(2,1)S(1)} %get-tuple-element.32), channel_id=1, source_target_pairs={{0,4},{2,6},{4,0},{6,2},{8,12},{10,14},{12,8},{14,10},{16,20},{18,... | collective-permute-start | bytes 344072 | tf_op jit(solution)/shard_map/ppermute | solution.py:179
  26.4 6.1 %collective-permute-start.15 = (bf16[16,3584]{1,0:T(8,128)(2,1)S(1)}, bf16[16,3584]{1,0:T(8,128)(2,1)S(1)}, u32[]{:S(2)}, u32[]{:S(2)}) collective-permute-start(bf16[16,3584]{1,0:T(8,128)(2,1)S(1)} %get-tuple-element.40), channel_id=1, source_target_pairs={{0,2},{2,0},{4,6},{6,4},{8,10},{10,8},{12,14},{14,12},{16,18},{18,... | collective-permute-start | bytes 344072 | tf_op jit(solution)/shard_map/ppermute | solution.py:179
  27.3 6.1 %collective-permute-start.5 = (bf16[16,3584]{1,0:T(8,128)(2,1)S(1)}, bf16[16,3584]{1,0:T(8,128)(2,1)S(1)}, u32[]{:S(2)}, u32[]{:S(2)}) collective-permute-start(bf16[16,3584]{1,0:T(8,128)(2,1)S(1)} %get-tuple-element.30), channel_id=1, source_target_pairs={{0,4},{2,6},{4,0},{6,2},{8,12},{10,14},{12,8},{14,10},{16,20},{18,... | collective-permute-start | bytes 344072 | tf_op jit(solution)/shard_map/ppermute | solution.py:179
  28.6 5.1 %collective-permute-start.7 = (bf16[16,3584]{1,0:T(8,128)(2,1)S(1)}, bf16[16,3584]{1,0:T(8,128)(2,1)S(1)}, u32[]{:S(2)}, u32[]{:S(2)}) collective-permute-start(bf16[16,3584]{1,0:T(8,128)(2,1)S(1)} %shard_map.79), channel_id=1, source_target_pairs={{0,2},{2,0},{4,6},{6,4},{8,10},{10,8},{12,14},{14,12},{16,18},{18,... | collective-permute-start | bytes 344072 | tf_op jit(solution)/shard_map/ppermute | solution.py:179
  29.4 7.4 %collective-permute-start.14 = (bf16[16,3584]{1,0:T(8,128)(2,1)S(1)}, bf16[16,3584]{1,0:T(8,128)(2,1)S(1)}, u32[]{:S(2)}, u32[]{:S(2)}) collective-permute-start(bf16[16,3584]{1,0:T(8,128)(2,1)S(1)} %get-tuple-element.38), channel_id=1, source_target_pairs={{0,2},{2,0},{4,6},{6,4},{8,10},{10,8},{12,14},{14,12},{16,18},{18,... | collective-permute-start | bytes 344072 | tf_op jit(solution)/shard_map/ppermute | solution.py:179
  32.5 4.9 %collective-permute-start.16 = (bf16[16,3584]{1,0:T(8,128)(2,1)S(1)}, bf16[16,3584]{1,0:T(8,128)(2,1)S(1)}, u32[]{:S(2)}, u32[]{:S(2)}) collective-permute-start(bf16[16,3584]{1,0:T(8,128)(2,1)S(1)} %shard_map.84), channel_id=1, source_target_pairs={{0,4},{2,6},{4,0},{6,2},{8,12},{10,14},{12,8},{14,10},{16,20},{18,... | collective-permute-start | bytes 344072 | tf_op jit(solution)/shard_map/ppermute | solution.py:179
  33.7 6.0 %collective-permute-start.8 = (bf16[8,3584]{1,0:T(8,128)(2,1)S(1)}, bf16[8,3584]{1,0:T(8,128)(2,1)S(1)}, u32[]{:S(2)}, u32[]{:S(2)}) collective-permute-start(bf16[8,3584]{1,0:T(8,128)(2,1)S(1)} %get-tuple-element.33), channel_id=1, source_target_pairs={{0,24},{2,26},{4,28},{6,30},{8,16},{10,18},{12,20},{14,22},{16,8},... | collective-permute-start | bytes 172040 | tf_op jit(solution)/shard_map/ppermute | solution.py:179
  36.8 5.2 %collective-permute-start.9 = (bf16[8,3584]{1,0:T(8,128)(2,1)S(1)}, bf16[8,3584]{1,0:T(8,128)(2,1)S(1)}, u32[]{:S(2)}, u32[]{:S(2)}) collective-permute-start(bf16[8,3584]{1,0:T(8,128)(2,1)S(1)} %get-tuple-element.34), channel_id=1, source_target_pairs={{0,16},{2,18},{4,20},{6,22},{8,24},{10,26},{12,28},{14,30},{16,0},... | collective-permute-start | bytes 172040 | tf_op jit(solution)/shard_map/ppermute | solution.py:179
  37.4 4.9 %collective-permute-start.17 = (bf16[8,3584]{1,0:T(8,128)(2,1)S(1)}, bf16[8,3584]{1,0:T(8,128)(2,1)S(1)}, u32[]{:S(2)}, u32[]{:S(2)}) collective-permute-start(bf16[8,3584]{1,0:T(8,128)(2,1)S(1)} %get-tuple-element.41), channel_id=1, source_target_pairs={{0,8},{2,10},{4,12},{6,14},{8,0},{10,2},{12,4},{14,6},{16,24},{18,... | collective-permute-start | bytes 172040 | tf_op jit(solution)/shard_map/ppermute | solution.py:179

commit v18 on v16

--- a/solution.py
+++ b/solution.py
@@ -40,6 +40,7 @@
     capacity = row_outs[0].shape[0]
     top_count, tok_count = expert_ids.shape
     own = lax.axis_index("expert") // group_size
+    core = lax.axis_index("dp") % 2
     copy_row = iota((slot_count, tok_count), 0)
     named = jnp.zeros_like(copy_row)
     before = jnp.zeros_like(copy_row)
@@ -50,7 +51,8 @@
         here = copy_row == p
         named = jnp.where(here, placement[p], named)
         d = lax.bitwise_xor(own, p)
-        relative = jnp.where(here, slot_count - 1 - d, relative)
+        place = jnp.where(core == 0, slot_count - 1 - d, (d + slot_count - 1) % slot_count)
+        relative = jnp.where(here, place, relative)
         seen = jnp.int32(0)
         for q in range(p):
             seen = seen + (placement[q] == placement[p]).astype(jnp.int32)
@@ -170,13 +172,22 @@
     tok_count, width = tokens.shape
     capacity = tok_count * expert_ids.shape[1] // slot_count
     slots = slot_count * capacity
-    offsets = range(slot_count - 1, -1, -1)
+    offsets = [(slot_count - 1 - i, (i + 1) % slot_count) for i in range(slot_count)]
     bf16 = jnp.bfloat16
     chunk = jax.ShapeDtypeStruct((capacity, width), bf16)
     half = jax.ShapeDtypeStruct((slots // 2, width), bf16)
 
     def swap(value, offset):
         return lax.ppermute(value, "expert", [(e, e ^ offset) for e in range(n_devices)])
+
+    def across(value, even, odd):
+        parts = lax.axis_size("dp")
+        pairs = [
+            (e * parts + part, (e ^ (group_size * (odd if part % 2 else even))) * parts + part)
+            for e in range(n_devices)
+            for part in range(parts)
+        ]
+        return lax.ppermute(value, ("expert", "dp"), pairs) if even else value
 
     def local(kernel, inputs, outs, limit=16 * MIB):
         return call(kernel, inputs, [VMEM] * len(inputs), outs, limit)
@@ -195,7 +206,7 @@
         + [pltpu.VMEM(s.shape, s.dtype) for s in sources[1:]]
         + [pltpu.SemaphoreType.DMA((5,))],
     )
-    chunks = [swap(c, d * group_size) if d else c for d, c in zip(offsets, chunks)]
+    chunks = [across(c, *d) for c, d in zip(chunks, offsets)]
     terms = jax.ShapeDtypeStruct((3 * tok_count, slots // 2), bf16)
     terms = local(terms_kernel, [combine], [terms, terms])
 
@@ -244,7 +255,7 @@
         else:
             result = [swap(v, q) if q else v for q, v in enumerate(result)]
         summed += local(functools.partial(sum_kernel, len(result)), result, [chunk] * count)
-    summed = [swap(v, d * group_size) if d else v for d, v in zip(offsets, summed)]
+    summed = [across(v, *d) for v, d in zip(summed, offsets)]
     near = local(
         near_kernel,
         [terms[0]] + summed[:count],

time: 42.5 us -> 43.7 us (1.028)
  waiting for transfers between devices: 9.76 us -> 11.1 us
    ppermute x18 -> x12, starting transfers between devices: 24 us -> 14.6 us  [swap(): lax.ppermute(value, 'expert', [(e, e ^ offset) for e in range(n_devices)])]
    ppermute x0 -> x6, starting transfers between devices: none -> 9.25 us  [across(): return lax.ppermute(value, ('expert', 'dp'), pairs) if even else value]
    ppermute x0 -> x6, waiting for transfers between devices: none -> 6.14 us  [across(): return lax.ppermute(value, ('expert', 'dp'), pairs) if even else value]
    ppermute x18 -> x12, waiting for transfers between devices: 9.76 us -> 4.97 us  [swap(): lax.ppermute(value, 'expert', [(e, e ^ offset) for e in range(n_devices)])]
  transfers between devices with their start and end apart: 18 -> 18, of which waited for: 9 -> 11; matrix products, arithmetic and copies ran while one was open for 0% -> 0% of each run, Pallas kernels for 15% -> 15%
where the time goes in v18:
time: 43.7 us; the launch traced here: 43.5 us
  starting transfers between devices  23.8 us (54%)
  waiting for transfers between devices  11.1 us (25%)
  Pallas kernels  8.49 us (19%)
    ppermute x12, starting transfers between devices, swap(): lax.ppermute(value, 'expert', [(e, e ^ offset) for e in range(n_devices)])  14.6 us
    ppermute x6, starting transfers between devices, across(): return lax.ppermute(value, ('expert', 'dp'), pairs) if even else value  9.25 us
    pallas_call x14, Pallas kernels, call(): pl.pallas_call(kernel, out_shape=outs, in_specs=in_specs, out_specs=jax.t...  8.49 us
    ppermute x6, waiting for transfers between devices, across(): return lax.ppermute(value, ('expert', 'dp'), pairs) if even else value  6.14 us
    ppermute x12, waiting for transfers between devices, swap(): lax.ppermute(value, 'expert', [(e, e ^ offset) for e in range(n_devices)])  4.97 us
  transfers between devices with their start and end apart: 18, of which 11 were waited for; matrix products, arithmetic and copies ran while one was open for 0% of the time, Pallas kernels for 15%

profile of v18, /device:TPU:0, one launch (start us, length us, event | category | flops | bytes accessed | tf_op | source)
XLA Modules:
  0.0 43.5 jit_solution(12297741219268629598)
XLA Ops:
  0.0 1.2 %shard_map.73 = (bf16[8,3584]{1,0:T(8,128)(2,1)S(1)}, bf16[8,3584]{1,0:T(8,128)(2,1)S(1)}, bf16[8,3584]{1,0:T(8,128)(2,1)S(1)}, bf16[8,3584]{1,0:T(8,128)(2,1)S(1)}, f32[32,16]{1,0:T(8,128)S(1)}) custom-call(s32[4]{0:T(128)} %refs_0_.3, s32[2,16]{1,0:T(2,128)} %bitcast.3, s32[2,16]{1,0:T(2,128)} %bitcast.4, f32[2,16]{1,0:T(2,128)} %bitcast.5, ...), custom_call_target="tpu_custom_call" | custom-call | tf_op jit(solution)/shard_map/pallas_call | solution.py:155
  1.2 5.1 %collective-permute-start = (bf16[8,3584]{1,0:T(8,128)(2,1)S(1)}, bf16[8,3584]{1,0:T(8,128)(2,1)S(1)}, u32[]{:S(2)}, u32[]{:S(2)}) collective-permute-start(bf16[8,3584]{1,0:T(8,128)(2,1)S(1)} %get-tuple-element.27), channel_id=1, source_target_pairs={{0,24},{1,9},{2,26},{3,11},{4,28},{5,13},{6,30},{7,15},{8,16},{9,1... | collective-permute-start | bytes 172040 | tf_op jit(solution)/shard_map/ppermute | solution.py:190
  6.3 0.6 %collective-permute-start.10 = (bf16[8,3584]{1,0:T(8,128)(2,1)S(1)}, bf16[8,3584]{1,0:T(8,128)(2,1)S(1)}, u32[]{:S(2)}, u32[]{:S(2)}) collective-permute-start(bf16[8,3584]{1,0:T(8,128)(2,1)S(1)} %get-tuple-element.35), channel_id=1, source_target_pairs={{0,8},{1,25},{2,10},{3,27},{4,12},{5,29},{6,14},{7,31},{8,0},{9,17... | collective-permute-start | bytes 172040 | tf_op jit(solution)/shard_map/ppermute | solution.py:190
  7.1 2.1 %shard_map.75.refs_2_.refs_4_ = bf16[2,3584,256]{2,1,0:T(8,128)(2,1)S(1)} custom-call(bf16[2,3584,256]{2,1,0:T(8,128)(2,1)} %refs_0_.4, bf16[48,16]{1,0:T(8,128)(2,1)S(1)} %get-tuple-element.26.refs_1_.terms), custom_call_target="tpu_custom_call" | custom-call | bytes 3670016 | tf_op jit(solution)/shard_map/pallas_call | solution.py:155
  9.2 3.0 %collective-permute-done.1.refs_1_ = bf16[8,3584]{1,0:T(8,128)(2,1)S(1)} collective-permute-done((bf16[8,3584]{1,0:T(8,128)(2,1)S(1)}, bf16[8,3584]{1,0:T(8,128)(2,1)S(1)}, u32[]{:S(2)}, u32[]{:S(2)}) %collective-permute-start.1) | collective-permute-done | bytes 57376 | tf_op jit(solution)/shard_map/ppermute | solution.py:190
  12.2 1.6 %collective-permute-start.2 = (bf16[16,3584]{1,0:T(8,128)(2,1)S(1)}, bf16[16,3584]{1,0:T(8,128)(2,1)S(1)}, u32[]{:S(2)}, u32[]{:S(2)}) collective-permute-start(bf16[16,3584]{1,0:T(8,128)(2,1)S(1)} %shard_map.76.refs_0_), channel_id=1, source_target_pairs={{0,2},{2,0},{4,6},{6,4},{8,10},{10,8},{12,14},{14,12},{16,18},{18,... | collective-permute-start | bytes 344072 | tf_op jit(solution)/shard_map/ppermute | solution.py:181
  13.8 1.6 %collective-permute-start.11 = (bf16[16,3584]{1,0:T(8,128)(2,1)S(1)}, bf16[16,3584]{1,0:T(8,128)(2,1)S(1)}, u32[]{:S(2)}, u32[]{:S(2)}) collective-permute-start(bf16[16,3584]{1,0:T(8,128)(2,1)S(1)} %shard_map.82.refs_0_), channel_id=1, source_target_pairs={{0,4},{2,6},{4,0},{6,2},{8,12},{10,14},{12,8},{14,10},{16,20},{18,... | collective-permute-start | bytes 344072 | tf_op jit(solution)/shard_map/ppermute | solution.py:181
  15.4 0.5 %collective-permute-start.3 = (bf16[16,3584]{1,0:T(8,128)(2,1)S(1)}, bf16[16,3584]{1,0:T(8,128)(2,1)S(1)}, u32[]{:S(2)}, u32[]{:S(2)}) collective-permute-start(bf16[16,3584]{1,0:T(8,128)(2,1)S(1)} %shard_map.76.refs_0_), channel_id=1, source_target_pairs={{0,4},{2,6},{4,0},{6,2},{8,12},{10,14},{12,8},{14,10},{16,20},{18,... | collective-permute-start | bytes 344072 | tf_op jit(solution)/shard_map/ppermute | solution.py:181
  15.9 1.2 %collective-permute-done.2.refs_1_ = bf16[16,3584]{1,0:T(8,128)(2,1)S(1)} collective-permute-done((bf16[16,3584]{1,0:T(8,128)(2,1)S(1)}, bf16[16,3584]{1,0:T(8,128)(2,1)S(1)}, u32[]{:S(2)}, u32[]{:S(2)}) %collective-permute-start.2) | collective-permute-done | bytes 114720 | tf_op jit(solution)/shard_map/ppermute | solution.py:181
  17.1 2.5 %collective-permute-start.4 = (bf16[16,3584]{1,0:T(8,128)(2,1)S(1)}, bf16[16,3584]{1,0:T(8,128)(2,1)S(1)}, u32[]{:S(2)}, u32[]{:S(2)}) collective-permute-start(bf16[16,3584]{1,0:T(8,128)(2,1)S(1)} %collective-permute-done.2.refs_1_), channel_id=1, source_target_pairs={{0,4},{2,6},{4,0},{6,2},{8,12},{10,14},{12,8},{14,10},{16,20},{18,... | collective-permute-start | bytes 344072 | tf_op jit(solution)/shard_map/ppermute | solution.py:181
  19.6 1.5 %collective-permute-start.12 = (bf16[16,3584]{1,0:T(8,128)(2,1)S(1)}, bf16[16,3584]{1,0:T(8,128)(2,1)S(1)}, u32[]{:S(2)}, u32[]{:S(2)}) collective-permute-start(bf16[16,3584]{1,0:T(8,128)(2,1)S(1)} %shard_map.82.refs_0_), channel_id=1, source_target_pairs={{0,2},{2,0},{4,6},{6,4},{8,10},{10,8},{12,14},{14,12},{16,18},{18,... | collective-permute-start | bytes 344072 | tf_op jit(solution)/shard_map/ppermute | solution.py:181
  21.0 0.5 %collective-permute-start.13 = (bf16[16,3584]{1,0:T(8,128)(2,1)S(1)}, bf16[16,3584]{1,0:T(8,128)(2,1)S(1)}, u32[]{:S(2)}, u32[]{:S(2)}) collective-permute-start(bf16[16,3584]{1,0:T(8,128)(2,1)S(1)} %collective-permute-done.11.refs_1_), channel_id=1, source_target_pairs={{0,2},{2,0},{4,6},{6,4},{8,10},{10,8},{12,14},{14,12},{16,18},{18,... | collective-permute-start | bytes 344072 | tf_op jit(solution)/shard_map/ppermute | solution.py:181
  21.6 1.5 %shard_map.77.refs_5_ = bf16[256,3584]{1,0:T(8,128)(2,1)S(1)} custom-call(bf16[256,3584]{1,0:T(8,128)(2,1)} %refs_0_.5, bf16[48,16]{1,0:T(8,128)(2,1)S(1)} %get-tuple-element.25.refs_1_.terms), custom_call_target="tpu_custom_call" | custom-call | bytes 1835008 | tf_op jit(solution)/shard_map/pallas_call | solution.py:155
  23.1 0.3 collective-permute-done.4.refs_3_
  23.3 1.2 %shard_map.78 = (bf16[16,3584]{1,0:T(8,128)(2,1)S(1)}, bf16[16,3584]{1,0:T(8,128)(2,1)S(1)}, bf16[16,3584]{1,0:T(8,128)(2,1)S(1)}, bf16[16,3584]{1,0:T(8,128)(2,1)S(1)}) custom-call(bf16[16,3584]{1,0:T(8,128)(2,1)S(1)} %shard_map.76.refs_0_, bf16[16,3584]{1,0:T(8,128)(2,1)S(1)} %collective-permute-done.2.refs_1_, ...), custom_call_target="tpu_custom_call" | custom-call | tf_op jit(solution)/shard_map/pallas_call | solution.py:155
  24.5 2.0 %collective-permute-start.6 = (bf16[16,3584]{1,0:T(8,128)(2,1)S(1)}, bf16[16,3584]{1,0:T(8,128)(2,1)S(1)}, u32[]{:S(2)}, u32[]{:S(2)}) collective-permute-start(bf16[16,3584]{1,0:T(8,128)(2,1)S(1)} %get-tuple-element.32), channel_id=1, source_target_pairs={{0,4},{2,6},{4,0},{6,2},{8,12},{10,14},{12,8},{14,10},{16,20},{18,... | collective-permute-start | bytes 344072 | tf_op jit(solution)/shard_map/ppermute | solution.py:181
  26.5 0.6 %collective-permute-done.13.refs_3_ = bf16[16,3584]{1,0:T(8,128)(2,1)S(1)} collective-permute-done((bf16[16,3584]{1,0:T(8,128)(2,1)S(1)}, bf16[16,3584]{1,0:T(8,128)(2,1)S(1)}, u32[]{:S(2)}, u32[]{:S(2)}) %collective-permute-start.13) | collective-permute-done | bytes 114720 | tf_op jit(solution)/shard_map/ppermute | solution.py:181
  27.1 1.2 %shard_map.83 = (bf16[16,3584]{1,0:T(8,128)(2,1)S(1)}, bf16[16,3584]{1,0:T(8,128)(2,1)S(1)}, bf16[16,3584]{1,0:T(8,128)(2,1)S(1)}, bf16[16,3584]{1,0:T(8,128)(2,1)S(1)}) custom-call(bf16[16,3584]{1,0:T(8,128)(2,1)S(1)} %shard_map.82.refs_0_, bf16[16,3584]{1,0:T(8,128)(2,1)S(1)} %collective-permute-done.11.refs_1_, ...), custom_call_target="tpu_custom_call" | custom-call | tf_op jit(solution)/shard_map/pallas_call | solution.py:155
  28.2 1.0 %collective-permute-start.15 = (bf16[16,3584]{1,0:T(8,128)(2,1)S(1)}, bf16[16,3584]{1,0:T(8,128)(2,1)S(1)}, u32[]{:S(2)}, u32[]{:S(2)}) collective-permute-start(bf16[16,3584]{1,0:T(8,128)(2,1)S(1)} %get-tuple-element.40), channel_id=1, source_target_pairs={{0,2},{2,0},{4,6},{6,4},{8,10},{10,8},{12,14},{14,12},{16,18},{18,... | collective-permute-start | bytes 344072 | tf_op jit(solution)/shard_map/ppermute | solution.py:181
  29.2 0.5 %collective-permute-done.6.refs_1_ = bf16[16,3584]{1,0:T(8,128)(2,1)S(1)} collective-permute-done((bf16[16,3584]{1,0:T(8,128)(2,1)S(1)}, bf16[16,3584]{1,0:T(8,128)(2,1)S(1)}, u32[]{:S(2)}, u32[]{:S(2)}) %collective-permute-start.6) | collective-permute-done | bytes 114720 | tf_op jit(solution)/shard_map/ppermute | solution.py:181
  29.8 1.7 %collective-permute-start.7 = (bf16[16,3584]{1,0:T(8,128)(2,1)S(1)}, bf16[16,3584]{1,0:T(8,128)(2,1)S(1)}, u32[]{:S(2)}, u32[]{:S(2)}) collective-permute-start(bf16[16,3584]{1,0:T(8,128)(2,1)S(1)} %shard_map.79), channel_id=1, source_target_pairs={{0,2},{2,0},{4,6},{6,4},{8,10},{10,8},{12,14},{14,12},{16,18},{18,... | collective-permute-start | bytes 344072 | tf_op jit(solution)/shard_map/ppermute | solution.py:181
  31.5 0.4 collective-permute-start.14
  31.9 1.2 %collective-permute-done.15.refs_1_ = bf16[16,3584]{1,0:T(8,128)(2,1)S(1)} collective-permute-done((bf16[16,3584]{1,0:T(8,128)(2,1)S(1)}, bf16[16,3584]{1,0:T(8,128)(2,1)S(1)}, u32[]{:S(2)}, u32[]{:S(2)}) %collective-permute-start.15) | collective-permute-done | bytes 114720 | tf_op jit(solution)/shard_map/ppermute | solution.py:181
  33.1 1.3 %collective-permute-start.16 = (bf16[16,3584]{1,0:T(8,128)(2,1)S(1)}, bf16[16,3584]{1,0:T(8,128)(2,1)S(1)}, u32[]{:S(2)}, u32[]{:S(2)}) collective-permute-start(bf16[16,3584]{1,0:T(8,128)(2,1)S(1)} %shard_map.84), channel_id=1, source_target_pairs={{0,4},{2,6},{4,0},{6,2},{8,12},{10,14},{12,8},{14,10},{16,20},{18,... | collective-permute-start | bytes 344072 | tf_op jit(solution)/shard_map/ppermute | solution.py:181
  34.7 2.3 %collective-permute-start.8 = (bf16[8,3584]{1,0:T(8,128)(2,1)S(1)}, bf16[8,3584]{1,0:T(8,128)(2,1)S(1)}, u32[]{:S(2)}, u32[]{:S(2)}) collective-permute-start(bf16[8,3584]{1,0:T(8,128)(2,1)S(1)} %get-tuple-element.33), channel_id=1, source_target_pairs={{0,24},{1,9},{2,26},{3,11},{4,28},{5,13},{6,30},{7,15},{8,16},{9,1... | collective-permute-start | bytes 172040 | tf_op jit(solution)/shard_map/ppermute | solution.py:190
  36.9 1.0 %collective-permute-done.16.refs_2_ = bf16[16,3584]{1,0:T(8,128)(2,1)S(1)} collective-permute-done((bf16[16,3584]{1,0:T(8,128)(2,1)S(1)}, bf16[16,3584]{1,0:T(8,128)(2,1)S(1)}, u32[]{:S(2)}, u32[]{:S(2)}) %collective-permute-start.16) | collective-permute-done | bytes 114720 | tf_op jit(solution)/shard_map/ppermute | solution.py:181
  38.0 1.2 %collective-permute-start.17 = (bf16[8,3584]{1,0:T(8,128)(2,1)S(1)}, bf16[8,3584]{1,0:T(8,128)(2,1)S(1)}, u32[]{:S(2)}, u32[]{:S(2)}) collective-permute-start(bf16[8,3584]{1,0:T(8,128)(2,1)S(1)} %get-tuple-element.41), channel_id=1, source_target_pairs={{0,8},{1,25},{2,10},{3,27},{4,12},{5,29},{6,14},{7,31},{8,0},{9,17... | collective-permute-start | bytes 172040 | tf_op jit(solution)/shard_map/ppermute | solution.py:190
  39.3 1.5 %collective-permute-done.8.refs_0_ = bf16[8,3584]{1,0:T(8,128)(2,1)S(1)} collective-permute-done((bf16[8,3584]{1,0:T(8,128)(2,1)S(1)}, bf16[8,3584]{1,0:T(8,128)(2,1)S(1)}, u32[]{:S(2)}, u32[]{:S(2)}) %collective-permute-start.8) | collective-permute-done | bytes 57376 | tf_op jit(solution)/shard_map/ppermute | solution.py:190
  40.7 1.3 %collective-permute-done.9.refs_1_ = bf16[8,3584]{1,0:T(8,128)(2,1)S(1)} collective-permute-done((bf16[8,3584]{1,0:T(8,128)(2,1)S(1)}, bf16[8,3584]{1,0:T(8,128)(2,1)S(1)}, u32[]{:S(2)}, u32[]{:S(2)}) %collective-permute-start.9) | collective-permute-done | bytes 57376 | tf_op jit(solution)/shard_map/ppermute | solution.py:190
  42.0 0.2 shard_map.81.near
  42.3 0.4 collective-permute-done.17.refs_0_
  42.6 0.9 %shard_map.86 = bf16[16,3584]{1,0:T(8,128)(2,1)} custom-call(bf16[48,16]{1,0:T(8,128)(2,1)S(1)} %get-tuple-element.25.refs_1_.terms, f32[16,3584]{1,0:T(8,128)S(1)} %shard_map.81.near, bf16[8,3584]{1,0:T(8,128)(2,1)S(1)} %collective-permute-done.17.refs_0_, bf16[8,3584]{1,0:T(8,128)(2,1)S(1)} %get-tuple-element.42.refs_1_), custom_call_target="tpu_custom_call" | custom-call | tf_op jit(solution)/shard_map/pallas_call | solution.py:155
  (18 shorter events, 0.6 us)
Async XLA Ops:
  1.2 8.0 %collective-permute-start = (bf16[8,3584]{1,0:T(8,128)(2,1)S(1)}, bf16[8,3584]{1,0:T(8,128)(2,1)S(1)}, u32[]{:S(2)}, u32[]{:S(2)}) collective-permute-start(bf16[8,3584]{1,0:T(8,128)(2,1)S(1)} %get-tuple-element.27), channel_id=1, source_target_pairs={{0,24},{1,9},{2,26},{3,11},{4,28},{5,13},{6,30},{7,15},{8,16},{9,1... | collective-permute-start | bytes 172040 | tf_op jit(solution)/shard_map/ppermute | solution.py:190
  6.3 5.9 %collective-permute-start.1 = (bf16[8,3584]{1,0:T(8,128)(2,1)S(1)}, bf16[8,3584]{1,0:T(8,128)(2,1)S(1)}, u32[]{:S(2)}, u32[]{:S(2)}) collective-permute-start(bf16[8,3584]{1,0:T(8,128)(2,1)S(1)} %get-tuple-element.28), channel_id=1, source_target_pairs={{0,16},{1,17},{2,18},{3,19},{4,20},{5,21},{6,22},{7,23},{8,24},{9,... | collective-permute-start | bytes 172040 | tf_op jit(solution)/shard_map/ppermute | solution.py:190
  6.3 7.5 %collective-permute-start.10 = (bf16[8,3584]{1,0:T(8,128)(2,1)S(1)}, bf16[8,3584]{1,0:T(8,128)(2,1)S(1)}, u32[]{:S(2)}, u32[]{:S(2)}) collective-permute-start(bf16[8,3584]{1,0:T(8,128)(2,1)S(1)} %get-tuple-element.35), channel_id=1, source_target_pairs={{0,8},{1,25},{2,10},{3,27},{4,12},{5,29},{6,14},{7,31},{8,0},{9,17... | collective-permute-start | bytes 172040 | tf_op jit(solution)/shard_map/ppermute | solution.py:190
  12.2 4.9 %collective-permute-start.2 = (bf16[16,3584]{1,0:T(8,128)(2,1)S(1)}, bf16[16,3584]{1,0:T(8,128)(2,1)S(1)}, u32[]{:S(2)}, u32[]{:S(2)}) collective-permute-start(bf16[16,3584]{1,0:T(8,128)(2,1)S(1)} %shard_map.76.refs_0_), channel_id=1, source_target_pairs={{0,2},{2,0},{4,6},{6,4},{8,10},{10,8},{12,14},{14,12},{16,18},{18,... | collective-permute-start | bytes 344072 | tf_op jit(solution)/shard_map/ppermute | solution.py:181
  13.8 7.3 %collective-permute-start.11 = (bf16[16,3584]{1,0:T(8,128)(2,1)S(1)}, bf16[16,3584]{1,0:T(8,128)(2,1)S(1)}, u32[]{:S(2)}, u32[]{:S(2)}) collective-permute-start(bf16[16,3584]{1,0:T(8,128)(2,1)S(1)} %shard_map.82.refs_0_), channel_id=1, source_target_pairs={{0,4},{2,6},{4,0},{6,2},{8,12},{10,14},{12,8},{14,10},{16,20},{18,... | collective-permute-start | bytes 344072 | tf_op jit(solution)/shard_map/ppermute | solution.py:181
  15.4 7.7 %collective-permute-start.3 = (bf16[16,3584]{1,0:T(8,128)(2,1)S(1)}, bf16[16,3584]{1,0:T(8,128)(2,1)S(1)}, u32[]{:S(2)}, u32[]{:S(2)}) collective-permute-start(bf16[16,3584]{1,0:T(8,128)(2,1)S(1)} %shard_map.76.refs_0_), channel_id=1, source_target_pairs={{0,4},{2,6},{4,0},{6,2},{8,12},{10,14},{12,8},{14,10},{16,20},{18,... | collective-permute-start | bytes 344072 | tf_op jit(solution)/shard_map/ppermute | solution.py:181
  17.1 6.3 %collective-permute-start.4 = (bf16[16,3584]{1,0:T(8,128)(2,1)S(1)}, bf16[16,3584]{1,0:T(8,128)(2,1)S(1)}, u32[]{:S(2)}, u32[]{:S(2)}) collective-permute-start(bf16[16,3584]{1,0:T(8,128)(2,1)S(1)} %collective-permute-done.2.refs_1_), channel_id=1, source_target_pairs={{0,4},{2,6},{4,0},{6,2},{8,12},{10,14},{12,8},{14,10},{16,20},{18,... | collective-permute-start | bytes 344072 | tf_op jit(solution)/shard_map/ppermute | solution.py:181
  19.6 6.9 %collective-permute-start.12 = (bf16[16,3584]{1,0:T(8,128)(2,1)S(1)}, bf16[16,3584]{1,0:T(8,128)(2,1)S(1)}, u32[]{:S(2)}, u32[]{:S(2)}) collective-permute-start(bf16[16,3584]{1,0:T(8,128)(2,1)S(1)} %shard_map.82.refs_0_), channel_id=1, source_target_pairs={{0,2},{2,0},{4,6},{6,4},{8,10},{10,8},{12,14},{14,12},{16,18},{18,... | collective-permute-start | bytes 344072 | tf_op jit(solution)/shard_map/ppermute | solution.py:181
  21.0 6.0 %collective-permute-start.13 = (bf16[16,3584]{1,0:T(8,128)(2,1)S(1)}, bf16[16,3584]{1,0:T(8,128)(2,1)S(1)}, u32[]{:S(2)}, u32[]{:S(2)}) collective-permute-start(bf16[16,3584]{1,0:T(8,128)(2,1)S(1)} %collective-permute-done.11.refs_1_), channel_id=1, source_target_pairs={{0,2},{2,0},{4,6},{6,4},{8,10},{10,8},{12,14},{14,12},{16,18},{18,... | collective-permute-start | bytes 344072 | tf_op jit(solution)/shard_map/ppermute | solution.py:181
  24.5 5.3 %collective-permute-start.6 = (bf16[16,3584]{1,0:T(8,128)(2,1)S(1)}, bf16[16,3584]{1,0:T(8,128)(2,1)S(1)}, u32[]{:S(2)}, u32[]{:S(2)}) collective-permute-start(bf16[16,3584]{1,0:T(8,128)(2,1)S(1)} %get-tuple-element.32), channel_id=1, source_target_pairs={{0,4},{2,6},{4,0},{6,2},{8,12},{10,14},{12,8},{14,10},{16,20},{18,... | collective-permute-start | bytes 344072 | tf_op jit(solution)/shard_map/ppermute | solution.py:181
  28.2 4.9 %collective-permute-start.15 = (bf16[16,3584]{1,0:T(8,128)(2,1)S(1)}, bf16[16,3584]{1,0:T(8,128)(2,1)S(1)}, u32[]{:S(2)}, u32[]{:S(2)}) collective-permute-start(bf16[16,3584]{1,0:T(8,128)(2,1)S(1)} %get-tuple-element.40), channel_id=1, source_target_pairs={{0,2},{2,0},{4,6},{6,4},{8,10},{10,8},{12,14},{14,12},{16,18},{18,... | collective-permute-start | bytes 344072 | tf_op jit(solution)/shard_map/ppermute | solution.py:181
  29.2 5.2 %collective-permute-start.5 = (bf16[16,3584]{1,0:T(8,128)(2,1)S(1)}, bf16[16,3584]{1,0:T(8,128)(2,1)S(1)}, u32[]{:S(2)}, u32[]{:S(2)}) collective-permute-start(bf16[16,3584]{1,0:T(8,128)(2,1)S(1)} %get-tuple-element.30), channel_id=1, source_target_pairs={{0,4},{2,6},{4,0},{6,2},{8,12},{10,14},{12,8},{14,10},{16,20},{18,... | collective-permute-start | bytes 344072 | tf_op jit(solution)/shard_map/ppermute | solution.py:181
  29.8 4.9 %collective-permute-start.7 = (bf16[16,3584]{1,0:T(8,128)(2,1)S(1)}, bf16[16,3584]{1,0:T(8,128)(2,1)S(1)}, u32[]{:S(2)}, u32[]{:S(2)}) collective-permute-start(bf16[16,3584]{1,0:T(8,128)(2,1)S(1)} %shard_map.79), channel_id=1, source_target_pairs={{0,2},{2,0},{4,6},{6,4},{8,10},{10,8},{12,14},{14,12},{16,18},{18,... | collective-permute-start | bytes 344072 | tf_op jit(solution)/shard_map/ppermute | solution.py:181
  31.5 5.5 %collective-permute-start.14 = (bf16[16,3584]{1,0:T(8,128)(2,1)S(1)}, bf16[16,3584]{1,0:T(8,128)(2,1)S(1)}, u32[]{:S(2)}, u32[]{:S(2)}) collective-permute-start(bf16[16,3584]{1,0:T(8,128)(2,1)S(1)} %get-tuple-element.38), channel_id=1, source_target_pairs={{0,2},{2,0},{4,6},{6,4},{8,10},{10,8},{12,14},{14,12},{16,18},{18,... | collective-permute-start | bytes 344072 | tf_op jit(solution)/shard_map/ppermute | solution.py:181
  33.1 4.9 %collective-permute-start.16 = (bf16[16,3584]{1,0:T(8,128)(2,1)S(1)}, bf16[16,3584]{1,0:T(8,128)(2,1)S(1)}, u32[]{:S(2)}, u32[]{:S(2)}) collective-permute-start(bf16[16,3584]{1,0:T(8,128)(2,1)S(1)} %shard_map.84), channel_id=1, source_target_pairs={{0,4},{2,6},{4,0},{6,2},{8,12},{10,14},{12,8},{14,10},{16,20},{18,... | collective-permute-start | bytes 344072 | tf_op jit(solution)/shard_map/ppermute | solution.py:181
  34.7 6.0 %collective-permute-start.8 = (bf16[8,3584]{1,0:T(8,128)(2,1)S(1)}, bf16[8,3584]{1,0:T(8,128)(2,1)S(1)}, u32[]{:S(2)}, u32[]{:S(2)}) collective-permute-start(bf16[8,3584]{1,0:T(8,128)(2,1)S(1)} %get-tuple-element.33), channel_id=1, source_target_pairs={{0,24},{1,9},{2,26},{3,11},{4,28},{5,13},{6,30},{7,15},{8,16},{9,1... | collective-permute-start | bytes 172040 | tf_op jit(solution)/shard_map/ppermute | solution.py:190
  36.9 5.1 %collective-permute-start.9 = (bf16[8,3584]{1,0:T(8,128)(2,1)S(1)}, bf16[8,3584]{1,0:T(8,128)(2,1)S(1)}, u32[]{:S(2)}, u32[]{:S(2)}) collective-permute-start(bf16[8,3584]{1,0:T(8,128)(2,1)S(1)} %get-tuple-element.34), channel_id=1, source_target_pairs={{0,16},{1,17},{2,18},{3,19},{4,20},{5,21},{6,22},{7,23},{8,24},{9,... | collective-permute-start | bytes 172040 | tf_op jit(solution)/shard_map/ppermute | solution.py:190
  38.0 4.6 %collective-permute-start.17 = (bf16[8,3584]{1,0:T(8,128)(2,1)S(1)}, bf16[8,3584]{1,0:T(8,128)(2,1)S(1)}, u32[]{:S(2)}, u32[]{:S(2)}) collective-permute-start(bf16[8,3584]{1,0:T(8,128)(2,1)S(1)} %get-tuple-element.41), channel_id=1, source_target_pairs={{0,8},{1,25},{2,10},{3,27},{4,12},{5,29},{6,14},{7,31},{8,0},{9,17... | collective-permute-start | bytes 172040 | tf_op jit(solution)/shard_map/ppermute | solution.py:190

commit v19 on v16

--- a/solution.py
+++ b/solution.py
@@ -228,7 +228,7 @@
             held = [own, held[a], held[b], swap(held[a], b)]
         else:
             held = [swap(own, q) if q else own for q in range(group_size)]
-        earlier = []
+        earlier = held[1:3]
         result = local(
             functools.partial(expert_kernel, group_size),
             held + [w_in, w_out],

time: 42.5 us -> 45.7 us (1.075)
  waiting for transfers between devices: 9.76 us -> 17 us
  starting transfers between devices: 24 us -> 20 us
    ppermute x18, waiting for transfers between devices: 9.76 us -> 17 us  [swap(): lax.ppermute(value, 'expert', [(e, e ^ offset) for e in range(n_devices)])]
    ppermute x18, starting transfers between devices: 24 us -> 20 us  [swap(): lax.ppermute(value, 'expert', [(e, e ^ offset) for e in range(n_devices)])]
  transfers between devices with their start and end apart: 18 -> 18, of which waited for: 9 -> 11; matrix products, arithmetic and copies ran while one was open for 0% -> 0% of each run, Pallas kernels for 15% -> 14%
where the time goes in v19:
time: 45.7 us; the launch traced here: 45.5 us
  starting transfers between devices  20 us (44%)
  waiting for transfers between devices  17 us (37%)
  Pallas kernels  8.5 us (19%)
    ppermute x18, starting transfers between devices, swap(): lax.ppermute(value, 'expert', [(e, e ^ offset) for e in range(n_devices)])  20 us
    ppermute x18, waiting for transfers between devices, swap(): lax.ppermute(value, 'expert', [(e, e ^ offset) for e in range(n_devices)])  17 us
    pallas_call x14, Pallas kernels, call(): pl.pallas_call(kernel, out_shape=outs, in_specs=in_specs, out_specs=jax.t...  8.5 us
  transfers between devices with their start and end apart: 18, of which 11 were waited for; matrix products, arithmetic and copies ran while one was open for 0% of the time, Pallas kernels for 14%

profile of v19, /device:TPU:0, one launch (start us, length us, event | category | flops | bytes accessed | tf_op | source)
XLA Modules:
  0.0 45.5 jit_solution(11809828696655403031)
XLA Ops:
  0.0 1.2 %shard_map.73 = (bf16[8,3584]{1,0:T(8,128)(2,1)S(1)}, bf16[8,3584]{1,0:T(8,128)(2,1)S(1)}, bf16[8,3584]{1,0:T(8,128)(2,1)S(1)}, bf16[8,3584]{1,0:T(8,128)(2,1)S(1)}, f32[32,16]{1,0:T(8,128)S(1)}) custom-call(s32[4]{0:T(128)} %refs_0_.3, s32[2,16]{1,0:T(2,128)} %bitcast.3, s32[2,16]{1,0:T(2,128)} %bitcast.4, f32[2,16]{1,0:T(2,128)} %bitcast.5, ...), custom_call_target="tpu_custom_call" | custom-call | tf_op jit(solution)/shard_map/pallas_call | solution.py:153
  1.2 5.1 %collective-permute-start = (bf16[8,3584]{1,0:T(8,128)(2,1)S(1)}, bf16[8,3584]{1,0:T(8,128)(2,1)S(1)}, u32[]{:S(2)}, u32[]{:S(2)}) collective-permute-start(bf16[8,3584]{1,0:T(8,128)(2,1)S(1)} %get-tuple-element.27), channel_id=1, source_target_pairs={{0,24},{2,26},{4,28},{6,30},{8,16},{10,18},{12,20},{14,22},{16,8},... | collective-permute-start | bytes 172040 | tf_op jit(solution)/shard_map/ppermute | solution.py:179
  6.3 0.2 shard_map.74
  6.5 2.1 %shard_map.75.refs_2_.refs_4_ = bf16[2,3584,256]{2,1,0:T(8,128)(2,1)S(1)} custom-call(bf16[2,3584,256]{2,1,0:T(8,128)(2,1)} %refs_0_.4, bf16[48,16]{1,0:T(8,128)(2,1)S(1)} %get-tuple-element.26.refs_1_.terms), custom_call_target="tpu_custom_call" | custom-call | bytes 3670016 | tf_op jit(solution)/shard_map/pallas_call | solution.py:153
  8.6 0.1 collective-permute-done.refs_0_
  8.7 2.7 %collective-permute-done.1.refs_1_ = bf16[8,3584]{1,0:T(8,128)(2,1)S(1)} collective-permute-done((bf16[8,3584]{1,0:T(8,128)(2,1)S(1)}, bf16[8,3584]{1,0:T(8,128)(2,1)S(1)}, u32[]{:S(2)}, u32[]{:S(2)}) %collective-permute-start.1) | collective-permute-done | bytes 57376 | tf_op jit(solution)/shard_map/ppermute | solution.py:179
  11.4 1.6 %collective-permute-start.2 = (bf16[16,3584]{1,0:T(8,128)(2,1)S(1)}, bf16[16,3584]{1,0:T(8,128)(2,1)S(1)}, u32[]{:S(2)}, u32[]{:S(2)}) collective-permute-start(bf16[16,3584]{1,0:T(8,128)(2,1)S(1)} %shard_map.76.refs_0_), channel_id=1, source_target_pairs={{0,2},{2,0},{4,6},{6,4},{8,10},{10,8},{12,14},{14,12},{16,18},{18,... | collective-permute-start | bytes 344072 | tf_op jit(solution)/shard_map/ppermute | solution.py:179
  12.9 1.5 %collective-permute-start.3 = (bf16[16,3584]{1,0:T(8,128)(2,1)S(1)}, bf16[16,3584]{1,0:T(8,128)(2,1)S(1)}, u32[]{:S(2)}, u32[]{:S(2)}) collective-permute-start(bf16[16,3584]{1,0:T(8,128)(2,1)S(1)} %shard_map.76.refs_0_), channel_id=1, source_target_pairs={{0,4},{2,6},{4,0},{6,2},{8,12},{10,14},{12,8},{14,10},{16,20},{18,... | collective-permute-start | bytes 344072 | tf_op jit(solution)/shard_map/ppermute | solution.py:179
  14.5 4.2 %collective-permute-done.10.refs_0_ = bf16[8,3584]{1,0:T(8,128)(2,1)S(1)} collective-permute-done((bf16[8,3584]{1,0:T(8,128)(2,1)S(1)}, bf16[8,3584]{1,0:T(8,128)(2,1)S(1)}, u32[]{:S(2)}, u32[]{:S(2)}) %collective-permute-start.10) | collective-permute-done | bytes 57376 | tf_op jit(solution)/shard_map/ppermute | solution.py:179
  18.7 0.7 %collective-permute-start.11 = (bf16[16,3584]{1,0:T(8,128)(2,1)S(1)}, bf16[16,3584]{1,0:T(8,128)(2,1)S(1)}, u32[]{:S(2)}, u32[]{:S(2)}) collective-permute-start(bf16[16,3584]{1,0:T(8,128)(2,1)S(1)} %shard_map.82.refs_0_), channel_id=1, source_target_pairs={{0,4},{2,6},{4,0},{6,2},{8,12},{10,14},{12,8},{14,10},{16,20},{18,... | collective-permute-start | bytes 344072 | tf_op jit(solution)/shard_map/ppermute | solution.py:179
  19.3 1.4 %collective-permute-start.4 = (bf16[16,3584]{1,0:T(8,128)(2,1)S(1)}, bf16[16,3584]{1,0:T(8,128)(2,1)S(1)}, u32[]{:S(2)}, u32[]{:S(2)}) collective-permute-start(bf16[16,3584]{1,0:T(8,128)(2,1)S(1)} %collective-permute-done.2.refs_1_.refs_2_), channel_id=1, source_target_pairs={{0,4},{2,6},{4,0},{6,2},{8,12},{10,14},{12,8},{14,10},{16,20},{18,... | collective-permute-start | bytes 344072 | tf_op jit(solution)/shard_map/ppermute | solution.py:179
  20.8 0.5 %collective-permute-start.12 = (bf16[16,3584]{1,0:T(8,128)(2,1)S(1)}, bf16[16,3584]{1,0:T(8,128)(2,1)S(1)}, u32[]{:S(2)}, u32[]{:S(2)}) collective-permute-start(bf16[16,3584]{1,0:T(8,128)(2,1)S(1)} %shard_map.82.refs_0_), channel_id=1, source_target_pairs={{0,2},{2,0},{4,6},{6,4},{8,10},{10,8},{12,14},{14,12},{16,18},{18,... | collective-permute-start | bytes 344072 | tf_op jit(solution)/shard_map/ppermute | solution.py:179
  21.3 2.2 %collective-permute-done.11.refs_1_ = bf16[16,3584]{1,0:T(8,128)(2,1)S(1)} collective-permute-done((bf16[16,3584]{1,0:T(8,128)(2,1)S(1)}, bf16[16,3584]{1,0:T(8,128)(2,1)S(1)}, u32[]{:S(2)}, u32[]{:S(2)}) %collective-permute-start.11) | collective-permute-done | bytes 114720 | tf_op jit(solution)/shard_map/ppermute | solution.py:179
  23.5 0.5 %collective-permute-start.13 = (bf16[16,3584]{1,0:T(8,128)(2,1)S(1)}, bf16[16,3584]{1,0:T(8,128)(2,1)S(1)}, u32[]{:S(2)}, u32[]{:S(2)}) collective-permute-start(bf16[16,3584]{1,0:T(8,128)(2,1)S(1)} %collective-permute-done.11.refs_1_), channel_id=1, source_target_pairs={{0,2},{2,0},{4,6},{6,4},{8,10},{10,8},{12,14},{14,12},{16,18},{18,... | collective-permute-start | bytes 344072 | tf_op jit(solution)/shard_map/ppermute | solution.py:179
  24.1 1.5 %shard_map.77.refs_5_ = bf16[256,3584]{1,0:T(8,128)(2,1)S(1)} custom-call(bf16[256,3584]{1,0:T(8,128)(2,1)} %refs_0_.5, bf16[48,16]{1,0:T(8,128)(2,1)S(1)} %get-tuple-element.25.refs_1_.terms), custom_call_target="tpu_custom_call" | custom-call | bytes 1835008 | tf_op jit(solution)/shard_map/pallas_call | solution.py:153
  25.5 1.2 %shard_map.78 = (bf16[16,3584]{1,0:T(8,128)(2,1)S(1)}, bf16[16,3584]{1,0:T(8,128)(2,1)S(1)}, bf16[16,3584]{1,0:T(8,128)(2,1)S(1)}, bf16[16,3584]{1,0:T(8,128)(2,1)S(1)}) custom-call(bf16[16,3584]{1,0:T(8,128)(2,1)S(1)} %shard_map.76.refs_0_, bf16[16,3584]{1,0:T(8,128)(2,1)S(1)} %collective-permute-done.2.refs_1_.refs_2_, ...), custom_call_target="tpu_custom_call" | custom-call | tf_op jit(solution)/shard_map/pallas_call | solution.py:153
  26.7 0.7 %collective-permute-start.6 = (bf16[16,3584]{1,0:T(8,128)(2,1)S(1)}, bf16[16,3584]{1,0:T(8,128)(2,1)S(1)}, u32[]{:S(2)}, u32[]{:S(2)}) collective-permute-start(bf16[16,3584]{1,0:T(8,128)(2,1)S(1)} %get-tuple-element.32), channel_id=1, source_target_pairs={{0,4},{2,6},{4,0},{6,2},{8,12},{10,14},{12,8},{14,10},{16,20},{18,... | collective-permute-start | bytes 344072 | tf_op jit(solution)/shard_map/ppermute | solution.py:179
  27.4 1.5 %collective-permute-done.13.refs_3_ = bf16[16,3584]{1,0:T(8,128)(2,1)S(1)} collective-permute-done((bf16[16,3584]{1,0:T(8,128)(2,1)S(1)}, bf16[16,3584]{1,0:T(8,128)(2,1)S(1)}, u32[]{:S(2)}, u32[]{:S(2)}) %collective-permute-start.13) | collective-permute-done | bytes 114720 | tf_op jit(solution)/shard_map/ppermute | solution.py:179
  28.8 1.2 %shard_map.83 = (bf16[16,3584]{1,0:T(8,128)(2,1)S(1)}, bf16[16,3584]{1,0:T(8,128)(2,1)S(1)}, bf16[16,3584]{1,0:T(8,128)(2,1)S(1)}, bf16[16,3584]{1,0:T(8,128)(2,1)S(1)}) custom-call(bf16[16,3584]{1,0:T(8,128)(2,1)S(1)} %shard_map.82.refs_0_, bf16[16,3584]{1,0:T(8,128)(2,1)S(1)} %collective-permute-done.11.refs_1_, ...), custom_call_target="tpu_custom_call" | custom-call | tf_op jit(solution)/shard_map/pallas_call | solution.py:153
  30.1 1.4 %collective-permute-start.5 = (bf16[16,3584]{1,0:T(8,128)(2,1)S(1)}, bf16[16,3584]{1,0:T(8,128)(2,1)S(1)}, u32[]{:S(2)}, u32[]{:S(2)}) collective-permute-start(bf16[16,3584]{1,0:T(8,128)(2,1)S(1)} %get-tuple-element.30), channel_id=1, source_target_pairs={{0,4},{2,6},{4,0},{6,2},{8,12},{10,14},{12,8},{14,10},{16,20},{18,... | collective-permute-start | bytes 344072 | tf_op jit(solution)/shard_map/ppermute | solution.py:179
  31.6 1.9 %collective-permute-start.7 = (bf16[16,3584]{1,0:T(8,128)(2,1)S(1)}, bf16[16,3584]{1,0:T(8,128)(2,1)S(1)}, u32[]{:S(2)}, u32[]{:S(2)}) collective-permute-start(bf16[16,3584]{1,0:T(8,128)(2,1)S(1)} %shard_map.79), channel_id=1, source_target_pairs={{0,2},{2,0},{4,6},{6,4},{8,10},{10,8},{12,14},{14,12},{16,18},{18,... | collective-permute-start | bytes 344072 | tf_op jit(solution)/shard_map/ppermute | solution.py:179
  33.5 0.2 collective-permute-start.14
  33.7 1.2 %collective-permute-done.15.refs_1_ = bf16[16,3584]{1,0:T(8,128)(2,1)S(1)} collective-permute-done((bf16[16,3584]{1,0:T(8,128)(2,1)S(1)}, bf16[16,3584]{1,0:T(8,128)(2,1)S(1)}, u32[]{:S(2)}, u32[]{:S(2)}) %collective-permute-start.15) | collective-permute-done | bytes 114720 | tf_op jit(solution)/shard_map/ppermute | solution.py:179
  34.9 0.3 collective-permute-start.16
  35.2 1.2 %collective-permute-done.7.refs_2_ = bf16[16,3584]{1,0:T(8,128)(2,1)S(1)} collective-permute-done((bf16[16,3584]{1,0:T(8,128)(2,1)S(1)}, bf16[16,3584]{1,0:T(8,128)(2,1)S(1)}, u32[]{:S(2)}, u32[]{:S(2)}) %collective-permute-start.7) | collective-permute-done | bytes 114720 | tf_op jit(solution)/shard_map/ppermute | solution.py:179
  36.5 2.7 %collective-permute-start.8 = (bf16[8,3584]{1,0:T(8,128)(2,1)S(1)}, bf16[8,3584]{1,0:T(8,128)(2,1)S(1)}, u32[]{:S(2)}, u32[]{:S(2)}) collective-permute-start(bf16[8,3584]{1,0:T(8,128)(2,1)S(1)} %get-tuple-element.33), channel_id=1, source_target_pairs={{0,24},{2,26},{4,28},{6,30},{8,16},{10,18},{12,20},{14,22},{16,8},... | collective-permute-start | bytes 172040 | tf_op jit(solution)/shard_map/ppermute | solution.py:179
  39.2 0.6 %collective-permute-done.16.refs_2_ = bf16[16,3584]{1,0:T(8,128)(2,1)S(1)} collective-permute-done((bf16[16,3584]{1,0:T(8,128)(2,1)S(1)}, bf16[16,3584]{1,0:T(8,128)(2,1)S(1)}, u32[]{:S(2)}, u32[]{:S(2)}) %collective-permute-start.16) | collective-permute-done | bytes 114720 | tf_op jit(solution)/shard_map/ppermute | solution.py:179
  39.8 1.3 %collective-permute-start.17 = (bf16[8,3584]{1,0:T(8,128)(2,1)S(1)}, bf16[8,3584]{1,0:T(8,128)(2,1)S(1)}, u32[]{:S(2)}, u32[]{:S(2)}) collective-permute-start(bf16[8,3584]{1,0:T(8,128)(2,1)S(1)} %get-tuple-element.41), channel_id=1, source_target_pairs={{0,8},{2,10},{4,12},{6,14},{8,0},{10,2},{12,4},{14,6},{16,24},{18,... | collective-permute-start | bytes 172040 | tf_op jit(solution)/shard_map/ppermute | solution.py:179
  41.1 1.5 %collective-permute-done.8.refs_0_ = bf16[8,3584]{1,0:T(8,128)(2,1)S(1)} collective-permute-done((bf16[8,3584]{1,0:T(8,128)(2,1)S(1)}, bf16[8,3584]{1,0:T(8,128)(2,1)S(1)}, u32[]{:S(2)}, u32[]{:S(2)}) %collective-permute-start.8) | collective-permute-done | bytes 57376 | tf_op jit(solution)/shard_map/ppermute | solution.py:179
  42.5 1.8 %collective-permute-done.9.refs_1_ = bf16[8,3584]{1,0:T(8,128)(2,1)S(1)} collective-permute-done((bf16[8,3584]{1,0:T(8,128)(2,1)S(1)}, bf16[8,3584]{1,0:T(8,128)(2,1)S(1)}, u32[]{:S(2)}, u32[]{:S(2)}) %collective-permute-start.9) | collective-permute-done | bytes 57376 | tf_op jit(solution)/shard_map/ppermute | solution.py:179
  44.4 0.2 shard_map.81.near
  44.7 0.9 %shard_map.86 = bf16[16,3584]{1,0:T(8,128)(2,1)} custom-call(bf16[48,16]{1,0:T(8,128)(2,1)S(1)} %get-tuple-element.25.refs_1_.terms, f32[16,3584]{1,0:T(8,128)S(1)} %shard_map.81.near, bf16[8,3584]{1,0:T(8,128)(2,1)S(1)} %collective-permute-done.17.refs_0_, bf16[8,3584]{1,0:T(8,128)(2,1)S(1)} %get-tuple-element.42.refs_1_), custom_call_target="tpu_custom_call" | custom-call | tf_op jit(solution)/shard_map/pallas_call | solution.py:153
  (18 shorter events, 0.4 us)
Async XLA Ops:
  1.2 7.5 %collective-permute-start = (bf16[8,3584]{1,0:T(8,128)(2,1)S(1)}, bf16[8,3584]{1,0:T(8,128)(2,1)S(1)}, u32[]{:S(2)}, u32[]{:S(2)}) collective-permute-start(bf16[8,3584]{1,0:T(8,128)(2,1)S(1)} %get-tuple-element.27), channel_id=1, source_target_pairs={{0,24},{2,26},{4,28},{6,30},{8,16},{10,18},{12,20},{14,22},{16,8},... | collective-permute-start | bytes 172040 | tf_op jit(solution)/shard_map/ppermute | solution.py:179
  6.3 5.1 %collective-permute-start.1 = (bf16[8,3584]{1,0:T(8,128)(2,1)S(1)}, bf16[8,3584]{1,0:T(8,128)(2,1)S(1)}, u32[]{:S(2)}, u32[]{:S(2)}) collective-permute-start(bf16[8,3584]{1,0:T(8,128)(2,1)S(1)} %get-tuple-element.28), channel_id=1, source_target_pairs={{0,16},{2,18},{4,20},{6,22},{8,24},{10,26},{12,28},{14,30},{16,0},... | collective-permute-start | bytes 172040 | tf_op jit(solution)/shard_map/ppermute | solution.py:179
  11.4 7.3 %collective-permute-start.2 = (bf16[16,3584]{1,0:T(8,128)(2,1)S(1)}, bf16[16,3584]{1,0:T(8,128)(2,1)S(1)}, u32[]{:S(2)}, u32[]{:S(2)}) collective-permute-start(bf16[16,3584]{1,0:T(8,128)(2,1)S(1)} %shard_map.76.refs_0_), channel_id=1, source_target_pairs={{0,2},{2,0},{4,6},{6,4},{8,10},{10,8},{12,14},{14,12},{16,18},{18,... | collective-permute-start | bytes 344072 | tf_op jit(solution)/shard_map/ppermute | solution.py:179
  12.9 5.7 %collective-permute-start.3 = (bf16[16,3584]{1,0:T(8,128)(2,1)S(1)}, bf16[16,3584]{1,0:T(8,128)(2,1)S(1)}, u32[]{:S(2)}, u32[]{:S(2)}) collective-permute-start(bf16[16,3584]{1,0:T(8,128)(2,1)S(1)} %shard_map.76.refs_0_), channel_id=1, source_target_pairs={{0,4},{2,6},{4,0},{6,2},{8,12},{10,14},{12,8},{14,10},{16,20},{18,... | collective-permute-start | bytes 344072 | tf_op jit(solution)/shard_map/ppermute | solution.py:179
  14.5 4.2 %collective-permute-start.10 = (bf16[8,3584]{1,0:T(8,128)(2,1)S(1)}, bf16[8,3584]{1,0:T(8,128)(2,1)S(1)}, u32[]{:S(2)}, u32[]{:S(2)}) collective-permute-start(bf16[8,3584]{1,0:T(8,128)(2,1)S(1)} %get-tuple-element.35), channel_id=1, source_target_pairs={{0,8},{2,10},{4,12},{6,14},{8,0},{10,2},{12,4},{14,6},{16,24},{18,... | collective-permute-start | bytes 172040 | tf_op jit(solution)/shard_map/ppermute | solution.py:179
  18.7 4.9 %collective-permute-start.11 = (bf16[16,3584]{1,0:T(8,128)(2,1)S(1)}, bf16[16,3584]{1,0:T(8,128)(2,1)S(1)}, u32[]{:S(2)}, u32[]{:S(2)}) collective-permute-start(bf16[16,3584]{1,0:T(8,128)(2,1)S(1)} %shard_map.82.refs_0_), channel_id=1, source_target_pairs={{0,4},{2,6},{4,0},{6,2},{8,12},{10,14},{12,8},{14,10},{16,20},{18,... | collective-permute-start | bytes 344072 | tf_op jit(solution)/shard_map/ppermute | solution.py:179
  19.3 6.2 %collective-permute-start.4 = (bf16[16,3584]{1,0:T(8,128)(2,1)S(1)}, bf16[16,3584]{1,0:T(8,128)(2,1)S(1)}, u32[]{:S(2)}, u32[]{:S(2)}) collective-permute-start(bf16[16,3584]{1,0:T(8,128)(2,1)S(1)} %collective-permute-done.2.refs_1_.refs_2_), channel_id=1, source_target_pairs={{0,4},{2,6},{4,0},{6,2},{8,12},{10,14},{12,8},{14,10},{16,20},{18,... | collective-permute-start | bytes 344072 | tf_op jit(solution)/shard_map/ppermute | solution.py:179
  20.8 6.6 %collective-permute-start.12 = (bf16[16,3584]{1,0:T(8,128)(2,1)S(1)}, bf16[16,3584]{1,0:T(8,128)(2,1)S(1)}, u32[]{:S(2)}, u32[]{:S(2)}) collective-permute-start(bf16[16,3584]{1,0:T(8,128)(2,1)S(1)} %shard_map.82.refs_0_), channel_id=1, source_target_pairs={{0,2},{2,0},{4,6},{6,4},{8,10},{10,8},{12,14},{14,12},{16,18},{18,... | collective-permute-start | bytes 344072 | tf_op jit(solution)/shard_map/ppermute | solution.py:179
  23.5 5.3 %collective-permute-start.13 = (bf16[16,3584]{1,0:T(8,128)(2,1)S(1)}, bf16[16,3584]{1,0:T(8,128)(2,1)S(1)}, u32[]{:S(2)}, u32[]{:S(2)}) collective-permute-start(bf16[16,3584]{1,0:T(8,128)(2,1)S(1)} %collective-permute-done.11.refs_1_), channel_id=1, source_target_pairs={{0,2},{2,0},{4,6},{6,4},{8,10},{10,8},{12,14},{14,12},{16,18},{18,... | collective-permute-start | bytes 344072 | tf_op jit(solution)/shard_map/ppermute | solution.py:179
  26.7 4.9 %collective-permute-start.6 = (bf16[16,3584]{1,0:T(8,128)(2,1)S(1)}, bf16[16,3584]{1,0:T(8,128)(2,1)S(1)}, u32[]{:S(2)}, u32[]{:S(2)}) collective-permute-start(bf16[16,3584]{1,0:T(8,128)(2,1)S(1)} %get-tuple-element.32), channel_id=1, source_target_pairs={{0,4},{2,6},{4,0},{6,2},{8,12},{10,14},{12,8},{14,10},{16,20},{18,... | collective-permute-start | bytes 344072 | tf_op jit(solution)/shard_map/ppermute | solution.py:179
  30.0 4.9 %collective-permute-start.15 = (bf16[16,3584]{1,0:T(8,128)(2,1)S(1)}, bf16[16,3584]{1,0:T(8,128)(2,1)S(1)}, u32[]{:S(2)}, u32[]{:S(2)}) collective-permute-start(bf16[16,3584]{1,0:T(8,128)(2,1)S(1)} %get-tuple-element.40), channel_id=1, source_target_pairs={{0,2},{2,0},{4,6},{6,4},{8,10},{10,8},{12,14},{14,12},{16,18},{18,... | collective-permute-start | bytes 344072 | tf_op jit(solution)/shard_map/ppermute | solution.py:179
  30.1 5.1 %collective-permute-start.5 = (bf16[16,3584]{1,0:T(8,128)(2,1)S(1)}, bf16[16,3584]{1,0:T(8,128)(2,1)S(1)}, u32[]{:S(2)}, u32[]{:S(2)}) collective-permute-start(bf16[16,3584]{1,0:T(8,128)(2,1)S(1)} %get-tuple-element.30), channel_id=1, source_target_pairs={{0,4},{2,6},{4,0},{6,2},{8,12},{10,14},{12,8},{14,10},{16,20},{18,... | collective-permute-start | bytes 344072 | tf_op jit(solution)/shard_map/ppermute | solution.py:179
  31.6 4.9 %collective-permute-start.7 = (bf16[16,3584]{1,0:T(8,128)(2,1)S(1)}, bf16[16,3584]{1,0:T(8,128)(2,1)S(1)}, u32[]{:S(2)}, u32[]{:S(2)}) collective-permute-start(bf16[16,3584]{1,0:T(8,128)(2,1)S(1)} %shard_map.79), channel_id=1, source_target_pairs={{0,2},{2,0},{4,6},{6,4},{8,10},{10,8},{12,14},{14,12},{16,18},{18,... | collective-permute-start | bytes 344072 | tf_op jit(solution)/shard_map/ppermute | solution.py:179
  33.5 5.7 %collective-permute-start.14 = (bf16[16,3584]{1,0:T(8,128)(2,1)S(1)}, bf16[16,3584]{1,0:T(8,128)(2,1)S(1)}, u32[]{:S(2)}, u32[]{:S(2)}) collective-permute-start(bf16[16,3584]{1,0:T(8,128)(2,1)S(1)} %get-tuple-element.38), channel_id=1, source_target_pairs={{0,2},{2,0},{4,6},{6,4},{8,10},{10,8},{12,14},{14,12},{16,18},{18,... | collective-permute-start | bytes 344072 | tf_op jit(solution)/shard_map/ppermute | solution.py:179
  34.9 4.9 %collective-permute-start.16 = (bf16[16,3584]{1,0:T(8,128)(2,1)S(1)}, bf16[16,3584]{1,0:T(8,128)(2,1)S(1)}, u32[]{:S(2)}, u32[]{:S(2)}) collective-permute-start(bf16[16,3584]{1,0:T(8,128)(2,1)S(1)} %shard_map.84), channel_id=1, source_target_pairs={{0,4},{2,6},{4,0},{6,2},{8,12},{10,14},{12,8},{14,10},{16,20},{18,... | collective-permute-start | bytes 344072 | tf_op jit(solution)/shard_map/ppermute | solution.py:179
  36.5 6.0 %collective-permute-start.8 = (bf16[8,3584]{1,0:T(8,128)(2,1)S(1)}, bf16[8,3584]{1,0:T(8,128)(2,1)S(1)}, u32[]{:S(2)}, u32[]{:S(2)}) collective-permute-start(bf16[8,3584]{1,0:T(8,128)(2,1)S(1)} %get-tuple-element.33), channel_id=1, source_target_pairs={{0,24},{2,26},{4,28},{6,30},{8,16},{10,18},{12,20},{14,22},{16,8},... | collective-permute-start | bytes 172040 | tf_op jit(solution)/shard_map/ppermute | solution.py:179
  39.2 5.2 %collective-permute-start.9 = (bf16[8,3584]{1,0:T(8,128)(2,1)S(1)}, bf16[8,3584]{1,0:T(8,128)(2,1)S(1)}, u32[]{:S(2)}, u32[]{:S(2)}) collective-permute-start(bf16[8,3584]{1,0:T(8,128)(2,1)S(1)} %get-tuple-element.34), channel_id=1, source_target_pairs={{0,16},{2,18},{4,20},{6,22},{8,24},{10,26},{12,28},{14,30},{16,0},... | collective-permute-start | bytes 172040 | tf_op jit(solution)/shard_map/ppermute | solution.py:179
  39.8 4.9 %collective-permute-start.17 = (bf16[8,3584]{1,0:T(8,128)(2,1)S(1)}, bf16[8,3584]{1,0:T(8,128)(2,1)S(1)}, u32[]{:S(2)}, u32[]{:S(2)}) collective-permute-start(bf16[8,3584]{1,0:T(8,128)(2,1)S(1)} %get-tuple-element.41), channel_id=1, source_target_pairs={{0,8},{2,10},{4,12},{6,14},{8,0},{10,2},{12,4},{14,6},{16,24},{18,... | collective-permute-start | bytes 172040 | tf_op jit(solution)/shard_map/ppermute | solution.py:179

commit v20 on v16

--- a/solution.py
+++ b/solution.py
@@ -97,10 +97,11 @@
         c.wait()
 
 
-def terms_kernel(combine, near_terms, far_terms):
-    slots = combine.shape[0] // 2
-    same = (iota((slots, slots), 0) == iota((slots, slots), 1)).astype(jnp.float32)
-    for start, out in ((0, near_terms), (slots, far_terms)):
+def terms_kernel(combine, first_terms, rest_terms):
+    start = 0
+    for out in (first_terms, rest_terms):
+        slots = out.shape[1]
+        same = (iota((slots, slots), 0) == iota((slots, slots), 1)).astype(jnp.float32)
         rest = combine[pl.ds(start, slots), :]
         terms = []
         for _ in range(3):
@@ -112,6 +113,7 @@
                 )
             )
         out[...] = jnp.concatenate(terms, axis=0).astype(jnp.bfloat16)
+        start += slots
 
 
 def stack_kernel(count, *refs):
@@ -140,12 +142,12 @@
     return product[2 * rows :] + product[rows : 2 * rows] + product[:rows]
 
 
-def near_kernel(terms, *refs):
+def first_kernel(terms, *refs):
     refs[-1][...] = combined(terms, refs[:-1], refs[-1].shape[0])
 
 
-def far_kernel(terms, near, *refs):
-    total = near[...] + combined(terms, refs[:-1], refs[-1].shape[0])
+def rest_kernel(terms, first, *refs):
+    total = first[...] + combined(terms, refs[:-1], refs[-1].shape[0])
     refs[-1][...] = total.astype(jnp.bfloat16)
 
 
@@ -196,8 +198,10 @@
         + [pltpu.SemaphoreType.DMA((5,))],
     )
     chunks = [swap(c, d * group_size) if d else c for d, c in zip(offsets, chunks)]
-    terms = jax.ShapeDtypeStruct((3 * tok_count, slots // 2), bf16)
-    terms = local(terms_kernel, [combine], [terms, terms])
+    terms = [
+        jax.ShapeDtypeStruct((3 * tok_count, n), bf16) for n in (capacity, slots - capacity)
+    ]
+    terms = local(terms_kernel, [combine], terms)
 
     def fetch(array, after):
         return call(
@@ -245,14 +249,14 @@
             result = [swap(v, q) if q else v for q, v in enumerate(result)]
         summed += local(functools.partial(sum_kernel, len(result)), result, [chunk] * count)
     summed = [swap(v, d * group_size) if d else v for d, v in zip(offsets, summed)]
-    near = local(
-        near_kernel,
-        [terms[0]] + summed[:count],
+    first = local(
+        first_kernel,
+        [terms[0]] + summed[:1],
         jax.ShapeDtypeStruct((tok_count, width), jnp.float32),
     )
     return local(
-        far_kernel,
-        [terms[1], near] + summed[count:],
+        rest_kernel,
+        [terms[1], first] + summed[1:],
         jax.ShapeDtypeStruct((tok_count, width), bf16),
     )
 

time: 42.5 us -> 42.5 us (level)
  transfers between devices with their start and end apart: 18 -> 18, of which waited for: 9 -> 10; matrix products, arithmetic and copies ran while one was open for 0% -> 0% of each run, Pallas kernels for 15% -> 15%
where the time goes in v20:
time: 42.5 us; the launch traced here: 42.3 us
  starting transfers between devices  24.3 us (57%)
  waiting for transfers between devices  9.49 us (22%)
  Pallas kernels  8.5 us (20%)
    ppermute x18, starting transfers between devices, swap(): lax.ppermute(value, 'expert', [(e, e ^ offset) for e in range(n_devices)])  24.3 us
    ppermute x18, waiting for transfers between devices, swap(): lax.ppermute(value, 'expert', [(e, e ^ offset) for e in range(n_devices)])  9.49 us
    pallas_call x14, Pallas kernels, call(): pl.pallas_call(kernel, out_shape=outs, in_specs=in_specs, out_specs=jax.t...  8.5 us
  transfers between devices with their start and end apart: 18, of which 10 were waited for; matrix products, arithmetic and copies ran while one was open for 0% of the time, Pallas kernels for 15%

profile of v20, /device:TPU:0, one launch (start us, length us, event | category | flops | bytes accessed | tf_op | source)
XLA Modules:
  0.0 42.3 jit_solution(1413458386127183769)
XLA Ops:
  0.0 1.2 %shard_map.73 = (bf16[8,3584]{1,0:T(8,128)(2,1)S(1)}, bf16[8,3584]{1,0:T(8,128)(2,1)S(1)}, bf16[8,3584]{1,0:T(8,128)(2,1)S(1)}, bf16[8,3584]{1,0:T(8,128)(2,1)S(1)}, f32[32,16]{1,0:T(8,128)S(1)}) custom-call(s32[4]{0:T(128)} %refs_0_.3, s32[2,16]{1,0:T(2,128)} %bitcast.3, s32[2,16]{1,0:T(2,128)} %bitcast.4, f32[2,16]{1,0:T(2,128)} %bitcast.5, ...), custom_call_target="tpu_custom_call" | custom-call | tf_op jit(solution)/shard_map/pallas_call | solution.py:155
  1.2 5.1 %collective-permute-start = (bf16[8,3584]{1,0:T(8,128)(2,1)S(1)}, bf16[8,3584]{1,0:T(8,128)(2,1)S(1)}, u32[]{:S(2)}, u32[]{:S(2)}) collective-permute-start(bf16[8,3584]{1,0:T(8,128)(2,1)S(1)} %get-tuple-element.27), channel_id=1, source_target_pairs={{0,24},{2,26},{4,28},{6,30},{8,16},{10,18},{12,20},{14,22},{16,8},... | collective-permute-start | bytes 172040 | tf_op jit(solution)/shard_map/ppermute | solution.py:181
  6.3 0.6 %collective-permute-start.10 = (bf16[8,3584]{1,0:T(8,128)(2,1)S(1)}, bf16[8,3584]{1,0:T(8,128)(2,1)S(1)}, u32[]{:S(2)}, u32[]{:S(2)}) collective-permute-start(bf16[8,3584]{1,0:T(8,128)(2,1)S(1)} %get-tuple-element.35), channel_id=1, source_target_pairs={{0,8},{2,10},{4,12},{6,14},{8,0},{10,2},{12,4},{14,6},{16,24},{18,... | collective-permute-start | bytes 172040 | tf_op jit(solution)/shard_map/ppermute | solution.py:181
  7.1 2.1 %shard_map.75.refs_2_.refs_4_ = bf16[2,3584,256]{2,1,0:T(8,128)(2,1)S(1)} custom-call(bf16[2,3584,256]{2,1,0:T(8,128)(2,1)} %refs_0_.4, bf16[48,8]{1,0:T(8,128)(2,1)S(1)} %get-tuple-element.26.refs_1_.terms), custom_call_target="tpu_custom_call" | custom-call | bytes 3670016 | tf_op jit(solution)/shard_map/pallas_call | solution.py:155
  9.2 2.1 %collective-permute-done.1.refs_1_ = bf16[8,3584]{1,0:T(8,128)(2,1)S(1)} collective-permute-done((bf16[8,3584]{1,0:T(8,128)(2,1)S(1)}, bf16[8,3584]{1,0:T(8,128)(2,1)S(1)}, u32[]{:S(2)}, u32[]{:S(2)}) %collective-permute-start.1) | collective-permute-done | bytes 57376 | tf_op jit(solution)/shard_map/ppermute | solution.py:181
  11.4 1.6 %collective-permute-start.2 = (bf16[16,3584]{1,0:T(8,128)(2,1)S(1)}, bf16[16,3584]{1,0:T(8,128)(2,1)S(1)}, u32[]{:S(2)}, u32[]{:S(2)}) collective-permute-start(bf16[16,3584]{1,0:T(8,128)(2,1)S(1)} %shard_map.76.refs_0_), channel_id=1, source_target_pairs={{0,2},{2,0},{4,6},{6,4},{8,10},{10,8},{12,14},{14,12},{16,18},{18,... | collective-permute-start | bytes 344072 | tf_op jit(solution)/shard_map/ppermute | solution.py:181
  13.0 1.6 %collective-permute-start.11 = (bf16[16,3584]{1,0:T(8,128)(2,1)S(1)}, bf16[16,3584]{1,0:T(8,128)(2,1)S(1)}, u32[]{:S(2)}, u32[]{:S(2)}) collective-permute-start(bf16[16,3584]{1,0:T(8,128)(2,1)S(1)} %shard_map.82.refs_0_), channel_id=1, source_target_pairs={{0,4},{2,6},{4,0},{6,2},{8,12},{10,14},{12,8},{14,10},{16,20},{18,... | collective-permute-start | bytes 344072 | tf_op jit(solution)/shard_map/ppermute | solution.py:181
  14.6 0.5 %collective-permute-start.3 = (bf16[16,3584]{1,0:T(8,128)(2,1)S(1)}, bf16[16,3584]{1,0:T(8,128)(2,1)S(1)}, u32[]{:S(2)}, u32[]{:S(2)}) collective-permute-start(bf16[16,3584]{1,0:T(8,128)(2,1)S(1)} %shard_map.76.refs_0_), channel_id=1, source_target_pairs={{0,4},{2,6},{4,0},{6,2},{8,12},{10,14},{12,8},{14,10},{16,20},{18,... | collective-permute-start | bytes 344072 | tf_op jit(solution)/shard_map/ppermute | solution.py:181
  15.1 1.2 %collective-permute-done.2.refs_1_ = bf16[16,3584]{1,0:T(8,128)(2,1)S(1)} collective-permute-done((bf16[16,3584]{1,0:T(8,128)(2,1)S(1)}, bf16[16,3584]{1,0:T(8,128)(2,1)S(1)}, u32[]{:S(2)}, u32[]{:S(2)}) %collective-permute-start.2) | collective-permute-done | bytes 114720 | tf_op jit(solution)/shard_map/ppermute | solution.py:181
  16.2 1.5 %collective-permute-start.4 = (bf16[16,3584]{1,0:T(8,128)(2,1)S(1)}, bf16[16,3584]{1,0:T(8,128)(2,1)S(1)}, u32[]{:S(2)}, u32[]{:S(2)}) collective-permute-start(bf16[16,3584]{1,0:T(8,128)(2,1)S(1)} %collective-permute-done.2.refs_1_), channel_id=1, source_target_pairs={{0,4},{2,6},{4,0},{6,2},{8,12},{10,14},{12,8},{14,10},{16,20},{18,... | collective-permute-start | bytes 344072 | tf_op jit(solution)/shard_map/ppermute | solution.py:181
  17.8 1.5 %collective-permute-start.12 = (bf16[16,3584]{1,0:T(8,128)(2,1)S(1)}, bf16[16,3584]{1,0:T(8,128)(2,1)S(1)}, u32[]{:S(2)}, u32[]{:S(2)}) collective-permute-start(bf16[16,3584]{1,0:T(8,128)(2,1)S(1)} %shard_map.82.refs_0_), channel_id=1, source_target_pairs={{0,2},{2,0},{4,6},{6,4},{8,10},{10,8},{12,14},{14,12},{16,18},{18,... | collective-permute-start | bytes 344072 | tf_op jit(solution)/shard_map/ppermute | solution.py:181
  19.3 0.5 %collective-permute-start.13 = (bf16[16,3584]{1,0:T(8,128)(2,1)S(1)}, bf16[16,3584]{1,0:T(8,128)(2,1)S(1)}, u32[]{:S(2)}, u32[]{:S(2)}) collective-permute-start(bf16[16,3584]{1,0:T(8,128)(2,1)S(1)} %collective-permute-done.11.refs_1_), channel_id=1, source_target_pairs={{0,2},{2,0},{4,6},{6,4},{8,10},{10,8},{12,14},{14,12},{16,18},{18,... | collective-permute-start | bytes 344072 | tf_op jit(solution)/shard_map/ppermute | solution.py:181
  19.8 1.5 %shard_map.77.refs_5_ = bf16[256,3584]{1,0:T(8,128)(2,1)S(1)} custom-call(bf16[256,3584]{1,0:T(8,128)(2,1)} %refs_0_.5, bf16[48,24]{1,0:T(8,128)(2,1)S(1)} %get-tuple-element.25.refs_1_.terms), custom_call_target="tpu_custom_call" | custom-call | bytes 1835008 | tf_op jit(solution)/shard_map/pallas_call | solution.py:155
  21.3 0.6 %collective-permute-done.4.refs_3_ = bf16[16,3584]{1,0:T(8,128)(2,1)S(1)} collective-permute-done((bf16[16,3584]{1,0:T(8,128)(2,1)S(1)}, bf16[16,3584]{1,0:T(8,128)(2,1)S(1)}, u32[]{:S(2)}, u32[]{:S(2)}) %collective-permute-start.4) | collective-permute-done | bytes 114720 | tf_op jit(solution)/shard_map/ppermute | solution.py:181
  22.0 1.2 %shard_map.78 = (bf16[16,3584]{1,0:T(8,128)(2,1)S(1)}, bf16[16,3584]{1,0:T(8,128)(2,1)S(1)}, bf16[16,3584]{1,0:T(8,128)(2,1)S(1)}, bf16[16,3584]{1,0:T(8,128)(2,1)S(1)}) custom-call(bf16[16,3584]{1,0:T(8,128)(2,1)S(1)} %shard_map.76.refs_0_, bf16[16,3584]{1,0:T(8,128)(2,1)S(1)} %collective-permute-done.2.refs_1_, ...), custom_call_target="tpu_custom_call" | custom-call | tf_op jit(solution)/shard_map/pallas_call | solution.py:155
  23.1 1.6 %collective-permute-start.6 = (bf16[16,3584]{1,0:T(8,128)(2,1)S(1)}, bf16[16,3584]{1,0:T(8,128)(2,1)S(1)}, u32[]{:S(2)}, u32[]{:S(2)}) collective-permute-start(bf16[16,3584]{1,0:T(8,128)(2,1)S(1)} %get-tuple-element.32), channel_id=1, source_target_pairs={{0,4},{2,6},{4,0},{6,2},{8,12},{10,14},{12,8},{14,10},{16,20},{18,... | collective-permute-start | bytes 344072 | tf_op jit(solution)/shard_map/ppermute | solution.py:181
  24.7 1.2 %shard_map.83 = (bf16[16,3584]{1,0:T(8,128)(2,1)S(1)}, bf16[16,3584]{1,0:T(8,128)(2,1)S(1)}, bf16[16,3584]{1,0:T(8,128)(2,1)S(1)}, bf16[16,3584]{1,0:T(8,128)(2,1)S(1)}) custom-call(bf16[16,3584]{1,0:T(8,128)(2,1)S(1)} %shard_map.82.refs_0_, bf16[16,3584]{1,0:T(8,128)(2,1)S(1)} %collective-permute-done.11.refs_1_, ...), custom_call_target="tpu_custom_call" | custom-call | tf_op jit(solution)/shard_map/pallas_call | solution.py:155
  25.9 0.8 %collective-permute-start.15 = (bf16[16,3584]{1,0:T(8,128)(2,1)S(1)}, bf16[16,3584]{1,0:T(8,128)(2,1)S(1)}, u32[]{:S(2)}, u32[]{:S(2)}) collective-permute-start(bf16[16,3584]{1,0:T(8,128)(2,1)S(1)} %get-tuple-element.40), channel_id=1, source_target_pairs={{0,2},{2,0},{4,6},{6,4},{8,10},{10,8},{12,14},{14,12},{16,18},{18,... | collective-permute-start | bytes 344072 | tf_op jit(solution)/shard_map/ppermute | solution.py:181
  26.6 0.7 %collective-permute-start.5 = (bf16[16,3584]{1,0:T(8,128)(2,1)S(1)}, bf16[16,3584]{1,0:T(8,128)(2,1)S(1)}, u32[]{:S(2)}, u32[]{:S(2)}) collective-permute-start(bf16[16,3584]{1,0:T(8,128)(2,1)S(1)} %get-tuple-element.30), channel_id=1, source_target_pairs={{0,4},{2,6},{4,0},{6,2},{8,12},{10,14},{12,8},{14,10},{16,20},{18,... | collective-permute-start | bytes 344072 | tf_op jit(solution)/shard_map/ppermute | solution.py:181
  27.3 1.6 %collective-permute-done.6.refs_1_ = bf16[16,3584]{1,0:T(8,128)(2,1)S(1)} collective-permute-done((bf16[16,3584]{1,0:T(8,128)(2,1)S(1)}, bf16[16,3584]{1,0:T(8,128)(2,1)S(1)}, u32[]{:S(2)}, u32[]{:S(2)}) %collective-permute-start.6) | collective-permute-done | bytes 114720 | tf_op jit(solution)/shard_map/ppermute | solution.py:181
  28.9 0.9 %collective-permute-start.7 = (bf16[16,3584]{1,0:T(8,128)(2,1)S(1)}, bf16[16,3584]{1,0:T(8,128)(2,1)S(1)}, u32[]{:S(2)}, u32[]{:S(2)}) collective-permute-start(bf16[16,3584]{1,0:T(8,128)(2,1)S(1)} %shard_map.79), channel_id=1, source_target_pairs={{0,2},{2,0},{4,6},{6,4},{8,10},{10,8},{12,14},{14,12},{16,18},{18,... | collective-permute-start | bytes 344072 | tf_op jit(solution)/shard_map/ppermute | solution.py:181
  29.9 1.1 %collective-permute-start.14 = (bf16[16,3584]{1,0:T(8,128)(2,1)S(1)}, bf16[16,3584]{1,0:T(8,128)(2,1)S(1)}, u32[]{:S(2)}, u32[]{:S(2)}) collective-permute-start(bf16[16,3584]{1,0:T(8,128)(2,1)S(1)} %get-tuple-element.38), channel_id=1, source_target_pairs={{0,2},{2,0},{4,6},{6,4},{8,10},{10,8},{12,14},{14,12},{16,18},{18,... | collective-permute-start | bytes 344072 | tf_op jit(solution)/shard_map/ppermute | solution.py:181
  31.0 0.3 collective-permute-done.15.refs_1_
  31.3 1.5 %collective-permute-start.16 = (bf16[16,3584]{1,0:T(8,128)(2,1)S(1)}, bf16[16,3584]{1,0:T(8,128)(2,1)S(1)}, u32[]{:S(2)}, u32[]{:S(2)}) collective-permute-start(bf16[16,3584]{1,0:T(8,128)(2,1)S(1)} %shard_map.84), channel_id=1, source_target_pairs={{0,4},{2,6},{4,0},{6,2},{8,12},{10,14},{12,8},{14,10},{16,20},{18,... | collective-permute-start | bytes 344072 | tf_op jit(solution)/shard_map/ppermute | solution.py:181
  32.8 1.0 %collective-permute-done.7.refs_2_ = bf16[16,3584]{1,0:T(8,128)(2,1)S(1)} collective-permute-done((bf16[16,3584]{1,0:T(8,128)(2,1)S(1)}, bf16[16,3584]{1,0:T(8,128)(2,1)S(1)}, u32[]{:S(2)}, u32[]{:S(2)}) %collective-permute-start.7) | collective-permute-done | bytes 114720 | tf_op jit(solution)/shard_map/ppermute | solution.py:181
  33.9 2.2 %collective-permute-start.8 = (bf16[8,3584]{1,0:T(8,128)(2,1)S(1)}, bf16[8,3584]{1,0:T(8,128)(2,1)S(1)}, u32[]{:S(2)}, u32[]{:S(2)}) collective-permute-start(bf16[8,3584]{1,0:T(8,128)(2,1)S(1)} %get-tuple-element.33), channel_id=1, source_target_pairs={{0,24},{2,26},{4,28},{6,30},{8,16},{10,18},{12,20},{14,22},{16,8},... | collective-permute-start | bytes 172040 | tf_op jit(solution)/shard_map/ppermute | solution.py:181
  36.3 2.4 %collective-permute-start.9 = (bf16[8,3584]{1,0:T(8,128)(2,1)S(1)}, bf16[8,3584]{1,0:T(8,128)(2,1)S(1)}, u32[]{:S(2)}, u32[]{:S(2)}) collective-permute-start(bf16[8,3584]{1,0:T(8,128)(2,1)S(1)} %get-tuple-element.34), channel_id=1, source_target_pairs={{0,16},{2,18},{4,20},{6,22},{8,24},{10,26},{12,28},{14,30},{16,0},... | collective-permute-start | bytes 172040 | tf_op jit(solution)/shard_map/ppermute | solution.py:181
  38.7 1.2 %collective-permute-done.8.refs_0_ = bf16[8,3584]{1,0:T(8,128)(2,1)S(1)} collective-permute-done((bf16[8,3584]{1,0:T(8,128)(2,1)S(1)}, bf16[8,3584]{1,0:T(8,128)(2,1)S(1)}, u32[]{:S(2)}, u32[]{:S(2)}) %collective-permute-start.8) | collective-permute-done | bytes 57376 | tf_op jit(solution)/shard_map/ppermute | solution.py:181
  39.9 0.2 shard_map.81.first
  40.1 0.4 collective-permute-done.17.refs_1_
  40.5 1.0 %collective-permute-done.9.refs_0_ = bf16[8,3584]{1,0:T(8,128)(2,1)S(1)} collective-permute-done((bf16[8,3584]{1,0:T(8,128)(2,1)S(1)}, bf16[8,3584]{1,0:T(8,128)(2,1)S(1)}, u32[]{:S(2)}, u32[]{:S(2)}) %collective-permute-start.9) | collective-permute-done | bytes 57376 | tf_op jit(solution)/shard_map/ppermute | solution.py:181
  41.5 0.9 %shard_map.86 = bf16[16,3584]{1,0:T(8,128)(2,1)} custom-call(bf16[48,24]{1,0:T(8,128)(2,1)S(1)} %get-tuple-element.25.refs_1_.terms, f32[16,3584]{1,0:T(8,128)S(1)} %shard_map.81.first, bf16[8,3584]{1,0:T(8,128)(2,1)S(1)} %collective-permute-done.9.refs_0_, bf16[8,3584]{1,0:T(8,128)(2,1)S(1)} %collective-permute-done.17.refs_1_, ...), custom_call_target="tpu_custom_call" | custom-call | tf_op jit(solution)/shard_map/pallas_call | solution.py:155
  (18 shorter events, 0.6 us)
Async XLA Ops:
  1.2 8.0 %collective-permute-start = (bf16[8,3584]{1,0:T(8,128)(2,1)S(1)}, bf16[8,3584]{1,0:T(8,128)(2,1)S(1)}, u32[]{:S(2)}, u32[]{:S(2)}) collective-permute-start(bf16[8,3584]{1,0:T(8,128)(2,1)S(1)} %get-tuple-element.27), channel_id=1, source_target_pairs={{0,24},{2,26},{4,28},{6,30},{8,16},{10,18},{12,20},{14,22},{16,8},... | collective-permute-start | bytes 172040 | tf_op jit(solution)/shard_map/ppermute | solution.py:181
  6.3 5.1 %collective-permute-start.1 = (bf16[8,3584]{1,0:T(8,128)(2,1)S(1)}, bf16[8,3584]{1,0:T(8,128)(2,1)S(1)}, u32[]{:S(2)}, u32[]{:S(2)}) collective-permute-start(bf16[8,3584]{1,0:T(8,128)(2,1)S(1)} %get-tuple-element.28), channel_id=1, source_target_pairs={{0,16},{2,18},{4,20},{6,22},{8,24},{10,26},{12,28},{14,30},{16,0},... | collective-permute-start | bytes 172040 | tf_op jit(solution)/shard_map/ppermute | solution.py:181
  6.3 6.7 %collective-permute-start.10 = (bf16[8,3584]{1,0:T(8,128)(2,1)S(1)}, bf16[8,3584]{1,0:T(8,128)(2,1)S(1)}, u32[]{:S(2)}, u32[]{:S(2)}) collective-permute-start(bf16[8,3584]{1,0:T(8,128)(2,1)S(1)} %get-tuple-element.35), channel_id=1, source_target_pairs={{0,8},{2,10},{4,12},{6,14},{8,0},{10,2},{12,4},{14,6},{16,24},{18,... | collective-permute-start | bytes 172040 | tf_op jit(solution)/shard_map/ppermute | solution.py:181
  11.4 4.9 %collective-permute-start.2 = (bf16[16,3584]{1,0:T(8,128)(2,1)S(1)}, bf16[16,3584]{1,0:T(8,128)(2,1)S(1)}, u32[]{:S(2)}, u32[]{:S(2)}) collective-permute-start(bf16[16,3584]{1,0:T(8,128)(2,1)S(1)} %shard_map.76.refs_0_), channel_id=1, source_target_pairs={{0,2},{2,0},{4,6},{6,4},{8,10},{10,8},{12,14},{14,12},{16,18},{18,... | collective-permute-start | bytes 344072 | tf_op jit(solution)/shard_map/ppermute | solution.py:181
  13.0 6.3 %collective-permute-start.11 = (bf16[16,3584]{1,0:T(8,128)(2,1)S(1)}, bf16[16,3584]{1,0:T(8,128)(2,1)S(1)}, u32[]{:S(2)}, u32[]{:S(2)}) collective-permute-start(bf16[16,3584]{1,0:T(8,128)(2,1)S(1)} %shard_map.82.refs_0_), channel_id=1, source_target_pairs={{0,4},{2,6},{4,0},{6,2},{8,12},{10,14},{12,8},{14,10},{16,20},{18,... | collective-permute-start | bytes 344072 | tf_op jit(solution)/shard_map/ppermute | solution.py:181
  14.6 6.7 %collective-permute-start.3 = (bf16[16,3584]{1,0:T(8,128)(2,1)S(1)}, bf16[16,3584]{1,0:T(8,128)(2,1)S(1)}, u32[]{:S(2)}, u32[]{:S(2)}) collective-permute-start(bf16[16,3584]{1,0:T(8,128)(2,1)S(1)} %shard_map.76.refs_0_), channel_id=1, source_target_pairs={{0,4},{2,6},{4,0},{6,2},{8,12},{10,14},{12,8},{14,10},{16,20},{18,... | collective-permute-start | bytes 344072 | tf_op jit(solution)/shard_map/ppermute | solution.py:181
  16.2 5.7 %collective-permute-start.4 = (bf16[16,3584]{1,0:T(8,128)(2,1)S(1)}, bf16[16,3584]{1,0:T(8,128)(2,1)S(1)}, u32[]{:S(2)}, u32[]{:S(2)}) collective-permute-start(bf16[16,3584]{1,0:T(8,128)(2,1)S(1)} %collective-permute-done.2.refs_1_), channel_id=1, source_target_pairs={{0,4},{2,6},{4,0},{6,2},{8,12},{10,14},{12,8},{14,10},{16,20},{18,... | collective-permute-start | bytes 344072 | tf_op jit(solution)/shard_map/ppermute | solution.py:181
  17.8 6.9 %collective-permute-start.12 = (bf16[16,3584]{1,0:T(8,128)(2,1)S(1)}, bf16[16,3584]{1,0:T(8,128)(2,1)S(1)}, u32[]{:S(2)}, u32[]{:S(2)}) collective-permute-start(bf16[16,3584]{1,0:T(8,128)(2,1)S(1)} %shard_map.82.refs_0_), channel_id=1, source_target_pairs={{0,2},{2,0},{4,6},{6,4},{8,10},{10,8},{12,14},{14,12},{16,18},{18,... | collective-permute-start | bytes 344072 | tf_op jit(solution)/shard_map/ppermute | solution.py:181
  19.3 5.4 %collective-permute-start.13 = (bf16[16,3584]{1,0:T(8,128)(2,1)S(1)}, bf16[16,3584]{1,0:T(8,128)(2,1)S(1)}, u32[]{:S(2)}, u32[]{:S(2)}) collective-permute-start(bf16[16,3584]{1,0:T(8,128)(2,1)S(1)} %collective-permute-done.11.refs_1_), channel_id=1, source_target_pairs={{0,2},{2,0},{4,6},{6,4},{8,10},{10,8},{12,14},{14,12},{16,18},{18,... | collective-permute-start | bytes 344072 | tf_op jit(solution)/shard_map/ppermute | solution.py:181
  23.1 5.8 %collective-permute-start.6 = (bf16[16,3584]{1,0:T(8,128)(2,1)S(1)}, bf16[16,3584]{1,0:T(8,128)(2,1)S(1)}, u32[]{:S(2)}, u32[]{:S(2)}) collective-permute-start(bf16[16,3584]{1,0:T(8,128)(2,1)S(1)} %get-tuple-element.32), channel_id=1, source_target_pairs={{0,4},{2,6},{4,0},{6,2},{8,12},{10,14},{12,8},{14,10},{16,20},{18,... | collective-permute-start | bytes 344072 | tf_op jit(solution)/shard_map/ppermute | solution.py:181
  25.9 5.4 %collective-permute-start.15 = (bf16[16,3584]{1,0:T(8,128)(2,1)S(1)}, bf16[16,3584]{1,0:T(8,128)(2,1)S(1)}, u32[]{:S(2)}, u32[]{:S(2)}) collective-permute-start(bf16[16,3584]{1,0:T(8,128)(2,1)S(1)} %get-tuple-element.40), channel_id=1, source_target_pairs={{0,2},{2,0},{4,6},{6,4},{8,10},{10,8},{12,14},{14,12},{16,18},{18,... | collective-permute-start | bytes 344072 | tf_op jit(solution)/shard_map/ppermute | solution.py:181
  26.6 6.2 %collective-permute-start.5 = (bf16[16,3584]{1,0:T(8,128)(2,1)S(1)}, bf16[16,3584]{1,0:T(8,128)(2,1)S(1)}, u32[]{:S(2)}, u32[]{:S(2)}) collective-permute-start(bf16[16,3584]{1,0:T(8,128)(2,1)S(1)} %get-tuple-element.30), channel_id=1, source_target_pairs={{0,4},{2,6},{4,0},{6,2},{8,12},{10,14},{12,8},{14,10},{16,20},{18,... | collective-permute-start | bytes 344072 | tf_op jit(solution)/shard_map/ppermute | solution.py:181
  28.9 4.9 %collective-permute-start.7 = (bf16[16,3584]{1,0:T(8,128)(2,1)S(1)}, bf16[16,3584]{1,0:T(8,128)(2,1)S(1)}, u32[]{:S(2)}, u32[]{:S(2)}) collective-permute-start(bf16[16,3584]{1,0:T(8,128)(2,1)S(1)} %shard_map.79), channel_id=1, source_target_pairs={{0,2},{2,0},{4,6},{6,4},{8,10},{10,8},{12,14},{14,12},{16,18},{18,... | collective-permute-start | bytes 344072 | tf_op jit(solution)/shard_map/ppermute | solution.py:181
  29.9 6.2 %collective-permute-start.14 = (bf16[16,3584]{1,0:T(8,128)(2,1)S(1)}, bf16[16,3584]{1,0:T(8,128)(2,1)S(1)}, u32[]{:S(2)}, u32[]{:S(2)}) collective-permute-start(bf16[16,3584]{1,0:T(8,128)(2,1)S(1)} %get-tuple-element.38), channel_id=1, source_target_pairs={{0,2},{2,0},{4,6},{6,4},{8,10},{10,8},{12,14},{14,12},{16,18},{18,... | collective-permute-start | bytes 344072 | tf_op jit(solution)/shard_map/ppermute | solution.py:181
  31.3 4.9 %collective-permute-start.16 = (bf16[16,3584]{1,0:T(8,128)(2,1)S(1)}, bf16[16,3584]{1,0:T(8,128)(2,1)S(1)}, u32[]{:S(2)}, u32[]{:S(2)}) collective-permute-start(bf16[16,3584]{1,0:T(8,128)(2,1)S(1)} %shard_map.84), channel_id=1, source_target_pairs={{0,4},{2,6},{4,0},{6,2},{8,12},{10,14},{12,8},{14,10},{16,20},{18,... | collective-permute-start | bytes 344072 | tf_op jit(solution)/shard_map/ppermute | solution.py:181
  33.9 6.0 %collective-permute-start.8 = (bf16[8,3584]{1,0:T(8,128)(2,1)S(1)}, bf16[8,3584]{1,0:T(8,128)(2,1)S(1)}, u32[]{:S(2)}, u32[]{:S(2)}) collective-permute-start(bf16[8,3584]{1,0:T(8,128)(2,1)S(1)} %get-tuple-element.33), channel_id=1, source_target_pairs={{0,24},{2,26},{4,28},{6,30},{8,16},{10,18},{12,20},{14,22},{16,8},... | collective-permute-start | bytes 172040 | tf_op jit(solution)/shard_map/ppermute | solution.py:181
  36.2 4.3 %collective-permute-start.17 = (bf16[8,3584]{1,0:T(8,128)(2,1)S(1)}, bf16[8,3584]{1,0:T(8,128)(2,1)S(1)}, u32[]{:S(2)}, u32[]{:S(2)}) collective-permute-start(bf16[8,3584]{1,0:T(8,128)(2,1)S(1)} %get-tuple-element.41), channel_id=1, source_target_pairs={{0,8},{2,10},{4,12},{6,14},{8,0},{10,2},{12,4},{14,6},{16,24},{18,... | collective-permute-start | bytes 172040 | tf_op jit(solution)/shard_map/ppermute | solution.py:181
  36.3 5.1 %collective-permute-start.9 = (bf16[8,3584]{1,0:T(8,128)(2,1)S(1)}, bf16[8,3584]{1,0:T(8,128)(2,1)S(1)}, u32[]{:S(2)}, u32[]{:S(2)}) collective-permute-start(bf16[8,3584]{1,0:T(8,128)(2,1)S(1)} %get-tuple-element.34), channel_id=1, source_target_pairs={{0,16},{2,18},{4,20},{6,22},{8,24},{10,26},{12,28},{14,30},{16,0},... | collective-permute-start | bytes 172040 | tf_op jit(solution)/shard_map/ppermute | solution.py:181

commit v21 on v20

--- a/solution.py
+++ b/solution.py
@@ -44,13 +44,17 @@
     named = jnp.zeros_like(copy_row)
     before = jnp.zeros_like(copy_row)
     relative = jnp.zeros_like(copy_row)
+    weighed = jnp.zeros_like(copy_row)
     for c in copies_in[:4]:
         c.wait()
     for p in range(slot_count):
         here = copy_row == p
         named = jnp.where(here, placement[p], named)
         d = lax.bitwise_xor(own, p)
-        relative = jnp.where(here, slot_count - 1 - d, relative)
+        weighed = jnp.where(here, slot_count - 1 - d, weighed)
+        far = d >= slot_count // 2
+        place = jnp.where(far, d - slot_count // 2, slot_count - 1 - d)
+        relative = jnp.where(here, place, relative)
         seen = jnp.int32(0)
         for q in range(p):
             seen = seen + (placement[q] == placement[p]).astype(jnp.int32)
@@ -76,6 +80,8 @@
         slot = jnp.where(rank < capacity, place * capacity + rank, -1)
         hot = slot_row == slot
         pick_rows = pick_rows + hot.astype(jnp.float32)
+        place = jnp.sum(chosen[k] * weighed, axis=0, keepdims=True)
+        hot = slot_row == jnp.where(rank < capacity, place * capacity + rank, -1)
         combine = combine + jnp.where(hot, gate_weights[pl.ds(k, 1), :], 0.0)
         earlier = earlier + chosen[k]
     combine_out[...] = combine
@@ -172,7 +178,7 @@
     tok_count, width = tokens.shape
     capacity = tok_count * expert_ids.shape[1] // slot_count
     slots = slot_count * capacity
-    offsets = range(slot_count - 1, -1, -1)
+    offsets = [*range(slot_count // 2, slot_count)] + [*range(slot_count // 2)][::-1]
     bf16 = jnp.bfloat16
     chunk = jax.ShapeDtypeStruct((capacity, width), bf16)
     half = jax.ShapeDtypeStruct((slots // 2, width), bf16)
@@ -249,6 +255,7 @@
             result = [swap(v, q) if q else v for q, v in enumerate(result)]
         summed += local(functools.partial(sum_kernel, len(result)), result, [chunk] * count)
     summed = [swap(v, d * group_size) if d else v for d, v in zip(offsets, summed)]
+    summed = summed[:count][::-1] + summed[count:]
     first = local(
         first_kernel,
         [terms[0]] + summed[:1],

time: 42.5 us -> 43.6 us (1.026)
  starting transfers between devices: 24.3 us -> 25.2 us
    ppermute x18, starting transfers between devices: 24.3 us -> 25.2 us  [swap(): lax.ppermute(value, 'expert', [(e, e ^ offset) for e in range(n_devices)])]
  transfers between devices with their start and end apart: 18 -> 18, of which waited for: 10 -> 8; matrix products, arithmetic and copies ran while one was open for 0% -> 0% of each run, Pallas kernels for 15% -> 15%
where the time goes in v21:
time: 43.6 us; the launch traced here: 43.4 us
  starting transfers between devices  25.2 us (58%)
  waiting for transfers between devices  9.57 us (22%)
  Pallas kernels  8.5 us (19%)
    ppermute x18, starting transfers between devices, swap(): lax.ppermute(value, 'expert', [(e, e ^ offset) for e in range(n_devices)])  25.2 us
    ppermute x18, waiting for transfers between devices, swap(): lax.ppermute(value, 'expert', [(e, e ^ offset) for e in range(n_devices)])  9.57 us
    pallas_call x14, Pallas kernels, call(): pl.pallas_call(kernel, out_shape=outs, in_specs=in_specs, out_specs=jax.t...  8.5 us
  transfers between devices with their start and end apart: 18, of which 8 were waited for; matrix products, arithmetic and copies ran while one was open for 0% of the time, Pallas kernels for 15%

profile of v21, /device:TPU:0, one launch (start us, length us, event | category | flops | bytes accessed | tf_op | source)
XLA Modules:
  0.0 43.4 jit_solution(17385405448410204946)
XLA Ops:
  0.0 1.2 %shard_map.73 = (bf16[8,3584]{1,0:T(8,128)(2,1)S(1)}, bf16[8,3584]{1,0:T(8,128)(2,1)S(1)}, bf16[8,3584]{1,0:T(8,128)(2,1)S(1)}, bf16[8,3584]{1,0:T(8,128)(2,1)S(1)}, f32[32,16]{1,0:T(8,128)S(1)}) custom-call(s32[4]{0:T(128)} %refs_0_.3, s32[2,16]{1,0:T(2,128)} %bitcast.3, s32[2,16]{1,0:T(2,128)} %bitcast.4, f32[2,16]{1,0:T(2,128)} %bitcast.5, ...), custom_call_target="tpu_custom_call" | custom-call | tf_op jit(solution)/shard_map/pallas_call | solution.py:161
  1.2 4.1 %collective-permute-start = (bf16[8,3584]{1,0:T(8,128)(2,1)S(1)}, bf16[8,3584]{1,0:T(8,128)(2,1)S(1)}, u32[]{:S(2)}, u32[]{:S(2)}) collective-permute-start(bf16[8,3584]{1,0:T(8,128)(2,1)S(1)} %get-tuple-element.27), channel_id=1, source_target_pairs={{0,16},{2,18},{4,20},{6,22},{8,24},{10,26},{12,28},{14,30},{16,0},... | collective-permute-start | bytes 172040 | tf_op jit(solution)/shard_map/ppermute | solution.py:187
  5.3 1.4 %collective-permute-start.1 = (bf16[8,3584]{1,0:T(8,128)(2,1)S(1)}, bf16[8,3584]{1,0:T(8,128)(2,1)S(1)}, u32[]{:S(2)}, u32[]{:S(2)}) collective-permute-start(bf16[8,3584]{1,0:T(8,128)(2,1)S(1)} %get-tuple-element.28), channel_id=1, source_target_pairs={{0,24},{2,26},{4,28},{6,30},{8,16},{10,18},{12,20},{14,22},{16,8},... | collective-permute-start | bytes 172040 | tf_op jit(solution)/shard_map/ppermute | solution.py:187
  6.6 0.2 collective-permute-start.10
  7.1 2.1 %shard_map.75.refs_2_.refs_4_ = bf16[2,3584,256]{2,1,0:T(8,128)(2,1)S(1)} custom-call(bf16[2,3584,256]{2,1,0:T(8,128)(2,1)} %refs_0_.4, bf16[48,8]{1,0:T(8,128)(2,1)S(1)} %get-tuple-element.26.refs_1_.terms), custom_call_target="tpu_custom_call" | custom-call | bytes 3670016 | tf_op jit(solution)/shard_map/pallas_call | solution.py:161
  9.2 2.2 %collective-permute-done.1.refs_1_ = bf16[8,3584]{1,0:T(8,128)(2,1)S(1)} collective-permute-done((bf16[8,3584]{1,0:T(8,128)(2,1)S(1)}, bf16[8,3584]{1,0:T(8,128)(2,1)S(1)}, u32[]{:S(2)}, u32[]{:S(2)}) %collective-permute-start.1) | collective-permute-done | bytes 57376 | tf_op jit(solution)/shard_map/ppermute | solution.py:187
  11.4 1.6 %collective-permute-start.2 = (bf16[16,3584]{1,0:T(8,128)(2,1)S(1)}, bf16[16,3584]{1,0:T(8,128)(2,1)S(1)}, u32[]{:S(2)}, u32[]{:S(2)}) collective-permute-start(bf16[16,3584]{1,0:T(8,128)(2,1)S(1)} %shard_map.76.refs_0_), channel_id=1, source_target_pairs={{0,2},{2,0},{4,6},{6,4},{8,10},{10,8},{12,14},{14,12},{16,18},{18,... | collective-permute-start | bytes 344072 | tf_op jit(solution)/shard_map/ppermute | solution.py:187
  13.0 1.6 %collective-permute-start.11 = (bf16[16,3584]{1,0:T(8,128)(2,1)S(1)}, bf16[16,3584]{1,0:T(8,128)(2,1)S(1)}, u32[]{:S(2)}, u32[]{:S(2)}) collective-permute-start(bf16[16,3584]{1,0:T(8,128)(2,1)S(1)} %shard_map.82.refs_0_), channel_id=1, source_target_pairs={{0,4},{2,6},{4,0},{6,2},{8,12},{10,14},{12,8},{14,10},{16,20},{18,... | collective-permute-start | bytes 344072 | tf_op jit(solution)/shard_map/ppermute | solution.py:187
  14.6 0.5 %collective-permute-start.3 = (bf16[16,3584]{1,0:T(8,128)(2,1)S(1)}, bf16[16,3584]{1,0:T(8,128)(2,1)S(1)}, u32[]{:S(2)}, u32[]{:S(2)}) collective-permute-start(bf16[16,3584]{1,0:T(8,128)(2,1)S(1)} %shard_map.76.refs_0_), channel_id=1, source_target_pairs={{0,4},{2,6},{4,0},{6,2},{8,12},{10,14},{12,8},{14,10},{16,20},{18,... | collective-permute-start | bytes 344072 | tf_op jit(solution)/shard_map/ppermute | solution.py:187
  15.1 1.1 %collective-permute-done.2.refs_1_ = bf16[16,3584]{1,0:T(8,128)(2,1)S(1)} collective-permute-done((bf16[16,3584]{1,0:T(8,128)(2,1)S(1)}, bf16[16,3584]{1,0:T(8,128)(2,1)S(1)}, u32[]{:S(2)}, u32[]{:S(2)}) %collective-permute-start.2) | collective-permute-done | bytes 114720 | tf_op jit(solution)/shard_map/ppermute | solution.py:187
  16.2 1.5 %collective-permute-start.4 = (bf16[16,3584]{1,0:T(8,128)(2,1)S(1)}, bf16[16,3584]{1,0:T(8,128)(2,1)S(1)}, u32[]{:S(2)}, u32[]{:S(2)}) collective-permute-start(bf16[16,3584]{1,0:T(8,128)(2,1)S(1)} %collective-permute-done.2.refs_1_), channel_id=1, source_target_pairs={{0,4},{2,6},{4,0},{6,2},{8,12},{10,14},{12,8},{14,10},{16,20},{18,... | collective-permute-start | bytes 344072 | tf_op jit(solution)/shard_map/ppermute | solution.py:187
  17.8 1.5 %collective-permute-start.12 = (bf16[16,3584]{1,0:T(8,128)(2,1)S(1)}, bf16[16,3584]{1,0:T(8,128)(2,1)S(1)}, u32[]{:S(2)}, u32[]{:S(2)}) collective-permute-start(bf16[16,3584]{1,0:T(8,128)(2,1)S(1)} %shard_map.82.refs_0_), channel_id=1, source_target_pairs={{0,2},{2,0},{4,6},{6,4},{8,10},{10,8},{12,14},{14,12},{16,18},{18,... | collective-permute-start | bytes 344072 | tf_op jit(solution)/shard_map/ppermute | solution.py:187
  19.3 0.5 %collective-permute-start.13 = (bf16[16,3584]{1,0:T(8,128)(2,1)S(1)}, bf16[16,3584]{1,0:T(8,128)(2,1)S(1)}, u32[]{:S(2)}, u32[]{:S(2)}) collective-permute-start(bf16[16,3584]{1,0:T(8,128)(2,1)S(1)} %collective-permute-done.11.refs_1_), channel_id=1, source_target_pairs={{0,2},{2,0},{4,6},{6,4},{8,10},{10,8},{12,14},{14,12},{16,18},{18,... | collective-permute-start | bytes 344072 | tf_op jit(solution)/shard_map/ppermute | solution.py:187
  19.8 1.5 %shard_map.77.refs_5_ = bf16[256,3584]{1,0:T(8,128)(2,1)S(1)} custom-call(bf16[256,3584]{1,0:T(8,128)(2,1)} %refs_0_.5, bf16[48,24]{1,0:T(8,128)(2,1)S(1)} %get-tuple-element.25.refs_1_.terms), custom_call_target="tpu_custom_call" | custom-call | bytes 1835008 | tf_op jit(solution)/shard_map/pallas_call | solution.py:161
  21.3 1.2 %shard_map.78 = (bf16[16,3584]{1,0:T(8,128)(2,1)S(1)}, bf16[16,3584]{1,0:T(8,128)(2,1)S(1)}, bf16[16,3584]{1,0:T(8,128)(2,1)S(1)}, bf16[16,3584]{1,0:T(8,128)(2,1)S(1)}) custom-call(bf16[16,3584]{1,0:T(8,128)(2,1)S(1)} %shard_map.76.refs_0_, bf16[16,3584]{1,0:T(8,128)(2,1)S(1)} %collective-permute-done.2.refs_1_, ...), custom_call_target="tpu_custom_call" | custom-call | tf_op jit(solution)/shard_map/pallas_call | solution.py:161
  22.5 1.3 %collective-permute-start.6 = (bf16[16,3584]{1,0:T(8,128)(2,1)S(1)}, bf16[16,3584]{1,0:T(8,128)(2,1)S(1)}, u32[]{:S(2)}, u32[]{:S(2)}) collective-permute-start(bf16[16,3584]{1,0:T(8,128)(2,1)S(1)} %get-tuple-element.32), channel_id=1, source_target_pairs={{0,4},{2,6},{4,0},{6,2},{8,12},{10,14},{12,8},{14,10},{16,20},{18,... | collective-permute-start | bytes 344072 | tf_op jit(solution)/shard_map/ppermute | solution.py:187
  23.8 0.3 collective-permute-done.13.refs_3_
  24.1 1.2 %shard_map.83 = (bf16[16,3584]{1,0:T(8,128)(2,1)S(1)}, bf16[16,3584]{1,0:T(8,128)(2,1)S(1)}, bf16[16,3584]{1,0:T(8,128)(2,1)S(1)}, bf16[16,3584]{1,0:T(8,128)(2,1)S(1)}) custom-call(bf16[16,3584]{1,0:T(8,128)(2,1)S(1)} %shard_map.82.refs_0_, bf16[16,3584]{1,0:T(8,128)(2,1)S(1)} %collective-permute-done.11.refs_1_, ...), custom_call_target="tpu_custom_call" | custom-call | tf_op jit(solution)/shard_map/pallas_call | solution.py:161
  25.2 1.3 %collective-permute-start.15 = (bf16[16,3584]{1,0:T(8,128)(2,1)S(1)}, bf16[16,3584]{1,0:T(8,128)(2,1)S(1)}, u32[]{:S(2)}, u32[]{:S(2)}) collective-permute-start(bf16[16,3584]{1,0:T(8,128)(2,1)S(1)} %get-tuple-element.40), channel_id=1, source_target_pairs={{0,2},{2,0},{4,6},{6,4},{8,10},{10,8},{12,14},{14,12},{16,18},{18,... | collective-permute-start | bytes 344072 | tf_op jit(solution)/shard_map/ppermute | solution.py:187
  26.5 0.8 %collective-permute-start.5 = (bf16[16,3584]{1,0:T(8,128)(2,1)S(1)}, bf16[16,3584]{1,0:T(8,128)(2,1)S(1)}, u32[]{:S(2)}, u32[]{:S(2)}) collective-permute-start(bf16[16,3584]{1,0:T(8,128)(2,1)S(1)} %get-tuple-element.30), channel_id=1, source_target_pairs={{0,4},{2,6},{4,0},{6,2},{8,12},{10,14},{12,8},{14,10},{16,20},{18,... | collective-permute-start | bytes 344072 | tf_op jit(solution)/shard_map/ppermute | solution.py:187
  27.3 1.3 %collective-permute-done.6.refs_1_ = bf16[16,3584]{1,0:T(8,128)(2,1)S(1)} collective-permute-done((bf16[16,3584]{1,0:T(8,128)(2,1)S(1)}, bf16[16,3584]{1,0:T(8,128)(2,1)S(1)}, u32[]{:S(2)}, u32[]{:S(2)}) %collective-permute-start.6) | collective-permute-done | bytes 114720 | tf_op jit(solution)/shard_map/ppermute | solution.py:187
  28.6 0.3 collective-permute-start.7
  28.9 1.7 %collective-permute-start.14 = (bf16[16,3584]{1,0:T(8,128)(2,1)S(1)}, bf16[16,3584]{1,0:T(8,128)(2,1)S(1)}, u32[]{:S(2)}, u32[]{:S(2)}) collective-permute-start(bf16[16,3584]{1,0:T(8,128)(2,1)S(1)} %get-tuple-element.38), channel_id=1, source_target_pairs={{0,2},{2,0},{4,6},{6,4},{8,10},{10,8},{12,14},{14,12},{16,18},{18,... | collective-permute-start | bytes 344072 | tf_op jit(solution)/shard_map/ppermute | solution.py:187
  30.7 0.9 %collective-permute-start.16 = (bf16[16,3584]{1,0:T(8,128)(2,1)S(1)}, bf16[16,3584]{1,0:T(8,128)(2,1)S(1)}, u32[]{:S(2)}, u32[]{:S(2)}) collective-permute-start(bf16[16,3584]{1,0:T(8,128)(2,1)S(1)} %shard_map.84), channel_id=1, source_target_pairs={{0,4},{2,6},{4,0},{6,2},{8,12},{10,14},{12,8},{14,10},{16,20},{18,... | collective-permute-start | bytes 344072 | tf_op jit(solution)/shard_map/ppermute | solution.py:187
  31.7 1.8 %collective-permute-done.7.refs_2_ = bf16[16,3584]{1,0:T(8,128)(2,1)S(1)} collective-permute-done((bf16[16,3584]{1,0:T(8,128)(2,1)S(1)}, bf16[16,3584]{1,0:T(8,128)(2,1)S(1)}, u32[]{:S(2)}, u32[]{:S(2)}) %collective-permute-start.7) | collective-permute-done | bytes 114720 | tf_op jit(solution)/shard_map/ppermute | solution.py:187
  33.5 2.2 %collective-permute-start.8 = (bf16[8,3584]{1,0:T(8,128)(2,1)S(1)}, bf16[8,3584]{1,0:T(8,128)(2,1)S(1)}, u32[]{:S(2)}, u32[]{:S(2)}) collective-permute-start(bf16[8,3584]{1,0:T(8,128)(2,1)S(1)} %get-tuple-element.33), channel_id=1, source_target_pairs={{0,24},{2,26},{4,28},{6,30},{8,16},{10,18},{12,20},{14,22},{16,8},... | collective-permute-start | bytes 172040 | tf_op jit(solution)/shard_map/ppermute | solution.py:187
  35.7 1.7 %collective-permute-start.17 = (bf16[8,3584]{1,0:T(8,128)(2,1)S(1)}, bf16[8,3584]{1,0:T(8,128)(2,1)S(1)}, u32[]{:S(2)}, u32[]{:S(2)}) collective-permute-start(bf16[8,3584]{1,0:T(8,128)(2,1)S(1)} %get-tuple-element.41), channel_id=1, source_target_pairs={{0,8},{2,10},{4,12},{6,14},{8,0},{10,2},{12,4},{14,6},{16,24},{18,... | collective-permute-start | bytes 172040 | tf_op jit(solution)/shard_map/ppermute | solution.py:187
  37.4 2.0 %collective-permute-start.9 = (bf16[8,3584]{1,0:T(8,128)(2,1)S(1)}, bf16[8,3584]{1,0:T(8,128)(2,1)S(1)}, u32[]{:S(2)}, u32[]{:S(2)}) collective-permute-start(bf16[8,3584]{1,0:T(8,128)(2,1)S(1)} %get-tuple-element.34), channel_id=1, source_target_pairs={{0,16},{2,18},{4,20},{6,22},{8,24},{10,26},{12,28},{14,30},{16,0},... | collective-permute-start | bytes 172040 | tf_op jit(solution)/shard_map/ppermute | solution.py:187
  39.6 0.2 shard_map.81.first
  39.8 0.4 collective-permute-done.17.refs_1_
  40.2 2.3 %collective-permute-done.9.refs_0_ = bf16[8,3584]{1,0:T(8,128)(2,1)S(1)} collective-permute-done((bf16[8,3584]{1,0:T(8,128)(2,1)S(1)}, bf16[8,3584]{1,0:T(8,128)(2,1)S(1)}, u32[]{:S(2)}, u32[]{:S(2)}) %collective-permute-start.9) | collective-permute-done | bytes 57376 | tf_op jit(solution)/shard_map/ppermute | solution.py:187
  42.5 0.9 %shard_map.86 = bf16[16,3584]{1,0:T(8,128)(2,1)} custom-call(bf16[48,24]{1,0:T(8,128)(2,1)S(1)} %get-tuple-element.25.refs_1_.terms, f32[16,3584]{1,0:T(8,128)S(1)} %shard_map.81.first, bf16[8,3584]{1,0:T(8,128)(2,1)S(1)} %collective-permute-done.9.refs_0_, bf16[8,3584]{1,0:T(8,128)(2,1)S(1)} %collective-permute-done.17.refs_1_, ...), custom_call_target="tpu_custom_call" | custom-call | tf_op jit(solution)/shard_map/pallas_call | solution.py:161
  (18 shorter events, 0.5 us)
Async XLA Ops:
  1.2 8.0 %collective-permute-start = (bf16[8,3584]{1,0:T(8,128)(2,1)S(1)}, bf16[8,3584]{1,0:T(8,128)(2,1)S(1)}, u32[]{:S(2)}, u32[]{:S(2)}) collective-permute-start(bf16[8,3584]{1,0:T(8,128)(2,1)S(1)} %get-tuple-element.27), channel_id=1, source_target_pairs={{0,16},{2,18},{4,20},{6,22},{8,24},{10,26},{12,28},{14,30},{16,0},... | collective-permute-start | bytes 172040 | tf_op jit(solution)/shard_map/ppermute | solution.py:187
  5.3 6.1 %collective-permute-start.1 = (bf16[8,3584]{1,0:T(8,128)(2,1)S(1)}, bf16[8,3584]{1,0:T(8,128)(2,1)S(1)}, u32[]{:S(2)}, u32[]{:S(2)}) collective-permute-start(bf16[8,3584]{1,0:T(8,128)(2,1)S(1)} %get-tuple-element.28), channel_id=1, source_target_pairs={{0,24},{2,26},{4,28},{6,30},{8,16},{10,18},{12,20},{14,22},{16,8},... | collective-permute-start | bytes 172040 | tf_op jit(solution)/shard_map/ppermute | solution.py:187
  6.6 6.3 %collective-permute-start.10 = (bf16[8,3584]{1,0:T(8,128)(2,1)S(1)}, bf16[8,3584]{1,0:T(8,128)(2,1)S(1)}, u32[]{:S(2)}, u32[]{:S(2)}) collective-permute-start(bf16[8,3584]{1,0:T(8,128)(2,1)S(1)} %get-tuple-element.35), channel_id=1, source_target_pairs={{0,8},{2,10},{4,12},{6,14},{8,0},{10,2},{12,4},{14,6},{16,24},{18,... | collective-permute-start | bytes 172040 | tf_op jit(solution)/shard_map/ppermute | solution.py:187
  11.4 4.9 %collective-permute-start.2 = (bf16[16,3584]{1,0:T(8,128)(2,1)S(1)}, bf16[16,3584]{1,0:T(8,128)(2,1)S(1)}, u32[]{:S(2)}, u32[]{:S(2)}) collective-permute-start(bf16[16,3584]{1,0:T(8,128)(2,1)S(1)} %shard_map.76.refs_0_), channel_id=1, source_target_pairs={{0,2},{2,0},{4,6},{6,4},{8,10},{10,8},{12,14},{14,12},{16,18},{18,... | collective-permute-start | bytes 344072 | tf_op jit(solution)/shard_map/ppermute | solution.py:187
  13.0 6.3 %collective-permute-start.11 = (bf16[16,3584]{1,0:T(8,128)(2,1)S(1)}, bf16[16,3584]{1,0:T(8,128)(2,1)S(1)}, u32[]{:S(2)}, u32[]{:S(2)}) collective-permute-start(bf16[16,3584]{1,0:T(8,128)(2,1)S(1)} %shard_map.82.refs_0_), channel_id=1, source_target_pairs={{0,4},{2,6},{4,0},{6,2},{8,12},{10,14},{12,8},{14,10},{16,20},{18,... | collective-permute-start | bytes 344072 | tf_op jit(solution)/shard_map/ppermute | solution.py:187
  14.6 6.7 %collective-permute-start.3 = (bf16[16,3584]{1,0:T(8,128)(2,1)S(1)}, bf16[16,3584]{1,0:T(8,128)(2,1)S(1)}, u32[]{:S(2)}, u32[]{:S(2)}) collective-permute-start(bf16[16,3584]{1,0:T(8,128)(2,1)S(1)} %shard_map.76.refs_0_), channel_id=1, source_target_pairs={{0,4},{2,6},{4,0},{6,2},{8,12},{10,14},{12,8},{14,10},{16,20},{18,... | collective-permute-start | bytes 344072 | tf_op jit(solution)/shard_map/ppermute | solution.py:187
  16.2 5.1 %collective-permute-start.4 = (bf16[16,3584]{1,0:T(8,128)(2,1)S(1)}, bf16[16,3584]{1,0:T(8,128)(2,1)S(1)}, u32[]{:S(2)}, u32[]{:S(2)}) collective-permute-start(bf16[16,3584]{1,0:T(8,128)(2,1)S(1)} %collective-permute-done.2.refs_1_), channel_id=1, source_target_pairs={{0,4},{2,6},{4,0},{6,2},{8,12},{10,14},{12,8},{14,10},{16,20},{18,... | collective-permute-start | bytes 344072 | tf_op jit(solution)/shard_map/ppermute | solution.py:187
  17.8 6.0 %collective-permute-start.12 = (bf16[16,3584]{1,0:T(8,128)(2,1)S(1)}, bf16[16,3584]{1,0:T(8,128)(2,1)S(1)}, u32[]{:S(2)}, u32[]{:S(2)}) collective-permute-start(bf16[16,3584]{1,0:T(8,128)(2,1)S(1)} %shard_map.82.refs_0_), channel_id=1, source_target_pairs={{0,2},{2,0},{4,6},{6,4},{8,10},{10,8},{12,14},{14,12},{16,18},{18,... | collective-permute-start | bytes 344072 | tf_op jit(solution)/shard_map/ppermute | solution.py:187
  19.3 4.8 %collective-permute-start.13 = (bf16[16,3584]{1,0:T(8,128)(2,1)S(1)}, bf16[16,3584]{1,0:T(8,128)(2,1)S(1)}, u32[]{:S(2)}, u32[]{:S(2)}) collective-permute-start(bf16[16,3584]{1,0:T(8,128)(2,1)S(1)} %collective-permute-done.11.refs_1_), channel_id=1, source_target_pairs={{0,2},{2,0},{4,6},{6,4},{8,10},{10,8},{12,14},{14,12},{16,18},{18,... | collective-permute-start | bytes 344072 | tf_op jit(solution)/shard_map/ppermute | solution.py:187
  22.5 6.1 %collective-permute-start.6 = (bf16[16,3584]{1,0:T(8,128)(2,1)S(1)}, bf16[16,3584]{1,0:T(8,128)(2,1)S(1)}, u32[]{:S(2)}, u32[]{:S(2)}) collective-permute-start(bf16[16,3584]{1,0:T(8,128)(2,1)S(1)} %get-tuple-element.32), channel_id=1, source_target_pairs={{0,4},{2,6},{4,0},{6,2},{8,12},{10,14},{12,8},{14,10},{16,20},{18,... | collective-permute-start | bytes 344072 | tf_op jit(solution)/shard_map/ppermute | solution.py:187
  25.2 5.5 %collective-permute-start.15 = (bf16[16,3584]{1,0:T(8,128)(2,1)S(1)}, bf16[16,3584]{1,0:T(8,128)(2,1)S(1)}, u32[]{:S(2)}, u32[]{:S(2)}) collective-permute-start(bf16[16,3584]{1,0:T(8,128)(2,1)S(1)} %get-tuple-element.40), channel_id=1, source_target_pairs={{0,2},{2,0},{4,6},{6,4},{8,10},{10,8},{12,14},{14,12},{16,18},{18,... | collective-permute-start | bytes 344072 | tf_op jit(solution)/shard_map/ppermute | solution.py:187
  26.5 5.1 %collective-permute-start.5 = (bf16[16,3584]{1,0:T(8,128)(2,1)S(1)}, bf16[16,3584]{1,0:T(8,128)(2,1)S(1)}, u32[]{:S(2)}, u32[]{:S(2)}) collective-permute-start(bf16[16,3584]{1,0:T(8,128)(2,1)S(1)} %get-tuple-element.30), channel_id=1, source_target_pairs={{0,4},{2,6},{4,0},{6,2},{8,12},{10,14},{12,8},{14,10},{16,20},{18,... | collective-permute-start | bytes 344072 | tf_op jit(solution)/shard_map/ppermute | solution.py:187
  28.6 4.9 %collective-permute-start.7 = (bf16[16,3584]{1,0:T(8,128)(2,1)S(1)}, bf16[16,3584]{1,0:T(8,128)(2,1)S(1)}, u32[]{:S(2)}, u32[]{:S(2)}) collective-permute-start(bf16[16,3584]{1,0:T(8,128)(2,1)S(1)} %shard_map.79), channel_id=1, source_target_pairs={{0,2},{2,0},{4,6},{6,4},{8,10},{10,8},{12,14},{14,12},{16,18},{18,... | collective-permute-start | bytes 344072 | tf_op jit(solution)/shard_map/ppermute | solution.py:187
  28.9 6.8 %collective-permute-start.14 = (bf16[16,3584]{1,0:T(8,128)(2,1)S(1)}, bf16[16,3584]{1,0:T(8,128)(2,1)S(1)}, u32[]{:S(2)}, u32[]{:S(2)}) collective-permute-start(bf16[16,3584]{1,0:T(8,128)(2,1)S(1)} %get-tuple-element.38), channel_id=1, source_target_pairs={{0,2},{2,0},{4,6},{6,4},{8,10},{10,8},{12,14},{14,12},{16,18},{18,... | collective-permute-start | bytes 344072 | tf_op jit(solution)/shard_map/ppermute | solution.py:187
  30.7 5.0 %collective-permute-start.16 = (bf16[16,3584]{1,0:T(8,128)(2,1)S(1)}, bf16[16,3584]{1,0:T(8,128)(2,1)S(1)}, u32[]{:S(2)}, u32[]{:S(2)}) collective-permute-start(bf16[16,3584]{1,0:T(8,128)(2,1)S(1)} %shard_map.84), channel_id=1, source_target_pairs={{0,4},{2,6},{4,0},{6,2},{8,12},{10,14},{12,8},{14,10},{16,20},{18,... | collective-permute-start | bytes 344072 | tf_op jit(solution)/shard_map/ppermute | solution.py:187
  33.5 6.1 %collective-permute-start.8 = (bf16[8,3584]{1,0:T(8,128)(2,1)S(1)}, bf16[8,3584]{1,0:T(8,128)(2,1)S(1)}, u32[]{:S(2)}, u32[]{:S(2)}) collective-permute-start(bf16[8,3584]{1,0:T(8,128)(2,1)S(1)} %get-tuple-element.33), channel_id=1, source_target_pairs={{0,24},{2,26},{4,28},{6,30},{8,16},{10,18},{12,20},{14,22},{16,8},... | collective-permute-start | bytes 172040 | tf_op jit(solution)/shard_map/ppermute | solution.py:187
  35.7 4.4 %collective-permute-start.17 = (bf16[8,3584]{1,0:T(8,128)(2,1)S(1)}, bf16[8,3584]{1,0:T(8,128)(2,1)S(1)}, u32[]{:S(2)}, u32[]{:S(2)}) collective-permute-start(bf16[8,3584]{1,0:T(8,128)(2,1)S(1)} %get-tuple-element.41), channel_id=1, source_target_pairs={{0,8},{2,10},{4,12},{6,14},{8,0},{10,2},{12,4},{14,6},{16,24},{18,... | collective-permute-start | bytes 172040 | tf_op jit(solution)/shard_map/ppermute | solution.py:187
  37.4 5.1 %collective-permute-start.9 = (bf16[8,3584]{1,0:T(8,128)(2,1)S(1)}, bf16[8,3584]{1,0:T(8,128)(2,1)S(1)}, u32[]{:S(2)}, u32[]{:S(2)}) collective-permute-start(bf16[8,3584]{1,0:T(8,128)(2,1)S(1)} %get-tuple-element.34), channel_id=1, source_target_pairs={{0,16},{2,18},{4,20},{6,22},{8,24},{10,26},{12,28},{14,30},{16,0},... | collective-permute-start | bytes 172040 | tf_op jit(solution)/shard_map/ppermute | solution.py:187

commit v22 on v20

--- a/solution.py
+++ b/solution.py
@@ -129,6 +129,19 @@
     unstack(jnp.dot(hidden, w_out[...], preferred_element_type=jnp.float32), outs)
 
 
+def fetching_expert_kernel(count, *refs):
+    blocks, (w_in, source), outs = refs[:count], refs[count : count + 2], refs[count + 2 : -2]
+    held, sem = refs[-2:]
+    copy = pltpu.make_async_copy(source, held, sem.at[0])
+    copy.start()
+    rows = stack(blocks).astype(jnp.bfloat16)
+    gate = jnp.dot(rows, w_in[0], preferred_element_type=jnp.float32)
+    upper = jnp.dot(rows, w_in[1], preferred_element_type=jnp.float32)
+    hidden = (gate / (1.0 + jnp.exp(-gate)) * upper).astype(jnp.bfloat16)
+    copy.wait()
+    unstack(jnp.dot(hidden, held[...], preferred_element_type=jnp.float32), outs)
+
+
 def sum_kernel(count, *refs):
     total = refs[0][...].astype(jnp.float32)
     for r in refs[1:count]:
@@ -215,7 +228,6 @@
         )
 
     w_in = fetch(w_in, terms[0])
-    w_out = fetch(w_out, terms[1])
 
     square = group_size == 4
     count = slot_count // 2
@@ -233,12 +245,22 @@
         else:
             held = [swap(own, q) if q else own for q in range(group_size)]
         earlier = []
-        result = local(
-            functools.partial(expert_kernel, group_size),
-            held + [w_in, w_out],
-            [half] * group_size,
-            40 * MIB,
-        )
+        if h == 0:
+            *result, w_out = call(
+                functools.partial(fetching_expert_kernel, group_size),
+                held + [w_in, *in_hbm(w_out)],
+                [VMEM] * (group_size + 1) + [HBM],
+                [half] * group_size + [jax.ShapeDtypeStruct(w_out.shape, bf16)],
+                40 * MIB,
+                [pltpu.SemaphoreType.DMA((1,))],
+            )
+        else:
+            result = local(
+                functools.partial(expert_kernel, group_size),
+                held + [w_in, w_out],
+                [half] * group_size,
+                40 * MIB,
+            )
         if square:
             mine, first, second, cross = result
             cross = swap(cross, b)

time: 42.5 us -> 43.1 us (1.014)
  waiting for transfers between devices: 9.49 us -> 11.5 us
  starting transfers between devices: 24.3 us -> 23.5 us
  Pallas kernels: 8.5 us -> 7.84 us
    ppermute x18, waiting for transfers between devices: 9.49 us -> 11.5 us  [swap(): lax.ppermute(value, 'expert', [(e, e ^ offset) for e in range(n_devices)])]
    ppermute x18, starting transfers between devices: 24.3 us -> 23.5 us  [swap(): lax.ppermute(value, 'expert', [(e, e ^ offset) for e in range(n_devices)])]
    pallas_call x14 -> x13, Pallas kernels: 8.5 us -> 7.84 us  [call(): pl.pallas_call(kernel, out_shape=outs, in_specs=in_specs, out_specs=jax.t...]
  transfers between devices with their start and end apart: 18 -> 18, of which waited for: 10 -> 10; matrix products, arithmetic and copies ran while one was open for 0% -> 0% of each run, Pallas kernels for 15% -> 13%
where the time goes in v22:
time: 43.1 us; the launch traced here: 42.9 us
  starting transfers between devices  23.5 us (55%)
  waiting for transfers between devices  11.5 us (27%)
  Pallas kernels  7.84 us (18%)
    ppermute x18, starting transfers between devices, swap(): lax.ppermute(value, 'expert', [(e, e ^ offset) for e in range(n_devices)])  23.5 us
    ppermute x18, waiting for transfers between devices, swap(): lax.ppermute(value, 'expert', [(e, e ^ offset) for e in range(n_devices)])  11.5 us
    pallas_call x13, Pallas kernels, call(): pl.pallas_call(kernel, out_shape=outs, in_specs=in_specs, out_specs=jax.t...  7.84 us
  transfers between devices with their start and end apart: 18, of which 10 were waited for; matrix products, arithmetic and copies ran while one was open for 0% of the time, Pallas kernels for 13%

profile of v22, /device:TPU:0, one launch (start us, length us, event | category | flops | bytes accessed | tf_op | source)
XLA Modules:
  0.0 42.9 jit_solution(5008557216646436772)
XLA Ops:
  0.0 1.2 %shard_map.73 = (bf16[8,3584]{1,0:T(8,128)(2,1)S(1)}, bf16[8,3584]{1,0:T(8,128)(2,1)S(1)}, bf16[8,3584]{1,0:T(8,128)(2,1)S(1)}, bf16[8,3584]{1,0:T(8,128)(2,1)S(1)}, f32[32,16]{1,0:T(8,128)S(1)}) custom-call(s32[4]{0:T(128)} %refs_0_.2, s32[2,16]{1,0:T(2,128)} %bitcast.3, s32[2,16]{1,0:T(2,128)} %bitcast.4, f32[2,16]{1,0:T(2,128)} %bitcast.5, ...), custom_call_target="tpu_custom_call" | custom-call | tf_op jit(solution)/shard_map/pallas_call | solution.py:168
  1.2 5.1 %collective-permute-start = (bf16[8,3584]{1,0:T(8,128)(2,1)S(1)}, bf16[8,3584]{1,0:T(8,128)(2,1)S(1)}, u32[]{:S(2)}, u32[]{:S(2)}) collective-permute-start(bf16[8,3584]{1,0:T(8,128)(2,1)S(1)} %get-tuple-element.28), channel_id=1, source_target_pairs={{0,24},{2,26},{4,28},{6,30},{8,16},{10,18},{12,20},{14,22},{16,8},... | collective-permute-start | bytes 172040 | tf_op jit(solution)/shard_map/ppermute | solution.py:194
  6.3 0.6 %collective-permute-start.10 = (bf16[8,3584]{1,0:T(8,128)(2,1)S(1)}, bf16[8,3584]{1,0:T(8,128)(2,1)S(1)}, u32[]{:S(2)}, u32[]{:S(2)}) collective-permute-start(bf16[8,3584]{1,0:T(8,128)(2,1)S(1)} %get-tuple-element.36), channel_id=1, source_target_pairs={{0,8},{2,10},{4,12},{6,14},{8,0},{10,2},{12,4},{14,6},{16,24},{18,... | collective-permute-start | bytes 172040 | tf_op jit(solution)/shard_map/ppermute | solution.py:194
  6.9 0.2 shard_map.74
  7.1 2.1 %shard_map.75.refs_2_.refs_4_ = bf16[2,3584,256]{2,1,0:T(8,128)(2,1)S(1)} custom-call(bf16[2,3584,256]{2,1,0:T(8,128)(2,1)} %refs_0_.3, bf16[48,8]{1,0:T(8,128)(2,1)S(1)} %get-tuple-element.27.refs_1_.terms), custom_call_target="tpu_custom_call" | custom-call | bytes 3670016 | tf_op jit(solution)/shard_map/pallas_call | solution.py:168
  9.2 2.1 %collective-permute-done.1.refs_1_ = bf16[8,3584]{1,0:T(8,128)(2,1)S(1)} collective-permute-done((bf16[8,3584]{1,0:T(8,128)(2,1)S(1)}, bf16[8,3584]{1,0:T(8,128)(2,1)S(1)}, u32[]{:S(2)}, u32[]{:S(2)}) %collective-permute-start.1) | collective-permute-done | bytes 57376 | tf_op jit(solution)/shard_map/ppermute | solution.py:194
  11.4 1.6 %collective-permute-start.2 = (bf16[16,3584]{1,0:T(8,128)(2,1)S(1)}, bf16[16,3584]{1,0:T(8,128)(2,1)S(1)}, u32[]{:S(2)}, u32[]{:S(2)}) collective-permute-start(bf16[16,3584]{1,0:T(8,128)(2,1)S(1)} %shard_map.76.refs_0_), channel_id=1, source_target_pairs={{0,2},{2,0},{4,6},{6,4},{8,10},{10,8},{12,14},{14,12},{16,18},{18,... | collective-permute-start | bytes 344072 | tf_op jit(solution)/shard_map/ppermute | solution.py:194
  13.0 1.6 %collective-permute-start.11 = (bf16[16,3584]{1,0:T(8,128)(2,1)S(1)}, bf16[16,3584]{1,0:T(8,128)(2,1)S(1)}, u32[]{:S(2)}, u32[]{:S(2)}) collective-permute-start(bf16[16,3584]{1,0:T(8,128)(2,1)S(1)} %shard_map.81.refs_0_), channel_id=1, source_target_pairs={{0,4},{2,6},{4,0},{6,2},{8,12},{10,14},{12,8},{14,10},{16,20},{18,... | collective-permute-start | bytes 344072 | tf_op jit(solution)/shard_map/ppermute | solution.py:194
  14.6 0.5 %collective-permute-start.3 = (bf16[16,3584]{1,0:T(8,128)(2,1)S(1)}, bf16[16,3584]{1,0:T(8,128)(2,1)S(1)}, u32[]{:S(2)}, u32[]{:S(2)}) collective-permute-start(bf16[16,3584]{1,0:T(8,128)(2,1)S(1)} %shard_map.76.refs_0_), channel_id=1, source_target_pairs={{0,4},{2,6},{4,0},{6,2},{8,12},{10,14},{12,8},{14,10},{16,20},{18,... | collective-permute-start | bytes 344072 | tf_op jit(solution)/shard_map/ppermute | solution.py:194
  15.1 1.2 %collective-permute-done.2.refs_1_ = bf16[16,3584]{1,0:T(8,128)(2,1)S(1)} collective-permute-done((bf16[16,3584]{1,0:T(8,128)(2,1)S(1)}, bf16[16,3584]{1,0:T(8,128)(2,1)S(1)}, u32[]{:S(2)}, u32[]{:S(2)}) %collective-permute-start.2) | collective-permute-done | bytes 114720 | tf_op jit(solution)/shard_map/ppermute | solution.py:194
  16.2 1.5 %collective-permute-start.4 = (bf16[16,3584]{1,0:T(8,128)(2,1)S(1)}, bf16[16,3584]{1,0:T(8,128)(2,1)S(1)}, u32[]{:S(2)}, u32[]{:S(2)}) collective-permute-start(bf16[16,3584]{1,0:T(8,128)(2,1)S(1)} %collective-permute-done.2.refs_1_), channel_id=1, source_target_pairs={{0,4},{2,6},{4,0},{6,2},{8,12},{10,14},{12,8},{14,10},{16,20},{18,... | collective-permute-start | bytes 344072 | tf_op jit(solution)/shard_map/ppermute | solution.py:194
  17.8 1.5 %collective-permute-start.12 = (bf16[16,3584]{1,0:T(8,128)(2,1)S(1)}, bf16[16,3584]{1,0:T(8,128)(2,1)S(1)}, u32[]{:S(2)}, u32[]{:S(2)}) collective-permute-start(bf16[16,3584]{1,0:T(8,128)(2,1)S(1)} %shard_map.81.refs_0_), channel_id=1, source_target_pairs={{0,2},{2,0},{4,6},{6,4},{8,10},{10,8},{12,14},{14,12},{16,18},{18,... | collective-permute-start | bytes 344072 | tf_op jit(solution)/shard_map/ppermute | solution.py:194
  19.3 0.5 %collective-permute-start.13 = (bf16[16,3584]{1,0:T(8,128)(2,1)S(1)}, bf16[16,3584]{1,0:T(8,128)(2,1)S(1)}, u32[]{:S(2)}, u32[]{:S(2)}) collective-permute-start(bf16[16,3584]{1,0:T(8,128)(2,1)S(1)} %collective-permute-done.11.refs_1_), channel_id=1, source_target_pairs={{0,2},{2,0},{4,6},{6,4},{8,10},{10,8},{12,14},{14,12},{16,18},{18,... | collective-permute-start | bytes 344072 | tf_op jit(solution)/shard_map/ppermute | solution.py:194
  19.8 0.9 %collective-permute-done.3.refs_2_ = bf16[16,3584]{1,0:T(8,128)(2,1)S(1)} collective-permute-done((bf16[16,3584]{1,0:T(8,128)(2,1)S(1)}, bf16[16,3584]{1,0:T(8,128)(2,1)S(1)}, u32[]{:S(2)}, u32[]{:S(2)}) %collective-permute-start.3) | collective-permute-done | bytes 114720 | tf_op jit(solution)/shard_map/ppermute | solution.py:194
  20.7 1.2 %collective-permute-done.4.refs_3_ = bf16[16,3584]{1,0:T(8,128)(2,1)S(1)} collective-permute-done((bf16[16,3584]{1,0:T(8,128)(2,1)S(1)}, bf16[16,3584]{1,0:T(8,128)(2,1)S(1)}, u32[]{:S(2)}, u32[]{:S(2)}) %collective-permute-start.4) | collective-permute-done | bytes 114720 | tf_op jit(solution)/shard_map/ppermute | solution.py:194
  22.0 2.0 %shard_map.77 = (bf16[16,3584]{1,0:T(8,128)(2,1)S(1)}, bf16[16,3584]{1,0:T(8,128)(2,1)S(1)}, bf16[16,3584]{1,0:T(8,128)(2,1)S(1)}, bf16[16,3584]{1,0:T(8,128)(2,1)S(1)}, bf16[256,3584]{1,0:T(8,128)(2,1)S(1)}) custom-call(bf16[16,3584]{1,0:T(8,128)(2,1)S(1)} %shard_map.76.refs_0_, bf16[16,3584]{1,0:T(8,128)(2,1)S(1)} %collective-permute-done.2.refs_1_, ...), custom_call_target="tpu_custom_call" | custom-call | tf_op jit(solution)/shard_map/pallas_call | solution.py:168
  23.9 1.6 %collective-permute-start.6 = (bf16[16,3584]{1,0:T(8,128)(2,1)S(1)}, bf16[16,3584]{1,0:T(8,128)(2,1)S(1)}, u32[]{:S(2)}, u32[]{:S(2)}) collective-permute-start(bf16[16,3584]{1,0:T(8,128)(2,1)S(1)} %get-tuple-element.33), channel_id=1, source_target_pairs={{0,4},{2,6},{4,0},{6,2},{8,12},{10,14},{12,8},{14,10},{16,20},{18,... | collective-permute-start | bytes 344072 | tf_op jit(solution)/shard_map/ppermute | solution.py:194
  25.5 1.2 %shard_map.82 = (bf16[16,3584]{1,0:T(8,128)(2,1)S(1)}, bf16[16,3584]{1,0:T(8,128)(2,1)S(1)}, bf16[16,3584]{1,0:T(8,128)(2,1)S(1)}, bf16[16,3584]{1,0:T(8,128)(2,1)S(1)}) custom-call(bf16[16,3584]{1,0:T(8,128)(2,1)S(1)} %shard_map.81.refs_0_, bf16[16,3584]{1,0:T(8,128)(2,1)S(1)} %collective-permute-done.11.refs_1_, ...), custom_call_target="tpu_custom_call" | custom-call | tf_op jit(solution)/shard_map/pallas_call | solution.py:168
  26.7 0.7 %collective-permute-start.15 = (bf16[16,3584]{1,0:T(8,128)(2,1)S(1)}, bf16[16,3584]{1,0:T(8,128)(2,1)S(1)}, u32[]{:S(2)}, u32[]{:S(2)}) collective-permute-start(bf16[16,3584]{1,0:T(8,128)(2,1)S(1)} %get-tuple-element.42), channel_id=1, source_target_pairs={{0,2},{2,0},{4,6},{6,4},{8,10},{10,8},{12,14},{14,12},{16,18},{18,... | collective-permute-start | bytes 344072 | tf_op jit(solution)/shard_map/ppermute | solution.py:194
  27.4 0.5 %collective-permute-start.5 = (bf16[16,3584]{1,0:T(8,128)(2,1)S(1)}, bf16[16,3584]{1,0:T(8,128)(2,1)S(1)}, u32[]{:S(2)}, u32[]{:S(2)}) collective-permute-start(bf16[16,3584]{1,0:T(8,128)(2,1)S(1)} %get-tuple-element.31), channel_id=1, source_target_pairs={{0,4},{2,6},{4,0},{6,2},{8,12},{10,14},{12,8},{14,10},{16,20},{18,... | collective-permute-start | bytes 344072 | tf_op jit(solution)/shard_map/ppermute | solution.py:194
  27.9 1.9 %collective-permute-done.6.refs_1_ = bf16[16,3584]{1,0:T(8,128)(2,1)S(1)} collective-permute-done((bf16[16,3584]{1,0:T(8,128)(2,1)S(1)}, bf16[16,3584]{1,0:T(8,128)(2,1)S(1)}, u32[]{:S(2)}, u32[]{:S(2)}) %collective-permute-start.6) | collective-permute-done | bytes 114720 | tf_op jit(solution)/shard_map/ppermute | solution.py:194
  29.8 0.4 collective-permute-start.7
  30.1 1.7 %collective-permute-start.14 = (bf16[16,3584]{1,0:T(8,128)(2,1)S(1)}, bf16[16,3584]{1,0:T(8,128)(2,1)S(1)}, u32[]{:S(2)}, u32[]{:S(2)}) collective-permute-start(bf16[16,3584]{1,0:T(8,128)(2,1)S(1)} %get-tuple-element.40), channel_id=1, source_target_pairs={{0,2},{2,0},{4,6},{6,4},{8,10},{10,8},{12,14},{14,12},{16,18},{18,... | collective-permute-start | bytes 344072 | tf_op jit(solution)/shard_map/ppermute | solution.py:194
  31.9 0.3 collective-permute-done.15.refs_1_
  32.2 1.2 %collective-permute-start.16 = (bf16[16,3584]{1,0:T(8,128)(2,1)S(1)}, bf16[16,3584]{1,0:T(8,128)(2,1)S(1)}, u32[]{:S(2)}, u32[]{:S(2)}) collective-permute-start(bf16[16,3584]{1,0:T(8,128)(2,1)S(1)} %shard_map.83), channel_id=1, source_target_pairs={{0,4},{2,6},{4,0},{6,2},{8,12},{10,14},{12,8},{14,10},{16,20},{18,... | collective-permute-start | bytes 344072 | tf_op jit(solution)/shard_map/ppermute | solution.py:194
  33.4 1.3 %collective-permute-done.7.refs_2_ = bf16[16,3584]{1,0:T(8,128)(2,1)S(1)} collective-permute-done((bf16[16,3584]{1,0:T(8,128)(2,1)S(1)}, bf16[16,3584]{1,0:T(8,128)(2,1)S(1)}, u32[]{:S(2)}, u32[]{:S(2)}) %collective-permute-start.7) | collective-permute-done | bytes 114720 | tf_op jit(solution)/shard_map/ppermute | solution.py:194
  34.7 2.2 %collective-permute-start.8 = (bf16[8,3584]{1,0:T(8,128)(2,1)S(1)}, bf16[8,3584]{1,0:T(8,128)(2,1)S(1)}, u32[]{:S(2)}, u32[]{:S(2)}) collective-permute-start(bf16[8,3584]{1,0:T(8,128)(2,1)S(1)} %get-tuple-element.34), channel_id=1, source_target_pairs={{0,24},{2,26},{4,28},{6,30},{8,16},{10,18},{12,20},{14,22},{16,8},... | collective-permute-start | bytes 172040 | tf_op jit(solution)/shard_map/ppermute | solution.py:194
  37.1 2.2 %collective-permute-start.17 = (bf16[8,3584]{1,0:T(8,128)(2,1)S(1)}, bf16[8,3584]{1,0:T(8,128)(2,1)S(1)}, u32[]{:S(2)}, u32[]{:S(2)}) collective-permute-start(bf16[8,3584]{1,0:T(8,128)(2,1)S(1)} %get-tuple-element.43), channel_id=1, source_target_pairs={{0,8},{2,10},{4,12},{6,14},{8,0},{10,2},{12,4},{14,6},{16,24},{18,... | collective-permute-start | bytes 172040 | tf_op jit(solution)/shard_map/ppermute | solution.py:194
  39.2 1.5 %collective-permute-done.8.refs_0_ = bf16[8,3584]{1,0:T(8,128)(2,1)S(1)} collective-permute-done((bf16[8,3584]{1,0:T(8,128)(2,1)S(1)}, bf16[8,3584]{1,0:T(8,128)(2,1)S(1)}, u32[]{:S(2)}, u32[]{:S(2)}) %collective-permute-start.8) | collective-permute-done | bytes 57376 | tf_op jit(solution)/shard_map/ppermute | solution.py:194
  40.7 0.2 shard_map.80.first
  40.9 1.1 %collective-permute-done.9.refs_0_ = bf16[8,3584]{1,0:T(8,128)(2,1)S(1)} collective-permute-done((bf16[8,3584]{1,0:T(8,128)(2,1)S(1)}, bf16[8,3584]{1,0:T(8,128)(2,1)S(1)}, u32[]{:S(2)}, u32[]{:S(2)}) %collective-permute-start.9) | collective-permute-done | bytes 57376 | tf_op jit(solution)/shard_map/ppermute | solution.py:194
  42.0 0.9 %shard_map.85 = bf16[16,3584]{1,0:T(8,128)(2,1)} custom-call(bf16[48,24]{1,0:T(8,128)(2,1)S(1)} %get-tuple-element.26.terms, f32[16,3584]{1,0:T(8,128)S(1)} %shard_map.80.first, bf16[8,3584]{1,0:T(8,128)(2,1)S(1)} %collective-permute-done.9.refs_0_, bf16[8,3584]{1,0:T(8,128)(2,1)S(1)} %collective-permute-done.17.refs_1_, ...), custom_call_target="tpu_custom_call" | custom-call | tf_op jit(solution)/shard_map/pallas_call | solution.py:168
  (17 shorter events, 0.3 us)
Async XLA Ops:
  1.2 8.0 %collective-permute-start = (bf16[8,3584]{1,0:T(8,128)(2,1)S(1)}, bf16[8,3584]{1,0:T(8,128)(2,1)S(1)}, u32[]{:S(2)}, u32[]{:S(2)}) collective-permute-start(bf16[8,3584]{1,0:T(8,128)(2,1)S(1)} %get-tuple-element.28), channel_id=1, source_target_pairs={{0,24},{2,26},{4,28},{6,30},{8,16},{10,18},{12,20},{14,22},{16,8},... | collective-permute-start | bytes 172040 | tf_op jit(solution)/shard_map/ppermute | solution.py:194
  6.3 5.1 %collective-permute-start.1 = (bf16[8,3584]{1,0:T(8,128)(2,1)S(1)}, bf16[8,3584]{1,0:T(8,128)(2,1)S(1)}, u32[]{:S(2)}, u32[]{:S(2)}) collective-permute-start(bf16[8,3584]{1,0:T(8,128)(2,1)S(1)} %get-tuple-element.29), channel_id=1, source_target_pairs={{0,16},{2,18},{4,20},{6,22},{8,24},{10,26},{12,28},{14,30},{16,0},... | collective-permute-start | bytes 172040 | tf_op jit(solution)/shard_map/ppermute | solution.py:194
  6.3 6.7 %collective-permute-start.10 = (bf16[8,3584]{1,0:T(8,128)(2,1)S(1)}, bf16[8,3584]{1,0:T(8,128)(2,1)S(1)}, u32[]{:S(2)}, u32[]{:S(2)}) collective-permute-start(bf16[8,3584]{1,0:T(8,128)(2,1)S(1)} %get-tuple-element.36), channel_id=1, source_target_pairs={{0,8},{2,10},{4,12},{6,14},{8,0},{10,2},{12,4},{14,6},{16,24},{18,... | collective-permute-start | bytes 172040 | tf_op jit(solution)/shard_map/ppermute | solution.py:194
  11.4 4.9 %collective-permute-start.2 = (bf16[16,3584]{1,0:T(8,128)(2,1)S(1)}, bf16[16,3584]{1,0:T(8,128)(2,1)S(1)}, u32[]{:S(2)}, u32[]{:S(2)}) collective-permute-start(bf16[16,3584]{1,0:T(8,128)(2,1)S(1)} %shard_map.76.refs_0_), channel_id=1, source_target_pairs={{0,2},{2,0},{4,6},{6,4},{8,10},{10,8},{12,14},{14,12},{16,18},{18,... | collective-permute-start | bytes 344072 | tf_op jit(solution)/shard_map/ppermute | solution.py:194
  13.0 6.3 %collective-permute-start.11 = (bf16[16,3584]{1,0:T(8,128)(2,1)S(1)}, bf16[16,3584]{1,0:T(8,128)(2,1)S(1)}, u32[]{:S(2)}, u32[]{:S(2)}) collective-permute-start(bf16[16,3584]{1,0:T(8,128)(2,1)S(1)} %shard_map.81.refs_0_), channel_id=1, source_target_pairs={{0,4},{2,6},{4,0},{6,2},{8,12},{10,14},{12,8},{14,10},{16,20},{18,... | collective-permute-start | bytes 344072 | tf_op jit(solution)/shard_map/ppermute | solution.py:194
  14.6 6.1 %collective-permute-start.3 = (bf16[16,3584]{1,0:T(8,128)(2,1)S(1)}, bf16[16,3584]{1,0:T(8,128)(2,1)S(1)}, u32[]{:S(2)}, u32[]{:S(2)}) collective-permute-start(bf16[16,3584]{1,0:T(8,128)(2,1)S(1)} %shard_map.76.refs_0_), channel_id=1, source_target_pairs={{0,4},{2,6},{4,0},{6,2},{8,12},{10,14},{12,8},{14,10},{16,20},{18,... | collective-permute-start | bytes 344072 | tf_op jit(solution)/shard_map/ppermute | solution.py:194
  16.2 5.7 %collective-permute-start.4 = (bf16[16,3584]{1,0:T(8,128)(2,1)S(1)}, bf16[16,3584]{1,0:T(8,128)(2,1)S(1)}, u32[]{:S(2)}, u32[]{:S(2)}) collective-permute-start(bf16[16,3584]{1,0:T(8,128)(2,1)S(1)} %collective-permute-done.2.refs_1_), channel_id=1, source_target_pairs={{0,4},{2,6},{4,0},{6,2},{8,12},{10,14},{12,8},{14,10},{16,20},{18,... | collective-permute-start | bytes 344072 | tf_op jit(solution)/shard_map/ppermute | solution.py:194
  17.8 7.7 %collective-permute-start.12 = (bf16[16,3584]{1,0:T(8,128)(2,1)S(1)}, bf16[16,3584]{1,0:T(8,128)(2,1)S(1)}, u32[]{:S(2)}, u32[]{:S(2)}) collective-permute-start(bf16[16,3584]{1,0:T(8,128)(2,1)S(1)} %shard_map.81.refs_0_), channel_id=1, source_target_pairs={{0,2},{2,0},{4,6},{6,4},{8,10},{10,8},{12,14},{14,12},{16,18},{18,... | collective-permute-start | bytes 344072 | tf_op jit(solution)/shard_map/ppermute | solution.py:194
  19.3 6.2 %collective-permute-start.13 = (bf16[16,3584]{1,0:T(8,128)(2,1)S(1)}, bf16[16,3584]{1,0:T(8,128)(2,1)S(1)}, u32[]{:S(2)}, u32[]{:S(2)}) collective-permute-start(bf16[16,3584]{1,0:T(8,128)(2,1)S(1)} %collective-permute-done.11.refs_1_), channel_id=1, source_target_pairs={{0,2},{2,0},{4,6},{6,4},{8,10},{10,8},{12,14},{14,12},{16,18},{18,... | collective-permute-start | bytes 344072 | tf_op jit(solution)/shard_map/ppermute | solution.py:194
  23.9 5.8 %collective-permute-start.6 = (bf16[16,3584]{1,0:T(8,128)(2,1)S(1)}, bf16[16,3584]{1,0:T(8,128)(2,1)S(1)}, u32[]{:S(2)}, u32[]{:S(2)}) collective-permute-start(bf16[16,3584]{1,0:T(8,128)(2,1)S(1)} %get-tuple-element.33), channel_id=1, source_target_pairs={{0,4},{2,6},{4,0},{6,2},{8,12},{10,14},{12,8},{14,10},{16,20},{18,... | collective-permute-start | bytes 344072 | tf_op jit(solution)/shard_map/ppermute | solution.py:194
  26.7 5.4 %collective-permute-start.15 = (bf16[16,3584]{1,0:T(8,128)(2,1)S(1)}, bf16[16,3584]{1,0:T(8,128)(2,1)S(1)}, u32[]{:S(2)}, u32[]{:S(2)}) collective-permute-start(bf16[16,3584]{1,0:T(8,128)(2,1)S(1)} %get-tuple-element.42), channel_id=1, source_target_pairs={{0,2},{2,0},{4,6},{6,4},{8,10},{10,8},{12,14},{14,12},{16,18},{18,... | collective-permute-start | bytes 344072 | tf_op jit(solution)/shard_map/ppermute | solution.py:194
  27.4 6.0 %collective-permute-start.5 = (bf16[16,3584]{1,0:T(8,128)(2,1)S(1)}, bf16[16,3584]{1,0:T(8,128)(2,1)S(1)}, u32[]{:S(2)}, u32[]{:S(2)}) collective-permute-start(bf16[16,3584]{1,0:T(8,128)(2,1)S(1)} %get-tuple-element.31), channel_id=1, source_target_pairs={{0,4},{2,6},{4,0},{6,2},{8,12},{10,14},{12,8},{14,10},{16,20},{18,... | collective-permute-start | bytes 344072 | tf_op jit(solution)/shard_map/ppermute | solution.py:194
  29.8 4.9 %collective-permute-start.7 = (bf16[16,3584]{1,0:T(8,128)(2,1)S(1)}, bf16[16,3584]{1,0:T(8,128)(2,1)S(1)}, u32[]{:S(2)}, u32[]{:S(2)}) collective-permute-start(bf16[16,3584]{1,0:T(8,128)(2,1)S(1)} %shard_map.78), channel_id=1, source_target_pairs={{0,2},{2,0},{4,6},{6,4},{8,10},{10,8},{12,14},{14,12},{16,18},{18,... | collective-permute-start | bytes 344072 | tf_op jit(solution)/shard_map/ppermute | solution.py:194
  30.1 6.7 %collective-permute-start.14 = (bf16[16,3584]{1,0:T(8,128)(2,1)S(1)}, bf16[16,3584]{1,0:T(8,128)(2,1)S(1)}, u32[]{:S(2)}, u32[]{:S(2)}) collective-permute-start(bf16[16,3584]{1,0:T(8,128)(2,1)S(1)} %get-tuple-element.40), channel_id=1, source_target_pairs={{0,2},{2,0},{4,6},{6,4},{8,10},{10,8},{12,14},{14,12},{16,18},{18,... | collective-permute-start | bytes 344072 | tf_op jit(solution)/shard_map/ppermute | solution.py:194
  32.2 4.9 %collective-permute-start.16 = (bf16[16,3584]{1,0:T(8,128)(2,1)S(1)}, bf16[16,3584]{1,0:T(8,128)(2,1)S(1)}, u32[]{:S(2)}, u32[]{:S(2)}) collective-permute-start(bf16[16,3584]{1,0:T(8,128)(2,1)S(1)} %shard_map.83), channel_id=1, source_target_pairs={{0,4},{2,6},{4,0},{6,2},{8,12},{10,14},{12,8},{14,10},{16,20},{18,... | collective-permute-start | bytes 344072 | tf_op jit(solution)/shard_map/ppermute | solution.py:194
  34.7 6.0 %collective-permute-start.8 = (bf16[8,3584]{1,0:T(8,128)(2,1)S(1)}, bf16[8,3584]{1,0:T(8,128)(2,1)S(1)}, u32[]{:S(2)}, u32[]{:S(2)}) collective-permute-start(bf16[8,3584]{1,0:T(8,128)(2,1)S(1)} %get-tuple-element.34), channel_id=1, source_target_pairs={{0,24},{2,26},{4,28},{6,30},{8,16},{10,18},{12,20},{14,22},{16,8},... | collective-permute-start | bytes 172040 | tf_op jit(solution)/shard_map/ppermute | solution.py:194
  36.9 5.1 %collective-permute-start.9 = (bf16[8,3584]{1,0:T(8,128)(2,1)S(1)}, bf16[8,3584]{1,0:T(8,128)(2,1)S(1)}, u32[]{:S(2)}, u32[]{:S(2)}) collective-permute-start(bf16[8,3584]{1,0:T(8,128)(2,1)S(1)} %get-tuple-element.35), channel_id=1, source_target_pairs={{0,16},{2,18},{4,20},{6,22},{8,24},{10,26},{12,28},{14,30},{16,0},... | collective-permute-start | bytes 172040 | tf_op jit(solution)/shard_map/ppermute | solution.py:194
  37.1 5.0 %collective-permute-start.17 = (bf16[8,3584]{1,0:T(8,128)(2,1)S(1)}, bf16[8,3584]{1,0:T(8,128)(2,1)S(1)}, u32[]{:S(2)}, u32[]{:S(2)}) collective-permute-start(bf16[8,3584]{1,0:T(8,128)(2,1)S(1)} %get-tuple-element.43), channel_id=1, source_target_pairs={{0,8},{2,10},{4,12},{6,14},{8,0},{10,2},{12,4},{14,6},{16,24},{18,... | collective-permute-start | bytes 172040 | tf_op jit(solution)/shard_map/ppermute | solution.py:194
